TPU v7x, 256 devices: a whole 4x4x8 slice. The times are simulated.
256 devices in a mesh: row: 16 (over x, z_hi, core), col: 16 (over z_lo, y).
Axes of the slice: x: 4, y: 4, z: 8 (z_hi: 2, z_lo: 4; z = z_hi * 4 + z_lo), core: 2. Of those that a mesh axis runs over, the one named last changes fastest.
Arguments:
- pair_valence: bfloat16 [1792, 2048], P('row'), may hold values from -0.125 to 0.125
- screening: bfloat16 [1792, 1792], P('row', 'col'), may hold values from -0.125 to 0.125
- pair_conduction: bfloat16 [1792, 98304], P(None, ('row', 'col')), may hold values from -6 to 6
Outputs:
- kernel: bfloat16 [2048, 98304], P(None, ('row', 'col'))
All inputs are finite; a program needn't handle non-finite values.
Results may differ from a plain program's by a relative error of at most 0.015.
Values may be sent and summed in bfloat16 or wider, within the bound.
No kernel may reach another device: no remote copies, remote signals or barrier semaphores. Data moves between devices by JAX's collectives and lax.ppermute only.
A program may use at most 64 MiB of HBM per device.

v0:
```python
import jax
import jax.numpy as jnp
from jax import lax
from jax.sharding import PartitionSpec as P


def per_device(pair_valence, screening, pair_conduction):
    row_panel = lax.all_gather(screening, "col", axis=1, tiled=True)
    screened = jnp.dot(
        lax.all_gather(row_panel, "row", axis=0, tiled=True),
        pair_conduction,
        preferred_element_type=jnp.float32,
    ).astype(jnp.bfloat16)
    kernel = lax.dot_general(
        lax.all_gather(pair_valence, "row", axis=0, tiled=True),
        screened,
        (((0,), (0,)), ((), ())),
        preferred_element_type=jnp.float32,
    )
    return kernel.astype(jnp.bfloat16)


def solution(mesh):
    placed = (P("row", None), P("row", "col"), P(None, ("row", "col")))
    return jax.shard_map(
        per_device, mesh=mesh, in_specs=placed, out_specs=P(None, ("row", "col")), check_vma=False
    )
```

profile of v0, /device:TPU:1, one launch (start us, length us, event | category | flops | bytes accessed | tf_op | source)
XLA Modules:
  0.0 265.7 jit_solution(11094987703653444182)
XLA Ops:
  6.5 0.0 copy-start
  6.5 0.0 all-gather.3.cloned.1.call-start
  6.5 1.0 copy.7
  7.5 40.2 %all_gather.9 = bf16[112,1792]{0,1:T(8,128)(2,1)S(1)} all-gather(bf16[112,112]{0,1:T(8,128)(2,1)S(1)} %copy.7), channel_id=1, replica_groups=mesh['row'=16,'col'=16] {'col'}, dimensions={1}, use_global_device_ids=true | all-gather | bytes 426496 | tf_op jit(solution)/shard_map/all_gather | solution.py:8
  47.7 1.0 copy.8
  48.7 0.0 all-gather.3.cloned.1.call-update
  48.7 0.0 all-gather.5.cloned.1.call-start
  48.7 0.7 all-gather.5.cloned.1.call-update
  49.4 98.2 %all-gather.3.cloned.1.call-done = bf16[1792,1792]{1,0:T(8,128)(2,1)} async-done(((bf16[112,1792]{1,0:T(8,128)(2,1)}), bf16[1792,1792]{1,0:T(8,128)(2,1)}) %all-gather.3.cloned.1.call-update) | async-done | bytes 6422544 | tf_op jit(solution)/shard_map/all_gather | solution.py:10
  147.7 98.4 %all-gather.5.cloned.1.call-done = bf16[1792,2048]{1,0:T(8,128)(2,1)} async-done(((bf16[112,2048]{1,0:T(8,128)(2,1)}), bf16[1792,2048]{1,0:T(8,128)(2,1)}) %all-gather.5.cloned.1.call-update) | async-done | bytes 7340048 | tf_op jit(solution)/shard_map/all_gather | solution.py:15
  246.0 0.0 copy-done
  246.0 11.3 %fusion = bf16[2048,384]{0,1:T(8,128)(2,1)S(1)} fusion(bf16[1792,2048]{1,0:T(8,128)(2,1)} %all-gather.5.cloned.1.call-done, bf16[1792,1792]{1,0:T(8,128)(2,1)} %all-gather.3.cloned.1.call-done, bf16[1792,384]{1,0:T(8,128)(2,1)S(1)} %copy-done), kind=kOutput, calls=%fused_computation.2 | convolution fusion | flops 5286297600 | bytes 16711680 | tf_op jit(solution)/shard_map/dot_general | solution.py:14
  257.3 1.6 copy.9
Async XLA Ops:
  6.5 239.5 %copy-start = (bf16[1792,384]{1,0:T(8,128)(2,1)S(1)}, bf16[1792,384]{1,0:T(8,128)(2,1)}, u32[]{:S(2)}) copy-start(bf16[1792,384]{1,0:T(8,128)(2,1)} %param.5) | copy-start | bytes 4128772
  6.5 141.1 %all-gather.3.cloned.1.call-start = ((), (), s32[]{:S(2)}) async-start(), calls=%async_computation | async-start | bytes 6823936 | tf_op jit(solution)/shard_map/all_gather | solution.py:10
  48.7 197.3 %all-gather.5.cloned.1.call-start = ((), (), s32[]{:S(2)}) async-start(), calls=%async_computation.1 | async-start | bytes 7798784 | tf_op jit(solution)/shard_map/all_gather | solution.py:15
Sparse Core Ops, SparseCore 0:
  48.8 98.7 all-gather.2
  150.3 95.6 all-gather.4
where the time goes:
time: 266 us
  waiting for transfers between devices  197 us (74%)
  blocking collectives  40.2 us (15%)
  between operations  13.4 us (5%)
  matrix products  11.3 us (4%)
  local copies, waits for them, and re-layouts  3.49 us (1%)
    all_gather x1, waiting for transfers between devices, per_device(): lax.all_gather(pair_valence, 'row', axis=0, tiled=True)  98.4 us
    all_gather x1, waiting for transfers between devices, per_device(): lax.all_gather(row_panel, 'row', axis=0, tiled=True)  98.2 us
    all_gather x1, blocking collectives, per_device(): row_panel = lax.all_gather(screening, 'col', axis=1, tiled=True)  40.2 us
    dot_general x1, matrix products, per_device(): lax.dot_general(lax.all_gather(pair_valence, 'row', axis=0, tiled=True),...  11.3 us
  transfers between devices with their start and end apart: 2, of which 2 were waited for; matrix products, arithmetic and copies ran while one was open for 0% of the time, Pallas kernels for 0%

commit v1 on v0

v1 whole, which is shorter than its diff:
```python
import jax
import jax.numpy as jnp
from jax import lax
from jax.sharding import Mesh, PartitionSpec as P

ROW = ("x", "z_hi", "core")
COL = ("z_lo", "y")
Z = ("z_hi", "z_lo")
BF16 = jnp.bfloat16
F32 = jnp.float32


def fetch(block, axis, size, ahead):
    return lax.ppermute(block, axis, [((i + ahead) % size, i) for i in range(size)])


def gather(block, axis, size):
    return [block] + [fetch(block, axis, size, ahead) for ahead in range(1, size)]


def in_order(blocks, me):
    size = len(blocks)
    twice = jnp.concatenate([jnp.stack(blocks)] * 2)
    return lax.dynamic_slice_in_dim(twice, size - me, size)


def ring4(block, axis):
    after = fetch(block, axis, 4, 1)
    before = fetch(block, axis, 4, -1)
    half = block.shape[0] // 2
    far = [fetch(after[:half], axis, 4, 1), fetch(before[half:], axis, 4, -1)]
    return [block, after, jnp.concatenate(far), before]


def pick(stack, index):
    return lax.dynamic_index_in_dim(stack, index, 0, keepdims=False)


def per_device(pair_valence, screening, pair_conduction):
    x, y = lax.axis_index("x"), lax.axis_index("y")
    z_hi, z_lo, core = lax.axis_index("z_hi"), lax.axis_index("z_lo"), lax.axis_index("core")
    pairs_other = fetch(pair_conduction, "core", 2, 1)

    some = in_order(gather(screening.T, "y", 4), y)
    columns = in_order(gather(some, "z_lo", 4), z_lo).reshape(1792, 112)

    panel = lax.dynamic_slice_in_dim(pair_valence, (y * 4 + z_lo) * 128, 128, 1)
    part = lax.dot_general(panel, columns, (((0,), (1,)), ((), ())), preferred_element_type=F32)

    part = part.reshape(2, 64, 1792)
    part = pick(part, core) + fetch(pick(part, 1 - core), "core", 2, 1)
    part = part.reshape(4, 16, 1792)
    part = pick(part, x) + sum(
        fetch(pick(part, (x + 4 - ahead) % 4), "x", 4, ahead) for ahead in (1, 2, 3)
    )
    part = part.reshape(2, 8, 1792)
    part = pick(part, z_hi) + fetch(pick(part, 1 - z_hi), "z_hi", 2, 1)
    rows = part.astype(BF16)

    line = in_order(gather(rows, Z, 8), z_hi * 4 + z_lo)
    first = jnp.stack(gather(line[:4].reshape(32, 1792), "x", 4), 0).reshape(128, 1792)
    second = jnp.stack(gather(line[4:].reshape(32, 1792), "y", 4), 0).reshape(128, 1792)
    first = jnp.stack(ring4(first, "y"))
    second = jnp.stack(ring4(second, "x"))

    both = jnp.concatenate([pair_conduction, pairs_other], 1)

    def times(a):
        return lax.dot_general(
            a.reshape(512, 1792), both, (((1,), (0,)), ((), ())), preferred_element_type=F32
        ).astype(BF16)

    first = times(first).reshape(4, 4, 4, 8, 768)
    second = times(second).reshape(4, 4, 4, 8, 768).swapaxes(0, 1)
    own = jnp.stack([first, second], 3)
    mine, theirs = own[..., :384], fetch(own[..., 384:], "core", 2, 1)
    halves = jnp.where(core == 0, jnp.stack([mine, theirs]), jnp.stack([theirs, mine]))
    halves = lax.dynamic_slice_in_dim(jnp.concatenate([halves] * 2, 1), 4 - y, 4, 1)
    halves = lax.dynamic_slice_in_dim(jnp.concatenate([halves] * 2, 2), 4 - x, 4, 2)
    return halves.transpose(1, 3, 0, 2, 4, 5, 6).reshape(2048, 384)


def solution(mesh):
    fine = Mesh(mesh.devices.reshape(4, 2, 2, 4, 4), ROW + COL)
    placed = (P(ROW, None), P(ROW, COL), P(None, ROW + COL))
    return jax.shard_map(
        per_device, mesh=fine, in_specs=placed, out_specs=P(None, ROW + COL), check_vma=False
    )
```

time: 266 us -> 119 us (0.45)
  waiting for transfers between devices: 197 us -> 42.3 us
  starting transfers between devices: 0.04 us -> 53.5 us
  blocking collectives: 40.2 us -> 0 us
  between operations: 13.4 us -> 0.35 us
  local copies, waits for them, and re-layouts: 3.49 us -> 14.8 us
  matrix products: 11.3 us -> 3.44 us
  other arithmetic: 0 us -> 4.21 us
    all_gather x2 -> x0, waiting for transfers between devices: 197 us -> none  [the longest x1 98.4 us: per_device(): lax.all_gather(pair_valence, 'row', axis=0, tiled=True)]
    ppermute x0 -> x34, starting transfers between devices: none -> 53.5 us  [fetch(): lax.ppermute(block, axis, [((i + ahead) % size, i) for i in range(size)])]
    ppermute x0 -> x34, waiting for transfers between devices: none -> 42.3 us  [fetch(): lax.ppermute(block, axis, [((i + ahead) % size, i) for i in range(size)])]
    all_gather x1 -> x0, blocking collectives: 40.2 us -> none  [per_device(): row_panel = lax.all_gather(screening, 'col', axis=1, tiled=True)]
    unnamed x3 -> x33, local copies, waits for them, and re-layouts: 0.96 us -> 10.4 us
    dot_general x1 -> x3, matrix products: 11.3 us -> 3.44 us  [the longest x2 3.17 us: times(): lax.dot_general(a.reshape(512, 1792), both, (((1,), (0,)), ((), ())), pre...]
  transfers between devices with their start and end apart: 2 -> 34, of which waited for: 2 -> 21; matrix products, arithmetic and copies ran while one was open for 0% -> 11% of each run, Pallas kernels for 0% -> 0%
where the time goes in v1:
time: 119 us
  starting transfers between devices  53.5 us (45%)
  waiting for transfers between devices  42.3 us (36%)
  local copies, waits for them, and re-layouts  14.8 us (12%)
  other arithmetic  4.21 us (4%)
  matrix products  3.44 us (3%)
    ppermute x34, starting transfers between devices, fetch(): lax.ppermute(block, axis, [((i + ahead) % size, i) for i in range(size)])  53.5 us
    ppermute x34, waiting for transfers between devices, fetch(): lax.ppermute(block, axis, [((i + ahead) % size, i) for i in range(size)])  42.3 us
    unnamed x33, local copies, waits for them, and re-layouts  10.4 us
    dot_general x2, matrix products, times(): lax.dot_general(a.reshape(512, 1792), both, (((1,), (0,)), ((), ())), pre...  3.17 us
  transfers between devices with their start and end apart: 34, of which 21 were waited for; matrix products, arithmetic and copies ran while one was open for 11% of the time, Pallas kernels for 0%

profile of v1, /device:TPU:1, one launch (start us, length us, event | category | flops | bytes accessed | tf_op | source)
XLA Modules:
  0.0 118.5 jit_solution(126083109734548221)
XLA Ops:
  0.0 3.6 %collective-permute-start = (bf16[112,112]{0,1:T(8,128)(2,1)}, bf16[112,112]{0,1:T(8,128)(2,1)S(1)}, u32[]{:S(2)}, u32[]{:S(2)}) collective-permute-start(bf16[112,112]{0,1:T(8,128)(2,1)} %bitcast.151), channel_id=1, source_target_pairs={{1,0},{2,1},{3,2},{0,3},{5,4},{6,5},{7,6},{4,7},{9,8},{10,9},{11,1... | collective-permute-start | bytes 75272 | tf_op jit(solution)/shard_map/ppermute | solution.py:14
  5.4 2.6 %collective-permute-done.1 = bf16[112,112]{0,1:T(8,128)(2,1)S(1)} collective-permute-done((bf16[112,112]{0,1:T(8,128)(2,1)}, bf16[112,112]{0,1:T(8,128)(2,1)S(1)}, u32[]{:S(2)}, u32[]{:S(2)}) %collective-permute-start.1) | collective-permute-done | bytes 25120 | tf_op jit(solution)/shard_map/ppermute | solution.py:14
  9.2 4.4 %collective-permute-start.3 = (bf16[4,112,112]{1,2,0:T(8,128)(2,1)S(1)}, bf16[4,112,112]{1,2,0:T(8,128)(2,1)S(1)}, u32[]{:S(2)}, u32[]{:S(2)}) collective-permute-start(bf16[4,112,112]{1,2,0:T(8,128)(2,1)S(1)} %get-tuple-element.8), channel_id=1, source_target_pairs={{4,0},{8,4},{12,8},{0,12},{5,1},{9,5},{13,9},{1,13},{6,2},{10,6},{... | collective-permute-start | bytes 301064 | tf_op jit(solution)/shard_map/ppermute | solution.py:14
  15.4 8.2 %collective-permute-done.4 = bf16[4,112,112]{1,2,0:T(8,128)(2,1)S(1)} collective-permute-done((bf16[4,112,112]{1,2,0:T(8,128)(2,1)S(1)}, bf16[4,112,112]{1,2,0:T(8,128)(2,1)S(1)}, u32[]{:S(2)}, u32[]{:S(2)}) %collective-permute-start.4) | collective-permute-done | bytes 100384 | tf_op jit(solution)/shard_map/ppermute | solution.py:14
  24.8 1.4 %collective-permute-start.6 = (f32[64,1792]{1,0:T(8,128)S(1)}, f32[64,1792]{1,0:T(8,128)}, u32[]{:S(2)}, u32[]{:S(2)}) collective-permute-start(f32[64,1792]{1,0:T(8,128)S(1)} %dynamic-slice_bitcast_fusion), channel_id=1, source_target_pairs={{16,0},{0,16},{17,1},{1,17},{18,2},{2,18},{19,3},{3,19},{20,4},{4,... | collective-permute-start | bytes 1376264 | tf_op jit(solution)/shard_map/ppermute | solution.py:14
  26.2 1.6 %collective-permute-done.6 = f32[64,1792]{1,0:T(8,128)} collective-permute-done((f32[64,1792]{1,0:T(8,128)S(1)}, f32[64,1792]{1,0:T(8,128)}, u32[]{:S(2)}, u32[]{:S(2)}) %collective-permute-start.6) | collective-permute-done | bytes 458784 | tf_op jit(solution)/shard_map/ppermute | solution.py:14
  28.9 2.6 %collective-permute-start.7 = (f32[16,1792]{1,0:T(8,128)S(1)}, f32[16,1792]{1,0:T(8,128)S(1)}, u32[]{:S(2)}, u32[]{:S(2)}) collective-permute-start(f32[16,1792]{1,0:T(8,128)S(1)} %get-tuple-element.17), channel_id=1, source_target_pairs={{64,0},{128,64},{192,128},{0,192},{65,1},{129,65},{193,129},{1,193... | collective-permute-start | bytes 344072 | tf_op jit(solution)/shard_map/ppermute | solution.py:14
  32.6 3.3 %collective-permute-done.7 = f32[16,1792]{1,0:T(8,128)S(1)} collective-permute-done((f32[16,1792]{1,0:T(8,128)S(1)}, f32[16,1792]{1,0:T(8,128)S(1)}, u32[]{:S(2)}, u32[]{:S(2)}) %collective-permute-start.7) | collective-permute-done | bytes 114720 | tf_op jit(solution)/shard_map/ppermute | solution.py:14
  37.0 3.4 %collective-permute-done.9 = f32[16,1792]{1,0:T(8,128)S(1)} collective-permute-done((f32[16,1792]{1,0:T(8,128)S(1)}, f32[16,1792]{1,0:T(8,128)S(1)}, u32[]{:S(2)}, u32[]{:S(2)}) %collective-permute-start.9) | collective-permute-done | bytes 114720 | tf_op jit(solution)/shard_map/ppermute | solution.py:14
  40.5 5.3 %collective-permute-start.10 = (f32[8,1792]{1,0:T(8,128)S(1)}, f32[8,1792]{1,0:T(8,128)S(1)}, u32[]{:S(2)}, u32[]{:S(2)}) collective-permute-start(f32[8,1792]{1,0:T(8,128)S(1)} %dynamic-slice_bitcast_fusion.8), channel_id=1, source_target_pairs={{32,0},{0,32},{33,1},{1,33},{34,2},{2,34},{35,3},{3,35},{36,4},{4,... | collective-permute-start | bytes 172040 | tf_op jit(solution)/shard_map/ppermute | solution.py:14
  45.8 1.8 %collective-permute-done.10 = f32[8,1792]{1,0:T(8,128)S(1)} collective-permute-done((f32[8,1792]{1,0:T(8,128)S(1)}, f32[8,1792]{1,0:T(8,128)S(1)}, u32[]{:S(2)}, u32[]{:S(2)}) %collective-permute-start.10) | collective-permute-done | bytes 57376 | tf_op jit(solution)/shard_map/ppermute | solution.py:14
  48.2 3.2 %collective-permute-start.11 = (bf16[8,1792]{1,0:T(8,128)(2,1)S(1)}, bf16[8,1792]{1,0:T(8,128)(2,1)S(1)}, u32[]{:S(2)}, u32[]{:S(2)}) collective-permute-start(bf16[8,1792]{1,0:T(8,128)(2,1)S(1)} %get-tuple-element.6), channel_id=1, source_target_pairs={{4,0},{8,4},{12,8},{32,12},{36,32},{40,36},{44,40},{0,44},{5,1},{9... | collective-permute-start | bytes 86024 | tf_op jit(solution)/shard_map/ppermute | solution.py:14
  51.4 1.6 %collective-permute-start.25 = (bf16[1792,384]{1,0:T(8,128)(2,1)S(1)}, bf16[1792,384]{1,0:T(8,128)(2,1)S(1)}, u32[]{:S(2)}, u32[]{:S(2)}) collective-permute-start(bf16[1792,384]{1,0:T(8,128)(2,1)S(1)} %copy-done.1), channel_id=1, source_target_pairs={{16,0},{0,16},{17,1},{1,17},{18,2},{2,18},{19,3},{3,19},{20,4},{4,... | collective-permute-start | bytes 4128776 | tf_op jit(solution)/shard_map/ppermute | solution.py:14
  52.9 2.3 %collective-permute-start.12 = (bf16[8,1792]{1,0:T(8,128)(2,1)S(1)}, bf16[8,1792]{1,0:T(8,128)(2,1)S(1)}, u32[]{:S(2)}, u32[]{:S(2)}) collective-permute-start(bf16[8,1792]{1,0:T(8,128)(2,1)S(1)} %get-tuple-element.6), channel_id=1, source_target_pairs={{8,0},{12,4},{32,8},{36,12},{40,32},{44,36},{0,40},{4,44},{9,1},{1... | collective-permute-start | bytes 86024 | tf_op jit(solution)/shard_map/ppermute | solution.py:14
  56.5 4.7 %collective-permute-start.14 = (bf16[8,1792]{1,0:T(8,128)(2,1)S(1)}, bf16[8,1792]{1,0:T(8,128)(2,1)S(1)}, u32[]{:S(2)}, u32[]{:S(2)}) collective-permute-start(bf16[8,1792]{1,0:T(8,128)(2,1)S(1)} %get-tuple-element.6), channel_id=1, source_target_pairs={{32,0},{36,4},{40,8},{44,12},{0,32},{4,36},{8,40},{12,44},{33,1},{... | collective-permute-start | bytes 86024 | tf_op jit(solution)/shard_map/ppermute | solution.py:14
  63.8 1.7 %collective-permute-start.17 = (bf16[8,1792]{1,0:T(8,128)(2,1)S(1)}, bf16[8,1792]{1,0:T(8,128)(2,1)S(1)}, u32[]{:S(2)}, u32[]{:S(2)}) collective-permute-start(bf16[8,1792]{1,0:T(8,128)(2,1)S(1)} %get-tuple-element.6), channel_id=1, source_target_pairs={{44,0},{0,4},{4,8},{8,12},{12,32},{32,36},{36,40},{40,44},{45,1},{... | collective-permute-start | bytes 86024 | tf_op jit(solution)/shard_map/ppermute | solution.py:14
  79.0 2.1 %collective-permute-done.27 = bf16[32,1792]{1,0:T(8,128)(2,1)S(1)} collective-permute-done((bf16[32,1792]{1,0:T(8,128)(2,1)S(1)}, bf16[32,1792]{1,0:T(8,128)(2,1)S(1)}, u32[]{:S(2)}, u32[]{:S(2)}) %collective-permute-start.27) | collective-permute-done | bytes 114720 | tf_op jit(solution)/shard_map/ppermute | solution.py:14
  82.3 1.6 %collective-permute-start.29 = (bf16[128,1792]{1,0:T(8,128)(2,1)S(1)}, bf16[128,1792]{1,0:T(8,128)(2,1)S(1)}, u32[]{:S(2)}, u32[]{:S(2)}) collective-permute-start(bf16[128,1792]{1,0:T(8,128)(2,1)S(1)} %bitcast.127), channel_id=1, source_target_pairs={{64,0},{128,64},{192,128},{0,192},{65,1},{129,65},{193,129},{1,193... | collective-permute-start | bytes 1376264 | tf_op jit(solution)/shard_map/ppermute | solution.py:14
  84.0 1.9 %collective-permute-done.20 = bf16[32,1792]{1,0:T(8,128)(2,1)S(1)} collective-permute-done((bf16[32,1792]{1,0:T(8,128)(2,1)S(1)}, bf16[32,1792]{1,0:T(8,128)(2,1)S(1)}, u32[]{:S(2)}, u32[]{:S(2)}) %collective-permute-start.20) | collective-permute-done | bytes 114720 | tf_op jit(solution)/shard_map/ppermute | solution.py:14
  86.0 1.7 %collective-permute-start.21 = (bf16[128,1792]{1,0:T(8,128)(2,1)S(1)}, bf16[128,1792]{1,0:T(8,128)(2,1)S(1)}, u32[]{:S(2)}, u32[]{:S(2)}) collective-permute-start(bf16[128,1792]{1,0:T(8,128)(2,1)S(1)} %bitcast.130), channel_id=1, source_target_pairs={{1,0},{2,1},{3,2},{0,3},{5,4},{6,5},{7,6},{4,7},{9,8},{10,9},{11,1... | collective-permute-start | bytes 1376264 | tf_op jit(solution)/shard_map/ppermute | solution.py:14
  87.6 1.6 %collective-permute-start.23 = (bf16[128,1792]{1,0:T(8,128)(2,1)S(1)}, bf16[128,1792]{1,0:T(8,128)(2,1)S(1)}, u32[]{:S(2)}, u32[]{:S(2)}) collective-permute-start(bf16[128,1792]{1,0:T(8,128)(2,1)S(1)} %bitcast.131), channel_id=1, source_target_pairs={{3,0},{0,1},{1,2},{2,3},{7,4},{4,5},{5,6},{6,7},{11,8},{8,9},{9,10... | collective-permute-start | bytes 1376264 | tf_op jit(solution)/shard_map/ppermute | solution.py:14
  89.4 3.0 %collective-permute-done.29 = bf16[128,1792]{1,0:T(8,128)(2,1)S(1)} collective-permute-done((bf16[128,1792]{1,0:T(8,128)(2,1)S(1)}, bf16[128,1792]{1,0:T(8,128)(2,1)S(1)}, u32[]{:S(2)}, u32[]{:S(2)}) %collective-permute-start.29) | collective-permute-done | bytes 458784 | tf_op jit(solution)/shard_map/ppermute | solution.py:14
  92.3 2.2 %collective-permute-start.30 = (bf16[64,1792]{1,0:T(8,128)(2,1)S(1)}, bf16[64,1792]{1,0:T(8,128)(2,1)S(1)}, u32[]{:S(2)}, u32[]{:S(2)}) collective-permute-start(bf16[64,1792]{1,0:T(8,128)(2,1)S(1)} %slice.34), channel_id=1, source_target_pairs={{64,0},{128,64},{192,128},{0,192},{65,1},{129,65},{193,129},{1,193... | collective-permute-start | bytes 688136 | tf_op jit(solution)/shard_map/ppermute | solution.py:14
  94.5 2.4 %collective-permute-done.31 = bf16[128,1792]{1,0:T(8,128)(2,1)S(1)} collective-permute-done((bf16[128,1792]{1,0:T(8,128)(2,1)S(1)}, bf16[128,1792]{1,0:T(8,128)(2,1)S(1)}, u32[]{:S(2)}, u32[]{:S(2)}) %collective-permute-start.31) | collective-permute-done | bytes 458784 | tf_op jit(solution)/shard_map/ppermute | solution.py:14
  97.1 3.1 %collective-permute-start.22 = (bf16[64,1792]{1,0:T(8,128)(2,1)S(1)}, bf16[64,1792]{1,0:T(8,128)(2,1)S(1)}, u32[]{:S(2)}, u32[]{:S(2)}) collective-permute-start(bf16[64,1792]{1,0:T(8,128)(2,1)S(1)} %slice.32), channel_id=1, source_target_pairs={{1,0},{2,1},{3,2},{0,3},{5,4},{6,5},{7,6},{4,7},{9,8},{10,9},{11,1... | collective-permute-start | bytes 688136 | tf_op jit(solution)/shard_map/ppermute | solution.py:14
  100.6 2.6 %collective-permute-done.32 = bf16[64,1792]{1,0:T(8,128)(2,1)S(1)} collective-permute-done((bf16[64,1792]{1,0:T(8,128)(2,1)S(1)}, bf16[64,1792]{1,0:T(8,128)(2,1)S(1)}, u32[]{:S(2)}, u32[]{:S(2)}) %collective-permute-start.32) | collective-permute-done | bytes 229408 | tf_op jit(solution)/shard_map/ppermute | solution.py:14
  103.6 1.6 %convolution_convert_fusion = bf16[512,768]{1,0:T(8,128)(2,1)S(1)} fusion(bf16[512,1792]{1,0:T(8,128)(2,1)S(1)} %bitcast.134, bf16[1792,768]{1,0:T(8,128)(2,1)S(1)} %constant_dynamic-update-slice_fusion.24), kind=kOutput, calls=%fused_computation.12 | convolution fusion | flops 1409679360 | bytes 5373952 | tf_op jit(solution)/shard_map/dot_general | solution.py:69
  105.2 1.5 %collective-permute-done.24 = bf16[64,1792]{1,0:T(8,128)(2,1)S(1)} collective-permute-done((bf16[64,1792]{1,0:T(8,128)(2,1)S(1)}, bf16[64,1792]{1,0:T(8,128)(2,1)S(1)}, u32[]{:S(2)}, u32[]{:S(2)}) %collective-permute-start.24) | collective-permute-done | bytes 229408 | tf_op jit(solution)/shard_map/ppermute | solution.py:14
  107.0 1.6 %convolution_convert_fusion.1 = bf16[512,768]{1,0:T(8,128)(2,1)S(1)} fusion(bf16[512,1792]{1,0:T(8,128)(2,1)S(1)} %bitcast.133, bf16[1792,768]{1,0:T(8,128)(2,1)S(1)} %constant_dynamic-update-slice_fusion.24), kind=kOutput, calls=%fused_computation.13 | convolution fusion | flops 1409679360 | bytes 5373952 | tf_op jit(solution)/shard_map/dot_general | solution.py:69
  108.8 4.7 %collective-permute-start.33 = (bf16[4,4,4,2,8,384]{5,4,2,1,0,3:T(8,128)(2,1)S(1)}, bf16[4,4,4,2,8,384]{5,4,2,1,0,3:T(8,128)(2,1)S(1)}, u32[]{:S(2)}, u32[]{:S(2)}) collective-permute-start(bf16[4,4,4,2,8,384]{5,4,2,1,0,3:T(8,128)(2,1)S(1)} %get-tuple-element.10), channel_id=1, source_target_pairs={{16,0},{0,16},{17,1},{1,17},{18,2},{2,18},{19,3},{3,19},{20,4},{4,... | collective-permute-start | bytes 2359304 | tf_op jit(solution)/shard_map/ppermute | solution.py:14
  113.6 1.9 %collective-permute-done.33 = bf16[4,4,4,2,8,384]{5,4,2,1,0,3:T(8,128)(2,1)S(1)} collective-permute-done((bf16[4,4,4,2,8,384]{5,4,2,1,0,3:T(8,128)(2,1)S(1)}, bf16[4,4,4,2,8,384]{5,4,2,1,0,3:T(8,128)(2,1)S(1)}, u32[]{:S(2)}, u32[]{:S(2)}) %collective-permute-start.33) | collective-permute-done | bytes 786464 | tf_op jit(solution)/shard_map/ppermute | solution.py:14
  117.1 1.4 %copy.7 = bf16[4,4,2,4,2,8,384]{6,5,4,3,2,1,0:T(8,128)(2,1)} copy(bf16[4,4,2,4,2,8,384]{6,5,1,3,0,4,2:T(8,128)(2,1)S(1)} %fusion.1) | data formatting | bytes 3145728 | tf_op jit(solution)/shard_map/transpose | solution.py:80
  (104 shorter events, 31.6 us)
Async XLA Ops:
  0.0 5.4 %collective-permute-start = (bf16[112,112]{0,1:T(8,128)(2,1)}, bf16[112,112]{0,1:T(8,128)(2,1)S(1)}, u32[]{:S(2)}, u32[]{:S(2)}) collective-permute-start(bf16[112,112]{0,1:T(8,128)(2,1)} %bitcast.151), channel_id=1, source_target_pairs={{1,0},{2,1},{3,2},{0,3},{5,4},{6,5},{7,6},{4,7},{9,8},{10,9},{11,1... | collective-permute-start | bytes 75272 | tf_op jit(solution)/shard_map/ppermute | solution.py:14
  3.6 4.5 %collective-permute-start.1 = (bf16[112,112]{0,1:T(8,128)(2,1)}, bf16[112,112]{0,1:T(8,128)(2,1)S(1)}, u32[]{:S(2)}, u32[]{:S(2)}) collective-permute-start(bf16[112,112]{0,1:T(8,128)(2,1)} %bitcast.152), channel_id=1, source_target_pairs={{2,0},{3,1},{0,2},{1,3},{6,4},{7,5},{4,6},{5,7},{10,8},{11,9},{8,1... | collective-permute-start | bytes 75272 | tf_op jit(solution)/shard_map/ppermute | solution.py:14
  3.9 4.4 %collective-permute-start.2 = (bf16[112,112]{0,1:T(8,128)(2,1)}, bf16[112,112]{0,1:T(8,128)(2,1)S(1)}, u32[]{:S(2)}, u32[]{:S(2)}) collective-permute-start(bf16[112,112]{0,1:T(8,128)(2,1)} %bitcast.153), channel_id=1, source_target_pairs={{3,0},{0,1},{1,2},{2,3},{7,4},{4,5},{5,6},{6,7},{11,8},{8,9},{9,10... | collective-permute-start | bytes 75272 | tf_op jit(solution)/shard_map/ppermute | solution.py:14
  9.2 6.2 %collective-permute-start.3 = (bf16[4,112,112]{1,2,0:T(8,128)(2,1)S(1)}, bf16[4,112,112]{1,2,0:T(8,128)(2,1)S(1)}, u32[]{:S(2)}, u32[]{:S(2)}) collective-permute-start(bf16[4,112,112]{1,2,0:T(8,128)(2,1)S(1)} %get-tuple-element.8), channel_id=1, source_target_pairs={{4,0},{8,4},{12,8},{0,12},{5,1},{9,5},{13,9},{1,13},{6,2},{10,6},{... | collective-permute-start | bytes 301064 | tf_op jit(solution)/shard_map/ppermute | solution.py:14
  13.7 9.8 %collective-permute-start.4 = (bf16[4,112,112]{1,2,0:T(8,128)(2,1)S(1)}, bf16[4,112,112]{1,2,0:T(8,128)(2,1)S(1)}, u32[]{:S(2)}, u32[]{:S(2)}) collective-permute-start(bf16[4,112,112]{1,2,0:T(8,128)(2,1)S(1)} %get-tuple-element.8), channel_id=1, source_target_pairs={{8,0},{12,4},{0,8},{4,12},{9,1},{13,5},{1,9},{5,13},{10,2},{14,6},... | collective-permute-start | bytes 301064 | tf_op jit(solution)/shard_map/ppermute | solution.py:14
  13.8 9.8 %collective-permute-start.5 = (bf16[4,112,112]{1,2,0:T(8,128)(2,1)S(1)}, bf16[4,112,112]{1,2,0:T(8,128)(2,1)S(1)}, u32[]{:S(2)}, u32[]{:S(2)}) collective-permute-start(bf16[4,112,112]{1,2,0:T(8,128)(2,1)S(1)} %get-tuple-element.8), channel_id=1, source_target_pairs={{12,0},{0,4},{4,8},{8,12},{13,1},{1,5},{5,9},{9,13},{14,2},{2,6},{... | collective-permute-start | bytes 301064 | tf_op jit(solution)/shard_map/ppermute | solution.py:14
  28.9 7.0 %collective-permute-start.7 = (f32[16,1792]{1,0:T(8,128)S(1)}, f32[16,1792]{1,0:T(8,128)S(1)}, u32[]{:S(2)}, u32[]{:S(2)}) collective-permute-start(f32[16,1792]{1,0:T(8,128)S(1)} %get-tuple-element.17), channel_id=1, source_target_pairs={{64,0},{128,64},{192,128},{0,192},{65,1},{129,65},{193,129},{1,193... | collective-permute-start | bytes 344072 | tf_op jit(solution)/shard_map/ppermute | solution.py:14
  31.4 5.5 %collective-permute-start.8 = (f32[16,1792]{1,0:T(8,128)S(1)}, f32[16,1792]{1,0:T(8,128)S(1)}, u32[]{:S(2)}, u32[]{:S(2)}) collective-permute-start(f32[16,1792]{1,0:T(8,128)S(1)} %get-tuple-element.15), channel_id=1, source_target_pairs={{128,0},{192,64},{0,128},{64,192},{129,1},{193,65},{1,129},{65,193... | collective-permute-start | bytes 344072 | tf_op jit(solution)/shard_map/ppermute | solution.py:14
  31.9 8.5 %collective-permute-start.9 = (f32[16,1792]{1,0:T(8,128)S(1)}, f32[16,1792]{1,0:T(8,128)S(1)}, u32[]{:S(2)}, u32[]{:S(2)}) collective-permute-start(f32[16,1792]{1,0:T(8,128)S(1)} %get-tuple-element.16), channel_id=1, source_target_pairs={{192,0},{0,64},{64,128},{128,192},{193,1},{1,65},{65,129},{129,193... | collective-permute-start | bytes 344072 | tf_op jit(solution)/shard_map/ppermute | solution.py:14
  40.5 7.1 %collective-permute-start.10 = (f32[8,1792]{1,0:T(8,128)S(1)}, f32[8,1792]{1,0:T(8,128)S(1)}, u32[]{:S(2)}, u32[]{:S(2)}) collective-permute-start(f32[8,1792]{1,0:T(8,128)S(1)} %dynamic-slice_bitcast_fusion.8), channel_id=1, source_target_pairs={{32,0},{0,32},{33,1},{1,33},{34,2},{2,34},{35,3},{3,35},{36,4},{4,... | collective-permute-start | bytes 172040 | tf_op jit(solution)/shard_map/ppermute | solution.py:14
  48.2 13.0 %collective-permute-start.11 = (bf16[8,1792]{1,0:T(8,128)(2,1)S(1)}, bf16[8,1792]{1,0:T(8,128)(2,1)S(1)}, u32[]{:S(2)}, u32[]{:S(2)}) collective-permute-start(bf16[8,1792]{1,0:T(8,128)(2,1)S(1)} %get-tuple-element.6), channel_id=1, source_target_pairs={{4,0},{8,4},{12,8},{32,12},{36,32},{40,36},{44,40},{0,44},{5,1},{9... | collective-permute-start | bytes 86024 | tf_op jit(solution)/shard_map/ppermute | solution.py:14
  51.4 49.0 %collective-permute-start.25 = (bf16[1792,384]{1,0:T(8,128)(2,1)S(1)}, bf16[1792,384]{1,0:T(8,128)(2,1)S(1)}, u32[]{:S(2)}, u32[]{:S(2)}) collective-permute-start(bf16[1792,384]{1,0:T(8,128)(2,1)S(1)} %copy-done.1), channel_id=1, source_target_pairs={{16,0},{0,16},{17,1},{1,17},{18,2},{2,18},{19,3},{3,19},{20,4},{4,... | collective-permute-start | bytes 4128776 | tf_op jit(solution)/shard_map/ppermute | solution.py:14
  52.9 8.8 %collective-permute-start.12 = (bf16[8,1792]{1,0:T(8,128)(2,1)S(1)}, bf16[8,1792]{1,0:T(8,128)(2,1)S(1)}, u32[]{:S(2)}, u32[]{:S(2)}) collective-permute-start(bf16[8,1792]{1,0:T(8,128)(2,1)S(1)} %get-tuple-element.6), channel_id=1, source_target_pairs={{8,0},{12,4},{32,8},{36,12},{40,32},{44,36},{0,40},{4,44},{9,1},{1... | collective-permute-start | bytes 86024 | tf_op jit(solution)/shard_map/ppermute | solution.py:14
  55.2 8.5 %collective-permute-start.13 = (bf16[8,1792]{1,0:T(8,128)(2,1)S(1)}, bf16[8,1792]{1,0:T(8,128)(2,1)S(1)}, u32[]{:S(2)}, u32[]{:S(2)}) collective-permute-start(bf16[8,1792]{1,0:T(8,128)(2,1)S(1)} %get-tuple-element.6), channel_id=1, source_target_pairs={{12,0},{32,4},{36,8},{40,12},{44,32},{0,36},{4,40},{8,44},{13,1},{... | collective-permute-start | bytes 86024 | tf_op jit(solution)/shard_map/ppermute | solution.py:14
  56.5 9.7 %collective-permute-start.14 = (bf16[8,1792]{1,0:T(8,128)(2,1)S(1)}, bf16[8,1792]{1,0:T(8,128)(2,1)S(1)}, u32[]{:S(2)}, u32[]{:S(2)}) collective-permute-start(bf16[8,1792]{1,0:T(8,128)(2,1)S(1)} %get-tuple-element.6), channel_id=1, source_target_pairs={{32,0},{36,4},{40,8},{44,12},{0,32},{4,36},{8,40},{12,44},{33,1},{... | collective-permute-start | bytes 86024 | tf_op jit(solution)/shard_map/ppermute | solution.py:14
  61.2 5.8 %collective-permute-start.15 = (bf16[8,1792]{1,0:T(8,128)(2,1)S(1)}, bf16[8,1792]{1,0:T(8,128)(2,1)S(1)}, u32[]{:S(2)}, u32[]{:S(2)}) collective-permute-start(bf16[8,1792]{1,0:T(8,128)(2,1)S(1)} %get-tuple-element.6), channel_id=1, source_target_pairs={{36,0},{40,4},{44,8},{0,12},{4,32},{8,36},{12,40},{32,44},{37,1},{... | collective-permute-start | bytes 86024 | tf_op jit(solution)/shard_map/ppermute | solution.py:14
  61.8 5.8 %collective-permute-start.16 = (bf16[8,1792]{1,0:T(8,128)(2,1)S(1)}, bf16[8,1792]{1,0:T(8,128)(2,1)S(1)}, u32[]{:S(2)}, u32[]{:S(2)}) collective-permute-start(bf16[8,1792]{1,0:T(8,128)(2,1)S(1)} %get-tuple-element.6), channel_id=1, source_target_pairs={{40,0},{44,4},{0,8},{4,12},{8,32},{12,36},{32,40},{36,44},{41,1},{... | collective-permute-start | bytes 86024 | tf_op jit(solution)/shard_map/ppermute | solution.py:14
  63.8 4.8 %collective-permute-start.17 = (bf16[8,1792]{1,0:T(8,128)(2,1)S(1)}, bf16[8,1792]{1,0:T(8,128)(2,1)S(1)}, u32[]{:S(2)}, u32[]{:S(2)}) collective-permute-start(bf16[8,1792]{1,0:T(8,128)(2,1)S(1)} %get-tuple-element.6), channel_id=1, source_target_pairs={{44,0},{0,4},{4,8},{8,12},{12,32},{32,36},{36,40},{40,44},{45,1},{... | collective-permute-start | bytes 86024 | tf_op jit(solution)/shard_map/ppermute | solution.py:14
  75.8 5.2 %collective-permute-start.27 = (bf16[32,1792]{1,0:T(8,128)(2,1)S(1)}, bf16[32,1792]{1,0:T(8,128)(2,1)S(1)}, u32[]{:S(2)}, u32[]{:S(2)}) collective-permute-start(bf16[32,1792]{1,0:T(8,128)(2,1)S(1)} %get-tuple-element.13), channel_id=1, source_target_pairs={{2,0},{3,1},{0,2},{1,3},{6,4},{7,5},{4,6},{5,7},{10,8},{11,9},{8,1... | collective-permute-start | bytes 344072 | tf_op jit(solution)/shard_map/ppermute | solution.py:14
  76.7 5.5 %collective-permute-start.28 = (bf16[32,1792]{1,0:T(8,128)(2,1)S(1)}, bf16[32,1792]{1,0:T(8,128)(2,1)S(1)}, u32[]{:S(2)}, u32[]{:S(2)}) collective-permute-start(bf16[32,1792]{1,0:T(8,128)(2,1)S(1)} %get-tuple-element.13), channel_id=1, source_target_pairs={{3,0},{0,1},{1,2},{2,3},{7,4},{4,5},{5,6},{6,7},{11,8},{8,9},{9,10... | collective-permute-start | bytes 344072 | tf_op jit(solution)/shard_map/ppermute | solution.py:14
  77.5 6.4 %collective-permute-start.18 = (bf16[32,1792]{1,0:T(8,128)(2,1)S(1)}, bf16[32,1792]{1,0:T(8,128)(2,1)S(1)}, u32[]{:S(2)}, u32[]{:S(2)}) collective-permute-start(bf16[32,1792]{1,0:T(8,128)(2,1)S(1)} %get-tuple-element.12), channel_id=1, source_target_pairs={{64,0},{128,64},{192,128},{0,192},{65,1},{129,65},{193,129},{1,193... | collective-permute-start | bytes 344072 | tf_op jit(solution)/shard_map/ppermute | solution.py:14
  78.8 5.2 %collective-permute-start.19 = (bf16[32,1792]{1,0:T(8,128)(2,1)S(1)}, bf16[32,1792]{1,0:T(8,128)(2,1)S(1)}, u32[]{:S(2)}, u32[]{:S(2)}) collective-permute-start(bf16[32,1792]{1,0:T(8,128)(2,1)S(1)} %get-tuple-element.12), channel_id=1, source_target_pairs={{128,0},{192,64},{0,128},{64,192},{129,1},{193,65},{1,129},{65,193... | collective-permute-start | bytes 344072 | tf_op jit(solution)/shard_map/ppermute | solution.py:14
  81.1 4.9 %collective-permute-start.20 = (bf16[32,1792]{1,0:T(8,128)(2,1)S(1)}, bf16[32,1792]{1,0:T(8,128)(2,1)S(1)}, u32[]{:S(2)}, u32[]{:S(2)}) collective-permute-start(bf16[32,1792]{1,0:T(8,128)(2,1)S(1)} %get-tuple-element.12), channel_id=1, source_target_pairs={{192,0},{0,64},{64,128},{128,192},{193,1},{1,65},{65,129},{129,193... | collective-permute-start | bytes 344072 | tf_op jit(solution)/shard_map/ppermute | solution.py:14
  82.3 10.0 %collective-permute-start.29 = (bf16[128,1792]{1,0:T(8,128)(2,1)S(1)}, bf16[128,1792]{1,0:T(8,128)(2,1)S(1)}, u32[]{:S(2)}, u32[]{:S(2)}) collective-permute-start(bf16[128,1792]{1,0:T(8,128)(2,1)S(1)} %bitcast.127), channel_id=1, source_target_pairs={{64,0},{128,64},{192,128},{0,192},{65,1},{129,65},{193,129},{1,193... | collective-permute-start | bytes 1376264 | tf_op jit(solution)/shard_map/ppermute | solution.py:14
  83.9 13.1 %collective-permute-start.31 = (bf16[128,1792]{1,0:T(8,128)(2,1)S(1)}, bf16[128,1792]{1,0:T(8,128)(2,1)S(1)}, u32[]{:S(2)}, u32[]{:S(2)}) collective-permute-start(bf16[128,1792]{1,0:T(8,128)(2,1)S(1)} %bitcast.128), channel_id=1, source_target_pairs={{192,0},{0,64},{64,128},{128,192},{193,1},{1,65},{65,129},{129,193... | collective-permute-start | bytes 1376264 | tf_op jit(solution)/shard_map/ppermute | solution.py:14
  86.0 11.1 %collective-permute-start.21 = (bf16[128,1792]{1,0:T(8,128)(2,1)S(1)}, bf16[128,1792]{1,0:T(8,128)(2,1)S(1)}, u32[]{:S(2)}, u32[]{:S(2)}) collective-permute-start(bf16[128,1792]{1,0:T(8,128)(2,1)S(1)} %bitcast.130), channel_id=1, source_target_pairs={{1,0},{2,1},{3,2},{0,3},{5,4},{6,5},{7,6},{4,7},{9,8},{10,9},{11,1... | collective-permute-start | bytes 1376264 | tf_op jit(solution)/shard_map/ppermute | solution.py:14
  87.6 12.6 %collective-permute-start.23 = (bf16[128,1792]{1,0:T(8,128)(2,1)S(1)}, bf16[128,1792]{1,0:T(8,128)(2,1)S(1)}, u32[]{:S(2)}, u32[]{:S(2)}) collective-permute-start(bf16[128,1792]{1,0:T(8,128)(2,1)S(1)} %bitcast.131), channel_id=1, source_target_pairs={{3,0},{0,1},{1,2},{2,3},{7,4},{4,5},{5,6},{6,7},{11,8},{8,9},{9,10... | collective-permute-start | bytes 1376264 | tf_op jit(solution)/shard_map/ppermute | solution.py:14
  92.3 8.3 %collective-permute-start.30 = (bf16[64,1792]{1,0:T(8,128)(2,1)S(1)}, bf16[64,1792]{1,0:T(8,128)(2,1)S(1)}, u32[]{:S(2)}, u32[]{:S(2)}) collective-permute-start(bf16[64,1792]{1,0:T(8,128)(2,1)S(1)} %slice.34), channel_id=1, source_target_pairs={{64,0},{128,64},{192,128},{0,192},{65,1},{129,65},{193,129},{1,193... | collective-permute-start | bytes 688136 | tf_op jit(solution)/shard_map/ppermute | solution.py:14
  97.0 6.3 %collective-permute-start.32 = (bf16[64,1792]{1,0:T(8,128)(2,1)S(1)}, bf16[64,1792]{1,0:T(8,128)(2,1)S(1)}, u32[]{:S(2)}, u32[]{:S(2)}) collective-permute-start(bf16[64,1792]{1,0:T(8,128)(2,1)S(1)} %slice.35), channel_id=1, source_target_pairs={{192,0},{0,64},{64,128},{128,192},{193,1},{1,65},{65,129},{129,193... | collective-permute-start | bytes 688136 | tf_op jit(solution)/shard_map/ppermute | solution.py:14
  97.1 8.1 %collective-permute-start.22 = (bf16[64,1792]{1,0:T(8,128)(2,1)S(1)}, bf16[64,1792]{1,0:T(8,128)(2,1)S(1)}, u32[]{:S(2)}, u32[]{:S(2)}) collective-permute-start(bf16[64,1792]{1,0:T(8,128)(2,1)S(1)} %slice.32), channel_id=1, source_target_pairs={{1,0},{2,1},{3,2},{0,3},{5,4},{6,5},{7,6},{4,7},{9,8},{10,9},{11,1... | collective-permute-start | bytes 688136 | tf_op jit(solution)/shard_map/ppermute | solution.py:14
  100.3 6.5 %collective-permute-start.24 = (bf16[64,1792]{1,0:T(8,128)(2,1)S(1)}, bf16[64,1792]{1,0:T(8,128)(2,1)S(1)}, u32[]{:S(2)}, u32[]{:S(2)}) collective-permute-start(bf16[64,1792]{1,0:T(8,128)(2,1)S(1)} %slice.33), channel_id=1, source_target_pairs={{3,0},{0,1},{1,2},{2,3},{7,4},{4,5},{5,6},{6,7},{11,8},{8,9},{9,10... | collective-permute-start | bytes 688136 | tf_op jit(solution)/shard_map/ppermute | solution.py:14
  108.8 6.6 %collective-permute-start.33 = (bf16[4,4,4,2,8,384]{5,4,2,1,0,3:T(8,128)(2,1)S(1)}, bf16[4,4,4,2,8,384]{5,4,2,1,0,3:T(8,128)(2,1)S(1)}, u32[]{:S(2)}, u32[]{:S(2)}) collective-permute-start(bf16[4,4,4,2,8,384]{5,4,2,1,0,3:T(8,128)(2,1)S(1)} %get-tuple-element.10), channel_id=1, source_target_pairs={{16,0},{0,16},{17,1},{1,17},{18,2},{2,18},{19,3},{3,19},{20,4},{4,... | collective-permute-start | bytes 2359304 | tf_op jit(solution)/shard_map/ppermute | solution.py:14
  (4 other events, 47.0 us)

commit v2 on v0

v2 whole, which is shorter than its diff:
```python
import jax
import jax.numpy as jnp
from jax import lax
from jax.experimental import pallas as pl
from jax.experimental.pallas import tpu as pltpu
from jax.sharding import Mesh, PartitionSpec as P

ROW = ("x", "z_hi", "core")
COL = ("z_lo", "y")
Z = ("z_hi", "z_lo")
BF16 = jnp.bfloat16
F32 = jnp.float32
VMEM = pl.BlockSpec(memory_space=pltpu.VMEM)
SMEM = pl.BlockSpec(memory_space=pltpu.SMEM)
ANY = pl.BlockSpec(memory_space=pl.ANY)
HBM = pl.BlockSpec(memory_space=pltpu.HBM)
PARAMS = pltpu.CompilerParams(vmem_limit_bytes=24 * 2**20)


def fetch(block, axis, size, ahead):
    return lax.ppermute(block, axis, [((i + ahead) % size, i) for i in range(size)])


def dot_t(left, right):
    return lax.dot_general(left, right, (((0,), (0,)), ((), ())), preferred_element_type=F32)


def partial_sums(place, screening, panel, keep, send, left, right, sems):
    core = place[2]
    copies = [pltpu.make_async_copy(screening, left, sems.at[2])]
    for half, base in enumerate((1 - core, core)):
        columns = pl.ds(pl.multiple_of(base * 1024, 1024), 1024)
        copies.append(pltpu.make_async_copy(panel.at[:, columns], right.at[half], sems.at[half]))
    for copy in copies:
        copy.start()
    copies[0].wait()
    for half, out in enumerate((send, keep)):
        copies[1 + half].wait()
        for slab in range(8):
            out[slab] = dot_t(left[...], right[half, :, pl.ds(slab * 128, 128)])


def wide(block, lead):
    return jnp.concatenate([block[i].reshape(-1, 128) for i in range(lead)], 1)


def order_pairs(place, own, other, both):
    for k in range(4):
        for j in range(4):
            y, z_lo = lax.rem(place[1] + k, 4), lax.rem(place[3] + j, 4)
            rows = pl.ds(pl.multiple_of((z_lo * 4 + y) * 112, 16), 112)
            both[k, pl.ds(j * 112, 112), :384] = own[rows]
            both[k, pl.ds(j * 112, 112), 384:] = other[rows]


def product_one(one, two, both, out):
    out[0] = dot_t(wide(one, 4), both[0])
    out[1, :128] = dot_t(two[...].reshape(1792, 128), both[...].reshape(1792, 768))


def product_two(after1, before1, after2, before2, both, start, out):
    out[0] = start[0] + dot_t(wide(after1, 4), both[1]) + dot_t(wide(before1, 4), both[3])
    out[1, :128] = start[1, :128]
    for block, ahead in ((after2, 1), (before2, 3)):
        rows = pl.ds(ahead * 128, 128)
        out[1, rows] = dot_t(block[...].reshape(1792, 128), both[...].reshape(1792, 768))


def product_three(place, low1, high1, low2, high2, both, start, mine, theirs):
    x = place[0]
    for half, block in ((0, low1), (1, high1)):
        rows = pl.ds(half * 256, 256)
        total = start[0, rows] + dot_t(wide(block, 2), both[2])
        total = total.astype(BF16).reshape(2, 128, 768)
        for i in range(2):
            slab = lax.rem(x + half * 2 + i, 4)
            mine[slab, 0] = total[i, :, :384]
            theirs[slab, 0] = total[i, :, 384:]
    for ahead in (0, 1, 3):
        slab = lax.rem(x + ahead, 4)
        total = start[1, pl.ds(ahead * 128, 128)].astype(BF16)
        mine[slab, 1] = total[:, :384]
        theirs[slab, 1] = total[:, 384:]
    slab = lax.rem(x + 2, 4)
    left = jnp.concatenate([low2[...].reshape(896, 128), high2[...].reshape(896, 128)], 0)
    total = dot_t(left, both[...].reshape(1792, 768)).astype(BF16)
    mine[slab, 1] = total[:, :384]
    theirs[slab, 1] = total[:, 384:]


def place_mine(place, block, out, sem):
    rows = pl.ds(pl.multiple_of(place[2] * 1024, 1024), 1024)
    copy = pltpu.make_async_copy(block, out.at[rows], sem)
    copy.start()
    copy.wait()


def place_theirs(place, block, given, out, sem):
    rows = pl.ds(pl.multiple_of((1 - place[2]) * 1024, 1024), 1024)
    copy = pltpu.make_async_copy(block, out.at[rows], sem)
    copy.start()
    copy.wait()


def call(kernel, out_shape, operands, out_specs=VMEM, specs=None, flops=0, **more):
    return pl.pallas_call(
        kernel,
        out_shape=out_shape,
        in_specs=specs or [SMEM] + [VMEM] * (len(operands) - 1),
        out_specs=out_specs,
        compiler_params=PARAMS,
        cost_estimate=pl.CostEstimate(flops=flops, bytes_accessed=2**21, transcendentals=0),
        **more,
    )(*operands)


def per_device(pair_valence, screening, pair_conduction):
    x, y, core, z_lo = (lax.axis_index(axis) for axis in ("x", "y", "core", "z_lo"))
    place = jnp.stack([x, y, core, z_lo]).astype(jnp.int32)

    slabs = jax.ShapeDtypeStruct((8, 112, 128), F32)
    keep, send = call(
        partial_sums,
        (slabs, slabs),
        (place, screening, pair_valence),
        (VMEM, VMEM),
        [SMEM, HBM, HBM],
        scratch_shapes=[
            pltpu.VMEM((112, 112), BF16),
            pltpu.VMEM((2, 112, 1024), BF16),
            pltpu.SemaphoreType.DMA((3,)),
        ],
    )
    received, own_pairs = lax.optimization_barrier((fetch(send, "core", 2, 1), pair_conduction))
    part = (keep + received).reshape(4, 2, 112, 128)
    sent = part.astype(BF16)
    part = lax.dynamic_index_in_dim(part, x, 0, keepdims=False)
    for ahead in (1, 3, 2):
        away = lax.dynamic_index_in_dim(sent, (x + 4 - ahead) % 4, 0, keepdims=False)
        part = part + fetch(away, "x", 4, ahead).astype(F32)

    other = fetch(own_pairs, "core", 2, 1)
    both = call(
        order_pairs, jax.ShapeDtypeStruct((4, 448, 768), BF16), (place, own_pairs, other)
    )

    own = part.astype(BF16)
    up1, down1 = fetch(own, Z, 8, 1), fetch(own, Z, 8, 7)
    up1, down1, both = lax.optimization_barrier((up1, down1, both))
    up2, down2 = fetch(up1, Z, 8, 1), fetch(down1, Z, 8, 7)
    up3, down3 = fetch(up2, Z, 8, 1), fetch(down2, Z, 8, 7)
    far = jnp.concatenate([fetch(up3[:1], Z, 8, 1), fetch(down3[1:], Z, 8, 7)])
    line = [own.astype(F32) + far, up1.astype(F32) + down3, up2.astype(F32) + down2, up3.astype(F32) + down1]
    line = jnp.stack(line, 1).astype(BF16)

    def ring(block, axis):
        after, before = fetch(block, axis, 4, 1), fetch(block, axis, 4, 3)
        low, high = fetch(after[:2], axis, 4, 1), fetch(before[2:], axis, 4, 3)
        return jnp.stack([block, after, jnp.concatenate([low, high]), before])

    one, two = ring(line[0], "x"), ring(line[1], "y")
    after1, before1 = fetch(one, "y", 4, 1), fetch(one, "y", 4, 3)
    after2, before2 = fetch(two, "x", 4, 1), fetch(two, "x", 4, 3)
    total = jax.ShapeDtypeStruct((2, 512, 768), F32)
    total_one = call(product_one, total, (one, two, both), specs=[VMEM] * 3, flops=10**9)
    after1, before1, after2, before2, total_one = lax.optimization_barrier(
        (after1, before1, after2, before2, total_one)
    )
    low1, high1 = fetch(after1[:2], "y", 4, 1), fetch(before1[2:], "y", 4, 3)
    low2, high2 = fetch(after2[:2], "x", 4, 1), fetch(before2[2:], "x", 4, 3)
    total_two = call(
        product_two,
        total,
        (after1, before1, after2, before2, both, total_one),
        specs=[VMEM] * 6,
        flops=10**9,
        input_output_aliases={5: 0},
    )
    half = jax.ShapeDtypeStruct((4, 2, 128, 384), BF16)
    mine, theirs = call(
        product_three,
        (half, half),
        (place, low1, high1, low2, high2, both, total_two),
        (VMEM, VMEM),
        flops=10**9,
    )

    theirs = fetch(theirs.reshape(1024, 384), "core", 2, 1)
    out = jax.ShapeDtypeStruct((2048, 384), BF16)
    sem = dict(scratch_shapes=[pltpu.SemaphoreType.DMA])
    kernel = call(place_mine, out, (place, mine.reshape(1024, 384)), ANY, [SMEM, VMEM], **sem)
    return call(
        place_theirs,
        out,
        (place, theirs, kernel),
        ANY,
        [SMEM, VMEM, ANY],
        input_output_aliases={2: 0},
        **sem,
    )


def solution(mesh):
    fine = Mesh(mesh.devices.reshape(4, 2, 2, 4, 4), ROW + COL)
    placed = (P(ROW, None), P(ROW, COL), P(None, ROW + COL))
    return jax.shard_map(
        per_device, mesh=fine, in_specs=placed, out_specs=P(None, ROW + COL), check_vma=False
    )
```

time: 266 us -> 93.6 us (0.35)
  waiting for transfers between devices: 197 us -> 24.2 us
  starting transfers between devices: 0.04 us -> 54.1 us
  blocking collectives: 40.2 us -> 0 us
  between operations: 13.4 us -> 0.44 us
  matrix products: 11.3 us -> 0 us
  Pallas kernels: 0 us -> 9.49 us
    all_gather x2 -> x0, waiting for transfers between devices: 197 us -> none  [the longest x1 98.4 us: per_device(): lax.all_gather(pair_valence, 'row', axis=0, tiled=True)]
    ppermute x0 -> x30, starting transfers between devices: none -> 54.1 us  [fetch(): lax.ppermute(block, axis, [((i + ahead) % size, i) for i in range(size)])]
    all_gather x1 -> x0, blocking collectives: 40.2 us -> none  [per_device(): row_panel = lax.all_gather(screening, 'col', axis=1, tiled=True)]
    ppermute x0 -> x30, waiting for transfers between devices: none -> 24.2 us  [fetch(): lax.ppermute(block, axis, [((i + ahead) % size, i) for i in range(size)])]
    dot_general x1 -> x0, matrix products: 11.3 us -> none  [per_device(): lax.dot_general(lax.all_gather(pair_valence, 'row', axis=0, tiled=True),...]
    pallas_call x0 -> x7, Pallas kernels: none -> 9.49 us  [call(): pl.pallas_call(kernel, out_shape=out_shape, in_specs=specs or [SMEM] + [V...]
  transfers between devices with their start and end apart: 2 -> 30, of which waited for: 2 -> 14; matrix products, arithmetic and copies ran while one was open for 0% -> 2% of each run, Pallas kernels for 0% -> 6%
where the time goes in v2:
time: 93.6 us; the launch traced here: 93.3 us
  starting transfers between devices  54.1 us (58%)
  waiting for transfers between devices  24.2 us (26%)
  Pallas kernels  9.49 us (10%)
  local copies, waits for them, and re-layouts  2.71 us (3%)
  other arithmetic  2.41 us (3%)
    ppermute x30, starting transfers between devices, fetch(): lax.ppermute(block, axis, [((i + ahead) % size, i) for i in range(size)])  54.1 us
    ppermute x30, waiting for transfers between devices, fetch(): lax.ppermute(block, axis, [((i + ahead) % size, i) for i in range(size)])  24.2 us
    pallas_call x7, Pallas kernels, call(): pl.pallas_call(kernel, out_shape=out_shape, in_specs=specs or [SMEM] + [V...  9.49 us
    unnamed x8, local copies, waits for them, and re-layouts  2.53 us
  transfers between devices with their start and end apart: 30, of which 14 were waited for; matrix products, arithmetic and copies ran while one was open for 2% of the time, Pallas kernels for 6%

profile of v2, /device:TPU:1, one launch (start us, length us, event | category | flops | bytes accessed | tf_op | source)
XLA Modules:
  0.0 93.3 jit_solution(7560982807618970339)
XLA Ops:
  1.8 1.3 %shard_map.37 = (f32[8,112,128]{2,1,0:T(8,128)S(1)}, f32[8,112,128]{2,1,0:T(8,128)S(1)}) custom-call(s32[4]{0:T(128)S(1)} %pad_add_fusion.place, bf16[112,112]{1,0:T(8,128)(2,1)S(1)} %copy-done.2, bf16[112,2048]{1,0:T(8,128)(2,1)S(1)} %copy-done.1), custom_call_target="tpu_custom_call" | custom-call | bytes 2097152 | tf_op jit(solution)/shard_map/pallas_call | solution.py:106
  3.2 3.3 %collective-permute-start = (f32[8,112,128]{2,1,0:T(8,128)S(1)}, f32[8,112,128]{2,1,0:T(8,128)}, u32[]{:S(2)}, u32[]{:S(2)}) collective-permute-start(f32[8,112,128]{2,1,0:T(8,128)S(1)} %get-tuple-element.20), channel_id=1, source_target_pairs={{16,0},{0,16},{17,1},{1,17},{18,2},{2,18},{19,3},{3,19},{20,4},{4,... | collective-permute-start | bytes 1376264 | tf_op jit(solution)/shard_map/ppermute | solution.py:21
  6.5 1.6 %collective-permute-done = f32[8,112,128]{2,1,0:T(8,128)} collective-permute-done((f32[8,112,128]{2,1,0:T(8,128)S(1)}, f32[8,112,128]{2,1,0:T(8,128)}, u32[]{:S(2)}, u32[]{:S(2)}) %collective-permute-start) | collective-permute-done | bytes 458784 | tf_op jit(solution)/shard_map/ppermute | solution.py:21
  8.4 1.1 %add.60 = f32[8,112,128]{2,1,0:T(8,128)S(1)} add(f32[8,112,128]{2,1,0:T(8,128)S(1)} %get-tuple-element.19, f32[8,112,128]{2,1,0:T(8,128)} %collective-permute-done) | non-fusion elementwise | flops 114688 | bytes 1376256 | tf_op jit(solution)/shard_map/add | solution.py:135
  12.3 1.2 %collective-permute-done.1 = bf16[2,112,128]{2,1,0:T(8,128)(2,1)S(1)} collective-permute-done((bf16[2,112,128]{2,1,0:T(8,128)(2,1)S(1)}, bf16[2,112,128]{2,1,0:T(8,128)(2,1)S(1)}, u32[]{:S(2)}, u32[]{:S(2)}) %collective-permute-start.1) | collective-permute-done | bytes 57376 | tf_op jit(solution)/shard_map/ppermute | solution.py:21
  13.5 2.3 %collective-permute-done.3 = bf16[2,112,128]{2,1,0:T(8,128)(2,1)S(1)} collective-permute-done((bf16[2,112,128]{2,1,0:T(8,128)(2,1)S(1)}, bf16[2,112,128]{2,1,0:T(8,128)(2,1)S(1)}, u32[]{:S(2)}, u32[]{:S(2)}) %collective-permute-start.3) | collective-permute-done | bytes 57376 | tf_op jit(solution)/shard_map/ppermute | solution.py:21
  15.8 1.8 %collective-permute-done.2 = bf16[2,112,128]{2,1,0:T(8,128)(2,1)S(1)} collective-permute-done((bf16[2,112,128]{2,1,0:T(8,128)(2,1)S(1)}, bf16[2,112,128]{2,1,0:T(8,128)(2,1)S(1)}, u32[]{:S(2)}, u32[]{:S(2)}) %collective-permute-start.2) | collective-permute-done | bytes 57376 | tf_op jit(solution)/shard_map/ppermute | solution.py:21
  18.5 1.5 %collective-permute-start.5 = (bf16[2,112,128]{2,1,0:T(8,128)(2,1)S(1)}, bf16[2,112,128]{2,1,0:T(8,128)(2,1)S(1)}, u32[]{:S(2)}, u32[]{:S(2)}) collective-permute-start(bf16[2,112,128]{2,1,0:T(8,128)(2,1)S(1)} %fusion.2), channel_id=1, source_target_pairs={{44,0},{0,4},{4,8},{8,12},{12,32},{32,36},{36,40},{40,44},{45,1},{... | collective-permute-start | bytes 172040 | tf_op jit(solution)/shard_map/ppermute | solution.py:21
  20.0 4.0 %collective-permute-start.4 = (bf16[2,112,128]{2,1,0:T(8,128)(2,1)S(1)}, bf16[2,112,128]{2,1,0:T(8,128)(2,1)S(1)}, u32[]{:S(2)}, u32[]{:S(2)}) collective-permute-start(bf16[2,112,128]{2,1,0:T(8,128)(2,1)S(1)} %fusion.2), channel_id=1, source_target_pairs={{4,0},{8,4},{12,8},{32,12},{36,32},{40,36},{44,40},{0,44},{5,1},{9... | collective-permute-start | bytes 172040 | tf_op jit(solution)/shard_map/ppermute | solution.py:21
  25.5 2.8 %collective-permute-start.7 = (bf16[2,112,128]{2,1,0:T(8,128)(2,1)S(1)}, bf16[2,112,128]{2,1,0:T(8,128)(2,1)S(1)}, u32[]{:S(2)}, u32[]{:S(2)}) collective-permute-start(bf16[2,112,128]{2,1,0:T(8,128)(2,1)S(1)} %collective-permute-done.4), channel_id=1, source_target_pairs={{4,0},{8,4},{12,8},{32,12},{36,32},{40,36},{44,40},{0,44},{5,1},{9... | collective-permute-start | bytes 172040 | tf_op jit(solution)/shard_map/ppermute | solution.py:21
  28.2 1.3 %collective-permute-done.7 = bf16[2,112,128]{2,1,0:T(8,128)(2,1)S(1)} collective-permute-done((bf16[2,112,128]{2,1,0:T(8,128)(2,1)S(1)}, bf16[2,112,128]{2,1,0:T(8,128)(2,1)S(1)}, u32[]{:S(2)}, u32[]{:S(2)}) %collective-permute-start.7) | collective-permute-done | bytes 57376 | tf_op jit(solution)/shard_map/ppermute | solution.py:21
  29.5 3.0 %collective-permute-start.8 = (bf16[2,112,128]{2,1,0:T(8,128)(2,1)S(1)}, bf16[2,112,128]{2,1,0:T(8,128)(2,1)S(1)}, u32[]{:S(2)}, u32[]{:S(2)}) collective-permute-start(bf16[2,112,128]{2,1,0:T(8,128)(2,1)S(1)} %collective-permute-done.7), channel_id=1, source_target_pairs={{4,0},{8,4},{12,8},{32,12},{36,32},{40,36},{44,40},{0,44},{5,1},{9... | collective-permute-start | bytes 172040 | tf_op jit(solution)/shard_map/ppermute | solution.py:21
  32.5 1.2 %collective-permute-done.8 = bf16[2,112,128]{2,1,0:T(8,128)(2,1)S(1)} collective-permute-done((bf16[2,112,128]{2,1,0:T(8,128)(2,1)S(1)}, bf16[2,112,128]{2,1,0:T(8,128)(2,1)S(1)}, u32[]{:S(2)}, u32[]{:S(2)}) %collective-permute-start.8) | collective-permute-done | bytes 57376 | tf_op jit(solution)/shard_map/ppermute | solution.py:21
  33.7 3.0 %collective-permute-start.9 = (bf16[1,112,128]{2,1,0:T(8,128)(2,1)S(1)}, bf16[1,112,128]{2,1,0:T(8,128)(2,1)S(1)}, u32[]{:S(2)}, u32[]{:S(2)}) collective-permute-start(bf16[1,112,128]{2,1,0:T(8,128)(2,1)S(1)} %slice.48), channel_id=1, source_target_pairs={{4,0},{8,4},{12,8},{32,12},{36,32},{40,36},{44,40},{0,44},{5,1},{9... | collective-permute-start | bytes 86024 | tf_op jit(solution)/shard_map/ppermute | solution.py:21
  37.7 3.6 %collective-permute-done.12 = bf16[1,112,128]{2,1,0:T(8,128)(2,1)S(1)} collective-permute-done((bf16[1,112,128]{2,1,0:T(8,128)(2,1)S(1)}, bf16[1,112,128]{2,1,0:T(8,128)(2,1)S(1)}, u32[]{:S(2)}, u32[]{:S(2)}) %collective-permute-start.12) | collective-permute-done | bytes 28704 | tf_op jit(solution)/shard_map/ppermute | solution.py:21
  41.4 1.4 %collective-permute-start.21 = (bf16[4,112,128]{2,1,0:T(8,128)(2,1)S(1)}, bf16[4,112,128]{2,1,0:T(8,128)(2,1)S(1)}, u32[]{:S(2)}, u32[]{:S(2)}) collective-permute-start(bf16[4,112,128]{2,1,0:T(8,128)(2,1)S(1)} %get-tuple-element.35), channel_id=1, source_target_pairs={{3,0},{0,1},{1,2},{2,3},{7,4},{4,5},{5,6},{6,7},{11,8},{8,9},{9,10... | collective-permute-start | bytes 344072 | tf_op jit(solution)/shard_map/ppermute | solution.py:21
  42.8 1.5 %collective-permute-start.19 = (bf16[4,112,128]{2,1,0:T(8,128)(2,1)S(1)}, bf16[4,112,128]{2,1,0:T(8,128)(2,1)S(1)}, u32[]{:S(2)}, u32[]{:S(2)}) collective-permute-start(bf16[4,112,128]{2,1,0:T(8,128)(2,1)S(1)} %get-tuple-element.35), channel_id=1, source_target_pairs={{1,0},{2,1},{3,2},{0,3},{5,4},{6,5},{7,6},{4,7},{9,8},{10,9},{11,1... | collective-permute-start | bytes 344072 | tf_op jit(solution)/shard_map/ppermute | solution.py:21
  44.3 2.7 %collective-permute-start.13 = (bf16[4,112,128]{2,1,0:T(8,128)(2,1)S(1)}, bf16[4,112,128]{2,1,0:T(8,128)(2,1)S(1)}, u32[]{:S(2)}, u32[]{:S(2)}) collective-permute-start(bf16[4,112,128]{2,1,0:T(8,128)(2,1)S(1)} %get-tuple-element.34), channel_id=1, source_target_pairs={{64,0},{128,64},{192,128},{0,192},{65,1},{129,65},{193,129},{1,193... | collective-permute-start | bytes 344072 | tf_op jit(solution)/shard_map/ppermute | solution.py:21
  47.1 2.8 %collective-permute-start.20 = (bf16[2,112,128]{2,1,0:T(8,128)(2,1)S(1)}, bf16[2,112,128]{2,1,0:T(8,128)(2,1)S(1)}, u32[]{:S(2)}, u32[]{:S(2)}) collective-permute-start(bf16[2,112,128]{2,1,0:T(8,128)(2,1)S(1)} %slice.54), channel_id=1, source_target_pairs={{1,0},{2,1},{3,2},{0,3},{5,4},{6,5},{7,6},{4,7},{9,8},{10,9},{11,1... | collective-permute-start | bytes 172040 | tf_op jit(solution)/shard_map/ppermute | solution.py:21
  50.0 2.7 %collective-permute-start.14 = (bf16[2,112,128]{2,1,0:T(8,128)(2,1)S(1)}, bf16[2,112,128]{2,1,0:T(8,128)(2,1)S(1)}, u32[]{:S(2)}, u32[]{:S(2)}) collective-permute-start(bf16[2,112,128]{2,1,0:T(8,128)(2,1)S(1)} %slice.51), channel_id=1, source_target_pairs={{64,0},{128,64},{192,128},{0,192},{65,1},{129,65},{193,129},{1,193... | collective-permute-start | bytes 172040 | tf_op jit(solution)/shard_map/ppermute | solution.py:21
  52.9 2.7 %collective-permute-start.23 = (bf16[4,4,112,128]{3,2,1,0:T(8,128)(2,1)S(1)}, bf16[4,4,112,128]{3,2,1,0:T(8,128)(2,1)S(1)}, u32[]{:S(2)}, u32[]{:S(2)}) collective-permute-start(bf16[4,4,112,128]{3,2,1,0:T(8,128)(2,1)S(1)} %pad_maximum_fusion.1.two), channel_id=1, source_target_pairs={{64,0},{128,64},{192,128},{0,192},{65,1},{129,65},{193,129},{1,193... | collective-permute-start | bytes 1376264 | tf_op jit(solution)/shard_map/ppermute | solution.py:21
  55.8 2.7 %collective-permute-start.17 = (bf16[4,4,112,128]{3,2,1,0:T(8,128)(2,1)S(1)}, bf16[4,4,112,128]{3,2,1,0:T(8,128)(2,1)S(1)}, u32[]{:S(2)}, u32[]{:S(2)}) collective-permute-start(bf16[4,4,112,128]{3,2,1,0:T(8,128)(2,1)S(1)} %pad_maximum_fusion.one), channel_id=1, source_target_pairs={{1,0},{2,1},{3,2},{0,3},{5,4},{6,5},{7,6},{4,7},{9,8},{10,9},{11,1... | collective-permute-start | bytes 1376264 | tf_op jit(solution)/shard_map/ppermute | solution.py:21
  59.4 2.6 %collective-permute-done.24.before2 = bf16[4,4,112,128]{3,2,1,0:T(8,128)(2,1)S(1)} collective-permute-done((bf16[4,4,112,128]{3,2,1,0:T(8,128)(2,1)S(1)}, bf16[4,4,112,128]{3,2,1,0:T(8,128)(2,1)S(1)}, u32[]{:S(2)}, u32[]{:S(2)}) %collective-permute-start.24) | collective-permute-done | bytes 458784 | tf_op jit(solution)/shard_map/ppermute | solution.py:21
  62.0 2.2 %collective-permute-done.18.before1 = bf16[4,4,112,128]{3,2,1,0:T(8,128)(2,1)S(1)} collective-permute-done((bf16[4,4,112,128]{3,2,1,0:T(8,128)(2,1)S(1)}, bf16[4,4,112,128]{3,2,1,0:T(8,128)(2,1)S(1)}, u32[]{:S(2)}, u32[]{:S(2)}) %collective-permute-start.18) | collective-permute-done | bytes 458784 | tf_op jit(solution)/shard_map/ppermute | solution.py:21
  64.4 3.0 %collective-permute-start.25 = (bf16[2,4,112,128]{3,2,1,0:T(8,128)(2,1)S(1)}, bf16[2,4,112,128]{3,2,1,0:T(8,128)(2,1)S(1)}, u32[]{:S(2)}, u32[]{:S(2)}) collective-permute-start(bf16[2,4,112,128]{3,2,1,0:T(8,128)(2,1)S(1)} %slice.44), channel_id=1, source_target_pairs={{1,0},{2,1},{3,2},{0,3},{5,4},{6,5},{7,6},{4,7},{9,8},{10,9},{11,1... | collective-permute-start | bytes 688136 | tf_op jit(solution)/shard_map/ppermute | solution.py:21
  68.9 2.0 %shard_map.40.start = f32[2,512,768]{2,1,0:T(8,128)S(1)} custom-call(bf16[4,4,112,128]{3,2,1,0:T(8,128)(2,1)S(1)} %collective-permute-done.17.after1, bf16[4,4,112,128]{3,2,1,0:T(8,128)(2,1)S(1)} %collective-permute-done.18.before1, bf16[4,4,112,128]{3,2,1,0:T(8,128)(2,1)S(1)} %collective-permute-done.23.after2, ...), custom_call_target="tpu_custom_call", output_to_operand_aliasing={{}: (5, {})} | custom-call | flops 1000000000 | bytes 2097152 | tf_op jit(solution)/shard_map/pallas_call | solution.py:106
  70.9 1.9 %collective-permute-done.25.low1 = bf16[2,4,112,128]{3,2,1,0:T(8,128)(2,1)S(1)} collective-permute-done((bf16[2,4,112,128]{3,2,1,0:T(8,128)(2,1)S(1)}, bf16[2,4,112,128]{3,2,1,0:T(8,128)(2,1)S(1)}, u32[]{:S(2)}, u32[]{:S(2)}) %collective-permute-start.25) | collective-permute-done | bytes 229408 | tf_op jit(solution)/shard_map/ppermute | solution.py:21
  72.8 2.5 %collective-permute-done.26.high1 = bf16[2,4,112,128]{3,2,1,0:T(8,128)(2,1)S(1)} collective-permute-done((bf16[2,4,112,128]{3,2,1,0:T(8,128)(2,1)S(1)}, bf16[2,4,112,128]{3,2,1,0:T(8,128)(2,1)S(1)}, u32[]{:S(2)}, u32[]{:S(2)}) %collective-permute-start.26) | collective-permute-done | bytes 229408 | tf_op jit(solution)/shard_map/ppermute | solution.py:21
  75.3 1.5 %shard_map.41 = (bf16[4,2,128,384]{3,2,1,0:T(8,128)(2,1)S(1)}, bf16[4,2,128,384]{3,2,1,0:T(8,128)(2,1)S(1)}) custom-call(s32[4]{0:T(128)S(1)} %pad_add_fusion.place, bf16[2,4,112,128]{3,2,1,0:T(8,128)(2,1)S(1)} %collective-permute-done.25.low1, bf16[2,4,112,128]{3,2,1,0:T(8,128)(2,1)S(1)} %collective-permute-done.26.high1, ...), custom_call_target="tpu_custom_call" | custom-call | flops 1000000000 | bytes 2097152 | tf_op jit(solution)/shard_map/pallas_call | solution.py:106
  76.9 12.9 %collective-permute-start.29 = (bf16[1024,384]{1,0:T(8,128)(2,1)S(1)}, bf16[1024,384]{1,0:T(8,128)(2,1)S(1)}, u32[]{:S(2)}, u32[]{:S(2)}) collective-permute-start(bf16[1024,384]{1,0:T(8,128)(2,1)S(1)} %bitcast.48), channel_id=1, source_target_pairs={{16,0},{0,16},{17,1},{1,17},{18,2},{2,18},{19,3},{3,19},{20,4},{4,... | collective-permute-start | bytes 2359304 | tf_op jit(solution)/shard_map/ppermute | solution.py:21
  89.8 1.4 %shard_map.42.given = bf16[2048,384]{1,0:T(8,128)(2,1)} custom-call(s32[4]{0:T(128)S(1)} %pad_add_fusion.place, bf16[1024,384]{1,0:T(8,128)(2,1)S(1)} %bitcast.47), custom_call_target="tpu_custom_call" | custom-call | bytes 2097152 | tf_op jit(solution)/shard_map/pallas_call | solution.py:106
  91.7 1.4 %shard_map.43 = bf16[2048,384]{1,0:T(8,128)(2,1)} custom-call(s32[4]{0:T(128)S(1)} %pad_add_fusion.place, bf16[1024,384]{1,0:T(8,128)(2,1)S(1)} %collective-permute-done.29.block, bf16[2048,384]{1,0:T(8,128)(2,1)} %shard_map.42.given), custom_call_target="tpu_custom_call", output_to_operand_aliasing={{}: (2, {})} | custom-call | bytes 2097152 | tf_op jit(solution)/shard_map/pallas_call | solution.py:106
  (68 shorter events, 12.0 us)
Async XLA Ops:
  0.1 1.0 %copy-start.1 = (bf16[112,2048]{1,0:T(8,128)(2,1)S(1)}, bf16[112,2048]{1,0:T(8,128)(2,1)}, u32[]{:S(2)}) copy-start(bf16[112,2048]{1,0:T(8,128)(2,1)} %panel.1) | copy-start | bytes 1376260
  1.8 22.2 %copy-start = (bf16[1792,384]{1,0:T(8,128)(2,1)S(1)}, bf16[1792,384]{1,0:T(8,128)(2,1)}, u32[]{:S(2)}) copy-start(bf16[1792,384]{1,0:T(8,128)(2,1)} %own) | copy-start | bytes 4128772
  3.2 4.9 %collective-permute-start = (f32[8,112,128]{2,1,0:T(8,128)S(1)}, f32[8,112,128]{2,1,0:T(8,128)}, u32[]{:S(2)}, u32[]{:S(2)}) collective-permute-start(f32[8,112,128]{2,1,0:T(8,128)S(1)} %get-tuple-element.20), channel_id=1, source_target_pairs={{16,0},{0,16},{17,1},{1,17},{18,2},{2,18},{19,3},{3,19},{20,4},{4,... | collective-permute-start | bytes 1376264 | tf_op jit(solution)/shard_map/ppermute | solution.py:21
  8.1 15.9 %collective-permute-start.6 = (bf16[1792,384]{1,0:T(8,128)(2,1)}, bf16[1792,384]{1,0:T(8,128)(2,1)S(1)}, u32[]{:S(2)}, u32[]{:S(2)}) collective-permute-start(bf16[1792,384]{1,0:T(8,128)(2,1)} %own), channel_id=1, source_target_pairs={{16,0},{0,16},{17,1},{1,17},{18,2},{2,18},{19,3},{3,19},{20,4},{4,... | collective-permute-start | bytes 4128776 | tf_op jit(solution)/shard_map/ppermute | solution.py:21
  10.4 3.1 %collective-permute-start.1 = (bf16[2,112,128]{2,1,0:T(8,128)(2,1)S(1)}, bf16[2,112,128]{2,1,0:T(8,128)(2,1)S(1)}, u32[]{:S(2)}, u32[]{:S(2)}) collective-permute-start(bf16[2,112,128]{2,1,0:T(8,128)(2,1)S(1)} %get-tuple-element.37), channel_id=1, source_target_pairs={{64,0},{128,64},{192,128},{0,192},{65,1},{129,65},{193,129},{1,193... | collective-permute-start | bytes 172040 | tf_op jit(solution)/shard_map/ppermute | solution.py:21
  11.2 4.6 %collective-permute-start.3 = (bf16[2,112,128]{2,1,0:T(8,128)(2,1)S(1)}, bf16[2,112,128]{2,1,0:T(8,128)(2,1)S(1)}, u32[]{:S(2)}, u32[]{:S(2)}) collective-permute-start(bf16[2,112,128]{2,1,0:T(8,128)(2,1)S(1)} %get-tuple-element.38), channel_id=1, source_target_pairs={{128,0},{192,64},{0,128},{64,192},{129,1},{193,65},{1,129},{65,193... | collective-permute-start | bytes 172040 | tf_op jit(solution)/shard_map/ppermute | solution.py:21
  11.7 5.8 %collective-permute-start.2 = (bf16[2,112,128]{2,1,0:T(8,128)(2,1)S(1)}, bf16[2,112,128]{2,1,0:T(8,128)(2,1)S(1)}, u32[]{:S(2)}, u32[]{:S(2)}) collective-permute-start(bf16[2,112,128]{2,1,0:T(8,128)(2,1)S(1)} %get-tuple-element.39), channel_id=1, source_target_pairs={{192,0},{0,64},{64,128},{128,192},{193,1},{1,65},{65,129},{129,193... | collective-permute-start | bytes 172040 | tf_op jit(solution)/shard_map/ppermute | solution.py:21
  18.5 7.0 %collective-permute-start.5 = (bf16[2,112,128]{2,1,0:T(8,128)(2,1)S(1)}, bf16[2,112,128]{2,1,0:T(8,128)(2,1)S(1)}, u32[]{:S(2)}, u32[]{:S(2)}) collective-permute-start(bf16[2,112,128]{2,1,0:T(8,128)(2,1)S(1)} %fusion.2), channel_id=1, source_target_pairs={{44,0},{0,4},{4,8},{8,12},{12,32},{32,36},{36,40},{40,44},{45,1},{... | collective-permute-start | bytes 172040 | tf_op jit(solution)/shard_map/ppermute | solution.py:21
  20.0 5.5 %collective-permute-start.4 = (bf16[2,112,128]{2,1,0:T(8,128)(2,1)S(1)}, bf16[2,112,128]{2,1,0:T(8,128)(2,1)S(1)}, u32[]{:S(2)}, u32[]{:S(2)}) collective-permute-start(bf16[2,112,128]{2,1,0:T(8,128)(2,1)S(1)} %fusion.2), channel_id=1, source_target_pairs={{4,0},{8,4},{12,8},{32,12},{36,32},{40,36},{44,40},{0,44},{5,1},{9... | collective-permute-start | bytes 172040 | tf_op jit(solution)/shard_map/ppermute | solution.py:21
  25.5 4.0 %collective-permute-start.7 = (bf16[2,112,128]{2,1,0:T(8,128)(2,1)S(1)}, bf16[2,112,128]{2,1,0:T(8,128)(2,1)S(1)}, u32[]{:S(2)}, u32[]{:S(2)}) collective-permute-start(bf16[2,112,128]{2,1,0:T(8,128)(2,1)S(1)} %collective-permute-done.4), channel_id=1, source_target_pairs={{4,0},{8,4},{12,8},{32,12},{36,32},{40,36},{44,40},{0,44},{5,1},{9... | collective-permute-start | bytes 172040 | tf_op jit(solution)/shard_map/ppermute | solution.py:21
  28.2 4.2 %collective-permute-start.10 = (bf16[2,112,128]{2,1,0:T(8,128)(2,1)S(1)}, bf16[2,112,128]{2,1,0:T(8,128)(2,1)S(1)}, u32[]{:S(2)}, u32[]{:S(2)}) collective-permute-start(bf16[2,112,128]{2,1,0:T(8,128)(2,1)S(1)} %collective-permute-done.5), channel_id=1, source_target_pairs={{44,0},{0,4},{4,8},{8,12},{12,32},{32,36},{36,40},{40,44},{45,1},{... | collective-permute-start | bytes 172040 | tf_op jit(solution)/shard_map/ppermute | solution.py:21
  29.5 4.2 %collective-permute-start.8 = (bf16[2,112,128]{2,1,0:T(8,128)(2,1)S(1)}, bf16[2,112,128]{2,1,0:T(8,128)(2,1)S(1)}, u32[]{:S(2)}, u32[]{:S(2)}) collective-permute-start(bf16[2,112,128]{2,1,0:T(8,128)(2,1)S(1)} %collective-permute-done.7), channel_id=1, source_target_pairs={{4,0},{8,4},{12,8},{32,12},{36,32},{40,36},{44,40},{0,44},{5,1},{9... | collective-permute-start | bytes 172040 | tf_op jit(solution)/shard_map/ppermute | solution.py:21
  32.5 4.2 %collective-permute-start.11 = (bf16[2,112,128]{2,1,0:T(8,128)(2,1)S(1)}, bf16[2,112,128]{2,1,0:T(8,128)(2,1)S(1)}, u32[]{:S(2)}, u32[]{:S(2)}) collective-permute-start(bf16[2,112,128]{2,1,0:T(8,128)(2,1)S(1)} %collective-permute-done.10), channel_id=1, source_target_pairs={{44,0},{0,4},{4,8},{8,12},{12,32},{32,36},{36,40},{40,44},{45,1},{... | collective-permute-start | bytes 172040 | tf_op jit(solution)/shard_map/ppermute | solution.py:21
  33.7 4.0 %collective-permute-start.9 = (bf16[1,112,128]{2,1,0:T(8,128)(2,1)S(1)}, bf16[1,112,128]{2,1,0:T(8,128)(2,1)S(1)}, u32[]{:S(2)}, u32[]{:S(2)}) collective-permute-start(bf16[1,112,128]{2,1,0:T(8,128)(2,1)S(1)} %slice.48), channel_id=1, source_target_pairs={{4,0},{8,4},{12,8},{32,12},{36,32},{40,36},{44,40},{0,44},{5,1},{9... | collective-permute-start | bytes 86024 | tf_op jit(solution)/shard_map/ppermute | solution.py:21
  36.7 4.5 %collective-permute-start.12 = (bf16[1,112,128]{2,1,0:T(8,128)(2,1)S(1)}, bf16[1,112,128]{2,1,0:T(8,128)(2,1)S(1)}, u32[]{:S(2)}, u32[]{:S(2)}) collective-permute-start(bf16[1,112,128]{2,1,0:T(8,128)(2,1)S(1)} %slice.49), channel_id=1, source_target_pairs={{44,0},{0,4},{4,8},{8,12},{12,32},{32,36},{36,40},{40,44},{45,1},{... | collective-permute-start | bytes 86024 | tf_op jit(solution)/shard_map/ppermute | solution.py:21
  41.4 5.6 %collective-permute-start.21 = (bf16[4,112,128]{2,1,0:T(8,128)(2,1)S(1)}, bf16[4,112,128]{2,1,0:T(8,128)(2,1)S(1)}, u32[]{:S(2)}, u32[]{:S(2)}) collective-permute-start(bf16[4,112,128]{2,1,0:T(8,128)(2,1)S(1)} %get-tuple-element.35), channel_id=1, source_target_pairs={{3,0},{0,1},{1,2},{2,3},{7,4},{4,5},{5,6},{6,7},{11,8},{8,9},{9,10... | collective-permute-start | bytes 344072 | tf_op jit(solution)/shard_map/ppermute | solution.py:21
  42.8 4.3 %collective-permute-start.19 = (bf16[4,112,128]{2,1,0:T(8,128)(2,1)S(1)}, bf16[4,112,128]{2,1,0:T(8,128)(2,1)S(1)}, u32[]{:S(2)}, u32[]{:S(2)}) collective-permute-start(bf16[4,112,128]{2,1,0:T(8,128)(2,1)S(1)} %get-tuple-element.35), channel_id=1, source_target_pairs={{1,0},{2,1},{3,2},{0,3},{5,4},{6,5},{7,6},{4,7},{9,8},{10,9},{11,1... | collective-permute-start | bytes 344072 | tf_op jit(solution)/shard_map/ppermute | solution.py:21
  44.3 5.6 %collective-permute-start.15 = (bf16[4,112,128]{2,1,0:T(8,128)(2,1)S(1)}, bf16[4,112,128]{2,1,0:T(8,128)(2,1)S(1)}, u32[]{:S(2)}, u32[]{:S(2)}) collective-permute-start(bf16[4,112,128]{2,1,0:T(8,128)(2,1)S(1)} %get-tuple-element.34), channel_id=1, source_target_pairs={{192,0},{0,64},{64,128},{128,192},{193,1},{1,65},{65,129},{129,193... | collective-permute-start | bytes 344072 | tf_op jit(solution)/shard_map/ppermute | solution.py:21
  44.3 5.7 %collective-permute-start.13 = (bf16[4,112,128]{2,1,0:T(8,128)(2,1)S(1)}, bf16[4,112,128]{2,1,0:T(8,128)(2,1)S(1)}, u32[]{:S(2)}, u32[]{:S(2)}) collective-permute-start(bf16[4,112,128]{2,1,0:T(8,128)(2,1)S(1)} %get-tuple-element.34), channel_id=1, source_target_pairs={{64,0},{128,64},{192,128},{0,192},{65,1},{129,65},{193,129},{1,193... | collective-permute-start | bytes 344072 | tf_op jit(solution)/shard_map/ppermute | solution.py:21
  47.0 5.7 %collective-permute-start.22 = (bf16[2,112,128]{2,1,0:T(8,128)(2,1)S(1)}, bf16[2,112,128]{2,1,0:T(8,128)(2,1)S(1)}, u32[]{:S(2)}, u32[]{:S(2)}) collective-permute-start(bf16[2,112,128]{2,1,0:T(8,128)(2,1)S(1)} %slice.55), channel_id=1, source_target_pairs={{3,0},{0,1},{1,2},{2,3},{7,4},{4,5},{5,6},{6,7},{11,8},{8,9},{9,10... | collective-permute-start | bytes 172040 | tf_op jit(solution)/shard_map/ppermute | solution.py:21
  47.1 5.6 %collective-permute-start.20 = (bf16[2,112,128]{2,1,0:T(8,128)(2,1)S(1)}, bf16[2,112,128]{2,1,0:T(8,128)(2,1)S(1)}, u32[]{:S(2)}, u32[]{:S(2)}) collective-permute-start(bf16[2,112,128]{2,1,0:T(8,128)(2,1)S(1)} %slice.54), channel_id=1, source_target_pairs={{1,0},{2,1},{3,2},{0,3},{5,4},{6,5},{7,6},{4,7},{9,8},{10,9},{11,1... | collective-permute-start | bytes 172040 | tf_op jit(solution)/shard_map/ppermute | solution.py:21
  49.9 5.7 %collective-permute-start.16 = (bf16[2,112,128]{2,1,0:T(8,128)(2,1)S(1)}, bf16[2,112,128]{2,1,0:T(8,128)(2,1)S(1)}, u32[]{:S(2)}, u32[]{:S(2)}) collective-permute-start(bf16[2,112,128]{2,1,0:T(8,128)(2,1)S(1)} %slice.52), channel_id=1, source_target_pairs={{192,0},{0,64},{64,128},{128,192},{193,1},{1,65},{65,129},{129,193... | collective-permute-start | bytes 172040 | tf_op jit(solution)/shard_map/ppermute | solution.py:21
  50.0 5.6 %collective-permute-start.14 = (bf16[2,112,128]{2,1,0:T(8,128)(2,1)S(1)}, bf16[2,112,128]{2,1,0:T(8,128)(2,1)S(1)}, u32[]{:S(2)}, u32[]{:S(2)}) collective-permute-start(bf16[2,112,128]{2,1,0:T(8,128)(2,1)S(1)} %slice.51), channel_id=1, source_target_pairs={{64,0},{128,64},{192,128},{0,192},{65,1},{129,65},{193,129},{1,193... | collective-permute-start | bytes 172040 | tf_op jit(solution)/shard_map/ppermute | solution.py:21
  52.8 9.2 %collective-permute-start.24 = (bf16[4,4,112,128]{3,2,1,0:T(8,128)(2,1)S(1)}, bf16[4,4,112,128]{3,2,1,0:T(8,128)(2,1)S(1)}, u32[]{:S(2)}, u32[]{:S(2)}) collective-permute-start(bf16[4,4,112,128]{3,2,1,0:T(8,128)(2,1)S(1)} %pad_maximum_fusion.1.two), channel_id=1, source_target_pairs={{192,0},{0,64},{64,128},{128,192},{193,1},{1,65},{65,129},{129,193... | collective-permute-start | bytes 1376264 | tf_op jit(solution)/shard_map/ppermute | solution.py:21
  52.9 9.1 %collective-permute-start.23 = (bf16[4,4,112,128]{3,2,1,0:T(8,128)(2,1)S(1)}, bf16[4,4,112,128]{3,2,1,0:T(8,128)(2,1)S(1)}, u32[]{:S(2)}, u32[]{:S(2)}) collective-permute-start(bf16[4,4,112,128]{3,2,1,0:T(8,128)(2,1)S(1)} %pad_maximum_fusion.1.two), channel_id=1, source_target_pairs={{64,0},{128,64},{192,128},{0,192},{65,1},{129,65},{193,129},{1,193... | collective-permute-start | bytes 1376264 | tf_op jit(solution)/shard_map/ppermute | solution.py:21
  55.7 8.6 %collective-permute-start.18 = (bf16[4,4,112,128]{3,2,1,0:T(8,128)(2,1)S(1)}, bf16[4,4,112,128]{3,2,1,0:T(8,128)(2,1)S(1)}, u32[]{:S(2)}, u32[]{:S(2)}) collective-permute-start(bf16[4,4,112,128]{3,2,1,0:T(8,128)(2,1)S(1)} %pad_maximum_fusion.one), channel_id=1, source_target_pairs={{3,0},{0,1},{1,2},{2,3},{7,4},{4,5},{5,6},{6,7},{11,8},{8,9},{9,10... | collective-permute-start | bytes 1376264 | tf_op jit(solution)/shard_map/ppermute | solution.py:21
  55.8 8.5 %collective-permute-start.17 = (bf16[4,4,112,128]{3,2,1,0:T(8,128)(2,1)S(1)}, bf16[4,4,112,128]{3,2,1,0:T(8,128)(2,1)S(1)}, u32[]{:S(2)}, u32[]{:S(2)}) collective-permute-start(bf16[4,4,112,128]{3,2,1,0:T(8,128)(2,1)S(1)} %pad_maximum_fusion.one), channel_id=1, source_target_pairs={{1,0},{2,1},{3,2},{0,3},{5,4},{6,5},{7,6},{4,7},{9,8},{10,9},{11,1... | collective-permute-start | bytes 1376264 | tf_op jit(solution)/shard_map/ppermute | solution.py:21
  64.4 8.5 %collective-permute-start.25 = (bf16[2,4,112,128]{3,2,1,0:T(8,128)(2,1)S(1)}, bf16[2,4,112,128]{3,2,1,0:T(8,128)(2,1)S(1)}, u32[]{:S(2)}, u32[]{:S(2)}) collective-permute-start(bf16[2,4,112,128]{3,2,1,0:T(8,128)(2,1)S(1)} %slice.44), channel_id=1, source_target_pairs={{1,0},{2,1},{3,2},{0,3},{5,4},{6,5},{7,6},{4,7},{9,8},{10,9},{11,1... | collective-permute-start | bytes 688136 | tf_op jit(solution)/shard_map/ppermute | solution.py:21
  67.4 7.9 %collective-permute-start.26 = (bf16[2,4,112,128]{3,2,1,0:T(8,128)(2,1)S(1)}, bf16[2,4,112,128]{3,2,1,0:T(8,128)(2,1)S(1)}, u32[]{:S(2)}, u32[]{:S(2)}) collective-permute-start(bf16[2,4,112,128]{3,2,1,0:T(8,128)(2,1)S(1)} %slice.45), channel_id=1, source_target_pairs={{3,0},{0,1},{1,2},{2,3},{7,4},{4,5},{5,6},{6,7},{11,8},{8,9},{9,10... | collective-permute-start | bytes 688136 | tf_op jit(solution)/shard_map/ppermute | solution.py:21
  67.4 7.9 %collective-permute-start.27 = (bf16[2,4,112,128]{3,2,1,0:T(8,128)(2,1)S(1)}, bf16[2,4,112,128]{3,2,1,0:T(8,128)(2,1)S(1)}, u32[]{:S(2)}, u32[]{:S(2)}) collective-permute-start(bf16[2,4,112,128]{3,2,1,0:T(8,128)(2,1)S(1)} %slice.46), channel_id=1, source_target_pairs={{64,0},{128,64},{192,128},{0,192},{65,1},{129,65},{193,129},{1,193... | collective-permute-start | bytes 688136 | tf_op jit(solution)/shard_map/ppermute | solution.py:21
  68.5 6.8 %collective-permute-start.28 = (bf16[2,4,112,128]{3,2,1,0:T(8,128)(2,1)S(1)}, bf16[2,4,112,128]{3,2,1,0:T(8,128)(2,1)S(1)}, u32[]{:S(2)}, u32[]{:S(2)}) collective-permute-start(bf16[2,4,112,128]{3,2,1,0:T(8,128)(2,1)S(1)} %slice.47), channel_id=1, source_target_pairs={{192,0},{0,64},{64,128},{128,192},{193,1},{1,65},{65,129},{129,193... | collective-permute-start | bytes 688136 | tf_op jit(solution)/shard_map/ppermute | solution.py:21
  76.9 14.8 %collective-permute-start.29 = (bf16[1024,384]{1,0:T(8,128)(2,1)S(1)}, bf16[1024,384]{1,0:T(8,128)(2,1)S(1)}, u32[]{:S(2)}, u32[]{:S(2)}) collective-permute-start(bf16[1024,384]{1,0:T(8,128)(2,1)S(1)} %bitcast.48), channel_id=1, source_target_pairs={{16,0},{0,16},{17,1},{1,17},{18,2},{2,18},{19,3},{3,19},{20,4},{4,... | collective-permute-start | bytes 2359304 | tf_op jit(solution)/shard_map/ppermute | solution.py:21
  (2 other events, 1.5 us)

commit v3 on v0

v3 whole, which is shorter than its diff:
```python
import itertools

import jax
import jax.numpy as jnp
from jax import lax
from jax.experimental import pallas as pl
from jax.experimental.pallas import tpu as pltpu
from jax.sharding import Mesh, PartitionSpec as P

ROW = ("x", "z_hi", "core")
COL = ("z_lo", "y")
Z = ("z_hi", "z_lo")
BF16 = jnp.bfloat16
F32 = jnp.float32
VMEM = pl.BlockSpec(memory_space=pltpu.VMEM)
SMEM = pl.BlockSpec(memory_space=pltpu.SMEM)
ANY = pl.BlockSpec(memory_space=pl.ANY)
PARAMS = pltpu.CompilerParams(vmem_limit_bytes=24 * 2**20)


def fetch(block, axis, size, ahead):
    return lax.ppermute(block, axis, [((i + ahead) % size, i) for i in range(size)])


def swap(block, axis, size, bits):
    return lax.ppermute(block, axis, [(i ^ bits, i) for i in range(size)])


def turn(block, order, ahead):
    pairs = []
    for x, z_hi, core, z_lo, y in itertools.product(*map(range, (4, 2, 2, 4, 4))):
        along_x = core == order
        source = ((x + ahead) % 4, y) if along_x else (x, (y + ahead) % 4)
        place = [((p * 2 + z_hi) * 2 + core) * 16 + z_lo * 4 + q for p, q in (source, (x, y))]
        pairs.append(tuple(place))
    return lax.ppermute(block, ROW + COL, pairs)


def dot_t(left, right):
    return lax.dot_general(left, right, (((0,), (0,)), ((), ())), preferred_element_type=F32)


def partial_sums(place, screening, panel, keep, send):
    core = place[2]
    for out, base in ((send, 1 - core), (keep, core)):
        for slab in range(8):
            columns = pl.ds(pl.multiple_of(base * 1024 + slab * 128, 128), 128)
            out[slab] = dot_t(screening[...], panel[:, columns])


def add_cores(place, keep, received, mine, *away):
    for back in range(4):
        for half in range(2):
            slab = lax.rem(place[0] + 4 - back, 4) * 2 + half
            total = keep[slab] + received[slab]
            if back:
                away[back - 1][half] = total.astype(BF16)
            else:
                mine[half] = total


def order_pairs(place, own, other, both):
    for k in range(4):
        for j in range(4):
            y, z_lo = lax.rem(place[1] + k, 4), place[3] ^ j
            rows = pl.ds(pl.multiple_of((z_lo * 4 + y) * 112, 16), 112)
            both[k, pl.ds(j * 112, 112), :384] = own[rows]
            both[k, pl.ds(j * 112, 112), 384:] = other[rows]


def on_core(place, core):
    return pl.when(place[2] == core)


def by_x(*slabs):
    return jnp.concatenate([slab[j].reshape(448, 128) for slab in slabs for j in range(2)], 1)


def by_y(*slabs):
    halves = [jnp.concatenate([slab[j].reshape(448, 128) for slab in slabs]) for j in range(2)]
    return jnp.concatenate(halves, 1)


def product_one(place, three, far, both, out):
    @on_core(place, 0)
    def _():
        out[:512] = dot_t(by_x(three[0], three[1]), both[0])
        out[512:] = dot_t(by_x(far, three[2]), both[0])

    @on_core(place, 1)
    def _():
        left = by_y(three[0], three[1], far, three[2])
        out[:256] = dot_t(left, both[...].reshape(1792, 768))


def product_two(place, after, after2, before, before2, both, start, out):
    @on_core(place, 0)
    def _():
        out[:512] = (
            start[:512]
            + dot_t(by_x(after[0], after[1]), both[1])
            + dot_t(by_x(before[0], before[1]), both[3])
        )
        out[512:] = (
            start[512:]
            + dot_t(by_x(after2, after[2]), both[1])
            + dot_t(by_x(before2, before[2]), both[3])
        )

    @on_core(place, 1)
    def _():
        right = both[...].reshape(1792, 768)
        out[:256] = start[:256]
        out[256:512] = dot_t(by_y(after[0], after[1], after2, after[2]), right)
        out[768:] = dot_t(by_y(before[0], before[1], before2, before[2]), right)


def product_three(place, low, both, start, mine, theirs):
    def keep(total):
        mine[...] = total[:, :384].astype(BF16)
        theirs[...] = total[:, 384:].astype(BF16)

    @on_core(place, 0)
    def _():
        keep(start[:512] + dot_t(by_x(low[0], low[1]), both[2]))

    @on_core(place, 1)
    def _():
        keep(start[:512])


def product_four(place, low, far2, far3, both, start, mine, theirs):
    def keep(rows, total):
        mine[rows] = total[:, :384].astype(BF16)
        theirs[rows] = total[:, 384:].astype(BF16)

    @on_core(place, 0)
    def _():
        keep(pl.ds(0, 512), start[512:] + dot_t(by_x(far2, far3), both[2]))

    @on_core(place, 1)
    def _():
        left = by_y(low[0], low[1], far2, far3)
        keep(pl.ds(0, 256), dot_t(left, both[...].reshape(1792, 768)))
        keep(pl.ds(256, 256), start[768:])


def place_rows(place, parts, out, sems):
    copies = []
    for block, core, first in parts:
        for i in range(2):
            row = core * 1024 + lax.rem(place[0] + first + i, 4) * 256
            rows = pl.ds(pl.multiple_of(row, 256), 256)
            sem = sems.at[len(copies)]
            copies.append(pltpu.make_async_copy(block.at[pl.ds(i * 256, 256)], out.at[rows], sem))
    for copy in copies:
        copy.start()
    for copy in copies:
        copy.wait()


def place_first(place, mine1, mine2, theirs1, out, sems):
    core = place[2]
    place_rows(place, [(mine1, core, 0), (mine2, core, 2), (theirs1, 1 - core, 0)], out, sems)


def place_last(place, theirs2, given, out, sems):
    place_rows(place, [(theirs2, 1 - place[2], 2)], out, sems)


def call(kernel, out_shape, operands, out_specs=VMEM, specs=None, flops=0, **more):
    return pl.pallas_call(
        kernel,
        out_shape=out_shape,
        in_specs=specs or [SMEM] + [VMEM] * (len(operands) - 1),
        out_specs=out_specs,
        compiler_params=PARAMS,
        cost_estimate=pl.CostEstimate(flops=flops, bytes_accessed=2**21, transcendentals=0),
        **more,
    )(*operands)


def per_device(pair_valence, screening, pair_conduction):
    x, y, core, z_lo = (lax.axis_index(axis) for axis in ("x", "y", "core", "z_lo"))
    place = jnp.stack([x, y, core, z_lo]).astype(jnp.int32)

    slabs = jax.ShapeDtypeStruct((8, 112, 128), F32)
    keep, send = call(partial_sums, (slabs, slabs), (place, screening, pair_valence), (VMEM, VMEM))
    two = jax.ShapeDtypeStruct((2, 112, 128), F32)
    sent = jax.ShapeDtypeStruct((2, 112, 128), BF16)
    part, *away = call(
        add_cores,
        (two, sent, sent, sent),
        (place, keep, fetch(send, "core", 2, 1)),
        (VMEM,) * 4,
    )
    for ahead in (1, 3, 2):
        part = part + fetch(away[ahead - 1], "x", 4, ahead).astype(F32)

    other = fetch(pair_conduction, "core", 2, 1)
    both = call(
        order_pairs, jax.ShapeDtypeStruct((4, 448, 768), BF16), (place, pair_conduction, other)
    )

    share, both = lax.optimization_barrier((swap(part.astype(BF16), "z_hi", 2, 1), both))
    part = (part + share.astype(F32)).astype(BF16)
    own = jnp.stack([part] + [swap(part, "z_lo", 4, bits) for bits in (1, 2, 3)], 1)

    after, before = turn(own, 0, 1), turn(own, 0, 3)
    three = jnp.stack([own, after, before])
    far = jnp.concatenate([turn(after[:1], 0, 1), turn(before[1:], 0, 3)])
    after, before = turn(three, 1, 1), turn(three, 1, 3)
    after2, before2 = turn(far, 1, 1), turn(far, 1, 3)
    total = jax.ShapeDtypeStruct((1024, 768), F32)
    total_one = call(product_one, total, (place, three, far, both), flops=10**9)
    after, before, total_one = lax.optimization_barrier((after, before, total_one))
    low = turn(after[:2], 1, 1)
    far3 = turn(before[2], 1, 3)
    far2 = turn(before2, 1, 3)
    total_two = call(
        product_two,
        total,
        (place, after, after2, before, before2, both, total_one),
        flops=10**9,
        input_output_aliases={6: 0},
    )
    half = jax.ShapeDtypeStruct((512, 384), BF16)
    mine1, theirs1 = call(
        product_three, (half, half), (place, low, both, total_two), (VMEM, VMEM), flops=10**9
    )
    theirs1 = fetch(theirs1, "core", 2, 1)
    mine2, theirs2 = call(
        product_four,
        (half, half),
        (place, low, far2, far3, both, total_two),
        (VMEM, VMEM),
        flops=10**9,
    )
    theirs2 = fetch(theirs2, "core", 2, 1)

    out = jax.ShapeDtypeStruct((2048, 384), BF16)
    sems = dict(scratch_shapes=[pltpu.SemaphoreType.DMA((6,))])
    kernel = call(place_first, out, (place, mine1, mine2, theirs1), ANY, **sems)
    return call(
        place_last,
        out,
        (place, theirs2, kernel),
        ANY,
        [SMEM, VMEM, ANY],
        input_output_aliases={2: 0},
        **sems,
    )


def solution(mesh):
    fine = Mesh(mesh.devices.reshape(4, 2, 2, 4, 4), ROW + COL)
    placed = (P(ROW, None), P(ROW, COL), P(None, ROW + COL))
    return jax.shard_map(
        per_device, mesh=fine, in_specs=placed, out_specs=P(None, ROW + COL), check_vma=False
    )
```

time: 266 us -> 80.4 us (0.30)
  waiting for transfers between devices: 197 us -> 33 us
  blocking collectives: 40.2 us -> 0 us
  starting transfers between devices: 0.04 us -> 33.4 us
  between operations: 13.4 us -> 0.32 us
  Pallas kernels: 0 us -> 11.4 us
  matrix products: 11.3 us -> 0 us
    all_gather x2 -> x0, waiting for transfers between devices: 197 us -> none  [the longest x1 98.4 us: per_device(): lax.all_gather(pair_valence, 'row', axis=0, tiled=True)]
    all_gather x1 -> x0, blocking collectives: 40.2 us -> none  [per_device(): row_panel = lax.all_gather(screening, 'col', axis=1, tiled=True)]
    ppermute x0 -> x22, starting transfers between devices: none -> 33.4 us  [the longest x7 15.5 us: fetch(): lax.ppermute(block, axis, [((i + ahead) % size, i) for i in range(size)])]
    ppermute x0 -> x22, waiting for transfers between devices: none -> 33 us  [the longest x11 22.1 us: turn(): return lax.ppermute(block, ROW + COL, pairs)]
    pallas_call x0 -> x9, Pallas kernels: none -> 11.4 us  [call(): pl.pallas_call(kernel, out_shape=out_shape, in_specs=specs or [SMEM] + [V...]
    dot_general x1 -> x0, matrix products: 11.3 us -> none  [per_device(): lax.dot_general(lax.all_gather(pair_valence, 'row', axis=0, tiled=True),...]
  transfers between devices with their start and end apart: 2 -> 22, of which waited for: 2 -> 17; matrix products, arithmetic and copies ran while one was open for 0% -> 0% of each run, Pallas kernels for 0% -> 12%
where the time goes in v3:
time: 80.4 us; the launch traced here: 80.2 us
  starting transfers between devices  33.4 us (42%)
  waiting for transfers between devices  33 us (41%)
  Pallas kernels  11.4 us (14%)
  local copies, waits for them, and re-layouts  1.86 us (2%)
    ppermute x11, waiting for transfers between devices, turn(): return lax.ppermute(block, ROW + COL, pairs)  22.1 us
    ppermute x7, starting transfers between devices, fetch(): lax.ppermute(block, axis, [((i + ahead) % size, i) for i in range(size)])  15.5 us
    pallas_call x9, Pallas kernels, call(): pl.pallas_call(kernel, out_shape=out_shape, in_specs=specs or [SMEM] + [V...  11.4 us
    ppermute x4, starting transfers between devices, swap(): return lax.ppermute(block, axis, [(i ^ bits, i) for i in range(size)])  11.1 us
    ppermute x11, starting transfers between devices, turn(): return lax.ppermute(block, ROW + COL, pairs)  6.82 us
    ppermute x7, waiting for transfers between devices, fetch(): lax.ppermute(block, axis, [((i + ahead) % size, i) for i in range(size)])  5.44 us
    ppermute x4, waiting for transfers between devices, swap(): return lax.ppermute(block, axis, [(i ^ bits, i) for i in range(size)])  5.41 us
    unnamed x7, local copies, waits for them, and re-layouts  1.78 us
  transfers between devices with their start and end apart: 22, of which 17 were waited for; matrix products, arithmetic and copies ran while one was open for 0% of the time, Pallas kernels for 12%

profile of v3, /device:TPU:1, one launch (start us, length us, event | category | flops | bytes accessed | tf_op | source)
XLA Modules:
  0.0 80.2 jit_solution(15346057877454689253)
XLA Ops:
  0.0 3.2 %collective-permute-start.5 = (bf16[1792,384]{1,0:T(8,128)(2,1)}, bf16[1792,384]{1,0:T(8,128)(2,1)S(1)}, u32[]{:S(2)}, u32[]{:S(2)}) collective-permute-start(bf16[1792,384]{1,0:T(8,128)(2,1)} %own.1), channel_id=1, source_target_pairs={{16,0},{0,16},{17,1},{1,17},{18,2},{2,18},{19,3},{3,19},{20,4},{4,... | collective-permute-start | bytes 4128776 | tf_op jit(solution)/shard_map/ppermute | solution.py:22
  3.3 1.0 %copy-done.1 = bf16[112,2048]{1,0:T(8,128)(2,1)S(1)} copy-done((bf16[112,2048]{1,0:T(8,128)(2,1)S(1)}, bf16[112,2048]{1,0:T(8,128)(2,1)}, u32[]{:S(2)}) %copy-start.1) | copy-done | bytes 458776
  5.1 1.0 %shard_map.37 = (f32[8,112,128]{2,1,0:T(8,128)S(1)}, f32[8,112,128]{2,1,0:T(8,128)S(1)}) custom-call(s32[4]{0:T(128)S(1)} %pad_add_fusion.place, bf16[112,112]{1,0:T(8,128)(2,1)S(1)} %copy-done.2, bf16[112,2048]{1,0:T(8,128)(2,1)S(1)} %copy-done.1), custom_call_target="tpu_custom_call" | custom-call | bytes 2097152 | tf_op jit(solution)/shard_map/pallas_call | solution.py:172
  6.2 1.7 %collective-permute-done.received = f32[8,112,128]{2,1,0:T(8,128)S(1)} collective-permute-done((f32[8,112,128]{2,1,0:T(8,128)S(1)}, f32[8,112,128]{2,1,0:T(8,128)S(1)}, u32[]{:S(2)}, u32[]{:S(2)}) %collective-permute-start) | collective-permute-done | bytes 458784 | tf_op jit(solution)/shard_map/ppermute | solution.py:22
  8.6 0.8 %collective-permute-start.1 = (bf16[2,112,128]{2,1,0:T(8,128)(2,1)S(1)}, bf16[2,112,128]{2,1,0:T(8,128)(2,1)S(1)}, u32[]{:S(2)}, u32[]{:S(2)}) collective-permute-start(bf16[2,112,128]{2,1,0:T(8,128)(2,1)S(1)} %get-tuple-element.23), channel_id=1, source_target_pairs={{64,0},{128,64},{192,128},{0,192},{65,1},{129,65},{193,129},{1,193... | collective-permute-start | bytes 172040 | tf_op jit(solution)/shard_map/ppermute | solution.py:22
  10.1 1.0 %collective-permute-start.3 = (bf16[2,112,128]{2,1,0:T(8,128)(2,1)S(1)}, bf16[2,112,128]{2,1,0:T(8,128)(2,1)S(1)}, u32[]{:S(2)}, u32[]{:S(2)}) collective-permute-start(bf16[2,112,128]{2,1,0:T(8,128)(2,1)S(1)} %get-tuple-element.25), channel_id=1, source_target_pairs={{128,0},{192,64},{0,128},{64,192},{129,1},{193,65},{1,129},{65,193... | collective-permute-start | bytes 172040 | tf_op jit(solution)/shard_map/ppermute | solution.py:22
  11.7 2.0 %collective-permute-done.2 = bf16[2,112,128]{2,1,0:T(8,128)(2,1)S(1)} collective-permute-done((bf16[2,112,128]{2,1,0:T(8,128)(2,1)S(1)}, bf16[2,112,128]{2,1,0:T(8,128)(2,1)S(1)}, u32[]{:S(2)}, u32[]{:S(2)}) %collective-permute-start.2) | collective-permute-done | bytes 57376 | tf_op jit(solution)/shard_map/ppermute | solution.py:22
  13.6 1.1 %collective-permute-done.3 = bf16[2,112,128]{2,1,0:T(8,128)(2,1)S(1)} collective-permute-done((bf16[2,112,128]{2,1,0:T(8,128)(2,1)S(1)}, bf16[2,112,128]{2,1,0:T(8,128)(2,1)S(1)}, u32[]{:S(2)}, u32[]{:S(2)}) %collective-permute-start.3) | collective-permute-done | bytes 57376 | tf_op jit(solution)/shard_map/ppermute | solution.py:22
  14.8 7.5 %collective-permute-start.4 = (bf16[2,112,128]{2,1,0:T(8,128)(2,1)S(1)}, bf16[2,112,128]{2,1,0:T(8,128)(2,1)S(1)}, u32[]{:S(2)}, u32[]{:S(2)}) collective-permute-start(bf16[2,112,128]{2,1,0:T(8,128)(2,1)S(1)} %fusion), channel_id=1, source_target_pairs={{32,0},{0,32},{33,1},{1,33},{34,2},{2,34},{35,3},{3,35},{36,4},{4,... | collective-permute-start | bytes 172040 | tf_op jit(solution)/shard_map/ppermute | solution.py:26
  22.3 0.8 shard_map.39.both
  23.1 0.8 collective-permute-done.4
  23.9 2.9 %collective-permute-start.8 = (bf16[2,112,128]{2,1,0:T(8,128)(2,1)S(1)}, bf16[2,112,128]{2,1,0:T(8,128)(2,1)S(1)}, u32[]{:S(2)}, u32[]{:S(2)}) collective-permute-start(bf16[2,112,128]{2,1,0:T(8,128)(2,1)S(1)} %add_convert_fusion), channel_id=1, source_target_pairs={{12,0},{8,4},{4,8},{0,12},{13,1},{9,5},{5,9},{1,13},{14,2},{10,6},... | collective-permute-start | bytes 172040 | tf_op jit(solution)/shard_map/ppermute | solution.py:26
  27.5 1.3 %collective-permute-done.8 = bf16[2,112,128]{2,1,0:T(8,128)(2,1)S(1)} collective-permute-done((bf16[2,112,128]{2,1,0:T(8,128)(2,1)S(1)}, bf16[2,112,128]{2,1,0:T(8,128)(2,1)S(1)}, u32[]{:S(2)}, u32[]{:S(2)}) %collective-permute-start.8) | collective-permute-done | bytes 57376 | tf_op jit(solution)/shard_map/ppermute | solution.py:26
  28.8 1.0 %collective-permute-done.6 = bf16[2,112,128]{2,1,0:T(8,128)(2,1)S(1)} collective-permute-done((bf16[2,112,128]{2,1,0:T(8,128)(2,1)S(1)}, bf16[2,112,128]{2,1,0:T(8,128)(2,1)S(1)}, u32[]{:S(2)}, u32[]{:S(2)}) %collective-permute-start.6) | collective-permute-done | bytes 57376 | tf_op jit(solution)/shard_map/ppermute | solution.py:26
  29.8 2.4 %collective-permute-done.7 = bf16[2,112,128]{2,1,0:T(8,128)(2,1)S(1)} collective-permute-done((bf16[2,112,128]{2,1,0:T(8,128)(2,1)S(1)}, bf16[2,112,128]{2,1,0:T(8,128)(2,1)S(1)}, u32[]{:S(2)}, u32[]{:S(2)}) %collective-permute-start.7) | collective-permute-done | bytes 57376 | tf_op jit(solution)/shard_map/ppermute | solution.py:26
  32.2 2.8 %collective-permute-start.9 = (bf16[2,4,112,128]{3,2,1,0:T(8,128)(2,1)S(1)}, bf16[2,4,112,128]{3,2,1,0:T(8,128)(2,1)S(1)}, u32[]{:S(2)}, u32[]{:S(2)}) collective-permute-start(bf16[2,4,112,128]{3,2,1,0:T(8,128)(2,1)S(1)} %get-tuple-element.36), channel_id=1, source_target_pairs={{64,0},{65,1},{66,2},{67,3},{68,4},{69,5},{70,6},{71,7},{72,8},{73... | collective-permute-start | bytes 688136 | tf_op jit(solution)/shard_map/ppermute | solution.py:36
  35.0 3.0 %collective-permute-done.9 = bf16[2,4,112,128]{3,2,1,0:T(8,128)(2,1)S(1)} collective-permute-done((bf16[2,4,112,128]{3,2,1,0:T(8,128)(2,1)S(1)}, bf16[2,4,112,128]{3,2,1,0:T(8,128)(2,1)S(1)}, u32[]{:S(2)}, u32[]{:S(2)}) %collective-permute-start.9) | collective-permute-done | bytes 229408 | tf_op jit(solution)/shard_map/ppermute | solution.py:36
  38.0 3.4 %collective-permute-done.10 = bf16[2,4,112,128]{3,2,1,0:T(8,128)(2,1)S(1)} collective-permute-done((bf16[2,4,112,128]{3,2,1,0:T(8,128)(2,1)S(1)}, bf16[2,4,112,128]{3,2,1,0:T(8,128)(2,1)S(1)}, u32[]{:S(2)}, u32[]{:S(2)}) %collective-permute-start.10) | collective-permute-done | bytes 229408 | tf_op jit(solution)/shard_map/ppermute | solution.py:36
  41.8 1.2 %collective-permute-start.12 = (bf16[3,2,4,112,128]{4,3,2,1,0:T(8,128)(2,1)S(1)}, bf16[3,2,4,112,128]{4,3,2,1,0:T(8,128)(2,1)S(1)}, u32[]{:S(2)}, u32[]{:S(2)}) collective-permute-start(bf16[3,2,4,112,128]{4,3,2,1,0:T(8,128)(2,1)S(1)} %pad_maximum_fusion.three), channel_id=1, source_target_pairs={{3,0},{0,1},{1,2},{2,3},{7,4},{4,5},{5,6},{6,7},{11,8},{8,9},{9,10... | collective-permute-start | bytes 2064392 | tf_op jit(solution)/shard_map/ppermute | solution.py:36
  43.2 1.5 %collective-permute-start.14 = (bf16[1,4,112,128]{3,2,1,0:T(8,128)(2,1)S(1)}, bf16[1,4,112,128]{3,2,1,0:T(8,128)(2,1)S(1)}, u32[]{:S(2)}, u32[]{:S(2)}) collective-permute-start(bf16[1,4,112,128]{3,2,1,0:T(8,128)(2,1)S(1)} %slice.17), channel_id=1, source_target_pairs={{192,0},{193,1},{194,2},{195,3},{196,4},{197,5},{198,6},{199,7},{2... | collective-permute-start | bytes 344072 | tf_op jit(solution)/shard_map/ppermute | solution.py:36
  44.7 2.1 %collective-permute-done.13 = bf16[1,4,112,128]{3,2,1,0:T(8,128)(2,1)S(1)} collective-permute-done((bf16[1,4,112,128]{3,2,1,0:T(8,128)(2,1)S(1)}, bf16[1,4,112,128]{3,2,1,0:T(8,128)(2,1)S(1)}, u32[]{:S(2)}, u32[]{:S(2)}) %collective-permute-start.13) | collective-permute-done | bytes 114720 | tf_op jit(solution)/shard_map/ppermute | solution.py:36
  46.8 1.3 %collective-permute-done.14 = bf16[1,4,112,128]{3,2,1,0:T(8,128)(2,1)S(1)} collective-permute-done((bf16[1,4,112,128]{3,2,1,0:T(8,128)(2,1)S(1)}, bf16[1,4,112,128]{3,2,1,0:T(8,128)(2,1)S(1)}, u32[]{:S(2)}, u32[]{:S(2)}) %collective-permute-start.14) | collective-permute-done | bytes 114720 | tf_op jit(solution)/shard_map/ppermute | solution.py:36
  48.2 1.7 %shard_map.40.start = f32[1024,768]{1,0:T(8,128)S(1)} custom-call(s32[4]{0:T(128)S(1)} %pad_add_fusion.place, bf16[3,2,4,112,128]{4,3,2,1,0:T(8,128)(2,1)S(1)} %pad_maximum_fusion.three, bf16[2,4,112,128]{3,2,1,0:T(8,128)(2,1)S(1)} %constant_dynamic-update-slice_fusion.far, bf16[4,448,768]{2,1,0:T(8,128)(2,1)S(1)} %shard_map.39.both), custom_call_target="tpu_custom_call" | custom-call | flops 1000000000 | bytes 2097152 | tf_op jit(solution)/shard_map/pallas_call | solution.py:172
  49.9 1.8 %collective-permute-done.11.after = bf16[3,2,4,112,128]{4,3,2,1,0:T(8,128)(2,1)S(1)} collective-permute-done((bf16[3,2,4,112,128]{4,3,2,1,0:T(8,128)(2,1)S(1)}, bf16[3,2,4,112,128]{4,3,2,1,0:T(8,128)(2,1)S(1)}, u32[]{:S(2)}, u32[]{:S(2)}) %collective-permute-start.11) | collective-permute-done | bytes 688160 | tf_op jit(solution)/shard_map/ppermute | solution.py:36
  51.7 1.5 %collective-permute-done.12.before = bf16[3,2,4,112,128]{4,3,2,1,0:T(8,128)(2,1)S(1)} collective-permute-done((bf16[3,2,4,112,128]{4,3,2,1,0:T(8,128)(2,1)S(1)}, bf16[3,2,4,112,128]{4,3,2,1,0:T(8,128)(2,1)S(1)}, u32[]{:S(2)}, u32[]{:S(2)}) %collective-permute-start.12) | collective-permute-done | bytes 688160 | tf_op jit(solution)/shard_map/ppermute | solution.py:36
  53.8 2.9 %collective-permute-done.16.before2 = bf16[2,4,112,128]{3,2,1,0:T(8,128)(2,1)S(1)} collective-permute-done((bf16[2,4,112,128]{3,2,1,0:T(8,128)(2,1)S(1)}, bf16[2,4,112,128]{3,2,1,0:T(8,128)(2,1)S(1)}, u32[]{:S(2)}, u32[]{:S(2)}) %collective-permute-start.16) | collective-permute-done | bytes 229408 | tf_op jit(solution)/shard_map/ppermute | solution.py:36
  56.9 6.1 %collective-permute-done.19.after2 = bf16[2,4,112,128]{3,2,1,0:T(8,128)(2,1)S(1)} collective-permute-done((bf16[2,4,112,128]{3,2,1,0:T(8,128)(2,1)S(1)}, bf16[2,4,112,128]{3,2,1,0:T(8,128)(2,1)S(1)}, u32[]{:S(2)}, u32[]{:S(2)}) %collective-permute-start.19) | collective-permute-done | bytes 229408 | tf_op jit(solution)/shard_map/ppermute | solution.py:36
  63.1 2.3 %shard_map.41.start = f32[1024,768]{1,0:T(8,128)S(1)} custom-call(s32[4]{0:T(128)S(1)} %pad_add_fusion.place, bf16[3,2,4,112,128]{4,3,2,1,0:T(8,128)(2,1)S(1)} %collective-permute-done.11.after, bf16[2,4,112,128]{3,2,1,0:T(8,128)(2,1)S(1)} %collective-permute-done.19.after2, ...), custom_call_target="tpu_custom_call", output_to_operand_aliasing={{}: (6, {})} | custom-call | flops 1000000000 | bytes 2097152 | tf_op jit(solution)/shard_map/pallas_call | solution.py:172
  66.0 9.4 %collective-permute-start.21 = (bf16[512,384]{1,0:T(8,128)(2,1)S(1)}, bf16[512,384]{1,0:T(8,128)(2,1)S(1)}, u32[]{:S(2)}, u32[]{:S(2)}) collective-permute-start(bf16[512,384]{1,0:T(8,128)(2,1)S(1)} %get-tuple-element.34), channel_id=1, source_target_pairs={{16,0},{0,16},{17,1},{1,17},{18,2},{2,18},{19,3},{3,19},{20,4},{4,... | collective-permute-start | bytes 1179656 | tf_op jit(solution)/shard_map/ppermute | solution.py:22
  75.4 1.5 %shard_map.42 = (bf16[512,384]{1,0:T(8,128)(2,1)S(1)}, bf16[512,384]{1,0:T(8,128)(2,1)S(1)}) custom-call(s32[4]{0:T(128)S(1)} %pad_add_fusion.place, bf16[2,2,4,112,128]{4,3,2,1,0:T(8,128)(2,1)S(1)} %collective-permute-done.15.low, bf16[2,4,112,128]{3,2,1,0:T(8,128)(2,1)S(1)} %collective-permute-done.17.far2, ...), custom_call_target="tpu_custom_call" | custom-call | flops 1000000000 | bytes 2097152 | tf_op jit(solution)/shard_map/pallas_call | solution.py:172
  77.0 1.6 %shard_map.44.given = bf16[2048,384]{1,0:T(8,128)(2,1)} custom-call(s32[4]{0:T(128)S(1)} %pad_add_fusion.place, bf16[512,384]{1,0:T(8,128)(2,1)S(1)} %get-tuple-element.32.mine1, bf16[512,384]{1,0:T(8,128)(2,1)S(1)} %get-tuple-element.33.mine2, bf16[512,384]{1,0:T(8,128)(2,1)S(1)} %collective-permute-done.21.theirs1), custom_call_target="tpu_custom_call" | custom-call | bytes 2097152 | tf_op jit(solution)/shard_map/pallas_call | solution.py:172
  78.7 1.3 %shard_map.45 = bf16[2048,384]{1,0:T(8,128)(2,1)} custom-call(s32[4]{0:T(128)S(1)} %pad_add_fusion.place, bf16[512,384]{1,0:T(8,128)(2,1)S(1)} %collective-permute-done.20.theirs2, bf16[2048,384]{1,0:T(8,128)(2,1)} %shard_map.44.given), custom_call_target="tpu_custom_call", output_to_operand_aliasing={{}: (2, {})} | custom-call | bytes 2097152 | tf_op jit(solution)/shard_map/pallas_call | solution.py:172
  (38 shorter events, 6.1 us)
Async XLA Ops:
  0.0 22.3 %copy-start = (bf16[1792,384]{1,0:T(8,128)(2,1)S(1)}, bf16[1792,384]{1,0:T(8,128)(2,1)}, u32[]{:S(2)}) copy-start(bf16[1792,384]{1,0:T(8,128)(2,1)} %own.1) | copy-start | bytes 4128772
  0.0 22.3 %collective-permute-start.5 = (bf16[1792,384]{1,0:T(8,128)(2,1)}, bf16[1792,384]{1,0:T(8,128)(2,1)S(1)}, u32[]{:S(2)}, u32[]{:S(2)}) collective-permute-start(bf16[1792,384]{1,0:T(8,128)(2,1)} %own.1), channel_id=1, source_target_pairs={{16,0},{0,16},{17,1},{1,17},{18,2},{2,18},{19,3},{3,19},{20,4},{4,... | collective-permute-start | bytes 4128776 | tf_op jit(solution)/shard_map/ppermute | solution.py:22
  3.3 1.0 %copy-start.1 = (bf16[112,2048]{1,0:T(8,128)(2,1)S(1)}, bf16[112,2048]{1,0:T(8,128)(2,1)}, u32[]{:S(2)}) copy-start(bf16[112,2048]{1,0:T(8,128)(2,1)} %panel.1) | copy-start | bytes 1376260
  4.3 0.7 copy-start.2
  6.1 1.9 %collective-permute-start = (f32[8,112,128]{2,1,0:T(8,128)S(1)}, f32[8,112,128]{2,1,0:T(8,128)S(1)}, u32[]{:S(2)}, u32[]{:S(2)}) collective-permute-start(f32[8,112,128]{2,1,0:T(8,128)S(1)} %get-tuple-element.21), channel_id=1, source_target_pairs={{16,0},{0,16},{17,1},{1,17},{18,2},{2,18},{19,3},{3,19},{20,4},{4,... | collective-permute-start | bytes 1376264 | tf_op jit(solution)/shard_map/ppermute | solution.py:22
  8.6 3.1 %collective-permute-start.1 = (bf16[2,112,128]{2,1,0:T(8,128)(2,1)S(1)}, bf16[2,112,128]{2,1,0:T(8,128)(2,1)S(1)}, u32[]{:S(2)}, u32[]{:S(2)}) collective-permute-start(bf16[2,112,128]{2,1,0:T(8,128)(2,1)S(1)} %get-tuple-element.23), channel_id=1, source_target_pairs={{64,0},{128,64},{192,128},{0,192},{65,1},{129,65},{193,129},{1,193... | collective-permute-start | bytes 172040 | tf_op jit(solution)/shard_map/ppermute | solution.py:22
  9.4 4.2 %collective-permute-start.2 = (bf16[2,112,128]{2,1,0:T(8,128)(2,1)S(1)}, bf16[2,112,128]{2,1,0:T(8,128)(2,1)S(1)}, u32[]{:S(2)}, u32[]{:S(2)}) collective-permute-start(bf16[2,112,128]{2,1,0:T(8,128)(2,1)S(1)} %get-tuple-element.24), channel_id=1, source_target_pairs={{192,0},{0,64},{64,128},{128,192},{193,1},{1,65},{65,129},{129,193... | collective-permute-start | bytes 172040 | tf_op jit(solution)/shard_map/ppermute | solution.py:22
  10.1 4.6 %collective-permute-start.3 = (bf16[2,112,128]{2,1,0:T(8,128)(2,1)S(1)}, bf16[2,112,128]{2,1,0:T(8,128)(2,1)S(1)}, u32[]{:S(2)}, u32[]{:S(2)}) collective-permute-start(bf16[2,112,128]{2,1,0:T(8,128)(2,1)S(1)} %get-tuple-element.25), channel_id=1, source_target_pairs={{128,0},{192,64},{0,128},{64,192},{129,1},{193,65},{1,129},{65,193... | collective-permute-start | bytes 172040 | tf_op jit(solution)/shard_map/ppermute | solution.py:22
  14.8 9.1 %collective-permute-start.4 = (bf16[2,112,128]{2,1,0:T(8,128)(2,1)S(1)}, bf16[2,112,128]{2,1,0:T(8,128)(2,1)S(1)}, u32[]{:S(2)}, u32[]{:S(2)}) collective-permute-start(bf16[2,112,128]{2,1,0:T(8,128)(2,1)S(1)} %fusion), channel_id=1, source_target_pairs={{32,0},{0,32},{33,1},{1,33},{34,2},{2,34},{35,3},{3,35},{36,4},{4,... | collective-permute-start | bytes 172040 | tf_op jit(solution)/shard_map/ppermute | solution.py:26
  23.9 4.9 %collective-permute-start.8 = (bf16[2,112,128]{2,1,0:T(8,128)(2,1)S(1)}, bf16[2,112,128]{2,1,0:T(8,128)(2,1)S(1)}, u32[]{:S(2)}, u32[]{:S(2)}) collective-permute-start(bf16[2,112,128]{2,1,0:T(8,128)(2,1)S(1)} %add_convert_fusion), channel_id=1, source_target_pairs={{12,0},{8,4},{4,8},{0,12},{13,1},{9,5},{5,9},{1,13},{14,2},{10,6},... | collective-permute-start | bytes 172040 | tf_op jit(solution)/shard_map/ppermute | solution.py:26
  26.8 3.0 %collective-permute-start.6 = (bf16[2,112,128]{2,1,0:T(8,128)(2,1)S(1)}, bf16[2,112,128]{2,1,0:T(8,128)(2,1)S(1)}, u32[]{:S(2)}, u32[]{:S(2)}) collective-permute-start(bf16[2,112,128]{2,1,0:T(8,128)(2,1)S(1)} %add_convert_fusion), channel_id=1, source_target_pairs={{4,0},{0,4},{12,8},{8,12},{5,1},{1,5},{13,9},{9,13},{6,2},{2,6},{1... | collective-permute-start | bytes 172040 | tf_op jit(solution)/shard_map/ppermute | solution.py:26
  26.8 5.4 %collective-permute-start.7 = (bf16[2,112,128]{2,1,0:T(8,128)(2,1)S(1)}, bf16[2,112,128]{2,1,0:T(8,128)(2,1)S(1)}, u32[]{:S(2)}, u32[]{:S(2)}) collective-permute-start(bf16[2,112,128]{2,1,0:T(8,128)(2,1)S(1)} %add_convert_fusion), channel_id=1, source_target_pairs={{8,0},{12,4},{0,8},{4,12},{9,1},{13,5},{1,9},{5,13},{10,2},{14,6},... | collective-permute-start | bytes 172040 | tf_op jit(solution)/shard_map/ppermute | solution.py:26
  32.2 5.8 %collective-permute-start.9 = (bf16[2,4,112,128]{3,2,1,0:T(8,128)(2,1)S(1)}, bf16[2,4,112,128]{3,2,1,0:T(8,128)(2,1)S(1)}, u32[]{:S(2)}, u32[]{:S(2)}) collective-permute-start(bf16[2,4,112,128]{3,2,1,0:T(8,128)(2,1)S(1)} %get-tuple-element.36), channel_id=1, source_target_pairs={{64,0},{65,1},{66,2},{67,3},{68,4},{69,5},{70,6},{71,7},{72,8},{73... | collective-permute-start | bytes 688136 | tf_op jit(solution)/shard_map/ppermute | solution.py:36
  35.0 6.4 %collective-permute-start.10 = (bf16[2,4,112,128]{3,2,1,0:T(8,128)(2,1)S(1)}, bf16[2,4,112,128]{3,2,1,0:T(8,128)(2,1)S(1)}, u32[]{:S(2)}, u32[]{:S(2)}) collective-permute-start(bf16[2,4,112,128]{3,2,1,0:T(8,128)(2,1)S(1)} %get-tuple-element.36), channel_id=1, source_target_pairs={{192,0},{193,1},{194,2},{195,3},{196,4},{197,5},{198,6},{199,7},{2... | collective-permute-start | bytes 688136 | tf_op jit(solution)/shard_map/ppermute | solution.py:36
  41.5 10.2 %collective-permute-start.11 = (bf16[3,2,4,112,128]{4,3,2,1,0:T(8,128)(2,1)S(1)}, bf16[3,2,4,112,128]{4,3,2,1,0:T(8,128)(2,1)S(1)}, u32[]{:S(2)}, u32[]{:S(2)}) collective-permute-start(bf16[3,2,4,112,128]{4,3,2,1,0:T(8,128)(2,1)S(1)} %pad_maximum_fusion.three), channel_id=1, source_target_pairs={{1,0},{2,1},{3,2},{0,3},{5,4},{6,5},{7,6},{4,7},{9,8},{10,9},{11,1... | collective-permute-start | bytes 2064392 | tf_op jit(solution)/shard_map/ppermute | solution.py:36
  41.8 11.4 %collective-permute-start.12 = (bf16[3,2,4,112,128]{4,3,2,1,0:T(8,128)(2,1)S(1)}, bf16[3,2,4,112,128]{4,3,2,1,0:T(8,128)(2,1)S(1)}, u32[]{:S(2)}, u32[]{:S(2)}) collective-permute-start(bf16[3,2,4,112,128]{4,3,2,1,0:T(8,128)(2,1)S(1)} %pad_maximum_fusion.three), channel_id=1, source_target_pairs={{3,0},{0,1},{1,2},{2,3},{7,4},{4,5},{5,6},{6,7},{11,8},{8,9},{9,10... | collective-permute-start | bytes 2064392 | tf_op jit(solution)/shard_map/ppermute | solution.py:36
  43.1 3.7 %collective-permute-start.13 = (bf16[1,4,112,128]{3,2,1,0:T(8,128)(2,1)S(1)}, bf16[1,4,112,128]{3,2,1,0:T(8,128)(2,1)S(1)}, u32[]{:S(2)}, u32[]{:S(2)}) collective-permute-start(bf16[1,4,112,128]{3,2,1,0:T(8,128)(2,1)S(1)} %slice.16), channel_id=1, source_target_pairs={{64,0},{65,1},{66,2},{67,3},{68,4},{69,5},{70,6},{71,7},{72,8},{73... | collective-permute-start | bytes 344072 | tf_op jit(solution)/shard_map/ppermute | solution.py:36
  43.2 4.9 %collective-permute-start.14 = (bf16[1,4,112,128]{3,2,1,0:T(8,128)(2,1)S(1)}, bf16[1,4,112,128]{3,2,1,0:T(8,128)(2,1)S(1)}, u32[]{:S(2)}, u32[]{:S(2)}) collective-permute-start(bf16[1,4,112,128]{3,2,1,0:T(8,128)(2,1)S(1)} %slice.17), channel_id=1, source_target_pairs={{192,0},{193,1},{194,2},{195,3},{196,4},{197,5},{198,6},{199,7},{2... | collective-permute-start | bytes 344072 | tf_op jit(solution)/shard_map/ppermute | solution.py:36
  48.1 8.7 %collective-permute-start.16 = (bf16[2,4,112,128]{3,2,1,0:T(8,128)(2,1)S(1)}, bf16[2,4,112,128]{3,2,1,0:T(8,128)(2,1)S(1)}, u32[]{:S(2)}, u32[]{:S(2)}) collective-permute-start(bf16[2,4,112,128]{3,2,1,0:T(8,128)(2,1)S(1)} %constant_dynamic-update-slice_fusion.far), channel_id=1, source_target_pairs={{3,0},{0,1},{1,2},{2,3},{7,4},{4,5},{5,6},{6,7},{11,8},{8,9},{9,10... | collective-permute-start | bytes 688136 | tf_op jit(solution)/shard_map/ppermute | solution.py:36
  53.2 12.1 %collective-permute-start.15 = (bf16[2,2,4,112,128]{4,3,2,1,0:T(8,128)(2,1)S(1)}, bf16[2,2,4,112,128]{4,3,2,1,0:T(8,128)(2,1)S(1)}, u32[]{:S(2)}, u32[]{:S(2)}) collective-permute-start(bf16[2,2,4,112,128]{4,3,2,1,0:T(8,128)(2,1)S(1)} %slice.14), channel_id=1, source_target_pairs={{1,0},{2,1},{3,2},{0,3},{5,4},{6,5},{7,6},{4,7},{9,8},{10,9},{11,1... | collective-permute-start | bytes 1376264 | tf_op jit(solution)/shard_map/ppermute | solution.py:36
  53.7 9.4 %collective-permute-start.19 = (bf16[2,4,112,128]{3,2,1,0:T(8,128)(2,1)S(1)}, bf16[2,4,112,128]{3,2,1,0:T(8,128)(2,1)S(1)}, u32[]{:S(2)}, u32[]{:S(2)}) collective-permute-start(bf16[2,4,112,128]{3,2,1,0:T(8,128)(2,1)S(1)} %constant_dynamic-update-slice_fusion.far), channel_id=1, source_target_pairs={{1,0},{2,1},{3,2},{0,3},{5,4},{6,5},{7,6},{4,7},{9,8},{10,9},{11,1... | collective-permute-start | bytes 688136 | tf_op jit(solution)/shard_map/ppermute | solution.py:36
  56.8 18.6 %collective-permute-start.17 = (bf16[2,4,112,128]{3,2,1,0:T(8,128)(2,1)S(1)}, bf16[2,4,112,128]{3,2,1,0:T(8,128)(2,1)S(1)}, u32[]{:S(2)}, u32[]{:S(2)}) collective-permute-start(bf16[2,4,112,128]{3,2,1,0:T(8,128)(2,1)S(1)} %collective-permute-done.16.before2), channel_id=1, source_target_pairs={{3,0},{0,1},{1,2},{2,3},{7,4},{4,5},{5,6},{6,7},{11,8},{8,9},{9,10... | collective-permute-start | bytes 688136 | tf_op jit(solution)/shard_map/ppermute | solution.py:36
  56.8 18.6 %collective-permute-start.18 = (bf16[2,4,112,128]{3,2,1,0:T(8,128)(2,1)S(1)}, bf16[2,4,112,128]{3,2,1,0:T(8,128)(2,1)S(1)}, u32[]{:S(2)}, u32[]{:S(2)}) collective-permute-start(bf16[2,4,112,128]{3,2,1,0:T(8,128)(2,1)S(1)} %slice_bitcast_fusion), channel_id=1, source_target_pairs={{3,0},{0,1},{1,2},{2,3},{7,4},{4,5},{5,6},{6,7},{11,8},{8,9},{9,10... | collective-permute-start | bytes 688136 | tf_op jit(solution)/shard_map/ppermute | solution.py:36
  66.0 11.0 %collective-permute-start.21 = (bf16[512,384]{1,0:T(8,128)(2,1)S(1)}, bf16[512,384]{1,0:T(8,128)(2,1)S(1)}, u32[]{:S(2)}, u32[]{:S(2)}) collective-permute-start(bf16[512,384]{1,0:T(8,128)(2,1)S(1)} %get-tuple-element.34), channel_id=1, source_target_pairs={{16,0},{0,16},{17,1},{1,17},{18,2},{2,18},{19,3},{3,19},{20,4},{4,... | collective-permute-start | bytes 1179656 | tf_op jit(solution)/shard_map/ppermute | solution.py:22
  76.9 1.8 %collective-permute-start.20 = (bf16[512,384]{1,0:T(8,128)(2,1)S(1)}, bf16[512,384]{1,0:T(8,128)(2,1)S(1)}, u32[]{:S(2)}, u32[]{:S(2)}) collective-permute-start(bf16[512,384]{1,0:T(8,128)(2,1)S(1)} %get-tuple-element.31), channel_id=1, source_target_pairs={{16,0},{0,16},{17,1},{1,17},{18,2},{2,18},{19,3},{3,19},{20,4},{4,... | collective-permute-start | bytes 1179656 | tf_op jit(solution)/shard_map/ppermute | solution.py:22

commit v4 on v3

--- a/solution.py
+++ b/solution.py
@@ -10,6 +10,7 @@
 ROW = ("x", "z_hi", "core")
 COL = ("z_lo", "y")
 Z = ("z_hi", "z_lo")
+ORDER = (0, 1, 3, 2)
 BF16 = jnp.bfloat16
 F32 = jnp.float32
 VMEM = pl.BlockSpec(memory_space=pltpu.VMEM)
@@ -60,9 +61,9 @@
 
 
 def order_pairs(place, own, other, both):
-    for k in range(4):
+    for k, ahead in enumerate(ORDER):
         for j in range(4):
-            y, z_lo = lax.rem(place[1] + k, 4), place[3] ^ j
+            y, z_lo = lax.rem(place[1] + ahead, 4), place[3] ^ j
             rows = pl.ds(pl.multiple_of((z_lo * 4 + y) * 112, 16), 112)
             both[k, pl.ds(j * 112, 112), :384] = own[rows]
             both[k, pl.ds(j * 112, 112), 384:] = other[rows]
@@ -81,78 +82,93 @@
     return jnp.concatenate(halves, 1)
 
 
-def product_one(place, three, far, both, out):
-    @on_core(place, 0)
-    def _():
-        out[:512] = dot_t(by_x(three[0], three[1]), both[0])
-        out[512:] = dot_t(by_x(far, three[2]), both[0])
-
-    @on_core(place, 1)
-    def _():
-        left = by_y(three[0], three[1], far, three[2])
-        out[:256] = dot_t(left, both[...].reshape(1792, 768))
-
-
-def product_two(place, after, after2, before, before2, both, start, out):
-    @on_core(place, 0)
-    def _():
-        out[:512] = (
-            start[:512]
-            + dot_t(by_x(after[0], after[1]), both[1])
-            + dot_t(by_x(before[0], before[1]), both[3])
+def slabs(block):
+    return [block[i] for i in range(block.shape[0])]
+
+
+def rows(first, count=1):
+    return pl.ds(first * 256, count * 256)
+
+
+def deep(both, first, count):
+    return both[pl.ds(first, count)].reshape(count * 448, 768)
+
+
+def product_one(place, own, after, before, both, out):
+    @on_core(place, 0)
+    def _():
+        out[rows(0, 3)] = dot_t(by_x(own, after, before), both[0])
+
+    @on_core(place, 1)
+    def _():
+        out[rows(0)] = dot_t(by_y(own, after, before), deep(both, 0, 3))
+
+
+def product_two(place, far, after, before, both, start, out):
+    @on_core(place, 0)
+    def _():
+        out[rows(0, 3)] = (
+            start[rows(0, 3)] + dot_t(by_x(*slabs(after)), both[1]) + dot_t(by_x(*slabs(before)), both[2])
         )
-        out[512:] = (
-            start[512:]
-            + dot_t(by_x(after2, after[2]), both[1])
-            + dot_t(by_x(before2, before[2]), both[3])
-        )
-
-    @on_core(place, 1)
-    def _():
-        right = both[...].reshape(1792, 768)
-        out[:256] = start[:256]
-        out[256:512] = dot_t(by_y(after[0], after[1], after2, after[2]), right)
-        out[768:] = dot_t(by_y(before[0], before[1], before2, before[2]), right)
-
-
-def product_three(place, low, both, start, mine, theirs):
+        out[rows(3)] = dot_t(by_x(far), both[0])
+
+    @on_core(place, 1)
+    def _():
+        out[rows(0)] = start[rows(0)] + dot_t(by_y(far), both[3])
+        out[rows(1)] = dot_t(by_y(*slabs(after)), deep(both, 0, 3))
+        out[rows(2)] = dot_t(by_y(*slabs(before)), deep(both, 0, 3))
+
+
+def product_three(place, after, before, both, start, out):
+    @on_core(place, 0)
+    def _():
+        out[rows(0, 3)] = start[rows(0, 3)]
+        out[rows(3)] = start[rows(3)] + dot_t(by_x(after), both[1]) + dot_t(by_x(before), both[2])
+
+    @on_core(place, 1)
+    def _():
+        out[rows(0)] = start[rows(0)]
+        out[rows(1)] = start[rows(1)] + dot_t(by_y(after), both[3])
+        out[rows(2)] = start[rows(2)] + dot_t(by_y(before), both[3])
+
+
+def product_four(place, low, both, start, mine, theirs):
     def keep(total):
         mine[...] = total[:, :384].astype(BF16)
         theirs[...] = total[:, 384:].astype(BF16)
 
     @on_core(place, 0)
     def _():
-        keep(start[:512] + dot_t(by_x(low[0], low[1]), both[2]))
-
-    @on_core(place, 1)
-    def _():
-        keep(start[:512])
-
-
-def product_four(place, low, far2, far3, both, start, mine, theirs):
-    def keep(rows, total):
-        mine[rows] = total[:, :384].astype(BF16)
-        theirs[rows] = total[:, 384:].astype(BF16)
-
-    @on_core(place, 0)
-    def _():
-        keep(pl.ds(0, 512), start[512:] + dot_t(by_x(far2, far3), both[2]))
-
-    @on_core(place, 1)
-    def _():
-        left = by_y(low[0], low[1], far2, far3)
-        keep(pl.ds(0, 256), dot_t(left, both[...].reshape(1792, 768)))
-        keep(pl.ds(256, 256), start[768:])
+        keep(start[rows(0, 2)] + dot_t(by_x(low[0], low[1]), both[3]))
+
+    @on_core(place, 1)
+    def _():
+        keep(start[rows(0, 2)])
+
+
+def product_five(place, low, far2, both, start, mine, theirs):
+    def keep(at, total):
+        mine[at] = total[:, :384].astype(BF16)
+        theirs[at] = total[:, 384:].astype(BF16)
+
+    @on_core(place, 0)
+    def _():
+        keep(rows(0, 2), start[rows(2, 2)] + dot_t(by_x(low[2], far2), both[3]))
+
+    @on_core(place, 1)
+    def _():
+        keep(rows(0), start[rows(2)])
+        keep(rows(1), dot_t(by_y(*slabs(low), far2), deep(both, 0, 4)))
 
 
 def place_rows(place, parts, out, sems):
     copies = []
-    for block, core, first in parts:
+    for block, core, which in parts:
         for i in range(2):
-            row = core * 1024 + lax.rem(place[0] + first + i, 4) * 256
-            rows = pl.ds(pl.multiple_of(row, 256), 256)
+            row = core * 1024 + lax.rem(place[0] + ORDER[which * 2 + i], 4) * 256
+            at = pl.ds(pl.multiple_of(row, 256), 256)
             sem = sems.at[len(copies)]
-            copies.append(pltpu.make_async_copy(block.at[pl.ds(i * 256, 256)], out.at[rows], sem))
+            copies.append(pltpu.make_async_copy(block.at[rows(i)], out.at[at], sem))
     for copy in copies:
         copy.start()
     for copy in copies:
@@ -161,11 +177,11 @@
 
 def place_first(place, mine1, mine2, theirs1, out, sems):
     core = place[2]
-    place_rows(place, [(mine1, core, 0), (mine2, core, 2), (theirs1, 1 - core, 0)], out, sems)
+    place_rows(place, [(mine1, core, 0), (mine2, core, 1), (theirs1, 1 - core, 0)], out, sems)
 
 
 def place_last(place, theirs2, given, out, sems):
-    place_rows(place, [(theirs2, 1 - place[2], 2)], out, sems)
+    place_rows(place, [(theirs2, 1 - place[2], 1)], out, sems)
 
 
 def call(kernel, out_shape, operands, out_specs=VMEM, specs=None, flops=0, **more):
@@ -206,33 +222,40 @@
     part = (part + share.astype(F32)).astype(BF16)
     own = jnp.stack([part] + [swap(part, "z_lo", 4, bits) for bits in (1, 2, 3)], 1)
 
-    after, before = turn(own, 0, 1), turn(own, 0, 3)
-    three = jnp.stack([own, after, before])
-    far = jnp.concatenate([turn(after[:1], 0, 1), turn(before[1:], 0, 3)])
-    after, before = turn(three, 1, 1), turn(three, 1, 3)
+    after, before, far = (turn(own, 0, ahead) for ahead in (1, 3, 2))
+    three = [own, after, before]
+    total = jax.ShapeDtypeStruct((1024, 768), F32)
+    total_one = call(product_one, total, (place, *three, both), flops=10**9)
+    sent = jnp.stack(three)
+    after, before = turn(sent, 1, 1), turn(sent, 1, 3)
+    far, total_one = lax.optimization_barrier((far, total_one))
     after2, before2 = turn(far, 1, 1), turn(far, 1, 3)
-    total = jax.ShapeDtypeStruct((1024, 768), F32)
-    total_one = call(product_one, total, (place, three, far, both), flops=10**9)
-    after, before, total_one = lax.optimization_barrier((after, before, total_one))
-    low = turn(after[:2], 1, 1)
-    far3 = turn(before[2], 1, 3)
-    far2 = turn(before2, 1, 3)
+    low = turn(after, 1, 1)
     total_two = call(
         product_two,
         total,
-        (place, after, after2, before, before2, both, total_one),
+        (place, far, after, before, both, total_one),
         flops=10**9,
-        input_output_aliases={6: 0},
+        input_output_aliases={5: 0},
+    )
+    after2, before2, total_two = lax.optimization_barrier((after2, before2, total_two))
+    far2 = turn(before2, 1, 3)
+    total_three = call(
+        product_three,
+        total,
+        (place, after2, before2, both, total_two),
+        flops=10**9,
+        input_output_aliases={4: 0},
     )
     half = jax.ShapeDtypeStruct((512, 384), BF16)
     mine1, theirs1 = call(
-        product_three, (half, half), (place, low, both, total_two), (VMEM, VMEM), flops=10**9
+        product_four, (half, half), (place, low, both, total_three), (VMEM, VMEM), flops=10**9
     )
     theirs1 = fetch(theirs1, "core", 2, 1)
     mine2, theirs2 = call(
-        product_four,
+        product_five,
         (half, half),
-        (place, low, far2, far3, both, total_two),
+        (place, low, far2, both, total_three),
         (VMEM, VMEM),
         flops=10**9,
     )

time: 80.4 us -> 89.4 us (1.11)
  starting transfers between devices: 33.4 us -> 41.8 us
  waiting for transfers between devices: 33 us -> 31.2 us
  local copies, waits for them, and re-layouts: 1.86 us -> 3.11 us
  Pallas kernels: 11.4 us -> 12.5 us
    ppermute x11 -> x9, starting transfers between devices: 6.82 us -> 11.1 us  [turn(): return lax.ppermute(block, ROW + COL, pairs)]
    ppermute x7, starting transfers between devices: 15.5 us -> 19.7 us  [fetch(): lax.ppermute(block, axis, [((i + ahead) % size, i) for i in range(size)])]
    ppermute x4, waiting for transfers between devices: 5.41 us -> 4.06 us  [swap(): return lax.ppermute(block, axis, [(i ^ bits, i) for i in range(size)])]
    unnamed x7 -> x6, local copies, waits for them, and re-layouts: 1.78 us -> 3.11 us
    pallas_call x9 -> x10, Pallas kernels: 11.4 us -> 12.5 us  [call(): pl.pallas_call(kernel, out_shape=out_shape, in_specs=specs or [SMEM] + [V...]
    ppermute x11 -> x9, waiting for transfers between devices: 22.1 us -> 21.7 us  [turn(): return lax.ppermute(block, ROW + COL, pairs)]
  transfers between devices with their start and end apart: 22 -> 20, of which waited for: 17 -> 12; matrix products, arithmetic and copies ran while one was open for 0% -> 0% of each run, Pallas kernels for 12% -> 12%
where the time goes in v4:
time: 89.4 us; the launch traced here: 89.2 us
  starting transfers between devices  41.8 us (47%)
  waiting for transfers between devices  31.2 us (35%)
  Pallas kernels  12.5 us (14%)
  local copies, waits for them, and re-layouts  3.11 us (3%)
    ppermute x9, waiting for transfers between devices, turn(): return lax.ppermute(block, ROW + COL, pairs)  21.7 us
    ppermute x7, starting transfers between devices, fetch(): lax.ppermute(block, axis, [((i + ahead) % size, i) for i in range(size)])  19.7 us
    pallas_call x10, Pallas kernels, call(): pl.pallas_call(kernel, out_shape=out_shape, in_specs=specs or [SMEM] + [V...  12.5 us
    ppermute x4, starting transfers between devices, swap(): return lax.ppermute(block, axis, [(i ^ bits, i) for i in range(size)])  11.1 us
    ppermute x9, starting transfers between devices, turn(): return lax.ppermute(block, ROW + COL, pairs)  11.1 us
    ppermute x7, waiting for transfers between devices, fetch(): lax.ppermute(block, axis, [((i + ahead) % size, i) for i in range(size)])  5.44 us
    ppermute x4, waiting for transfers between devices, swap(): return lax.ppermute(block, axis, [(i ^ bits, i) for i in range(size)])  4.06 us
    unnamed x6, local copies, waits for them, and re-layouts  3.11 us
  transfers between devices with their start and end apart: 20, of which 12 were waited for; matrix products, arithmetic and copies ran while one was open for 0% of the time, Pallas kernels for 12%

profile of v4, /device:TPU:1, one launch (start us, length us, event | category | flops | bytes accessed | tf_op | source)
XLA Modules:
  0.0 89.2 jit_solution(15752992474289539781)
XLA Ops:
  0.0 3.2 %collective-permute-start.5 = (bf16[1792,384]{1,0:T(8,128)(2,1)}, bf16[1792,384]{1,0:T(8,128)(2,1)S(1)}, u32[]{:S(2)}, u32[]{:S(2)}) collective-permute-start(bf16[1792,384]{1,0:T(8,128)(2,1)} %own.1), channel_id=1, source_target_pairs={{16,0},{0,16},{17,1},{1,17},{18,2},{2,18},{19,3},{3,19},{20,4},{4,... | collective-permute-start | bytes 4128776 | tf_op jit(solution)/shard_map/ppermute | solution.py:23
  3.3 1.0 %copy-done.1 = bf16[112,2048]{1,0:T(8,128)(2,1)S(1)} copy-done((bf16[112,2048]{1,0:T(8,128)(2,1)S(1)}, bf16[112,2048]{1,0:T(8,128)(2,1)}, u32[]{:S(2)}) %copy-start.1) | copy-done | bytes 458776
  5.1 1.0 %shard_map.37 = (f32[8,112,128]{2,1,0:T(8,128)S(1)}, f32[8,112,128]{2,1,0:T(8,128)S(1)}) custom-call(s32[4]{0:T(128)S(1)} %pad_add_fusion.place, bf16[112,112]{1,0:T(8,128)(2,1)S(1)} %copy-done.2, bf16[112,2048]{1,0:T(8,128)(2,1)S(1)} %copy-done.1), custom_call_target="tpu_custom_call" | custom-call | bytes 2097152 | tf_op jit(solution)/shard_map/pallas_call | solution.py:188
  6.2 1.8 %collective-permute-done.received = f32[8,112,128]{2,1,0:T(8,128)S(1)} collective-permute-done((f32[8,112,128]{2,1,0:T(8,128)S(1)}, f32[8,112,128]{2,1,0:T(8,128)S(1)}, u32[]{:S(2)}, u32[]{:S(2)}) %collective-permute-start) | collective-permute-done | bytes 458784 | tf_op jit(solution)/shard_map/ppermute | solution.py:23
  10.1 1.0 %collective-permute-start.3 = (bf16[2,112,128]{2,1,0:T(8,128)(2,1)S(1)}, bf16[2,112,128]{2,1,0:T(8,128)(2,1)S(1)}, u32[]{:S(2)}, u32[]{:S(2)}) collective-permute-start(bf16[2,112,128]{2,1,0:T(8,128)(2,1)S(1)} %get-tuple-element.27), channel_id=1, source_target_pairs={{128,0},{192,64},{0,128},{64,192},{129,1},{193,65},{1,129},{65,193... | collective-permute-start | bytes 172040 | tf_op jit(solution)/shard_map/ppermute | solution.py:23
  11.7 2.0 %collective-permute-done.2 = bf16[2,112,128]{2,1,0:T(8,128)(2,1)S(1)} collective-permute-done((bf16[2,112,128]{2,1,0:T(8,128)(2,1)S(1)}, bf16[2,112,128]{2,1,0:T(8,128)(2,1)S(1)}, u32[]{:S(2)}, u32[]{:S(2)}) %collective-permute-start.2) | collective-permute-done | bytes 57376 | tf_op jit(solution)/shard_map/ppermute | solution.py:23
  13.6 1.1 %collective-permute-done.3 = bf16[2,112,128]{2,1,0:T(8,128)(2,1)S(1)} collective-permute-done((bf16[2,112,128]{2,1,0:T(8,128)(2,1)S(1)}, bf16[2,112,128]{2,1,0:T(8,128)(2,1)S(1)}, u32[]{:S(2)}, u32[]{:S(2)}) %collective-permute-start.3) | collective-permute-done | bytes 57376 | tf_op jit(solution)/shard_map/ppermute | solution.py:23
  14.8 7.5 %collective-permute-start.4 = (bf16[2,112,128]{2,1,0:T(8,128)(2,1)S(1)}, bf16[2,112,128]{2,1,0:T(8,128)(2,1)S(1)}, u32[]{:S(2)}, u32[]{:S(2)}) collective-permute-start(bf16[2,112,128]{2,1,0:T(8,128)(2,1)S(1)} %fusion), channel_id=1, source_target_pairs={{32,0},{0,32},{33,1},{1,33},{34,2},{2,34},{35,3},{3,35},{36,4},{4,... | collective-permute-start | bytes 172040 | tf_op jit(solution)/shard_map/ppermute | solution.py:27
  22.3 1.3 %copy-done = bf16[1792,384]{1,0:T(8,128)(2,1)S(1)} copy-done((bf16[1792,384]{1,0:T(8,128)(2,1)S(1)}, bf16[1792,384]{1,0:T(8,128)(2,1)}, u32[]{:S(2)}) %copy-start) | copy-done | bytes 1376280
  24.5 2.3 %collective-permute-start.8 = (bf16[2,112,128]{2,1,0:T(8,128)(2,1)S(1)}, bf16[2,112,128]{2,1,0:T(8,128)(2,1)S(1)}, u32[]{:S(2)}, u32[]{:S(2)}) collective-permute-start(bf16[2,112,128]{2,1,0:T(8,128)(2,1)S(1)} %add_convert_fusion), channel_id=1, source_target_pairs={{12,0},{8,4},{4,8},{0,12},{13,1},{9,5},{5,9},{1,13},{14,2},{10,6},... | collective-permute-start | bytes 172040 | tf_op jit(solution)/shard_map/ppermute | solution.py:27
  26.8 1.3 %collective-permute-start.7 = (bf16[2,112,128]{2,1,0:T(8,128)(2,1)S(1)}, bf16[2,112,128]{2,1,0:T(8,128)(2,1)S(1)}, u32[]{:S(2)}, u32[]{:S(2)}) collective-permute-start(bf16[2,112,128]{2,1,0:T(8,128)(2,1)S(1)} %add_convert_fusion), channel_id=1, source_target_pairs={{8,0},{12,4},{0,8},{4,12},{9,1},{13,5},{1,9},{5,13},{10,2},{14,6},... | collective-permute-start | bytes 172040 | tf_op jit(solution)/shard_map/ppermute | solution.py:27
  28.1 1.3 %collective-permute-done.8 = bf16[2,112,128]{2,1,0:T(8,128)(2,1)S(1)} collective-permute-done((bf16[2,112,128]{2,1,0:T(8,128)(2,1)S(1)}, bf16[2,112,128]{2,1,0:T(8,128)(2,1)S(1)}, u32[]{:S(2)}, u32[]{:S(2)}) %collective-permute-start.8) | collective-permute-done | bytes 57376 | tf_op jit(solution)/shard_map/ppermute | solution.py:27
  30.0 2.2 %collective-permute-done.7 = bf16[2,112,128]{2,1,0:T(8,128)(2,1)S(1)} collective-permute-done((bf16[2,112,128]{2,1,0:T(8,128)(2,1)S(1)}, bf16[2,112,128]{2,1,0:T(8,128)(2,1)S(1)}, u32[]{:S(2)}, u32[]{:S(2)}) %collective-permute-start.7) | collective-permute-done | bytes 57376 | tf_op jit(solution)/shard_map/ppermute | solution.py:27
  32.2 1.4 %collective-permute-start.10 = (bf16[2,4,112,128]{3,2,1,0:T(8,128)(2,1)S(1)}, bf16[2,4,112,128]{3,2,1,0:T(8,128)(2,1)S(1)}, u32[]{:S(2)}, u32[]{:S(2)}) collective-permute-start(bf16[2,4,112,128]{3,2,1,0:T(8,128)(2,1)S(1)} %get-tuple-element.40.own), channel_id=1, source_target_pairs={{192,0},{193,1},{194,2},{195,3},{196,4},{197,5},{198,6},{199,7},{2... | collective-permute-start | bytes 688136 | tf_op jit(solution)/shard_map/ppermute | solution.py:37
  33.6 1.5 %collective-permute-start.9 = (bf16[2,4,112,128]{3,2,1,0:T(8,128)(2,1)S(1)}, bf16[2,4,112,128]{3,2,1,0:T(8,128)(2,1)S(1)}, u32[]{:S(2)}, u32[]{:S(2)}) collective-permute-start(bf16[2,4,112,128]{3,2,1,0:T(8,128)(2,1)S(1)} %get-tuple-element.40.own), channel_id=1, source_target_pairs={{64,0},{65,1},{66,2},{67,3},{68,4},{69,5},{70,6},{71,7},{72,8},{73... | collective-permute-start | bytes 688136 | tf_op jit(solution)/shard_map/ppermute | solution.py:37
  35.1 3.6 %collective-permute-done.10.before = bf16[2,4,112,128]{3,2,1,0:T(8,128)(2,1)S(1)} collective-permute-done((bf16[2,4,112,128]{3,2,1,0:T(8,128)(2,1)S(1)}, bf16[2,4,112,128]{3,2,1,0:T(8,128)(2,1)S(1)}, u32[]{:S(2)}, u32[]{:S(2)}) %collective-permute-start.10) | collective-permute-done | bytes 229408 | tf_op jit(solution)/shard_map/ppermute | solution.py:37
  38.9 1.5 %collective-permute-start.16 = (bf16[3,2,4,112,128]{4,3,2,1,0:T(8,128)(2,1)S(1)}, bf16[3,2,4,112,128]{4,3,2,1,0:T(8,128)(2,1)S(1)}, u32[]{:S(2)}, u32[]{:S(2)}) collective-permute-start(bf16[3,2,4,112,128]{4,3,2,1,0:T(8,128)(2,1)S(1)} %pad_maximum_fusion), channel_id=1, source_target_pairs={{3,0},{0,1},{1,2},{2,3},{7,4},{4,5},{5,6},{6,7},{11,8},{8,9},{9,10... | collective-permute-start | bytes 2064392 | tf_op jit(solution)/shard_map/ppermute | solution.py:37
  40.4 8.6 %collective-permute-done.11.after = bf16[3,2,4,112,128]{4,3,2,1,0:T(8,128)(2,1)S(1)} collective-permute-done((bf16[3,2,4,112,128]{4,3,2,1,0:T(8,128)(2,1)S(1)}, bf16[3,2,4,112,128]{4,3,2,1,0:T(8,128)(2,1)S(1)}, u32[]{:S(2)}, u32[]{:S(2)}) %collective-permute-start.11) | collective-permute-done | bytes 688160 | tf_op jit(solution)/shard_map/ppermute | solution.py:37
  49.0 2.2 %collective-permute-start.12 = (bf16[3,2,4,112,128]{4,3,2,1,0:T(8,128)(2,1)S(1)}, bf16[3,2,4,112,128]{4,3,2,1,0:T(8,128)(2,1)S(1)}, u32[]{:S(2)}, u32[]{:S(2)}) collective-permute-start(bf16[3,2,4,112,128]{4,3,2,1,0:T(8,128)(2,1)S(1)} %collective-permute-done.11.after), channel_id=1, source_target_pairs={{1,0},{2,1},{3,2},{0,3},{5,4},{6,5},{7,6},{4,7},{9,8},{10,9},{11,1... | collective-permute-start | bytes 2064392 | tf_op jit(solution)/shard_map/ppermute | solution.py:37
  51.2 2.9 %collective-permute-start.13 = (bf16[2,4,112,128]{3,2,1,0:T(8,128)(2,1)S(1)}, bf16[2,4,112,128]{3,2,1,0:T(8,128)(2,1)S(1)}, u32[]{:S(2)}, u32[]{:S(2)}) collective-permute-start(bf16[2,4,112,128]{3,2,1,0:T(8,128)(2,1)S(1)} %get-tuple-element.40.own), channel_id=1, source_target_pairs={{128,0},{129,1},{130,2},{131,3},{132,4},{133,5},{134,6},{135,7},{1... | collective-permute-start | bytes 688136 | tf_op jit(solution)/shard_map/ppermute | solution.py:37
  54.1 1.4 %shard_map.40.start = f32[1024,768]{1,0:T(8,128)S(1)} custom-call(s32[4]{0:T(128)S(1)} %pad_add_fusion.place, bf16[2,4,112,128]{3,2,1,0:T(8,128)(2,1)S(1)} %get-tuple-element.40.own, bf16[2,4,112,128]{3,2,1,0:T(8,128)(2,1)S(1)} %collective-permute-done.9.after, bf16[2,4,112,128]{3,2,1,0:T(8,128)(2,1)S(1)} %collective-permute-done.10.before, ...), custom_call_target="tpu_custom_call" | custom-call | flops 1000000000 | bytes 2097152 | tf_op jit(solution)/shard_map/pallas_call | solution.py:188
  55.5 3.4 %collective-permute-done.13.far = bf16[2,4,112,128]{3,2,1,0:T(8,128)(2,1)S(1)} collective-permute-done((bf16[2,4,112,128]{3,2,1,0:T(8,128)(2,1)S(1)}, bf16[2,4,112,128]{3,2,1,0:T(8,128)(2,1)S(1)}, u32[]{:S(2)}, u32[]{:S(2)}) %collective-permute-start.13) | collective-permute-done | bytes 229408 | tf_op jit(solution)/shard_map/ppermute | solution.py:37
  58.9 1.4 %collective-permute-start.14 = (bf16[2,4,112,128]{3,2,1,0:T(8,128)(2,1)S(1)}, bf16[2,4,112,128]{3,2,1,0:T(8,128)(2,1)S(1)}, u32[]{:S(2)}, u32[]{:S(2)}) collective-permute-start(bf16[2,4,112,128]{3,2,1,0:T(8,128)(2,1)S(1)} %collective-permute-done.13.far), channel_id=1, source_target_pairs={{1,0},{2,1},{3,2},{0,3},{5,4},{6,5},{7,6},{4,7},{9,8},{10,9},{11,1... | collective-permute-start | bytes 688136 | tf_op jit(solution)/shard_map/ppermute | solution.py:37
  60.3 2.4 %shard_map.41.start = f32[1024,768]{1,0:T(8,128)S(1)} custom-call(s32[4]{0:T(128)S(1)} %pad_add_fusion.place, bf16[2,4,112,128]{3,2,1,0:T(8,128)(2,1)S(1)} %collective-permute-done.13.far, bf16[3,2,4,112,128]{4,3,2,1,0:T(8,128)(2,1)S(1)} %collective-permute-done.11.after, ...), custom_call_target="tpu_custom_call", output_to_operand_aliasing={{}: (5, {})} | custom-call | flops 1000000000 | bytes 2097152 | tf_op jit(solution)/shard_map/pallas_call | solution.py:188
  62.7 1.3 %collective-permute-done.14.after = bf16[2,4,112,128]{3,2,1,0:T(8,128)(2,1)S(1)} collective-permute-done((bf16[2,4,112,128]{3,2,1,0:T(8,128)(2,1)S(1)}, bf16[2,4,112,128]{3,2,1,0:T(8,128)(2,1)S(1)}, u32[]{:S(2)}, u32[]{:S(2)}) %collective-permute-start.14) | collective-permute-done | bytes 229408 | tf_op jit(solution)/shard_map/ppermute | solution.py:37
  64.0 4.8 %collective-permute-done.15.before = bf16[2,4,112,128]{3,2,1,0:T(8,128)(2,1)S(1)} collective-permute-done((bf16[2,4,112,128]{3,2,1,0:T(8,128)(2,1)S(1)}, bf16[2,4,112,128]{3,2,1,0:T(8,128)(2,1)S(1)}, u32[]{:S(2)}, u32[]{:S(2)}) %collective-permute-start.15) | collective-permute-done | bytes 229408 | tf_op jit(solution)/shard_map/ppermute | solution.py:37
  68.8 1.3 %shard_map.42.start = f32[1024,768]{1,0:T(8,128)S(1)} custom-call(s32[4]{0:T(128)S(1)} %pad_add_fusion.place, bf16[2,4,112,128]{3,2,1,0:T(8,128)(2,1)S(1)} %collective-permute-done.14.after, bf16[2,4,112,128]{3,2,1,0:T(8,128)(2,1)S(1)} %collective-permute-done.15.before, bf16[4,448,768]{2,1,0:T(8,128)(2,1)S(1)} %shard_map.39.both, ...), custom_call_target="tpu_custom_call", output_to_operand_aliasing={{}: (4, {})} | custom-call | flops 1000000000 | bytes 2097152 | tf_op jit(solution)/shard_map/pallas_call | solution.py:188
  70.8 9.7 %collective-permute-start.19 = (bf16[512,384]{1,0:T(8,128)(2,1)S(1)}, bf16[512,384]{1,0:T(8,128)(2,1)S(1)}, u32[]{:S(2)}, u32[]{:S(2)}) collective-permute-start(bf16[512,384]{1,0:T(8,128)(2,1)S(1)} %get-tuple-element.38), channel_id=1, source_target_pairs={{16,0},{0,16},{17,1},{1,17},{18,2},{2,18},{19,3},{3,19},{20,4},{4,... | collective-permute-start | bytes 1179656 | tf_op jit(solution)/shard_map/ppermute | solution.py:23
  80.5 1.5 %shard_map.43 = (bf16[512,384]{1,0:T(8,128)(2,1)S(1)}, bf16[512,384]{1,0:T(8,128)(2,1)S(1)}) custom-call(s32[4]{0:T(128)S(1)} %pad_add_fusion.place, bf16[3,2,4,112,128]{4,3,2,1,0:T(8,128)(2,1)S(1)} %collective-permute-done.12.low, bf16[2,4,112,128]{3,2,1,0:T(8,128)(2,1)S(1)} %collective-permute-done.17.far2, bf16[4,448,768]{2,1,0:T(8,128)(2,1)S(1)} %shard_map.39.both, ...), custom_call_target="tpu_custom_call" | custom-call | flops 1000000000 | bytes 2097152 | tf_op jit(solution)/shard_map/pallas_call | solution.py:188
  81.9 4.1 %collective-permute-start.18 = (bf16[512,384]{1,0:T(8,128)(2,1)S(1)}, bf16[512,384]{1,0:T(8,128)(2,1)S(1)}, u32[]{:S(2)}, u32[]{:S(2)}) collective-permute-start(bf16[512,384]{1,0:T(8,128)(2,1)S(1)} %get-tuple-element.35), channel_id=1, source_target_pairs={{16,0},{0,16},{17,1},{1,17},{18,2},{2,18},{19,3},{3,19},{20,4},{4,... | collective-permute-start | bytes 1179656 | tf_op jit(solution)/shard_map/ppermute | solution.py:23
  86.1 1.6 %shard_map.45.given = bf16[2048,384]{1,0:T(8,128)(2,1)} custom-call(s32[4]{0:T(128)S(1)} %pad_add_fusion.place, bf16[512,384]{1,0:T(8,128)(2,1)S(1)} %get-tuple-element.36.mine1, bf16[512,384]{1,0:T(8,128)(2,1)S(1)} %get-tuple-element.37.mine2, bf16[512,384]{1,0:T(8,128)(2,1)S(1)} %collective-permute-done.19.theirs1), custom_call_target="tpu_custom_call" | custom-call | bytes 2097152 | tf_op jit(solution)/shard_map/pallas_call | solution.py:188
  87.7 1.3 %shard_map.46 = bf16[2048,384]{1,0:T(8,128)(2,1)} custom-call(s32[4]{0:T(128)S(1)} %pad_add_fusion.place, bf16[512,384]{1,0:T(8,128)(2,1)S(1)} %collective-permute-done.18.theirs2, bf16[2048,384]{1,0:T(8,128)(2,1)} %shard_map.45.given), custom_call_target="tpu_custom_call", output_to_operand_aliasing={{}: (2, {})} | custom-call | bytes 2097152 | tf_op jit(solution)/shard_map/pallas_call | solution.py:188
  (29 shorter events, 6.0 us)
Async XLA Ops:
  0.0 22.3 %collective-permute-start.5 = (bf16[1792,384]{1,0:T(8,128)(2,1)}, bf16[1792,384]{1,0:T(8,128)(2,1)S(1)}, u32[]{:S(2)}, u32[]{:S(2)}) collective-permute-start(bf16[1792,384]{1,0:T(8,128)(2,1)} %own.1), channel_id=1, source_target_pairs={{16,0},{0,16},{17,1},{1,17},{18,2},{2,18},{19,3},{3,19},{20,4},{4,... | collective-permute-start | bytes 4128776 | tf_op jit(solution)/shard_map/ppermute | solution.py:23
  3.3 1.0 %copy-start.1 = (bf16[112,2048]{1,0:T(8,128)(2,1)S(1)}, bf16[112,2048]{1,0:T(8,128)(2,1)}, u32[]{:S(2)}) copy-start(bf16[112,2048]{1,0:T(8,128)(2,1)} %panel.1) | copy-start | bytes 1376260
  4.3 0.7 copy-start.2
  6.1 1.9 %collective-permute-start = (f32[8,112,128]{2,1,0:T(8,128)S(1)}, f32[8,112,128]{2,1,0:T(8,128)S(1)}, u32[]{:S(2)}, u32[]{:S(2)}) collective-permute-start(f32[8,112,128]{2,1,0:T(8,128)S(1)} %get-tuple-element.23), channel_id=1, source_target_pairs={{16,0},{0,16},{17,1},{1,17},{18,2},{2,18},{19,3},{3,19},{20,4},{4,... | collective-permute-start | bytes 1376264 | tf_op jit(solution)/shard_map/ppermute | solution.py:23
  8.6 3.1 %collective-permute-start.1 = (bf16[2,112,128]{2,1,0:T(8,128)(2,1)S(1)}, bf16[2,112,128]{2,1,0:T(8,128)(2,1)S(1)}, u32[]{:S(2)}, u32[]{:S(2)}) collective-permute-start(bf16[2,112,128]{2,1,0:T(8,128)(2,1)S(1)} %get-tuple-element.25), channel_id=1, source_target_pairs={{64,0},{128,64},{192,128},{0,192},{65,1},{129,65},{193,129},{1,193... | collective-permute-start | bytes 172040 | tf_op jit(solution)/shard_map/ppermute | solution.py:23
  9.4 4.2 %collective-permute-start.2 = (bf16[2,112,128]{2,1,0:T(8,128)(2,1)S(1)}, bf16[2,112,128]{2,1,0:T(8,128)(2,1)S(1)}, u32[]{:S(2)}, u32[]{:S(2)}) collective-permute-start(bf16[2,112,128]{2,1,0:T(8,128)(2,1)S(1)} %get-tuple-element.26), channel_id=1, source_target_pairs={{192,0},{0,64},{64,128},{128,192},{193,1},{1,65},{65,129},{129,193... | collective-permute-start | bytes 172040 | tf_op jit(solution)/shard_map/ppermute | solution.py:23
  10.1 4.6 %collective-permute-start.3 = (bf16[2,112,128]{2,1,0:T(8,128)(2,1)S(1)}, bf16[2,112,128]{2,1,0:T(8,128)(2,1)S(1)}, u32[]{:S(2)}, u32[]{:S(2)}) collective-permute-start(bf16[2,112,128]{2,1,0:T(8,128)(2,1)S(1)} %get-tuple-element.27), channel_id=1, source_target_pairs={{128,0},{192,64},{0,128},{64,192},{129,1},{193,65},{1,129},{65,193... | collective-permute-start | bytes 172040 | tf_op jit(solution)/shard_map/ppermute | solution.py:23
  14.8 9.6 %collective-permute-start.4 = (bf16[2,112,128]{2,1,0:T(8,128)(2,1)S(1)}, bf16[2,112,128]{2,1,0:T(8,128)(2,1)S(1)}, u32[]{:S(2)}, u32[]{:S(2)}) collective-permute-start(bf16[2,112,128]{2,1,0:T(8,128)(2,1)S(1)} %fusion), channel_id=1, source_target_pairs={{32,0},{0,32},{33,1},{1,33},{34,2},{2,34},{35,3},{3,35},{36,4},{4,... | collective-permute-start | bytes 172040 | tf_op jit(solution)/shard_map/ppermute | solution.py:27
  22.3 1.3 %copy-start = (bf16[1792,384]{1,0:T(8,128)(2,1)S(1)}, bf16[1792,384]{1,0:T(8,128)(2,1)}, u32[]{:S(2)}) copy-start(bf16[1792,384]{1,0:T(8,128)(2,1)} %own.1) | copy-start | bytes 4128772
  24.5 4.9 %collective-permute-start.8 = (bf16[2,112,128]{2,1,0:T(8,128)(2,1)S(1)}, bf16[2,112,128]{2,1,0:T(8,128)(2,1)S(1)}, u32[]{:S(2)}, u32[]{:S(2)}) collective-permute-start(bf16[2,112,128]{2,1,0:T(8,128)(2,1)S(1)} %add_convert_fusion), channel_id=1, source_target_pairs={{12,0},{8,4},{4,8},{0,12},{13,1},{9,5},{5,9},{1,13},{14,2},{10,6},... | collective-permute-start | bytes 172040 | tf_op jit(solution)/shard_map/ppermute | solution.py:27
  26.8 3.2 %collective-permute-start.6 = (bf16[2,112,128]{2,1,0:T(8,128)(2,1)S(1)}, bf16[2,112,128]{2,1,0:T(8,128)(2,1)S(1)}, u32[]{:S(2)}, u32[]{:S(2)}) collective-permute-start(bf16[2,112,128]{2,1,0:T(8,128)(2,1)S(1)} %add_convert_fusion), channel_id=1, source_target_pairs={{4,0},{0,4},{12,8},{8,12},{5,1},{1,5},{13,9},{9,13},{6,2},{2,6},{1... | collective-permute-start | bytes 172040 | tf_op jit(solution)/shard_map/ppermute | solution.py:27
  26.8 5.4 %collective-permute-start.7 = (bf16[2,112,128]{2,1,0:T(8,128)(2,1)S(1)}, bf16[2,112,128]{2,1,0:T(8,128)(2,1)S(1)}, u32[]{:S(2)}, u32[]{:S(2)}) collective-permute-start(bf16[2,112,128]{2,1,0:T(8,128)(2,1)S(1)} %add_convert_fusion), channel_id=1, source_target_pairs={{8,0},{12,4},{0,8},{4,12},{9,1},{13,5},{1,9},{5,13},{10,2},{14,6},... | collective-permute-start | bytes 172040 | tf_op jit(solution)/shard_map/ppermute | solution.py:27
  32.2 6.5 %collective-permute-start.10 = (bf16[2,4,112,128]{3,2,1,0:T(8,128)(2,1)S(1)}, bf16[2,4,112,128]{3,2,1,0:T(8,128)(2,1)S(1)}, u32[]{:S(2)}, u32[]{:S(2)}) collective-permute-start(bf16[2,4,112,128]{3,2,1,0:T(8,128)(2,1)S(1)} %get-tuple-element.40.own), channel_id=1, source_target_pairs={{192,0},{193,1},{194,2},{195,3},{196,4},{197,5},{198,6},{199,7},{2... | collective-permute-start | bytes 688136 | tf_op jit(solution)/shard_map/ppermute | solution.py:37
  33.6 5.2 %collective-permute-start.9 = (bf16[2,4,112,128]{3,2,1,0:T(8,128)(2,1)S(1)}, bf16[2,4,112,128]{3,2,1,0:T(8,128)(2,1)S(1)}, u32[]{:S(2)}, u32[]{:S(2)}) collective-permute-start(bf16[2,4,112,128]{3,2,1,0:T(8,128)(2,1)S(1)} %get-tuple-element.40.own), channel_id=1, source_target_pairs={{64,0},{65,1},{66,2},{67,3},{68,4},{69,5},{70,6},{71,7},{72,8},{73... | collective-permute-start | bytes 688136 | tf_op jit(solution)/shard_map/ppermute | solution.py:37
  38.8 10.2 %collective-permute-start.11 = (bf16[3,2,4,112,128]{4,3,2,1,0:T(8,128)(2,1)S(1)}, bf16[3,2,4,112,128]{4,3,2,1,0:T(8,128)(2,1)S(1)}, u32[]{:S(2)}, u32[]{:S(2)}) collective-permute-start(bf16[3,2,4,112,128]{4,3,2,1,0:T(8,128)(2,1)S(1)} %pad_maximum_fusion), channel_id=1, source_target_pairs={{1,0},{2,1},{3,2},{0,3},{5,4},{6,5},{7,6},{4,7},{9,8},{10,9},{11,1... | collective-permute-start | bytes 2064392 | tf_op jit(solution)/shard_map/ppermute | solution.py:37
  38.9 21.4 %collective-permute-start.16 = (bf16[3,2,4,112,128]{4,3,2,1,0:T(8,128)(2,1)S(1)}, bf16[3,2,4,112,128]{4,3,2,1,0:T(8,128)(2,1)S(1)}, u32[]{:S(2)}, u32[]{:S(2)}) collective-permute-start(bf16[3,2,4,112,128]{4,3,2,1,0:T(8,128)(2,1)S(1)} %pad_maximum_fusion), channel_id=1, source_target_pairs={{3,0},{0,1},{1,2},{2,3},{7,4},{4,5},{5,6},{6,7},{11,8},{8,9},{9,10... | collective-permute-start | bytes 2064392 | tf_op jit(solution)/shard_map/ppermute | solution.py:37
  49.0 21.1 %collective-permute-start.12 = (bf16[3,2,4,112,128]{4,3,2,1,0:T(8,128)(2,1)S(1)}, bf16[3,2,4,112,128]{4,3,2,1,0:T(8,128)(2,1)S(1)}, u32[]{:S(2)}, u32[]{:S(2)}) collective-permute-start(bf16[3,2,4,112,128]{4,3,2,1,0:T(8,128)(2,1)S(1)} %collective-permute-done.11.after), channel_id=1, source_target_pairs={{1,0},{2,1},{3,2},{0,3},{5,4},{6,5},{7,6},{4,7},{9,8},{10,9},{11,1... | collective-permute-start | bytes 2064392 | tf_op jit(solution)/shard_map/ppermute | solution.py:37
  51.2 7.7 %collective-permute-start.13 = (bf16[2,4,112,128]{3,2,1,0:T(8,128)(2,1)S(1)}, bf16[2,4,112,128]{3,2,1,0:T(8,128)(2,1)S(1)}, u32[]{:S(2)}, u32[]{:S(2)}) collective-permute-start(bf16[2,4,112,128]{3,2,1,0:T(8,128)(2,1)S(1)} %get-tuple-element.40.own), channel_id=1, source_target_pairs={{128,0},{129,1},{130,2},{131,3},{132,4},{133,5},{134,6},{135,7},{1... | collective-permute-start | bytes 688136 | tf_op jit(solution)/shard_map/ppermute | solution.py:37
  58.9 5.2 %collective-permute-start.14 = (bf16[2,4,112,128]{3,2,1,0:T(8,128)(2,1)S(1)}, bf16[2,4,112,128]{3,2,1,0:T(8,128)(2,1)S(1)}, u32[]{:S(2)}, u32[]{:S(2)}) collective-permute-start(bf16[2,4,112,128]{3,2,1,0:T(8,128)(2,1)S(1)} %collective-permute-done.13.far), channel_id=1, source_target_pairs={{1,0},{2,1},{3,2},{0,3},{5,4},{6,5},{7,6},{4,7},{9,8},{10,9},{11,1... | collective-permute-start | bytes 688136 | tf_op jit(solution)/shard_map/ppermute | solution.py:37
  60.3 8.5 %collective-permute-start.15 = (bf16[2,4,112,128]{3,2,1,0:T(8,128)(2,1)S(1)}, bf16[2,4,112,128]{3,2,1,0:T(8,128)(2,1)S(1)}, u32[]{:S(2)}, u32[]{:S(2)}) collective-permute-start(bf16[2,4,112,128]{3,2,1,0:T(8,128)(2,1)S(1)} %collective-permute-done.13.far), channel_id=1, source_target_pairs={{3,0},{0,1},{1,2},{2,3},{7,4},{4,5},{5,6},{6,7},{11,8},{8,9},{9,10... | collective-permute-start | bytes 688136 | tf_op jit(solution)/shard_map/ppermute | solution.py:37
  68.8 11.6 %collective-permute-start.17 = (bf16[2,4,112,128]{3,2,1,0:T(8,128)(2,1)S(1)}, bf16[2,4,112,128]{3,2,1,0:T(8,128)(2,1)S(1)}, u32[]{:S(2)}, u32[]{:S(2)}) collective-permute-start(bf16[2,4,112,128]{3,2,1,0:T(8,128)(2,1)S(1)} %collective-permute-done.15.before), channel_id=1, source_target_pairs={{3,0},{0,1},{1,2},{2,3},{7,4},{4,5},{5,6},{6,7},{11,8},{8,9},{9,10... | collective-permute-start | bytes 688136 | tf_op jit(solution)/shard_map/ppermute | solution.py:37
  70.8 15.3 %collective-permute-start.19 = (bf16[512,384]{1,0:T(8,128)(2,1)S(1)}, bf16[512,384]{1,0:T(8,128)(2,1)S(1)}, u32[]{:S(2)}, u32[]{:S(2)}) collective-permute-start(bf16[512,384]{1,0:T(8,128)(2,1)S(1)} %get-tuple-element.38), channel_id=1, source_target_pairs={{16,0},{0,16},{17,1},{1,17},{18,2},{2,18},{19,3},{3,19},{20,4},{4,... | collective-permute-start | bytes 1179656 | tf_op jit(solution)/shard_map/ppermute | solution.py:23
  81.9 5.7 %collective-permute-start.18 = (bf16[512,384]{1,0:T(8,128)(2,1)S(1)}, bf16[512,384]{1,0:T(8,128)(2,1)S(1)}, u32[]{:S(2)}, u32[]{:S(2)}) collective-permute-start(bf16[512,384]{1,0:T(8,128)(2,1)S(1)} %get-tuple-element.35), channel_id=1, source_target_pairs={{16,0},{0,16},{17,1},{1,17},{18,2},{2,18},{19,3},{3,19},{20,4},{4,... | collective-permute-start | bytes 1179656 | tf_op jit(solution)/shard_map/ppermute | solution.py:23

commit v5 on v4

--- a/solution.py
+++ b/solution.py
@@ -83,7 +83,7 @@
 
 
 def slabs(block):
-    return [block[i] for i in range(block.shape[0])]
+    return [block.at[i] for i in range(block.shape[0])]
 
 
 def rows(first, count=1):
@@ -108,7 +108,9 @@
     @on_core(place, 0)
     def _():
         out[rows(0, 3)] = (
-            start[rows(0, 3)] + dot_t(by_x(*slabs(after)), both[1]) + dot_t(by_x(*slabs(before)), both[2])
+            start[rows(0, 3)]
+            + dot_t(by_x(*slabs(after)), both[1])
+            + dot_t(by_x(*slabs(before)), both[2])
         )
         out[rows(3)] = dot_t(by_x(far), both[0])
 
@@ -146,19 +148,19 @@
         keep(start[rows(0, 2)])
 
 
-def product_five(place, low, far2, both, start, mine, theirs):
+def product_five(place, low, high, both, start, mine, theirs):
     def keep(at, total):
         mine[at] = total[:, :384].astype(BF16)
         theirs[at] = total[:, 384:].astype(BF16)
 
     @on_core(place, 0)
     def _():
-        keep(rows(0, 2), start[rows(2, 2)] + dot_t(by_x(low[2], far2), both[3]))
+        keep(rows(0, 2), start[rows(2, 2)] + dot_t(by_x(*slabs(high)), both[3]))
 
     @on_core(place, 1)
     def _():
         keep(rows(0), start[rows(2)])
-        keep(rows(1), dot_t(by_y(*slabs(low), far2), deep(both, 0, 4)))
+        keep(rows(1), dot_t(by_y(*slabs(low), *slabs(high)), deep(both, 0, 4)))
 
 
 def place_rows(place, parts, out, sems):
@@ -184,14 +186,14 @@
     place_rows(place, [(theirs2, 1 - place[2], 1)], out, sems)
 
 
-def call(kernel, out_shape, operands, out_specs=VMEM, specs=None, flops=0, **more):
+def call(kernel, out_shape, operands, out_specs=VMEM, specs=None, **more):
     return pl.pallas_call(
         kernel,
         out_shape=out_shape,
         in_specs=specs or [SMEM] + [VMEM] * (len(operands) - 1),
         out_specs=out_specs,
         compiler_params=PARAMS,
-        cost_estimate=pl.CostEstimate(flops=flops, bytes_accessed=2**21, transcendentals=0),
+        cost_estimate=pl.CostEstimate(flops=0, bytes_accessed=0, transcendentals=0),
         **more,
     )(*operands)
 
@@ -222,42 +224,37 @@
     part = (part + share.astype(F32)).astype(BF16)
     own = jnp.stack([part] + [swap(part, "z_lo", 4, bits) for bits in (1, 2, 3)], 1)
 
-    after, before, far = (turn(own, 0, ahead) for ahead in (1, 3, 2))
-    three = [own, after, before]
+    after, before = turn(own, 0, 1), turn(own, 0, 3)
+    far = jnp.concatenate([turn(after[:1], 0, 1), turn(before[1:], 0, 3)])
     total = jax.ShapeDtypeStruct((1024, 768), F32)
-    total_one = call(product_one, total, (place, *three, both), flops=10**9)
-    sent = jnp.stack(three)
-    after, before = turn(sent, 1, 1), turn(sent, 1, 3)
+    total_one = call(product_one, total, (place, own, after, before, both))
+    sent = jnp.stack([own, after, before])
+    after1, before1 = turn(sent, 1, 1), turn(sent, 1, 3)
     far, total_one = lax.optimization_barrier((far, total_one))
     after2, before2 = turn(far, 1, 1), turn(far, 1, 3)
-    low = turn(after, 1, 1)
+    low, high = turn(after1[:2], 1, 1), turn(jnp.stack([before1[2], before2]), 1, 3)
     total_two = call(
         product_two,
         total,
-        (place, far, after, before, both, total_one),
-        flops=10**9,
+        (place, far, after1, before1, both, total_one),
         input_output_aliases={5: 0},
     )
-    after2, before2, total_two = lax.optimization_barrier((after2, before2, total_two))
-    far2 = turn(before2, 1, 3)
     total_three = call(
         product_three,
         total,
         (place, after2, before2, both, total_two),
-        flops=10**9,
         input_output_aliases={4: 0},
     )
     half = jax.ShapeDtypeStruct((512, 384), BF16)
     mine1, theirs1 = call(
-        product_four, (half, half), (place, low, both, total_three), (VMEM, VMEM), flops=10**9
+        product_four, (half, half), (place, low, both, total_three), (VMEM, VMEM)
     )
     theirs1 = fetch(theirs1, "core", 2, 1)
     mine2, theirs2 = call(
         product_five,
         (half, half),
-        (place, low, far2, both, total_three),
+        (place, low, high, both, total_three),
         (VMEM, VMEM),
-        flops=10**9,
     )
     theirs2 = fetch(theirs2, "core", 2, 1)
 

time: 89.4 us -> 79.2 us (0.89)
  waiting for transfers between devices: 31.2 us -> 22.3 us
  starting transfers between devices: 41.8 us -> 40 us
    ppermute x9 -> x10, waiting for transfers between devices: 21.7 us -> 12.7 us  [turn(): return lax.ppermute(block, ROW + COL, pairs)]
    ppermute x7, starting transfers between devices: 19.7 us -> 16.2 us  [fetch(): lax.ppermute(block, axis, [((i + ahead) % size, i) for i in range(size)])]
    ppermute x9 -> x10, starting transfers between devices: 11.1 us -> 12.7 us  [turn(): return lax.ppermute(block, ROW + COL, pairs)]
  transfers between devices with their start and end apart: 20 -> 21, of which waited for: 12 -> 14; matrix products, arithmetic and copies ran while one was open for 0% -> 0% of each run, Pallas kernels for 12% -> 14%
where the time goes in v5:
time: 79.2 us; the launch traced here: 78.6 us
  starting transfers between devices  40 us (51%)
  waiting for transfers between devices  22.3 us (28%)
  Pallas kernels  12.5 us (16%)
  local copies, waits for them, and re-layouts  3.17 us (4%)
    ppermute x7, starting transfers between devices, fetch(): lax.ppermute(block, axis, [((i + ahead) % size, i) for i in range(size)])  16.2 us
    ppermute x10, waiting for transfers between devices, turn(): return lax.ppermute(block, ROW + COL, pairs)  12.7 us
    ppermute x10, starting transfers between devices, turn(): return lax.ppermute(block, ROW + COL, pairs)  12.7 us
    pallas_call x10, Pallas kernels, call(): pl.pallas_call(kernel, out_shape=out_shape, in_specs=specs or [SMEM] + [V...  12.5 us
    ppermute x4, starting transfers between devices, swap(): return lax.ppermute(block, axis, [(i ^ bits, i) for i in range(size)])  11.1 us
    ppermute x7, waiting for transfers between devices, fetch(): lax.ppermute(block, axis, [((i + ahead) % size, i) for i in range(size)])  5.53 us
    ppermute x4, waiting for transfers between devices, swap(): return lax.ppermute(block, axis, [(i ^ bits, i) for i in range(size)])  4.06 us
    unnamed x6, local copies, waits for them, and re-layouts  3.11 us
  transfers between devices with their start and end apart: 21, of which 14 were waited for; matrix products, arithmetic and copies ran while one was open for 0% of the time, Pallas kernels for 14%

profile of v5, /device:TPU:1, one launch (start us, length us, event | category | flops | bytes accessed | tf_op | source)
XLA Modules:
  0.0 78.6 jit_solution(6450844712608636367)
XLA Ops:
  0.0 3.2 %collective-permute-start.5 = (bf16[1792,384]{1,0:T(8,128)(2,1)}, bf16[1792,384]{1,0:T(8,128)(2,1)S(1)}, u32[]{:S(2)}, u32[]{:S(2)}) collective-permute-start(bf16[1792,384]{1,0:T(8,128)(2,1)} %own.1), channel_id=1, source_target_pairs={{16,0},{0,16},{17,1},{1,17},{18,2},{2,18},{19,3},{3,19},{20,4},{4,... | collective-permute-start | bytes 4128776 | tf_op jit(solution)/shard_map/ppermute | solution.py:23
  3.3 1.0 %copy-done.1 = bf16[112,2048]{1,0:T(8,128)(2,1)S(1)} copy-done((bf16[112,2048]{1,0:T(8,128)(2,1)S(1)}, bf16[112,2048]{1,0:T(8,128)(2,1)}, u32[]{:S(2)}) %copy-start.1) | copy-done | bytes 458776
  4.3 0.7 copy-done.2
  5.1 1.0 %shard_map.37 = (f32[8,112,128]{2,1,0:T(8,128)S(1)}, f32[8,112,128]{2,1,0:T(8,128)S(1)}) custom-call(s32[4]{0:T(128)S(1)} %pad_add_fusion.place, bf16[112,112]{1,0:T(8,128)(2,1)S(1)} %copy-done.2, bf16[112,2048]{1,0:T(8,128)(2,1)S(1)} %copy-done.1), custom_call_target="tpu_custom_call" | custom-call | tf_op jit(solution)/shard_map/pallas_call | solution.py:190
  6.2 1.8 %collective-permute-done.received = f32[8,112,128]{2,1,0:T(8,128)S(1)} collective-permute-done((f32[8,112,128]{2,1,0:T(8,128)S(1)}, f32[8,112,128]{2,1,0:T(8,128)S(1)}, u32[]{:S(2)}, u32[]{:S(2)}) %collective-permute-start) | collective-permute-done | bytes 458784 | tf_op jit(solution)/shard_map/ppermute | solution.py:23
  8.6 0.8 %collective-permute-start.1 = (bf16[2,112,128]{2,1,0:T(8,128)(2,1)S(1)}, bf16[2,112,128]{2,1,0:T(8,128)(2,1)S(1)}, u32[]{:S(2)}, u32[]{:S(2)}) collective-permute-start(bf16[2,112,128]{2,1,0:T(8,128)(2,1)S(1)} %get-tuple-element.22), channel_id=1, source_target_pairs={{64,0},{128,64},{192,128},{0,192},{65,1},{129,65},{193,129},{1,193... | collective-permute-start | bytes 172040 | tf_op jit(solution)/shard_map/ppermute | solution.py:23
  10.1 1.0 %collective-permute-start.3 = (bf16[2,112,128]{2,1,0:T(8,128)(2,1)S(1)}, bf16[2,112,128]{2,1,0:T(8,128)(2,1)S(1)}, u32[]{:S(2)}, u32[]{:S(2)}) collective-permute-start(bf16[2,112,128]{2,1,0:T(8,128)(2,1)S(1)} %get-tuple-element.24), channel_id=1, source_target_pairs={{128,0},{192,64},{0,128},{64,192},{129,1},{193,65},{1,129},{65,193... | collective-permute-start | bytes 172040 | tf_op jit(solution)/shard_map/ppermute | solution.py:23
  11.7 2.0 %collective-permute-done.2 = bf16[2,112,128]{2,1,0:T(8,128)(2,1)S(1)} collective-permute-done((bf16[2,112,128]{2,1,0:T(8,128)(2,1)S(1)}, bf16[2,112,128]{2,1,0:T(8,128)(2,1)S(1)}, u32[]{:S(2)}, u32[]{:S(2)}) %collective-permute-start.2) | collective-permute-done | bytes 57376 | tf_op jit(solution)/shard_map/ppermute | solution.py:23
  13.6 1.1 %collective-permute-done.3 = bf16[2,112,128]{2,1,0:T(8,128)(2,1)S(1)} collective-permute-done((bf16[2,112,128]{2,1,0:T(8,128)(2,1)S(1)}, bf16[2,112,128]{2,1,0:T(8,128)(2,1)S(1)}, u32[]{:S(2)}, u32[]{:S(2)}) %collective-permute-start.3) | collective-permute-done | bytes 57376 | tf_op jit(solution)/shard_map/ppermute | solution.py:23
  14.8 7.5 %collective-permute-start.4 = (bf16[2,112,128]{2,1,0:T(8,128)(2,1)S(1)}, bf16[2,112,128]{2,1,0:T(8,128)(2,1)S(1)}, u32[]{:S(2)}, u32[]{:S(2)}) collective-permute-start(bf16[2,112,128]{2,1,0:T(8,128)(2,1)S(1)} %fusion), channel_id=1, source_target_pairs={{32,0},{0,32},{33,1},{1,33},{34,2},{2,34},{35,3},{3,35},{36,4},{4,... | collective-permute-start | bytes 172040 | tf_op jit(solution)/shard_map/ppermute | solution.py:27
  22.3 1.3 %copy-done = bf16[1792,384]{1,0:T(8,128)(2,1)S(1)} copy-done((bf16[1792,384]{1,0:T(8,128)(2,1)S(1)}, bf16[1792,384]{1,0:T(8,128)(2,1)}, u32[]{:S(2)}) %copy-start) | copy-done | bytes 1376280
  23.6 0.8 %shard_map.39.both = bf16[4,448,768]{2,1,0:T(8,128)(2,1)S(1)} custom-call(s32[4]{0:T(128)S(1)} %pad_add_fusion.place, bf16[1792,384]{1,0:T(8,128)(2,1)S(1)} %copy-done, bf16[1792,384]{1,0:T(8,128)(2,1)S(1)} %collective-permute-done.5.other), custom_call_target="tpu_custom_call" | custom-call | tf_op jit(solution)/shard_map/pallas_call | solution.py:190
  24.5 2.3 %collective-permute-start.8 = (bf16[2,112,128]{2,1,0:T(8,128)(2,1)S(1)}, bf16[2,112,128]{2,1,0:T(8,128)(2,1)S(1)}, u32[]{:S(2)}, u32[]{:S(2)}) collective-permute-start(bf16[2,112,128]{2,1,0:T(8,128)(2,1)S(1)} %add_convert_fusion), channel_id=1, source_target_pairs={{12,0},{8,4},{4,8},{0,12},{13,1},{9,5},{5,9},{1,13},{14,2},{10,6},... | collective-permute-start | bytes 172040 | tf_op jit(solution)/shard_map/ppermute | solution.py:27
  26.8 1.3 %collective-permute-start.7 = (bf16[2,112,128]{2,1,0:T(8,128)(2,1)S(1)}, bf16[2,112,128]{2,1,0:T(8,128)(2,1)S(1)}, u32[]{:S(2)}, u32[]{:S(2)}) collective-permute-start(bf16[2,112,128]{2,1,0:T(8,128)(2,1)S(1)} %add_convert_fusion), channel_id=1, source_target_pairs={{8,0},{12,4},{0,8},{4,12},{9,1},{13,5},{1,9},{5,13},{10,2},{14,6},... | collective-permute-start | bytes 172040 | tf_op jit(solution)/shard_map/ppermute | solution.py:27
  28.1 1.3 %collective-permute-done.8 = bf16[2,112,128]{2,1,0:T(8,128)(2,1)S(1)} collective-permute-done((bf16[2,112,128]{2,1,0:T(8,128)(2,1)S(1)}, bf16[2,112,128]{2,1,0:T(8,128)(2,1)S(1)}, u32[]{:S(2)}, u32[]{:S(2)}) %collective-permute-start.8) | collective-permute-done | bytes 57376 | tf_op jit(solution)/shard_map/ppermute | solution.py:27
  30.0 2.2 %collective-permute-done.7 = bf16[2,112,128]{2,1,0:T(8,128)(2,1)S(1)} collective-permute-done((bf16[2,112,128]{2,1,0:T(8,128)(2,1)S(1)}, bf16[2,112,128]{2,1,0:T(8,128)(2,1)S(1)}, u32[]{:S(2)}, u32[]{:S(2)}) %collective-permute-start.7) | collective-permute-done | bytes 57376 | tf_op jit(solution)/shard_map/ppermute | solution.py:27
  32.2 1.4 %collective-permute-start.10 = (bf16[2,4,112,128]{3,2,1,0:T(8,128)(2,1)S(1)}, bf16[2,4,112,128]{3,2,1,0:T(8,128)(2,1)S(1)}, u32[]{:S(2)}, u32[]{:S(2)}) collective-permute-start(bf16[2,4,112,128]{3,2,1,0:T(8,128)(2,1)S(1)} %get-tuple-element.34.own), channel_id=1, source_target_pairs={{192,0},{193,1},{194,2},{195,3},{196,4},{197,5},{198,6},{199,7},{2... | collective-permute-start | bytes 688136 | tf_op jit(solution)/shard_map/ppermute | solution.py:37
  33.6 1.5 %collective-permute-start.9 = (bf16[2,4,112,128]{3,2,1,0:T(8,128)(2,1)S(1)}, bf16[2,4,112,128]{3,2,1,0:T(8,128)(2,1)S(1)}, u32[]{:S(2)}, u32[]{:S(2)}) collective-permute-start(bf16[2,4,112,128]{3,2,1,0:T(8,128)(2,1)S(1)} %get-tuple-element.34.own), channel_id=1, source_target_pairs={{64,0},{65,1},{66,2},{67,3},{68,4},{69,5},{70,6},{71,7},{72,8},{73... | collective-permute-start | bytes 688136 | tf_op jit(solution)/shard_map/ppermute | solution.py:37
  35.1 3.6 %collective-permute-done.10.before = bf16[2,4,112,128]{3,2,1,0:T(8,128)(2,1)S(1)} collective-permute-done((bf16[2,4,112,128]{3,2,1,0:T(8,128)(2,1)S(1)}, bf16[2,4,112,128]{3,2,1,0:T(8,128)(2,1)S(1)}, u32[]{:S(2)}, u32[]{:S(2)}) %collective-permute-start.10) | collective-permute-done | bytes 229408 | tf_op jit(solution)/shard_map/ppermute | solution.py:37
  38.9 1.5 %collective-permute-start.13 = (bf16[3,2,4,112,128]{4,3,2,1,0:T(8,128)(2,1)S(1)}, bf16[3,2,4,112,128]{4,3,2,1,0:T(8,128)(2,1)S(1)}, u32[]{:S(2)}, u32[]{:S(2)}) collective-permute-start(bf16[3,2,4,112,128]{4,3,2,1,0:T(8,128)(2,1)S(1)} %pad_maximum_fusion), channel_id=1, source_target_pairs={{3,0},{0,1},{1,2},{2,3},{7,4},{4,5},{5,6},{6,7},{11,8},{8,9},{9,10... | collective-permute-start | bytes 2064392 | tf_op jit(solution)/shard_map/ppermute | solution.py:37
  40.4 2.8 %collective-permute-start.14 = (bf16[1,4,112,128]{3,2,1,0:T(8,128)(2,1)S(1)}, bf16[1,4,112,128]{3,2,1,0:T(8,128)(2,1)S(1)}, u32[]{:S(2)}, u32[]{:S(2)}) collective-permute-start(bf16[1,4,112,128]{3,2,1,0:T(8,128)(2,1)S(1)} %slice.18), channel_id=1, source_target_pairs={{64,0},{65,1},{66,2},{67,3},{68,4},{69,5},{70,6},{71,7},{72,8},{73... | collective-permute-start | bytes 344072 | tf_op jit(solution)/shard_map/ppermute | solution.py:37
  43.3 1.4 %shard_map.40.start = f32[1024,768]{1,0:T(8,128)S(1)} custom-call(s32[4]{0:T(128)S(1)} %pad_add_fusion.place, bf16[2,4,112,128]{3,2,1,0:T(8,128)(2,1)S(1)} %get-tuple-element.34.own, bf16[2,4,112,128]{3,2,1,0:T(8,128)(2,1)S(1)} %collective-permute-done.9.after, bf16[2,4,112,128]{3,2,1,0:T(8,128)(2,1)S(1)} %collective-permute-done.10.before, ...), custom_call_target="tpu_custom_call" | custom-call | tf_op jit(solution)/shard_map/pallas_call | solution.py:190
  45.0 3.1 %collective-permute-done.15 = bf16[1,4,112,128]{3,2,1,0:T(8,128)(2,1)S(1)} collective-permute-done((bf16[1,4,112,128]{3,2,1,0:T(8,128)(2,1)S(1)}, bf16[1,4,112,128]{3,2,1,0:T(8,128)(2,1)S(1)}, u32[]{:S(2)}, u32[]{:S(2)}) %collective-permute-start.15) | collective-permute-done | bytes 114720 | tf_op jit(solution)/shard_map/ppermute | solution.py:37
  49.0 2.3 %collective-permute-start.12 = (bf16[2,2,4,112,128]{4,3,2,1,0:T(8,128)(2,1)S(1)}, bf16[2,2,4,112,128]{4,3,2,1,0:T(8,128)(2,1)S(1)}, u32[]{:S(2)}, u32[]{:S(2)}) collective-permute-start(bf16[2,2,4,112,128]{4,3,2,1,0:T(8,128)(2,1)S(1)} %slice.16), channel_id=1, source_target_pairs={{1,0},{2,1},{3,2},{0,3},{5,4},{6,5},{7,6},{4,7},{9,8},{10,9},{11,1... | collective-permute-start | bytes 1376264 | tf_op jit(solution)/shard_map/ppermute | solution.py:37
  51.4 4.5 %collective-permute-done.16.before = bf16[2,4,112,128]{3,2,1,0:T(8,128)(2,1)S(1)} collective-permute-done((bf16[2,4,112,128]{3,2,1,0:T(8,128)(2,1)S(1)}, bf16[2,4,112,128]{3,2,1,0:T(8,128)(2,1)S(1)}, u32[]{:S(2)}, u32[]{:S(2)}) %collective-permute-start.16) | collective-permute-done | bytes 229408 | tf_op jit(solution)/shard_map/ppermute | solution.py:37
  56.0 2.7 %collective-permute-start.18 = (bf16[2,4,112,128]{3,2,1,0:T(8,128)(2,1)S(1)}, bf16[2,4,112,128]{3,2,1,0:T(8,128)(2,1)S(1)}, u32[]{:S(2)}, u32[]{:S(2)}) collective-permute-start(bf16[2,4,112,128]{3,2,1,0:T(8,128)(2,1)S(1)} %pad_maximum_fusion.3.far), channel_id=1, source_target_pairs={{1,0},{2,1},{3,2},{0,3},{5,4},{6,5},{7,6},{4,7},{9,8},{10,9},{11,1... | collective-permute-start | bytes 688136 | tf_op jit(solution)/shard_map/ppermute | solution.py:37
  58.6 2.4 %shard_map.41.start = f32[1024,768]{1,0:T(8,128)S(1)} custom-call(s32[4]{0:T(128)S(1)} %pad_add_fusion.place, bf16[2,4,112,128]{3,2,1,0:T(8,128)(2,1)S(1)} %pad_maximum_fusion.3.far, bf16[3,2,4,112,128]{4,3,2,1,0:T(8,128)(2,1)S(1)} %collective-permute-done.11.after, ...), custom_call_target="tpu_custom_call", output_to_operand_aliasing={{}: (5, {})} | custom-call | tf_op jit(solution)/shard_map/pallas_call | solution.py:190
  61.6 1.3 %shard_map.42.start = f32[1024,768]{1,0:T(8,128)S(1)} custom-call(s32[4]{0:T(128)S(1)} %pad_add_fusion.place, bf16[2,4,112,128]{3,2,1,0:T(8,128)(2,1)S(1)} %collective-permute-done.18.after, bf16[2,4,112,128]{3,2,1,0:T(8,128)(2,1)S(1)} %collective-permute-done.16.before, bf16[4,448,768]{2,1,0:T(8,128)(2,1)S(1)} %shard_map.39.both, ...), custom_call_target="tpu_custom_call", output_to_operand_aliasing={{}: (4, {})} | custom-call | tf_op jit(solution)/shard_map/pallas_call | solution.py:190
  63.5 10.2 %collective-permute-start.20 = (bf16[512,384]{1,0:T(8,128)(2,1)S(1)}, bf16[512,384]{1,0:T(8,128)(2,1)S(1)}, u32[]{:S(2)}, u32[]{:S(2)}) collective-permute-start(bf16[512,384]{1,0:T(8,128)(2,1)S(1)} %get-tuple-element.32), channel_id=1, source_target_pairs={{16,0},{0,16},{17,1},{1,17},{18,2},{2,18},{19,3},{3,19},{20,4},{4,... | collective-permute-start | bytes 1179656 | tf_op jit(solution)/shard_map/ppermute | solution.py:23
  73.8 1.5 %shard_map.43 = (bf16[512,384]{1,0:T(8,128)(2,1)S(1)}, bf16[512,384]{1,0:T(8,128)(2,1)S(1)}) custom-call(s32[4]{0:T(128)S(1)} %pad_add_fusion.place, bf16[2,2,4,112,128]{4,3,2,1,0:T(8,128)(2,1)S(1)} %collective-permute-done.12.low, bf16[2,2,4,112,128]{4,3,2,1,0:T(8,128)(2,1)S(1)} %collective-permute-done.17.high, bf16[4,448,768]{2,1,0:T(8,128)(2,1)S(1)} %shard_map.39.both, ...), custom_call_target="tpu_custom_call" | custom-call | tf_op jit(solution)/shard_map/pallas_call | solution.py:190
  75.4 1.6 %shard_map.45.given = bf16[2048,384]{1,0:T(8,128)(2,1)} custom-call(s32[4]{0:T(128)S(1)} %pad_add_fusion.place, bf16[512,384]{1,0:T(8,128)(2,1)S(1)} %get-tuple-element.30.mine1, bf16[512,384]{1,0:T(8,128)(2,1)S(1)} %get-tuple-element.31.mine2, bf16[512,384]{1,0:T(8,128)(2,1)S(1)} %collective-permute-done.20.theirs1), custom_call_target="tpu_custom_call" | custom-call | tf_op jit(solution)/shard_map/pallas_call | solution.py:190
  77.1 1.3 %shard_map.46 = bf16[2048,384]{1,0:T(8,128)(2,1)} custom-call(s32[4]{0:T(128)S(1)} %pad_add_fusion.place, bf16[512,384]{1,0:T(8,128)(2,1)S(1)} %collective-permute-done.19.theirs2, bf16[2048,384]{1,0:T(8,128)(2,1)} %shard_map.45.given), custom_call_target="tpu_custom_call", output_to_operand_aliasing={{}: (2, {})} | custom-call | tf_op jit(solution)/shard_map/pallas_call | solution.py:190
  (37 shorter events, 5.8 us)
Async XLA Ops:
  0.0 22.3 %collective-permute-start.5 = (bf16[1792,384]{1,0:T(8,128)(2,1)}, bf16[1792,384]{1,0:T(8,128)(2,1)S(1)}, u32[]{:S(2)}, u32[]{:S(2)}) collective-permute-start(bf16[1792,384]{1,0:T(8,128)(2,1)} %own.1), channel_id=1, source_target_pairs={{16,0},{0,16},{17,1},{1,17},{18,2},{2,18},{19,3},{3,19},{20,4},{4,... | collective-permute-start | bytes 4128776 | tf_op jit(solution)/shard_map/ppermute | solution.py:23
  3.3 1.0 %copy-start.1 = (bf16[112,2048]{1,0:T(8,128)(2,1)S(1)}, bf16[112,2048]{1,0:T(8,128)(2,1)}, u32[]{:S(2)}) copy-start(bf16[112,2048]{1,0:T(8,128)(2,1)} %panel.1) | copy-start | bytes 1376260
  4.3 0.7 copy-start.2
  6.1 1.9 %collective-permute-start = (f32[8,112,128]{2,1,0:T(8,128)S(1)}, f32[8,112,128]{2,1,0:T(8,128)S(1)}, u32[]{:S(2)}, u32[]{:S(2)}) collective-permute-start(f32[8,112,128]{2,1,0:T(8,128)S(1)} %get-tuple-element.20), channel_id=1, source_target_pairs={{16,0},{0,16},{17,1},{1,17},{18,2},{2,18},{19,3},{3,19},{20,4},{4,... | collective-permute-start | bytes 1376264 | tf_op jit(solution)/shard_map/ppermute | solution.py:23
  8.6 3.1 %collective-permute-start.1 = (bf16[2,112,128]{2,1,0:T(8,128)(2,1)S(1)}, bf16[2,112,128]{2,1,0:T(8,128)(2,1)S(1)}, u32[]{:S(2)}, u32[]{:S(2)}) collective-permute-start(bf16[2,112,128]{2,1,0:T(8,128)(2,1)S(1)} %get-tuple-element.22), channel_id=1, source_target_pairs={{64,0},{128,64},{192,128},{0,192},{65,1},{129,65},{193,129},{1,193... | collective-permute-start | bytes 172040 | tf_op jit(solution)/shard_map/ppermute | solution.py:23
  9.4 4.2 %collective-permute-start.2 = (bf16[2,112,128]{2,1,0:T(8,128)(2,1)S(1)}, bf16[2,112,128]{2,1,0:T(8,128)(2,1)S(1)}, u32[]{:S(2)}, u32[]{:S(2)}) collective-permute-start(bf16[2,112,128]{2,1,0:T(8,128)(2,1)S(1)} %get-tuple-element.23), channel_id=1, source_target_pairs={{192,0},{0,64},{64,128},{128,192},{193,1},{1,65},{65,129},{129,193... | collective-permute-start | bytes 172040 | tf_op jit(solution)/shard_map/ppermute | solution.py:23
  10.1 4.6 %collective-permute-start.3 = (bf16[2,112,128]{2,1,0:T(8,128)(2,1)S(1)}, bf16[2,112,128]{2,1,0:T(8,128)(2,1)S(1)}, u32[]{:S(2)}, u32[]{:S(2)}) collective-permute-start(bf16[2,112,128]{2,1,0:T(8,128)(2,1)S(1)} %get-tuple-element.24), channel_id=1, source_target_pairs={{128,0},{192,64},{0,128},{64,192},{129,1},{193,65},{1,129},{65,193... | collective-permute-start | bytes 172040 | tf_op jit(solution)/shard_map/ppermute | solution.py:23
  14.8 9.6 %collective-permute-start.4 = (bf16[2,112,128]{2,1,0:T(8,128)(2,1)S(1)}, bf16[2,112,128]{2,1,0:T(8,128)(2,1)S(1)}, u32[]{:S(2)}, u32[]{:S(2)}) collective-permute-start(bf16[2,112,128]{2,1,0:T(8,128)(2,1)S(1)} %fusion), channel_id=1, source_target_pairs={{32,0},{0,32},{33,1},{1,33},{34,2},{2,34},{35,3},{3,35},{36,4},{4,... | collective-permute-start | bytes 172040 | tf_op jit(solution)/shard_map/ppermute | solution.py:27
  22.3 1.3 %copy-start = (bf16[1792,384]{1,0:T(8,128)(2,1)S(1)}, bf16[1792,384]{1,0:T(8,128)(2,1)}, u32[]{:S(2)}) copy-start(bf16[1792,384]{1,0:T(8,128)(2,1)} %own.1) | copy-start | bytes 4128772
  24.5 4.9 %collective-permute-start.8 = (bf16[2,112,128]{2,1,0:T(8,128)(2,1)S(1)}, bf16[2,112,128]{2,1,0:T(8,128)(2,1)S(1)}, u32[]{:S(2)}, u32[]{:S(2)}) collective-permute-start(bf16[2,112,128]{2,1,0:T(8,128)(2,1)S(1)} %add_convert_fusion), channel_id=1, source_target_pairs={{12,0},{8,4},{4,8},{0,12},{13,1},{9,5},{5,9},{1,13},{14,2},{10,6},... | collective-permute-start | bytes 172040 | tf_op jit(solution)/shard_map/ppermute | solution.py:27
  26.8 3.2 %collective-permute-start.6 = (bf16[2,112,128]{2,1,0:T(8,128)(2,1)S(1)}, bf16[2,112,128]{2,1,0:T(8,128)(2,1)S(1)}, u32[]{:S(2)}, u32[]{:S(2)}) collective-permute-start(bf16[2,112,128]{2,1,0:T(8,128)(2,1)S(1)} %add_convert_fusion), channel_id=1, source_target_pairs={{4,0},{0,4},{12,8},{8,12},{5,1},{1,5},{13,9},{9,13},{6,2},{2,6},{1... | collective-permute-start | bytes 172040 | tf_op jit(solution)/shard_map/ppermute | solution.py:27
  26.8 5.4 %collective-permute-start.7 = (bf16[2,112,128]{2,1,0:T(8,128)(2,1)S(1)}, bf16[2,112,128]{2,1,0:T(8,128)(2,1)S(1)}, u32[]{:S(2)}, u32[]{:S(2)}) collective-permute-start(bf16[2,112,128]{2,1,0:T(8,128)(2,1)S(1)} %add_convert_fusion), channel_id=1, source_target_pairs={{8,0},{12,4},{0,8},{4,12},{9,1},{13,5},{1,9},{5,13},{10,2},{14,6},... | collective-permute-start | bytes 172040 | tf_op jit(solution)/shard_map/ppermute | solution.py:27
  32.2 6.5 %collective-permute-start.10 = (bf16[2,4,112,128]{3,2,1,0:T(8,128)(2,1)S(1)}, bf16[2,4,112,128]{3,2,1,0:T(8,128)(2,1)S(1)}, u32[]{:S(2)}, u32[]{:S(2)}) collective-permute-start(bf16[2,4,112,128]{3,2,1,0:T(8,128)(2,1)S(1)} %get-tuple-element.34.own), channel_id=1, source_target_pairs={{192,0},{193,1},{194,2},{195,3},{196,4},{197,5},{198,6},{199,7},{2... | collective-permute-start | bytes 688136 | tf_op jit(solution)/shard_map/ppermute | solution.py:37
  33.6 5.2 %collective-permute-start.9 = (bf16[2,4,112,128]{3,2,1,0:T(8,128)(2,1)S(1)}, bf16[2,4,112,128]{3,2,1,0:T(8,128)(2,1)S(1)}, u32[]{:S(2)}, u32[]{:S(2)}) collective-permute-start(bf16[2,4,112,128]{3,2,1,0:T(8,128)(2,1)S(1)} %get-tuple-element.34.own), channel_id=1, source_target_pairs={{64,0},{65,1},{66,2},{67,3},{68,4},{69,5},{70,6},{71,7},{72,8},{73... | collective-permute-start | bytes 688136 | tf_op jit(solution)/shard_map/ppermute | solution.py:37
  38.8 10.2 %collective-permute-start.11 = (bf16[3,2,4,112,128]{4,3,2,1,0:T(8,128)(2,1)S(1)}, bf16[3,2,4,112,128]{4,3,2,1,0:T(8,128)(2,1)S(1)}, u32[]{:S(2)}, u32[]{:S(2)}) collective-permute-start(bf16[3,2,4,112,128]{4,3,2,1,0:T(8,128)(2,1)S(1)} %pad_maximum_fusion), channel_id=1, source_target_pairs={{1,0},{2,1},{3,2},{0,3},{5,4},{6,5},{7,6},{4,7},{9,8},{10,9},{11,1... | collective-permute-start | bytes 2064392 | tf_op jit(solution)/shard_map/ppermute | solution.py:37
  38.9 12.4 %collective-permute-start.13 = (bf16[3,2,4,112,128]{4,3,2,1,0:T(8,128)(2,1)S(1)}, bf16[3,2,4,112,128]{4,3,2,1,0:T(8,128)(2,1)S(1)}, u32[]{:S(2)}, u32[]{:S(2)}) collective-permute-start(bf16[3,2,4,112,128]{4,3,2,1,0:T(8,128)(2,1)S(1)} %pad_maximum_fusion), channel_id=1, source_target_pairs={{3,0},{0,1},{1,2},{2,3},{7,4},{4,5},{5,6},{6,7},{11,8},{8,9},{9,10... | collective-permute-start | bytes 2064392 | tf_op jit(solution)/shard_map/ppermute | solution.py:37
  40.4 4.6 %collective-permute-start.14 = (bf16[1,4,112,128]{3,2,1,0:T(8,128)(2,1)S(1)}, bf16[1,4,112,128]{3,2,1,0:T(8,128)(2,1)S(1)}, u32[]{:S(2)}, u32[]{:S(2)}) collective-permute-start(bf16[1,4,112,128]{3,2,1,0:T(8,128)(2,1)S(1)} %slice.18), channel_id=1, source_target_pairs={{64,0},{65,1},{66,2},{67,3},{68,4},{69,5},{70,6},{71,7},{72,8},{73... | collective-permute-start | bytes 344072 | tf_op jit(solution)/shard_map/ppermute | solution.py:37
  43.2 4.9 %collective-permute-start.15 = (bf16[1,4,112,128]{3,2,1,0:T(8,128)(2,1)S(1)}, bf16[1,4,112,128]{3,2,1,0:T(8,128)(2,1)S(1)}, u32[]{:S(2)}, u32[]{:S(2)}) collective-permute-start(bf16[1,4,112,128]{3,2,1,0:T(8,128)(2,1)S(1)} %slice.19), channel_id=1, source_target_pairs={{192,0},{193,1},{194,2},{195,3},{196,4},{197,5},{198,6},{199,7},{2... | collective-permute-start | bytes 344072 | tf_op jit(solution)/shard_map/ppermute | solution.py:37
  48.2 7.6 %collective-permute-start.16 = (bf16[2,4,112,128]{3,2,1,0:T(8,128)(2,1)S(1)}, bf16[2,4,112,128]{3,2,1,0:T(8,128)(2,1)S(1)}, u32[]{:S(2)}, u32[]{:S(2)}) collective-permute-start(bf16[2,4,112,128]{3,2,1,0:T(8,128)(2,1)S(1)} %pad_maximum_fusion.3.far), channel_id=1, source_target_pairs={{3,0},{0,1},{1,2},{2,3},{7,4},{4,5},{5,6},{6,7},{11,8},{8,9},{9,10... | collective-permute-start | bytes 688136 | tf_op jit(solution)/shard_map/ppermute | solution.py:37
  49.0 13.8 %collective-permute-start.12 = (bf16[2,2,4,112,128]{4,3,2,1,0:T(8,128)(2,1)S(1)}, bf16[2,2,4,112,128]{4,3,2,1,0:T(8,128)(2,1)S(1)}, u32[]{:S(2)}, u32[]{:S(2)}) collective-permute-start(bf16[2,2,4,112,128]{4,3,2,1,0:T(8,128)(2,1)S(1)} %slice.16), channel_id=1, source_target_pairs={{1,0},{2,1},{3,2},{0,3},{5,4},{6,5},{7,6},{4,7},{9,8},{10,9},{11,1... | collective-permute-start | bytes 1376264 | tf_op jit(solution)/shard_map/ppermute | solution.py:37
  55.9 17.9 %collective-permute-start.17 = (bf16[2,2,4,112,128]{4,3,2,1,0:T(8,128)(2,1)S(1)}, bf16[2,2,4,112,128]{4,3,2,1,0:T(8,128)(2,1)S(1)}, u32[]{:S(2)}, u32[]{:S(2)}) collective-permute-start(bf16[2,2,4,112,128]{4,3,2,1,0:T(8,128)(2,1)S(1)} %pad_maximum_fusion.1), channel_id=1, source_target_pairs={{3,0},{0,1},{1,2},{2,3},{7,4},{4,5},{5,6},{6,7},{11,8},{8,9},{9,10... | collective-permute-start | bytes 1376264 | tf_op jit(solution)/shard_map/ppermute | solution.py:37
  56.0 5.6 %collective-permute-start.18 = (bf16[2,4,112,128]{3,2,1,0:T(8,128)(2,1)S(1)}, bf16[2,4,112,128]{3,2,1,0:T(8,128)(2,1)S(1)}, u32[]{:S(2)}, u32[]{:S(2)}) collective-permute-start(bf16[2,4,112,128]{3,2,1,0:T(8,128)(2,1)S(1)} %pad_maximum_fusion.3.far), channel_id=1, source_target_pairs={{1,0},{2,1},{3,2},{0,3},{5,4},{6,5},{7,6},{4,7},{9,8},{10,9},{11,1... | collective-permute-start | bytes 688136 | tf_op jit(solution)/shard_map/ppermute | solution.py:37
  63.5 11.8 %collective-permute-start.20 = (bf16[512,384]{1,0:T(8,128)(2,1)S(1)}, bf16[512,384]{1,0:T(8,128)(2,1)S(1)}, u32[]{:S(2)}, u32[]{:S(2)}) collective-permute-start(bf16[512,384]{1,0:T(8,128)(2,1)S(1)} %get-tuple-element.32), channel_id=1, source_target_pairs={{16,0},{0,16},{17,1},{1,17},{18,2},{2,18},{19,3},{3,19},{20,4},{4,... | collective-permute-start | bytes 1179656 | tf_op jit(solution)/shard_map/ppermute | solution.py:23
  75.3 1.8 %collective-permute-start.19 = (bf16[512,384]{1,0:T(8,128)(2,1)S(1)}, bf16[512,384]{1,0:T(8,128)(2,1)S(1)}, u32[]{:S(2)}, u32[]{:S(2)}) collective-permute-start(bf16[512,384]{1,0:T(8,128)(2,1)S(1)} %get-tuple-element.29), channel_id=1, source_target_pairs={{16,0},{0,16},{17,1},{1,17},{18,2},{2,18},{19,3},{3,19},{20,4},{4,... | collective-permute-start | bytes 1179656 | tf_op jit(solution)/shard_map/ppermute | solution.py:23

commit v6 on v5

--- a/solution.py
+++ b/solution.py
@@ -23,8 +23,12 @@
     return lax.ppermute(block, axis, [((i + ahead) % size, i) for i in range(size)])
 
 
-def swap(block, axis, size, bits):
-    return lax.ppermute(block, axis, [(i ^ bits, i) for i in range(size)])
+def on_one(block, axis, size, source):
+    if axis == "z_lo":
+        pairs = [(size + source(i), size + i) for i in range(size)]
+        return lax.ppermute(block, ("core", axis), pairs)
+    pairs = [(source(i) * 2 + 1, i * 2 + 1) for i in range(size)]
+    return lax.ppermute(block, (axis, "core"), pairs)
 
 
 def turn(block, order, ahead):
@@ -41,23 +45,23 @@
     return lax.dot_general(left, right, (((0,), (0,)), ((), ())), preferred_element_type=F32)
 
 
-def partial_sums(place, screening, panel, keep, send):
-    core = place[2]
-    for out, base in ((send, 1 - core), (keep, core)):
-        for slab in range(8):
-            columns = pl.ds(pl.multiple_of(base * 1024 + slab * 128, 128), 128)
-            out[slab] = dot_t(screening[...], panel[:, columns])
+def partial_sums(screening, panel, keep, send):
+    for slab in range(16):
+        total = dot_t(screening[...], panel[:, pl.ds(slab * 128, 128)])
+        keep[slab] = total
+        send[slab] = total.astype(BF16)
 
 
 def add_cores(place, keep, received, mine, *away):
     for back in range(4):
         for half in range(2):
-            slab = lax.rem(place[0] + 4 - back, 4) * 2 + half
-            total = keep[slab] + received[slab]
-            if back:
-                away[back - 1][half] = total.astype(BF16)
-            else:
-                mine[half] = total
+            for z_hi in range(2):
+                slab = half * 8 + lax.rem(place[0] + 4 - back, 4) * 2 + z_hi
+                total = keep[slab] + received[slab].astype(F32)
+                if back:
+                    away[back - 1][half * 2 + z_hi] = total.astype(BF16)
+                else:
+                    mine[half * 2 + z_hi] = total
 
 
 def order_pairs(place, own, other, both):
@@ -202,27 +206,35 @@
     x, y, core, z_lo = (lax.axis_index(axis) for axis in ("x", "y", "core", "z_lo"))
     place = jnp.stack([x, y, core, z_lo]).astype(jnp.int32)
 
-    slabs = jax.ShapeDtypeStruct((8, 112, 128), F32)
-    keep, send = call(partial_sums, (slabs, slabs), (place, screening, pair_valence), (VMEM, VMEM))
-    two = jax.ShapeDtypeStruct((2, 112, 128), F32)
-    sent = jax.ShapeDtypeStruct((2, 112, 128), BF16)
+    keep, send = call(
+        partial_sums,
+        (jax.ShapeDtypeStruct((16, 112, 128), F32), jax.ShapeDtypeStruct((16, 112, 128), BF16)),
+        (screening, pair_valence),
+        (VMEM, VMEM),
+        [VMEM, VMEM],
+    )
+    sent = jax.ShapeDtypeStruct((4, 112, 128), BF16)
     part, *away = call(
         add_cores,
-        (two, sent, sent, sent),
-        (place, keep, fetch(send, "core", 2, 1)),
+        (jax.ShapeDtypeStruct((4, 112, 128), F32), sent, sent, sent),
+        (place, keep, lax.ppermute(send, "core", [(0, 1)])),
         (VMEM,) * 4,
     )
     for ahead in (1, 3, 2):
-        part = part + fetch(away[ahead - 1], "x", 4, ahead).astype(F32)
+        block = on_one(away[ahead - 1], "x", 4, lambda i: (i + ahead) % 4)
+        part = part + block.astype(F32)
 
     other = fetch(pair_conduction, "core", 2, 1)
     both = call(
         order_pairs, jax.ShapeDtypeStruct((4, 448, 768), BF16), (place, pair_conduction, other)
     )
 
-    share, both = lax.optimization_barrier((swap(part.astype(BF16), "z_hi", 2, 1), both))
+    share = on_one(part.astype(BF16), "z_hi", 2, lambda i: i ^ 1)
+    share, both = lax.optimization_barrier((share, both))
     part = (part + share.astype(F32)).astype(BF16)
-    own = jnp.stack([part] + [swap(part, "z_lo", 4, bits) for bits in (1, 2, 3)], 1)
+    line = [part] + [on_one(part, "z_lo", 4, lambda i: i ^ bits) for bits in (1, 2, 3)]
+    line = jnp.stack(line, 1)
+    own = jnp.where(core == 0, lax.ppermute(line[:2], "core", [(1, 0)]), line[2:])
 
     after, before = turn(own, 0, 1), turn(own, 0, 3)
     far = jnp.concatenate([turn(after[:1], 0, 1), turn(before[1:], 0, 3)])
@@ -232,6 +244,7 @@
     after1, before1 = turn(sent, 1, 1), turn(sent, 1, 3)
     far, total_one = lax.optimization_barrier((far, total_one))
     after2, before2 = turn(far, 1, 1), turn(far, 1, 3)
+    after2, before2 = lax.optimization_barrier((after2, before2))
     low, high = turn(after1[:2], 1, 1), turn(jnp.stack([before1[2], before2]), 1, 3)
     total_two = call(
         product_two,

time: 79.2 us -> 97.5 us (1.23)
  starting transfers between devices: 40 us -> 51.9 us
  waiting for transfers between devices: 22.3 us -> 27.9 us
  local copies, waits for them, and re-layouts: 3.17 us -> 4.26 us
    ppermute x4 -> x9, starting transfers between devices: 11.1 us -> 28.9 us  [the longest x4 16.3 us: on_one(): return lax.ppermute(block, (axis, 'core'), pairs)]
    ppermute x4 -> x9, waiting for transfers between devices: 4.06 us -> 11.2 us  [the longest x3 4.2 us: on_one(): return lax.ppermute(block, ('core', axis), pairs)]
    ppermute x7 -> x3, starting transfers between devices: 16.2 us -> 10.3 us  [fetch(): lax.ppermute(block, axis, [((i + ahead) % size, i) for i in range(size)])]
    ppermute x7 -> x3, waiting for transfers between devices: 5.53 us -> 0.1 us  [fetch(): lax.ppermute(block, axis, [((i + ahead) % size, i) for i in range(size)])]
    ppermute x10, waiting for transfers between devices: 12.7 us -> 16.6 us  [turn(): return lax.ppermute(block, ROW + COL, pairs)]
    unnamed x6 -> x10, local copies, waits for them, and re-layouts: 3.11 us -> 4.18 us
  transfers between devices with their start and end apart: 21 -> 22, of which waited for: 14 -> 13; matrix products, arithmetic and copies ran while one was open for 0% -> 0% of each run, Pallas kernels for 14% -> 11%
where the time goes in v6:
time: 97.5 us; the launch traced here: 97 us
  starting transfers between devices  51.9 us (53%)
  waiting for transfers between devices  27.9 us (29%)
  Pallas kernels  12.1 us (12%)
  local copies, waits for them, and re-layouts  4.26 us (4%)
    ppermute x10, waiting for transfers between devices, turn(): return lax.ppermute(block, ROW + COL, pairs)  16.6 us
    ppermute x4, starting transfers between devices, on_one(): return lax.ppermute(block, (axis, 'core'), pairs)  16.3 us
    ppermute x10, starting transfers between devices, turn(): return lax.ppermute(block, ROW + COL, pairs)  12.7 us
    pallas_call x10, Pallas kernels, call(): pl.pallas_call(kernel, out_shape=out_shape, in_specs=specs or [SMEM] + [V...  12.1 us
    ppermute x3, starting transfers between devices, fetch(): lax.ppermute(block, axis, [((i + ahead) % size, i) for i in range(size)])  10.3 us
    ppermute x3, starting transfers between devices, on_one(): return lax.ppermute(block, ('core', axis), pairs)  9.27 us
    ppermute x3, waiting for transfers between devices, on_one(): return lax.ppermute(block, ('core', axis), pairs)  4.2 us
    unnamed x10, local copies, waits for them, and re-layouts  4.18 us
  transfers between devices with their start and end apart: 22, of which 13 were waited for; matrix products, arithmetic and copies ran while one was open for 0% of the time, Pallas kernels for 11%

profile of v6, /device:TPU:1, one launch (start us, length us, event | category | flops | bytes accessed | tf_op | source)
XLA Modules:
  0.0 97.0 jit_solution(8322348996277087126)
XLA Ops:
  0.0 3.2 %collective-permute-start.5 = (bf16[1792,384]{1,0:T(8,128)(2,1)}, bf16[1792,384]{1,0:T(8,128)(2,1)S(1)}, u32[]{:S(2)}, u32[]{:S(2)}) collective-permute-start(bf16[1792,384]{1,0:T(8,128)(2,1)} %own.1), channel_id=1, source_target_pairs={{16,0},{0,16},{17,1},{1,17},{18,2},{2,18},{19,3},{3,19},{20,4},{4,... | collective-permute-start | bytes 4128776 | tf_op jit(solution)/shard_map/ppermute | solution.py:23
  5.4 1.3 %collective-permute-start = (bf16[16,112,128]{2,1,0:T(8,128)(2,1)S(1)}, bf16[16,112,128]{2,1,0:T(8,128)(2,1)S(1)}, u32[]{:S(2)}, u32[]{:S(2)}) collective-permute-start(bf16[16,112,128]{2,1,0:T(8,128)(2,1)S(1)} %get-tuple-element.22), channel_id=1, source_target_pairs={{0,16},{1,17},{2,18},{3,19},{4,20},{5,21},{6,22},{7,23},{8,24},{9,... | collective-permute-start | bytes 1376264 | tf_op jit(solution)/shard_map/ppermute | solution.py:220
  6.8 2.3 %collective-permute-done.received = bf16[16,112,128]{2,1,0:T(8,128)(2,1)S(1)} collective-permute-done((bf16[16,112,128]{2,1,0:T(8,128)(2,1)S(1)}, bf16[16,112,128]{2,1,0:T(8,128)(2,1)S(1)}, u32[]{:S(2)}, u32[]{:S(2)}) %collective-permute-start) | collective-permute-done | bytes 458784 | tf_op jit(solution)/shard_map/ppermute | solution.py:220
  9.8 2.7 %collective-permute-start.1 = (bf16[4,112,128]{2,1,0:T(8,128)(2,1)S(1)}, bf16[4,112,128]{2,1,0:T(8,128)(2,1)S(1)}, u32[]{:S(2)}, u32[]{:S(2)}) collective-permute-start(bf16[4,112,128]{2,1,0:T(8,128)(2,1)S(1)} %get-tuple-element.24), channel_id=1, source_target_pairs={{80,16},{144,80},{208,144},{16,208},{81,17},{145,81},{209,145},{17... | collective-permute-start | bytes 344072 | tf_op jit(solution)/shard_map/ppermute | solution.py:31
  12.5 2.6 %collective-permute-start.2 = (bf16[4,112,128]{2,1,0:T(8,128)(2,1)S(1)}, bf16[4,112,128]{2,1,0:T(8,128)(2,1)S(1)}, u32[]{:S(2)}, u32[]{:S(2)}) collective-permute-start(bf16[4,112,128]{2,1,0:T(8,128)(2,1)S(1)} %get-tuple-element.25), channel_id=1, source_target_pairs={{208,16},{16,80},{80,144},{144,208},{209,17},{17,81},{81,145},{145... | collective-permute-start | bytes 344072 | tf_op jit(solution)/shard_map/ppermute | solution.py:31
  15.1 2.9 %collective-permute-start.3 = (bf16[4,112,128]{2,1,0:T(8,128)(2,1)S(1)}, bf16[4,112,128]{2,1,0:T(8,128)(2,1)S(1)}, u32[]{:S(2)}, u32[]{:S(2)}) collective-permute-start(bf16[4,112,128]{2,1,0:T(8,128)(2,1)S(1)} %get-tuple-element.26), channel_id=1, source_target_pairs={{144,16},{208,80},{16,144},{80,208},{145,17},{209,81},{17,145},{81... | collective-permute-start | bytes 344072 | tf_op jit(solution)/shard_map/ppermute | solution.py:31
  19.2 2.9 %collective-permute-done.3 = bf16[4,112,128]{2,1,0:T(8,128)(2,1)S(1)} collective-permute-done((bf16[4,112,128]{2,1,0:T(8,128)(2,1)S(1)}, bf16[4,112,128]{2,1,0:T(8,128)(2,1)S(1)}, u32[]{:S(2)}, u32[]{:S(2)}) %collective-permute-start.3) | collective-permute-done | bytes 114720 | tf_op jit(solution)/shard_map/ppermute | solution.py:31
  22.2 8.1 %collective-permute-start.4 = (bf16[4,112,128]{2,1,0:T(8,128)(2,1)S(1)}, bf16[4,112,128]{2,1,0:T(8,128)(2,1)S(1)}, u32[]{:S(2)}, u32[]{:S(2)}) collective-permute-start(bf16[4,112,128]{2,1,0:T(8,128)(2,1)S(1)} %fusion), channel_id=1, source_target_pairs={{48,16},{16,48},{49,17},{17,49},{50,18},{18,50},{51,19},{19,51},{5... | collective-permute-start | bytes 344072 | tf_op jit(solution)/shard_map/ppermute | solution.py:31
  31.4 1.3 %copy-done.2 = bf16[1792,384]{1,0:T(8,128)(2,1)S(1)} copy-done((bf16[1792,384]{1,0:T(8,128)(2,1)S(1)}, bf16[1792,384]{1,0:T(8,128)(2,1)}, u32[]{:S(2)}) %copy-start.2) | copy-done | bytes 1376280
  33.6 3.6 %collective-permute-start.8 = (bf16[4,112,128]{2,1,0:T(8,128)(2,1)S(1)}, bf16[4,112,128]{2,1,0:T(8,128)(2,1)S(1)}, u32[]{:S(2)}, u32[]{:S(2)}) collective-permute-start(bf16[4,112,128]{2,1,0:T(8,128)(2,1)S(1)} %add_convert_fusion), channel_id=1, source_target_pairs={{28,16},{24,20},{20,24},{16,28},{29,17},{25,21},{21,25},{17,29},{3... | collective-permute-start | bytes 344072 | tf_op jit(solution)/shard_map/ppermute | solution.py:29
  37.3 2.2 %collective-permute-start.6 = (bf16[4,112,128]{2,1,0:T(8,128)(2,1)S(1)}, bf16[4,112,128]{2,1,0:T(8,128)(2,1)S(1)}, u32[]{:S(2)}, u32[]{:S(2)}) collective-permute-start(bf16[4,112,128]{2,1,0:T(8,128)(2,1)S(1)} %add_convert_fusion), channel_id=1, source_target_pairs={{20,16},{16,20},{28,24},{24,28},{21,17},{17,21},{29,25},{25,29},{2... | collective-permute-start | bytes 344072 | tf_op jit(solution)/shard_map/ppermute | solution.py:29
  39.5 3.4 %collective-permute-start.7 = (bf16[4,112,128]{2,1,0:T(8,128)(2,1)S(1)}, bf16[4,112,128]{2,1,0:T(8,128)(2,1)S(1)}, u32[]{:S(2)}, u32[]{:S(2)}) collective-permute-start(bf16[4,112,128]{2,1,0:T(8,128)(2,1)S(1)} %add_convert_fusion), channel_id=1, source_target_pairs={{24,16},{28,20},{16,24},{20,28},{25,17},{29,21},{17,25},{21,29},{2... | collective-permute-start | bytes 344072 | tf_op jit(solution)/shard_map/ppermute | solution.py:29
  43.0 4.2 %collective-permute-done.7 = bf16[4,112,128]{2,1,0:T(8,128)(2,1)S(1)} collective-permute-done((bf16[4,112,128]{2,1,0:T(8,128)(2,1)S(1)}, bf16[4,112,128]{2,1,0:T(8,128)(2,1)S(1)}, u32[]{:S(2)}, u32[]{:S(2)}) %collective-permute-start.7) | collective-permute-done | bytes 114720 | tf_op jit(solution)/shard_map/ppermute | solution.py:29
  47.2 2.0 %collective-permute-start.9 = (bf16[2,4,112,128]{3,2,1,0:T(8,128)(2,1)S(1)}, bf16[2,4,112,128]{3,2,1,0:T(8,128)(2,1)}, u32[]{:S(2)}, u32[]{:S(2)}) collective-permute-start(bf16[2,4,112,128]{3,2,1,0:T(8,128)(2,1)S(1)} %slice.24), channel_id=1, source_target_pairs={{16,0},{17,1},{18,2},{19,3},{20,4},{21,5},{22,6},{23,7},{24,8},{25... | collective-permute-start | bytes 688136 | tf_op jit(solution)/shard_map/ppermute | solution.py:237
  49.8 2.8 %collective-permute-start.10 = (bf16[2,4,112,128]{3,2,1,0:T(8,128)(2,1)S(1)}, bf16[2,4,112,128]{3,2,1,0:T(8,128)(2,1)S(1)}, u32[]{:S(2)}, u32[]{:S(2)}) collective-permute-start(bf16[2,4,112,128]{3,2,1,0:T(8,128)(2,1)S(1)} %slice_select_fusion.own), channel_id=1, source_target_pairs={{64,0},{65,1},{66,2},{67,3},{68,4},{69,5},{70,6},{71,7},{72,8},{73... | collective-permute-start | bytes 688136 | tf_op jit(solution)/shard_map/ppermute | solution.py:41
  52.6 3.0 %collective-permute-done.10.after = bf16[2,4,112,128]{3,2,1,0:T(8,128)(2,1)S(1)} collective-permute-done((bf16[2,4,112,128]{3,2,1,0:T(8,128)(2,1)S(1)}, bf16[2,4,112,128]{3,2,1,0:T(8,128)(2,1)S(1)}, u32[]{:S(2)}, u32[]{:S(2)}) %collective-permute-start.10) | collective-permute-done | bytes 229408 | tf_op jit(solution)/shard_map/ppermute | solution.py:41
  55.6 3.4 %collective-permute-done.11.before = bf16[2,4,112,128]{3,2,1,0:T(8,128)(2,1)S(1)} collective-permute-done((bf16[2,4,112,128]{3,2,1,0:T(8,128)(2,1)S(1)}, bf16[2,4,112,128]{3,2,1,0:T(8,128)(2,1)S(1)}, u32[]{:S(2)}, u32[]{:S(2)}) %collective-permute-start.11) | collective-permute-done | bytes 229408 | tf_op jit(solution)/shard_map/ppermute | solution.py:41
  59.1 2.4 %collective-permute-start.12 = (bf16[3,2,4,112,128]{4,3,2,1,0:T(8,128)(2,1)S(1)}, bf16[3,2,4,112,128]{4,3,2,1,0:T(8,128)(2,1)S(1)}, u32[]{:S(2)}, u32[]{:S(2)}) collective-permute-start(bf16[3,2,4,112,128]{4,3,2,1,0:T(8,128)(2,1)S(1)} %pad_maximum_fusion), channel_id=1, source_target_pairs={{1,0},{2,1},{3,2},{0,3},{5,4},{6,5},{7,6},{4,7},{9,8},{10,9},{11,1... | collective-permute-start | bytes 2064392 | tf_op jit(solution)/shard_map/ppermute | solution.py:41
  61.9 1.3 %collective-permute-start.16 = (bf16[1,4,112,128]{3,2,1,0:T(8,128)(2,1)S(1)}, bf16[1,4,112,128]{3,2,1,0:T(8,128)(2,1)S(1)}, u32[]{:S(2)}, u32[]{:S(2)}) collective-permute-start(bf16[1,4,112,128]{3,2,1,0:T(8,128)(2,1)S(1)} %slice.29), channel_id=1, source_target_pairs={{192,0},{193,1},{194,2},{195,3},{196,4},{197,5},{198,6},{199,7},{2... | collective-permute-start | bytes 344072 | tf_op jit(solution)/shard_map/ppermute | solution.py:41
  63.2 1.4 %shard_map.40.start = f32[1024,768]{1,0:T(8,128)S(1)} custom-call(s32[4]{0:T(128)S(1)} %pad_add_fusion.place, bf16[2,4,112,128]{3,2,1,0:T(8,128)(2,1)S(1)} %slice_select_fusion.own, bf16[2,4,112,128]{3,2,1,0:T(8,128)(2,1)S(1)} %collective-permute-done.10.after, bf16[2,4,112,128]{3,2,1,0:T(8,128)(2,1)S(1)} %collective-permute-done.11.before, ...), custom_call_target="tpu_custom_call" | custom-call | tf_op jit(solution)/shard_map/pallas_call | solution.py:194
  64.6 1.9 %collective-permute-done.15 = bf16[1,4,112,128]{3,2,1,0:T(8,128)(2,1)S(1)} collective-permute-done((bf16[1,4,112,128]{3,2,1,0:T(8,128)(2,1)S(1)}, bf16[1,4,112,128]{3,2,1,0:T(8,128)(2,1)S(1)}, u32[]{:S(2)}, u32[]{:S(2)}) %collective-permute-start.15) | collective-permute-done | bytes 114720 | tf_op jit(solution)/shard_map/ppermute | solution.py:41
  66.9 4.2 %collective-permute-start.17 = (bf16[2,4,112,128]{3,2,1,0:T(8,128)(2,1)S(1)}, bf16[2,4,112,128]{3,2,1,0:T(8,128)(2,1)S(1)}, u32[]{:S(2)}, u32[]{:S(2)}) collective-permute-start(bf16[2,4,112,128]{3,2,1,0:T(8,128)(2,1)S(1)} %pad_maximum_fusion.3.far), channel_id=1, source_target_pairs={{1,0},{2,1},{3,2},{0,3},{5,4},{6,5},{7,6},{4,7},{9,8},{10,9},{11,1... | collective-permute-start | bytes 688136 | tf_op jit(solution)/shard_map/ppermute | solution.py:41
  71.1 3.0 %collective-permute-done.17.after = bf16[2,4,112,128]{3,2,1,0:T(8,128)(2,1)S(1)} collective-permute-done((bf16[2,4,112,128]{3,2,1,0:T(8,128)(2,1)S(1)}, bf16[2,4,112,128]{3,2,1,0:T(8,128)(2,1)S(1)}, u32[]{:S(2)}, u32[]{:S(2)}) %collective-permute-start.17) | collective-permute-done | bytes 229408 | tf_op jit(solution)/shard_map/ppermute | solution.py:41
  74.1 3.1 %collective-permute-done.18.before = bf16[2,4,112,128]{3,2,1,0:T(8,128)(2,1)S(1)} collective-permute-done((bf16[2,4,112,128]{3,2,1,0:T(8,128)(2,1)S(1)}, bf16[2,4,112,128]{3,2,1,0:T(8,128)(2,1)S(1)}, u32[]{:S(2)}, u32[]{:S(2)}) %collective-permute-start.18) | collective-permute-done | bytes 229408 | tf_op jit(solution)/shard_map/ppermute | solution.py:41
  77.4 1.5 %collective-permute-start.19 = (bf16[2,2,4,112,128]{4,3,2,1,0:T(8,128)(2,1)S(1)}, bf16[2,2,4,112,128]{4,3,2,1,0:T(8,128)(2,1)S(1)}, u32[]{:S(2)}, u32[]{:S(2)}) collective-permute-start(bf16[2,2,4,112,128]{4,3,2,1,0:T(8,128)(2,1)S(1)} %pad_maximum_fusion.2), channel_id=1, source_target_pairs={{3,0},{0,1},{1,2},{2,3},{7,4},{4,5},{5,6},{6,7},{11,8},{8,9},{9,10... | collective-permute-start | bytes 1376264 | tf_op jit(solution)/shard_map/ppermute | solution.py:41
  78.9 2.5 %shard_map.41.start = f32[1024,768]{1,0:T(8,128)S(1)} custom-call(s32[4]{0:T(128)S(1)} %pad_add_fusion.place, bf16[2,4,112,128]{3,2,1,0:T(8,128)(2,1)S(1)} %pad_maximum_fusion.3.far, bf16[3,2,4,112,128]{4,3,2,1,0:T(8,128)(2,1)S(1)} %collective-permute-done.12.after, ...), custom_call_target="tpu_custom_call", output_to_operand_aliasing={{}: (5, {})} | custom-call | tf_op jit(solution)/shard_map/pallas_call | solution.py:194
  81.5 1.3 %shard_map.42.start = f32[1024,768]{1,0:T(8,128)S(1)} custom-call(s32[4]{0:T(128)S(1)} %pad_add_fusion.place, bf16[2,4,112,128]{3,2,1,0:T(8,128)(2,1)S(1)} %collective-permute-done.17.after, bf16[2,4,112,128]{3,2,1,0:T(8,128)(2,1)S(1)} %collective-permute-done.18.before, bf16[4,448,768]{2,1,0:T(8,128)(2,1)S(1)} %shard_map.39.both, ...), custom_call_target="tpu_custom_call", output_to_operand_aliasing={{}: (4, {})} | custom-call | tf_op jit(solution)/shard_map/pallas_call | solution.py:194
  82.8 1.9 %collective-permute-done.13.low = bf16[2,2,4,112,128]{4,3,2,1,0:T(8,128)(2,1)S(1)} collective-permute-done((bf16[2,2,4,112,128]{4,3,2,1,0:T(8,128)(2,1)S(1)}, bf16[2,2,4,112,128]{4,3,2,1,0:T(8,128)(2,1)S(1)}, u32[]{:S(2)}, u32[]{:S(2)}) %collective-permute-start.13) | collective-permute-done | bytes 458784 | tf_op jit(solution)/shard_map/ppermute | solution.py:41
  85.3 6.9 %collective-permute-start.21 = (bf16[512,384]{1,0:T(8,128)(2,1)S(1)}, bf16[512,384]{1,0:T(8,128)(2,1)S(1)}, u32[]{:S(2)}, u32[]{:S(2)}) collective-permute-start(bf16[512,384]{1,0:T(8,128)(2,1)S(1)} %get-tuple-element.36), channel_id=1, source_target_pairs={{16,0},{0,16},{17,1},{1,17},{18,2},{2,18},{19,3},{3,19},{20,4},{4,... | collective-permute-start | bytes 1179656 | tf_op jit(solution)/shard_map/ppermute | solution.py:23
  92.2 1.5 %shard_map.43 = (bf16[512,384]{1,0:T(8,128)(2,1)S(1)}, bf16[512,384]{1,0:T(8,128)(2,1)S(1)}) custom-call(s32[4]{0:T(128)S(1)} %pad_add_fusion.place, bf16[2,2,4,112,128]{4,3,2,1,0:T(8,128)(2,1)S(1)} %collective-permute-done.13.low, bf16[2,2,4,112,128]{4,3,2,1,0:T(8,128)(2,1)S(1)} %collective-permute-done.19.high, bf16[4,448,768]{2,1,0:T(8,128)(2,1)S(1)} %shard_map.39.both, ...), custom_call_target="tpu_custom_call" | custom-call | tf_op jit(solution)/shard_map/pallas_call | solution.py:194
  93.8 1.6 %shard_map.45.given = bf16[2048,384]{1,0:T(8,128)(2,1)} custom-call(s32[4]{0:T(128)S(1)} %pad_add_fusion.place, bf16[512,384]{1,0:T(8,128)(2,1)S(1)} %get-tuple-element.34.mine1, bf16[512,384]{1,0:T(8,128)(2,1)S(1)} %get-tuple-element.35.mine2, bf16[512,384]{1,0:T(8,128)(2,1)S(1)} %collective-permute-done.21.theirs1), custom_call_target="tpu_custom_call" | custom-call | tf_op jit(solution)/shard_map/pallas_call | solution.py:194
  95.5 1.3 %shard_map.46 = bf16[2048,384]{1,0:T(8,128)(2,1)} custom-call(s32[4]{0:T(128)S(1)} %pad_add_fusion.place, bf16[512,384]{1,0:T(8,128)(2,1)S(1)} %collective-permute-done.20.theirs2, bf16[2048,384]{1,0:T(8,128)(2,1)} %shard_map.45.given), custom_call_target="tpu_custom_call", output_to_operand_aliasing={{}: (2, {})} | custom-call | tf_op jit(solution)/shard_map/pallas_call | solution.py:194
  (45 shorter events, 8.6 us)
Async XLA Ops:
  0.0 30.3 %collective-permute-start.5 = (bf16[1792,384]{1,0:T(8,128)(2,1)}, bf16[1792,384]{1,0:T(8,128)(2,1)S(1)}, u32[]{:S(2)}, u32[]{:S(2)}) collective-permute-start(bf16[1792,384]{1,0:T(8,128)(2,1)} %own.1), channel_id=1, source_target_pairs={{16,0},{0,16},{17,1},{1,17},{18,2},{2,18},{19,3},{3,19},{20,4},{4,... | collective-permute-start | bytes 4128776 | tf_op jit(solution)/shard_map/ppermute | solution.py:23
  3.2 1.0 %copy-start.3 = (bf16[112,2048]{1,0:T(8,128)(2,1)S(1)}, bf16[112,2048]{1,0:T(8,128)(2,1)}, u32[]{:S(2)}) copy-start(bf16[112,2048]{1,0:T(8,128)(2,1)} %panel.1) | copy-start | bytes 1376260
  4.3 0.7 copy-start.4
  5.4 3.7 %collective-permute-start = (bf16[16,112,128]{2,1,0:T(8,128)(2,1)S(1)}, bf16[16,112,128]{2,1,0:T(8,128)(2,1)S(1)}, u32[]{:S(2)}, u32[]{:S(2)}) collective-permute-start(bf16[16,112,128]{2,1,0:T(8,128)(2,1)S(1)} %get-tuple-element.22), channel_id=1, source_target_pairs={{0,16},{1,17},{2,18},{3,19},{4,20},{5,21},{6,22},{7,23},{8,24},{9,... | collective-permute-start | bytes 1376264 | tf_op jit(solution)/shard_map/ppermute | solution.py:220
  6.8 24.7 %copy-start = (bf16[1792,384]{1,0:T(8,128)(2,1)S(1)}, bf16[1792,384]{1,0:T(8,128)(2,1)}, u32[]{:S(2)}) copy-start(bf16[1792,384]{1,0:T(8,128)(2,1)} %own.1) | copy-start | bytes 4128772
  9.8 8.2 %collective-permute-start.1 = (bf16[4,112,128]{2,1,0:T(8,128)(2,1)S(1)}, bf16[4,112,128]{2,1,0:T(8,128)(2,1)S(1)}, u32[]{:S(2)}, u32[]{:S(2)}) collective-permute-start(bf16[4,112,128]{2,1,0:T(8,128)(2,1)S(1)} %get-tuple-element.24), channel_id=1, source_target_pairs={{80,16},{144,80},{208,144},{16,208},{81,17},{145,81},{209,145},{17... | collective-permute-start | bytes 344072 | tf_op jit(solution)/shard_map/ppermute | solution.py:31
  12.5 6.7 %collective-permute-start.2 = (bf16[4,112,128]{2,1,0:T(8,128)(2,1)S(1)}, bf16[4,112,128]{2,1,0:T(8,128)(2,1)S(1)}, u32[]{:S(2)}, u32[]{:S(2)}) collective-permute-start(bf16[4,112,128]{2,1,0:T(8,128)(2,1)S(1)} %get-tuple-element.25), channel_id=1, source_target_pairs={{208,16},{16,80},{80,144},{144,208},{209,17},{17,81},{81,145},{145... | collective-permute-start | bytes 344072 | tf_op jit(solution)/shard_map/ppermute | solution.py:31
  15.1 7.0 %collective-permute-start.3 = (bf16[4,112,128]{2,1,0:T(8,128)(2,1)S(1)}, bf16[4,112,128]{2,1,0:T(8,128)(2,1)S(1)}, u32[]{:S(2)}, u32[]{:S(2)}) collective-permute-start(bf16[4,112,128]{2,1,0:T(8,128)(2,1)S(1)} %get-tuple-element.26), channel_id=1, source_target_pairs={{144,16},{208,80},{16,144},{80,208},{145,17},{209,81},{17,145},{81... | collective-permute-start | bytes 344072 | tf_op jit(solution)/shard_map/ppermute | solution.py:31
  22.2 11.4 %collective-permute-start.4 = (bf16[4,112,128]{2,1,0:T(8,128)(2,1)S(1)}, bf16[4,112,128]{2,1,0:T(8,128)(2,1)S(1)}, u32[]{:S(2)}, u32[]{:S(2)}) collective-permute-start(bf16[4,112,128]{2,1,0:T(8,128)(2,1)S(1)} %fusion), channel_id=1, source_target_pairs={{48,16},{16,48},{49,17},{17,49},{50,18},{18,50},{51,19},{19,51},{5... | collective-permute-start | bytes 344072 | tf_op jit(solution)/shard_map/ppermute | solution.py:31
  30.3 1.1 %copy-start.1 = (bf16[1792,384]{1,0:T(8,128)(2,1)}, bf16[1792,384]{1,0:T(8,128)(2,1)S(1)}, u32[]{:S(2)}) copy-start(bf16[1792,384]{1,0:T(8,128)(2,1)S(1)} %collective-permute-done.5.other) | copy-start | bytes 4128772
  31.4 1.3 %copy-start.2 = (bf16[1792,384]{1,0:T(8,128)(2,1)S(1)}, bf16[1792,384]{1,0:T(8,128)(2,1)}, u32[]{:S(2)}) copy-start(bf16[1792,384]{1,0:T(8,128)(2,1)} %copy-done.1) | copy-start | bytes 4128772
  33.6 9.3 %collective-permute-start.8 = (bf16[4,112,128]{2,1,0:T(8,128)(2,1)S(1)}, bf16[4,112,128]{2,1,0:T(8,128)(2,1)S(1)}, u32[]{:S(2)}, u32[]{:S(2)}) collective-permute-start(bf16[4,112,128]{2,1,0:T(8,128)(2,1)S(1)} %add_convert_fusion), channel_id=1, source_target_pairs={{28,16},{24,20},{20,24},{16,28},{29,17},{25,21},{21,25},{17,29},{3... | collective-permute-start | bytes 344072 | tf_op jit(solution)/shard_map/ppermute | solution.py:29
  37.3 5.7 %collective-permute-start.6 = (bf16[4,112,128]{2,1,0:T(8,128)(2,1)S(1)}, bf16[4,112,128]{2,1,0:T(8,128)(2,1)S(1)}, u32[]{:S(2)}, u32[]{:S(2)}) collective-permute-start(bf16[4,112,128]{2,1,0:T(8,128)(2,1)S(1)} %add_convert_fusion), channel_id=1, source_target_pairs={{20,16},{16,20},{28,24},{24,28},{21,17},{17,21},{29,25},{25,29},{2... | collective-permute-start | bytes 344072 | tf_op jit(solution)/shard_map/ppermute | solution.py:29
  39.5 7.7 %collective-permute-start.7 = (bf16[4,112,128]{2,1,0:T(8,128)(2,1)S(1)}, bf16[4,112,128]{2,1,0:T(8,128)(2,1)S(1)}, u32[]{:S(2)}, u32[]{:S(2)}) collective-permute-start(bf16[4,112,128]{2,1,0:T(8,128)(2,1)S(1)} %add_convert_fusion), channel_id=1, source_target_pairs={{24,16},{28,20},{16,24},{20,28},{25,17},{29,21},{17,25},{21,29},{2... | collective-permute-start | bytes 344072 | tf_op jit(solution)/shard_map/ppermute | solution.py:29
  47.2 2.5 %collective-permute-start.9 = (bf16[2,4,112,128]{3,2,1,0:T(8,128)(2,1)S(1)}, bf16[2,4,112,128]{3,2,1,0:T(8,128)(2,1)}, u32[]{:S(2)}, u32[]{:S(2)}) collective-permute-start(bf16[2,4,112,128]{3,2,1,0:T(8,128)(2,1)S(1)} %slice.24), channel_id=1, source_target_pairs={{16,0},{17,1},{18,2},{19,3},{20,4},{21,5},{22,6},{23,7},{24,8},{25... | collective-permute-start | bytes 688136 | tf_op jit(solution)/shard_map/ppermute | solution.py:237
  49.8 5.8 %collective-permute-start.10 = (bf16[2,4,112,128]{3,2,1,0:T(8,128)(2,1)S(1)}, bf16[2,4,112,128]{3,2,1,0:T(8,128)(2,1)S(1)}, u32[]{:S(2)}, u32[]{:S(2)}) collective-permute-start(bf16[2,4,112,128]{3,2,1,0:T(8,128)(2,1)S(1)} %slice_select_fusion.own), channel_id=1, source_target_pairs={{64,0},{65,1},{66,2},{67,3},{68,4},{69,5},{70,6},{71,7},{72,8},{73... | collective-permute-start | bytes 688136 | tf_op jit(solution)/shard_map/ppermute | solution.py:41
  52.6 6.4 %collective-permute-start.11 = (bf16[2,4,112,128]{3,2,1,0:T(8,128)(2,1)S(1)}, bf16[2,4,112,128]{3,2,1,0:T(8,128)(2,1)S(1)}, u32[]{:S(2)}, u32[]{:S(2)}) collective-permute-start(bf16[2,4,112,128]{3,2,1,0:T(8,128)(2,1)S(1)} %slice_select_fusion.own), channel_id=1, source_target_pairs={{192,0},{193,1},{194,2},{195,3},{196,4},{197,5},{198,6},{199,7},{2... | collective-permute-start | bytes 688136 | tf_op jit(solution)/shard_map/ppermute | solution.py:41
  59.1 18.1 %collective-permute-start.12 = (bf16[3,2,4,112,128]{4,3,2,1,0:T(8,128)(2,1)S(1)}, bf16[3,2,4,112,128]{4,3,2,1,0:T(8,128)(2,1)S(1)}, u32[]{:S(2)}, u32[]{:S(2)}) collective-permute-start(bf16[3,2,4,112,128]{4,3,2,1,0:T(8,128)(2,1)S(1)} %pad_maximum_fusion), channel_id=1, source_target_pairs={{1,0},{2,1},{3,2},{0,3},{5,4},{6,5},{7,6},{4,7},{9,8},{10,9},{11,1... | collective-permute-start | bytes 2064392 | tf_op jit(solution)/shard_map/ppermute | solution.py:41
  61.5 15.8 %collective-permute-start.14 = (bf16[3,2,4,112,128]{4,3,2,1,0:T(8,128)(2,1)S(1)}, bf16[3,2,4,112,128]{4,3,2,1,0:T(8,128)(2,1)S(1)}, u32[]{:S(2)}, u32[]{:S(2)}) collective-permute-start(bf16[3,2,4,112,128]{4,3,2,1,0:T(8,128)(2,1)S(1)} %pad_maximum_fusion), channel_id=1, source_target_pairs={{3,0},{0,1},{1,2},{2,3},{7,4},{4,5},{5,6},{6,7},{11,8},{8,9},{9,10... | collective-permute-start | bytes 2064392 | tf_op jit(solution)/shard_map/ppermute | solution.py:41
  61.5 5.0 %collective-permute-start.15 = (bf16[1,4,112,128]{3,2,1,0:T(8,128)(2,1)S(1)}, bf16[1,4,112,128]{3,2,1,0:T(8,128)(2,1)S(1)}, u32[]{:S(2)}, u32[]{:S(2)}) collective-permute-start(bf16[1,4,112,128]{3,2,1,0:T(8,128)(2,1)S(1)} %slice.28), channel_id=1, source_target_pairs={{64,0},{65,1},{66,2},{67,3},{68,4},{69,5},{70,6},{71,7},{72,8},{73... | collective-permute-start | bytes 344072 | tf_op jit(solution)/shard_map/ppermute | solution.py:41
  61.9 4.9 %collective-permute-start.16 = (bf16[1,4,112,128]{3,2,1,0:T(8,128)(2,1)S(1)}, bf16[1,4,112,128]{3,2,1,0:T(8,128)(2,1)S(1)}, u32[]{:S(2)}, u32[]{:S(2)}) collective-permute-start(bf16[1,4,112,128]{3,2,1,0:T(8,128)(2,1)S(1)} %slice.29), channel_id=1, source_target_pairs={{192,0},{193,1},{194,2},{195,3},{196,4},{197,5},{198,6},{199,7},{2... | collective-permute-start | bytes 344072 | tf_op jit(solution)/shard_map/ppermute | solution.py:41
  66.9 7.2 %collective-permute-start.17 = (bf16[2,4,112,128]{3,2,1,0:T(8,128)(2,1)S(1)}, bf16[2,4,112,128]{3,2,1,0:T(8,128)(2,1)S(1)}, u32[]{:S(2)}, u32[]{:S(2)}) collective-permute-start(bf16[2,4,112,128]{3,2,1,0:T(8,128)(2,1)S(1)} %pad_maximum_fusion.3.far), channel_id=1, source_target_pairs={{1,0},{2,1},{3,2},{0,3},{5,4},{6,5},{7,6},{4,7},{9,8},{10,9},{11,1... | collective-permute-start | bytes 688136 | tf_op jit(solution)/shard_map/ppermute | solution.py:41
  71.1 6.1 %collective-permute-start.18 = (bf16[2,4,112,128]{3,2,1,0:T(8,128)(2,1)S(1)}, bf16[2,4,112,128]{3,2,1,0:T(8,128)(2,1)S(1)}, u32[]{:S(2)}, u32[]{:S(2)}) collective-permute-start(bf16[2,4,112,128]{3,2,1,0:T(8,128)(2,1)S(1)} %pad_maximum_fusion.3.far), channel_id=1, source_target_pairs={{3,0},{0,1},{1,2},{2,3},{7,4},{4,5},{5,6},{6,7},{11,8},{8,9},{9,10... | collective-permute-start | bytes 688136 | tf_op jit(solution)/shard_map/ppermute | solution.py:41
  77.2 7.4 %collective-permute-start.13 = (bf16[2,2,4,112,128]{4,3,2,1,0:T(8,128)(2,1)S(1)}, bf16[2,2,4,112,128]{4,3,2,1,0:T(8,128)(2,1)S(1)}, u32[]{:S(2)}, u32[]{:S(2)}) collective-permute-start(bf16[2,2,4,112,128]{4,3,2,1,0:T(8,128)(2,1)S(1)} %slice.26), channel_id=1, source_target_pairs={{1,0},{2,1},{3,2},{0,3},{5,4},{6,5},{7,6},{4,7},{9,8},{10,9},{11,1... | collective-permute-start | bytes 1376264 | tf_op jit(solution)/shard_map/ppermute | solution.py:41
  77.4 14.8 %collective-permute-start.19 = (bf16[2,2,4,112,128]{4,3,2,1,0:T(8,128)(2,1)S(1)}, bf16[2,2,4,112,128]{4,3,2,1,0:T(8,128)(2,1)S(1)}, u32[]{:S(2)}, u32[]{:S(2)}) collective-permute-start(bf16[2,2,4,112,128]{4,3,2,1,0:T(8,128)(2,1)S(1)} %pad_maximum_fusion.2), channel_id=1, source_target_pairs={{3,0},{0,1},{1,2},{2,3},{7,4},{4,5},{5,6},{6,7},{11,8},{8,9},{9,10... | collective-permute-start | bytes 1376264 | tf_op jit(solution)/shard_map/ppermute | solution.py:41
  85.3 8.6 %collective-permute-start.21 = (bf16[512,384]{1,0:T(8,128)(2,1)S(1)}, bf16[512,384]{1,0:T(8,128)(2,1)S(1)}, u32[]{:S(2)}, u32[]{:S(2)}) collective-permute-start(bf16[512,384]{1,0:T(8,128)(2,1)S(1)} %get-tuple-element.36), channel_id=1, source_target_pairs={{16,0},{0,16},{17,1},{1,17},{18,2},{2,18},{19,3},{3,19},{20,4},{4,... | collective-permute-start | bytes 1179656 | tf_op jit(solution)/shard_map/ppermute | solution.py:23
  93.7 1.8 %collective-permute-start.20 = (bf16[512,384]{1,0:T(8,128)(2,1)S(1)}, bf16[512,384]{1,0:T(8,128)(2,1)S(1)}, u32[]{:S(2)}, u32[]{:S(2)}) collective-permute-start(bf16[512,384]{1,0:T(8,128)(2,1)S(1)} %get-tuple-element.33), channel_id=1, source_target_pairs={{16,0},{0,16},{17,1},{1,17},{18,2},{2,18},{19,3},{3,19},{20,4},{4,... | collective-permute-start | bytes 1179656 | tf_op jit(solution)/shard_map/ppermute | solution.py:23

commit v7 on v5

--- a/solution.py
+++ b/solution.py
@@ -27,11 +27,10 @@
     return lax.ppermute(block, axis, [(i ^ bits, i) for i in range(size)])
 
 
-def turn(block, order, ahead):
+def turn(block, order, bits):
     pairs = []
     for x, z_hi, core, z_lo, y in itertools.product(*map(range, (4, 2, 2, 4, 4))):
-        along_x = core == order
-        source = ((x + ahead) % 4, y) if along_x else (x, (y + ahead) % 4)
+        source = (x ^ bits, y) if core == order else (x, y ^ bits)
         place = [((p * 2 + z_hi) * 2 + core) * 16 + z_lo * 4 + q for p, q in (source, (x, y))]
         pairs.append(tuple(place))
     return lax.ppermute(block, ROW + COL, pairs)
@@ -50,20 +49,20 @@
 
 
 def add_cores(place, keep, received, mine, *away):
-    for back in range(4):
+    for bits in range(4):
         for half in range(2):
-            slab = lax.rem(place[0] + 4 - back, 4) * 2 + half
+            slab = (place[0] ^ bits) * 2 + half
             total = keep[slab] + received[slab]
-            if back:
-                away[back - 1][half] = total.astype(BF16)
+            if bits:
+                away[bits - 1][half] = total.astype(BF16)
             else:
                 mine[half] = total
 
 
 def order_pairs(place, own, other, both):
-    for k, ahead in enumerate(ORDER):
+    for k, bits in enumerate(ORDER):
         for j in range(4):
-            y, z_lo = lax.rem(place[1] + ahead, 4), place[3] ^ j
+            y, z_lo = place[1] ^ bits, place[3] ^ j
             rows = pl.ds(pl.multiple_of((z_lo * 4 + y) * 112, 16), 112)
             both[k, pl.ds(j * 112, 112), :384] = own[rows]
             both[k, pl.ds(j * 112, 112), 384:] = other[rows]
@@ -94,80 +93,84 @@
     return both[pl.ds(first, count)].reshape(count * 448, 768)
 
 
-def product_one(place, own, after, before, both, out):
-    @on_core(place, 0)
-    def _():
-        out[rows(0, 3)] = dot_t(by_x(own, after, before), both[0])
-
-    @on_core(place, 1)
-    def _():
-        out[rows(0)] = dot_t(by_y(own, after, before), deep(both, 0, 3))
-
-
-def product_two(place, far, after, before, both, start, out):
-    @on_core(place, 0)
-    def _():
-        out[rows(0, 3)] = (
-            start[rows(0, 3)]
-            + dot_t(by_x(*slabs(after)), both[1])
-            + dot_t(by_x(*slabs(before)), both[2])
+def product_one(place, first, both, out):
+    @on_core(place, 0)
+    def _():
+        out[rows(0, 2)] = dot_t(by_x(*slabs(first)), both[0])
+
+    @on_core(place, 1)
+    def _():
+        out[rows(0)] = dot_t(by_y(*slabs(first)), deep(both, 0, 2))
+
+
+def product_two(place, last, one, three, both, start, out):
+    last, one, three = slabs(last), slabs(one), slabs(three)
+
+    @on_core(place, 0)
+    def _():
+        out[rows(0, 2)] = (
+            start[rows(0, 2)] + dot_t(by_x(*one), both[1]) + dot_t(by_x(*three), both[2])
         )
-        out[rows(3)] = dot_t(by_x(far), both[0])
-
-    @on_core(place, 1)
-    def _():
-        out[rows(0)] = start[rows(0)] + dot_t(by_y(far), both[3])
-        out[rows(1)] = dot_t(by_y(*slabs(after)), deep(both, 0, 3))
-        out[rows(2)] = dot_t(by_y(*slabs(before)), deep(both, 0, 3))
-
-
-def product_three(place, after, before, both, start, out):
-    @on_core(place, 0)
-    def _():
-        out[rows(0, 3)] = start[rows(0, 3)]
-        out[rows(3)] = start[rows(3)] + dot_t(by_x(after), both[1]) + dot_t(by_x(before), both[2])
+        out[rows(2, 2)] = dot_t(by_x(*last), both[0])
+
+    @on_core(place, 1)
+    def _():
+        out[rows(0)] = start[rows(0)] + dot_t(by_y(*last), deep(both, 2, 2))
+        out[rows(1)] = dot_t(by_y(*one), deep(both, 0, 2))
+        out[rows(2)] = dot_t(by_y(*three), deep(both, 0, 2))
+
+
+def product_three(place, one, three, both, start, out):
+    one, three = slabs(one), slabs(three)
+
+    @on_core(place, 0)
+    def _():
+        out[rows(0, 2)] = start[rows(0, 2)]
+        out[rows(2, 2)] = (
+            start[rows(2, 2)] + dot_t(by_x(*one), both[1]) + dot_t(by_x(*three), both[2])
+        )
 
     @on_core(place, 1)
     def _():
         out[rows(0)] = start[rows(0)]
-        out[rows(1)] = start[rows(1)] + dot_t(by_y(after), both[3])
-        out[rows(2)] = start[rows(2)] + dot_t(by_y(before), both[3])
-
-
-def product_four(place, low, both, start, mine, theirs):
+        out[rows(1)] = start[rows(1)] + dot_t(by_y(*one), deep(both, 2, 2))
+        out[rows(2)] = start[rows(2)] + dot_t(by_y(*three), deep(both, 2, 2))
+
+
+def product_four(place, first, both, start, mine, theirs):
     def keep(total):
         mine[...] = total[:, :384].astype(BF16)
         theirs[...] = total[:, 384:].astype(BF16)
 
     @on_core(place, 0)
     def _():
-        keep(start[rows(0, 2)] + dot_t(by_x(low[0], low[1]), both[3]))
+        keep(start[rows(0, 2)] + dot_t(by_x(*slabs(first)), both[3]))
 
     @on_core(place, 1)
     def _():
         keep(start[rows(0, 2)])
 
 
-def product_five(place, low, high, both, start, mine, theirs):
+def product_five(place, first, last, both, start, mine, theirs):
     def keep(at, total):
         mine[at] = total[:, :384].astype(BF16)
         theirs[at] = total[:, 384:].astype(BF16)
 
     @on_core(place, 0)
     def _():
-        keep(rows(0, 2), start[rows(2, 2)] + dot_t(by_x(*slabs(high)), both[3]))
+        keep(rows(0, 2), start[rows(2, 2)] + dot_t(by_x(*slabs(last)), both[3]))
 
     @on_core(place, 1)
     def _():
         keep(rows(0), start[rows(2)])
-        keep(rows(1), dot_t(by_y(*slabs(low), *slabs(high)), deep(both, 0, 4)))
+        keep(rows(1), dot_t(by_y(*slabs(first), *slabs(last)), deep(both, 0, 4)))
 
 
 def place_rows(place, parts, out, sems):
     copies = []
     for block, core, which in parts:
         for i in range(2):
-            row = core * 1024 + lax.rem(place[0] + ORDER[which * 2 + i], 4) * 256
+            row = core * 1024 + (place[0] ^ ORDER[which * 2 + i]) * 256
             at = pl.ds(pl.multiple_of(row, 256), 256)
             sem = sems.at[len(copies)]
             copies.append(pltpu.make_async_copy(block.at[rows(i)], out.at[at], sem))
@@ -212,8 +215,8 @@
         (place, keep, fetch(send, "core", 2, 1)),
         (VMEM,) * 4,
     )
-    for ahead in (1, 3, 2):
-        part = part + fetch(away[ahead - 1], "x", 4, ahead).astype(F32)
+    for bits in (1, 3, 2):
+        part = part + swap(away[bits - 1], "x", 4, bits).astype(F32)
 
     other = fetch(pair_conduction, "core", 2, 1)
     both = call(
@@ -224,37 +227,34 @@
     part = (part + share.astype(F32)).astype(BF16)
     own = jnp.stack([part] + [swap(part, "z_lo", 4, bits) for bits in (1, 2, 3)], 1)
 
-    after, before = turn(own, 0, 1), turn(own, 0, 3)
-    far = jnp.concatenate([turn(after[:1], 0, 1), turn(before[1:], 0, 3)])
+    first = jnp.stack([own, turn(own, 0, 1)])
+    last = turn(first, 0, 3)
+    one1, three1 = turn(first, 1, 1), turn(first, 1, 3)
     total = jax.ShapeDtypeStruct((1024, 768), F32)
-    total_one = call(product_one, total, (place, own, after, before, both))
-    sent = jnp.stack([own, after, before])
-    after1, before1 = turn(sent, 1, 1), turn(sent, 1, 3)
-    far, total_one = lax.optimization_barrier((far, total_one))
-    after2, before2 = turn(far, 1, 1), turn(far, 1, 3)
-    low, high = turn(after1[:2], 1, 1), turn(jnp.stack([before1[2], before2]), 1, 3)
+    total_one = call(product_one, total, (place, first, both))
+    last, total_one = lax.optimization_barrier((last, total_one))
+    one2, three2 = turn(last, 1, 1), turn(last, 1, 3)
+    one1, three1 = lax.optimization_barrier((one1, three1))
+    far1, far2 = turn(three1, 1, 1), turn(one2, 1, 3)
     total_two = call(
         product_two,
         total,
-        (place, far, after1, before1, both, total_one),
+        (place, last, one1, three1, both, total_one),
         input_output_aliases={5: 0},
     )
     total_three = call(
         product_three,
         total,
-        (place, after2, before2, both, total_two),
+        (place, one2, three2, both, total_two),
         input_output_aliases={4: 0},
     )
     half = jax.ShapeDtypeStruct((512, 384), BF16)
     mine1, theirs1 = call(
-        product_four, (half, half), (place, low, both, total_three), (VMEM, VMEM)
+        product_four, (half, half), (place, far1, both, total_three), (VMEM, VMEM)
     )
     theirs1 = fetch(theirs1, "core", 2, 1)
     mine2, theirs2 = call(
-        product_five,
-        (half, half),
-        (place, low, high, both, total_three),
-        (VMEM, VMEM),
+        product_five, (half, half), (place, far1, far2, both, total_three), (VMEM, VMEM)
     )
     theirs2 = fetch(theirs2, "core", 2, 1)
 

time: 79.2 us -> 78.6 us (level)
  waiting for transfers between devices: 22.3 us -> 21.4 us
    ppermute x10 -> x8, starting transfers between devices: 12.7 us -> 8.93 us  [turn(): return lax.ppermute(block, ROW + COL, pairs)]
    ppermute x7 -> x4, waiting for transfers between devices: 5.53 us -> 1.81 us  [fetch(): lax.ppermute(block, axis, [((i + ahead) % size, i) for i in range(size)])]
    ppermute x4 -> x7, starting transfers between devices: 11.1 us -> 14 us  [swap(): return lax.ppermute(block, axis, [(i ^ bits, i) for i in range(size)])]
    ppermute x7 -> x4, starting transfers between devices: 16.2 us -> 17.9 us  [fetch(): lax.ppermute(block, axis, [((i + ahead) % size, i) for i in range(size)])]
    ppermute x4 -> x7, waiting for transfers between devices: 4.06 us -> 5.51 us  [swap(): return lax.ppermute(block, axis, [(i ^ bits, i) for i in range(size)])]
    ppermute x10 -> x8, waiting for transfers between devices: 12.7 us -> 14.1 us  [turn(): return lax.ppermute(block, ROW + COL, pairs)]
  transfers between devices with their start and end apart: 21 -> 19, of which waited for: 14 -> 12; matrix products, arithmetic and copies ran while one was open for 0% -> 0% of each run, Pallas kernels for 14% -> 14%
where the time goes in v7:
time: 78.6 us; the launch traced here: 78.4 us
  starting transfers between devices  40.7 us (52%)
  waiting for transfers between devices  21.4 us (27%)
  Pallas kernels  12.7 us (16%)
  local copies, waits for them, and re-layouts  3.11 us (4%)
    ppermute x4, starting transfers between devices, fetch(): lax.ppermute(block, axis, [((i + ahead) % size, i) for i in range(size)])  17.9 us
    ppermute x8, waiting for transfers between devices, turn(): return lax.ppermute(block, ROW + COL, pairs)  14.1 us
    ppermute x7, starting transfers between devices, swap(): return lax.ppermute(block, axis, [(i ^ bits, i) for i in range(size)])  14 us
    pallas_call x10, Pallas kernels, call(): pl.pallas_call(kernel, out_shape=out_shape, in_specs=specs or [SMEM] + [V...  12.7 us
    ppermute x8, starting transfers between devices, turn(): return lax.ppermute(block, ROW + COL, pairs)  8.93 us
    ppermute x7, waiting for transfers between devices, swap(): return lax.ppermute(block, axis, [(i ^ bits, i) for i in range(size)])  5.51 us
    unnamed x6, local copies, waits for them, and re-layouts  3.11 us
    ppermute x4, waiting for transfers between devices, fetch(): lax.ppermute(block, axis, [((i + ahead) % size, i) for i in range(size)])  1.81 us
  transfers between devices with their start and end apart: 19, of which 12 were waited for; matrix products, arithmetic and copies ran while one was open for 0% of the time, Pallas kernels for 14%

profile of v7, /device:TPU:1, one launch (start us, length us, event | category | flops | bytes accessed | tf_op | source)
XLA Modules:
  0.0 78.4 jit_solution(10722490433375491746)
XLA Ops:
  0.0 3.2 %collective-permute-start.5 = (bf16[1792,384]{1,0:T(8,128)(2,1)}, bf16[1792,384]{1,0:T(8,128)(2,1)S(1)}, u32[]{:S(2)}, u32[]{:S(2)}) collective-permute-start(bf16[1792,384]{1,0:T(8,128)(2,1)} %own.1), channel_id=1, source_target_pairs={{16,0},{0,16},{17,1},{1,17},{18,2},{2,18},{19,3},{3,19},{20,4},{4,... | collective-permute-start | bytes 4128776 | tf_op jit(solution)/shard_map/ppermute | solution.py:23
  3.3 1.0 %copy-done.1 = bf16[112,2048]{1,0:T(8,128)(2,1)S(1)} copy-done((bf16[112,2048]{1,0:T(8,128)(2,1)S(1)}, bf16[112,2048]{1,0:T(8,128)(2,1)}, u32[]{:S(2)}) %copy-start.1) | copy-done | bytes 458776
  5.1 1.0 %shard_map.37 = (f32[8,112,128]{2,1,0:T(8,128)S(1)}, f32[8,112,128]{2,1,0:T(8,128)S(1)}) custom-call(s32[4]{0:T(128)S(1)} %pad_add_fusion.place, bf16[112,112]{1,0:T(8,128)(2,1)S(1)} %copy-done.2, bf16[112,2048]{1,0:T(8,128)(2,1)S(1)} %copy-done.1), custom_call_target="tpu_custom_call" | custom-call | tf_op jit(solution)/shard_map/pallas_call | solution.py:193
  6.2 1.8 %collective-permute-done.received = f32[8,112,128]{2,1,0:T(8,128)S(1)} collective-permute-done((f32[8,112,128]{2,1,0:T(8,128)S(1)}, f32[8,112,128]{2,1,0:T(8,128)S(1)}, u32[]{:S(2)}, u32[]{:S(2)}) %collective-permute-start) | collective-permute-done | bytes 458784 | tf_op jit(solution)/shard_map/ppermute | solution.py:23
  8.7 1.3 %collective-permute-start.2 = (bf16[2,112,128]{2,1,0:T(8,128)(2,1)S(1)}, bf16[2,112,128]{2,1,0:T(8,128)(2,1)S(1)}, u32[]{:S(2)}, u32[]{:S(2)}) collective-permute-start(bf16[2,112,128]{2,1,0:T(8,128)(2,1)S(1)} %get-tuple-element.25), channel_id=1, source_target_pairs={{192,0},{128,64},{64,128},{0,192},{193,1},{129,65},{65,129},{1,193... | collective-permute-start | bytes 172040 | tf_op jit(solution)/shard_map/ppermute | solution.py:27
  10.0 2.0 %collective-permute-start.3 = (bf16[2,112,128]{2,1,0:T(8,128)(2,1)S(1)}, bf16[2,112,128]{2,1,0:T(8,128)(2,1)S(1)}, u32[]{:S(2)}, u32[]{:S(2)}) collective-permute-start(bf16[2,112,128]{2,1,0:T(8,128)(2,1)S(1)} %get-tuple-element.26), channel_id=1, source_target_pairs={{128,0},{192,64},{0,128},{64,192},{129,1},{193,65},{1,129},{65,193... | collective-permute-start | bytes 172040 | tf_op jit(solution)/shard_map/ppermute | solution.py:27
  11.9 1.1 %collective-permute-done.2 = bf16[2,112,128]{2,1,0:T(8,128)(2,1)S(1)} collective-permute-done((bf16[2,112,128]{2,1,0:T(8,128)(2,1)S(1)}, bf16[2,112,128]{2,1,0:T(8,128)(2,1)S(1)}, u32[]{:S(2)}, u32[]{:S(2)}) %collective-permute-start.2) | collective-permute-done | bytes 57376 | tf_op jit(solution)/shard_map/ppermute | solution.py:27
  13.0 1.5 %collective-permute-done.3 = bf16[2,112,128]{2,1,0:T(8,128)(2,1)S(1)} collective-permute-done((bf16[2,112,128]{2,1,0:T(8,128)(2,1)S(1)}, bf16[2,112,128]{2,1,0:T(8,128)(2,1)S(1)}, u32[]{:S(2)}, u32[]{:S(2)}) %collective-permute-start.3) | collective-permute-done | bytes 57376 | tf_op jit(solution)/shard_map/ppermute | solution.py:27
  14.5 7.0 %collective-permute-start.4 = (bf16[2,112,128]{2,1,0:T(8,128)(2,1)S(1)}, bf16[2,112,128]{2,1,0:T(8,128)(2,1)S(1)}, u32[]{:S(2)}, u32[]{:S(2)}) collective-permute-start(bf16[2,112,128]{2,1,0:T(8,128)(2,1)S(1)} %fusion), channel_id=1, source_target_pairs={{32,0},{0,32},{33,1},{1,33},{34,2},{2,34},{35,3},{3,35},{36,4},{4,... | collective-permute-start | bytes 172040 | tf_op jit(solution)/shard_map/ppermute | solution.py:27
  21.5 1.3 %copy-done = bf16[1792,384]{1,0:T(8,128)(2,1)S(1)} copy-done((bf16[1792,384]{1,0:T(8,128)(2,1)S(1)}, bf16[1792,384]{1,0:T(8,128)(2,1)}, u32[]{:S(2)}) %copy-start) | copy-done | bytes 1376280
  23.7 2.4 %collective-permute-start.8 = (bf16[2,112,128]{2,1,0:T(8,128)(2,1)S(1)}, bf16[2,112,128]{2,1,0:T(8,128)(2,1)S(1)}, u32[]{:S(2)}, u32[]{:S(2)}) collective-permute-start(bf16[2,112,128]{2,1,0:T(8,128)(2,1)S(1)} %add_convert_fusion), channel_id=1, source_target_pairs={{12,0},{8,4},{4,8},{0,12},{13,1},{9,5},{5,9},{1,13},{14,2},{10,6},... | collective-permute-start | bytes 172040 | tf_op jit(solution)/shard_map/ppermute | solution.py:27
  26.1 1.2 %collective-permute-start.7 = (bf16[2,112,128]{2,1,0:T(8,128)(2,1)S(1)}, bf16[2,112,128]{2,1,0:T(8,128)(2,1)S(1)}, u32[]{:S(2)}, u32[]{:S(2)}) collective-permute-start(bf16[2,112,128]{2,1,0:T(8,128)(2,1)S(1)} %add_convert_fusion), channel_id=1, source_target_pairs={{8,0},{12,4},{0,8},{4,12},{9,1},{13,5},{1,9},{5,13},{10,2},{14,6},... | collective-permute-start | bytes 172040 | tf_op jit(solution)/shard_map/ppermute | solution.py:27
  27.4 1.3 %collective-permute-done.8 = bf16[2,112,128]{2,1,0:T(8,128)(2,1)S(1)} collective-permute-done((bf16[2,112,128]{2,1,0:T(8,128)(2,1)S(1)}, bf16[2,112,128]{2,1,0:T(8,128)(2,1)S(1)}, u32[]{:S(2)}, u32[]{:S(2)}) %collective-permute-start.8) | collective-permute-done | bytes 57376 | tf_op jit(solution)/shard_map/ppermute | solution.py:27
  29.3 1.0 %collective-permute-done.7 = bf16[2,112,128]{2,1,0:T(8,128)(2,1)S(1)} collective-permute-done((bf16[2,112,128]{2,1,0:T(8,128)(2,1)S(1)}, bf16[2,112,128]{2,1,0:T(8,128)(2,1)S(1)}, u32[]{:S(2)}, u32[]{:S(2)}) %collective-permute-start.7) | collective-permute-done | bytes 57376 | tf_op jit(solution)/shard_map/ppermute | solution.py:27
  30.3 1.4 %collective-permute-start.9 = (bf16[2,4,112,128]{3,2,1,0:T(8,128)(2,1)S(1)}, bf16[2,4,112,128]{3,2,1,0:T(8,128)(2,1)S(1)}, u32[]{:S(2)}, u32[]{:S(2)}) collective-permute-start(bf16[2,4,112,128]{3,2,1,0:T(8,128)(2,1)S(1)} %get-tuple-element.38), channel_id=1, source_target_pairs={{64,0},{65,1},{66,2},{67,3},{68,4},{69,5},{70,6},{71,7},{72,8},{73... | collective-permute-start | bytes 688136 | tf_op jit(solution)/shard_map/ppermute | solution.py:36
  31.7 3.6 %collective-permute-done.9 = bf16[2,4,112,128]{3,2,1,0:T(8,128)(2,1)S(1)} collective-permute-done((bf16[2,4,112,128]{3,2,1,0:T(8,128)(2,1)S(1)}, bf16[2,4,112,128]{3,2,1,0:T(8,128)(2,1)S(1)}, u32[]{:S(2)}, u32[]{:S(2)}) %collective-permute-start.9) | collective-permute-done | bytes 229408 | tf_op jit(solution)/shard_map/ppermute | solution.py:36
  35.3 2.8 %collective-permute-start.13 = (bf16[2,2,4,112,128]{4,3,2,1,0:T(8,128)(2,1)S(1)}, bf16[2,2,4,112,128]{4,3,2,1,0:T(8,128)(2,1)S(1)}, u32[]{:S(2)}, u32[]{:S(2)}) collective-permute-start(bf16[2,2,4,112,128]{4,3,2,1,0:T(8,128)(2,1)S(1)} %pad_maximum_fusion.first), channel_id=1, source_target_pairs={{192,0},{193,1},{194,2},{195,3},{196,4},{197,5},{198,6},{199,7},{2... | collective-permute-start | bytes 1376264 | tf_op jit(solution)/shard_map/ppermute | solution.py:36
  38.5 1.1 %collective-permute-start.11 = (bf16[2,2,4,112,128]{4,3,2,1,0:T(8,128)(2,1)S(1)}, bf16[2,2,4,112,128]{4,3,2,1,0:T(8,128)(2,1)S(1)}, u32[]{:S(2)}, u32[]{:S(2)}) collective-permute-start(bf16[2,2,4,112,128]{4,3,2,1,0:T(8,128)(2,1)S(1)} %pad_maximum_fusion.first), channel_id=1, source_target_pairs={{3,0},{2,1},{1,2},{0,3},{7,4},{6,5},{5,6},{4,7},{11,8},{10,9},{9,1... | collective-permute-start | bytes 1376264 | tf_op jit(solution)/shard_map/ppermute | solution.py:36
  39.6 1.2 %shard_map.40.start = f32[1024,768]{1,0:T(8,128)S(1)} custom-call(s32[4]{0:T(128)S(1)} %pad_add_fusion.place, bf16[2,2,4,112,128]{4,3,2,1,0:T(8,128)(2,1)S(1)} %pad_maximum_fusion.first, bf16[4,448,768]{2,1,0:T(8,128)(2,1)S(1)} %shard_map.39.both), custom_call_target="tpu_custom_call" | custom-call | tf_op jit(solution)/shard_map/pallas_call | solution.py:193
  40.8 3.3 %collective-permute-done.13.last = bf16[2,2,4,112,128]{4,3,2,1,0:T(8,128)(2,1)S(1)} collective-permute-done((bf16[2,2,4,112,128]{4,3,2,1,0:T(8,128)(2,1)S(1)}, bf16[2,2,4,112,128]{4,3,2,1,0:T(8,128)(2,1)S(1)}, u32[]{:S(2)}, u32[]{:S(2)}) %collective-permute-start.13) | collective-permute-done | bytes 458784 | tf_op jit(solution)/shard_map/ppermute | solution.py:36
  44.3 1.1 %collective-permute-start.16 = (bf16[2,2,4,112,128]{4,3,2,1,0:T(8,128)(2,1)S(1)}, bf16[2,2,4,112,128]{4,3,2,1,0:T(8,128)(2,1)S(1)}, u32[]{:S(2)}, u32[]{:S(2)}) collective-permute-start(bf16[2,2,4,112,128]{4,3,2,1,0:T(8,128)(2,1)S(1)} %collective-permute-done.13.last), channel_id=1, source_target_pairs={{3,0},{2,1},{1,2},{0,3},{7,4},{6,5},{5,6},{4,7},{11,8},{10,9},{9,1... | collective-permute-start | bytes 1376264 | tf_op jit(solution)/shard_map/ppermute | solution.py:36
  45.8 3.7 %collective-permute-done.11.three = bf16[2,2,4,112,128]{4,3,2,1,0:T(8,128)(2,1)S(1)} collective-permute-done((bf16[2,2,4,112,128]{4,3,2,1,0:T(8,128)(2,1)S(1)}, bf16[2,2,4,112,128]{4,3,2,1,0:T(8,128)(2,1)S(1)}, u32[]{:S(2)}, u32[]{:S(2)}) %collective-permute-start.11) | collective-permute-done | bytes 458784 | tf_op jit(solution)/shard_map/ppermute | solution.py:36
  49.5 0.8 %collective-permute-start.12 = (bf16[2,2,4,112,128]{4,3,2,1,0:T(8,128)(2,1)S(1)}, bf16[2,2,4,112,128]{4,3,2,1,0:T(8,128)(2,1)S(1)}, u32[]{:S(2)}, u32[]{:S(2)}) collective-permute-start(bf16[2,2,4,112,128]{4,3,2,1,0:T(8,128)(2,1)S(1)} %collective-permute-done.11.three), channel_id=1, source_target_pairs={{1,0},{0,1},{3,2},{2,3},{5,4},{4,5},{7,6},{6,7},{9,8},{8,9},{11,10... | collective-permute-start | bytes 1376264 | tf_op jit(solution)/shard_map/ppermute | solution.py:36
  50.3 1.4 %collective-permute-done.14.one = bf16[2,2,4,112,128]{4,3,2,1,0:T(8,128)(2,1)S(1)} collective-permute-done((bf16[2,2,4,112,128]{4,3,2,1,0:T(8,128)(2,1)S(1)}, bf16[2,2,4,112,128]{4,3,2,1,0:T(8,128)(2,1)S(1)}, u32[]{:S(2)}, u32[]{:S(2)}) %collective-permute-start.14) | collective-permute-done | bytes 458784 | tf_op jit(solution)/shard_map/ppermute | solution.py:36
  51.7 1.1 %collective-permute-start.15 = (bf16[2,2,4,112,128]{4,3,2,1,0:T(8,128)(2,1)S(1)}, bf16[2,2,4,112,128]{4,3,2,1,0:T(8,128)(2,1)S(1)}, u32[]{:S(2)}, u32[]{:S(2)}) collective-permute-start(bf16[2,2,4,112,128]{4,3,2,1,0:T(8,128)(2,1)S(1)} %collective-permute-done.14.one), channel_id=1, source_target_pairs={{3,0},{2,1},{1,2},{0,3},{7,4},{6,5},{5,6},{4,7},{11,8},{10,9},{9,1... | collective-permute-start | bytes 1376264 | tf_op jit(solution)/shard_map/ppermute | solution.py:36
  52.7 2.3 %shard_map.41.start = f32[1024,768]{1,0:T(8,128)S(1)} custom-call(s32[4]{0:T(128)S(1)} %pad_add_fusion.place, bf16[2,2,4,112,128]{4,3,2,1,0:T(8,128)(2,1)S(1)} %collective-permute-done.13.last, bf16[2,2,4,112,128]{4,3,2,1,0:T(8,128)(2,1)S(1)} %collective-permute-done.10.one, ...), custom_call_target="tpu_custom_call", output_to_operand_aliasing={{}: (5, {})} | custom-call | tf_op jit(solution)/shard_map/pallas_call | solution.py:193
  55.0 1.8 %collective-permute-done.16.three = bf16[2,2,4,112,128]{4,3,2,1,0:T(8,128)(2,1)S(1)} collective-permute-done((bf16[2,2,4,112,128]{4,3,2,1,0:T(8,128)(2,1)S(1)}, bf16[2,2,4,112,128]{4,3,2,1,0:T(8,128)(2,1)S(1)}, u32[]{:S(2)}, u32[]{:S(2)}) %collective-permute-start.16) | collective-permute-done | bytes 458784 | tf_op jit(solution)/shard_map/ppermute | solution.py:36
  56.8 1.8 %shard_map.42.start = f32[1024,768]{1,0:T(8,128)S(1)} custom-call(s32[4]{0:T(128)S(1)} %pad_add_fusion.place, bf16[2,2,4,112,128]{4,3,2,1,0:T(8,128)(2,1)S(1)} %collective-permute-done.14.one, bf16[2,2,4,112,128]{4,3,2,1,0:T(8,128)(2,1)S(1)} %collective-permute-done.16.three, ...), custom_call_target="tpu_custom_call", output_to_operand_aliasing={{}: (4, {})} | custom-call | tf_op jit(solution)/shard_map/pallas_call | solution.py:193
  59.3 14.1 %collective-permute-start.18 = (bf16[512,384]{1,0:T(8,128)(2,1)S(1)}, bf16[512,384]{1,0:T(8,128)(2,1)S(1)}, u32[]{:S(2)}, u32[]{:S(2)}) collective-permute-start(bf16[512,384]{1,0:T(8,128)(2,1)S(1)} %get-tuple-element.36), channel_id=1, source_target_pairs={{16,0},{0,16},{17,1},{1,17},{18,2},{2,18},{19,3},{3,19},{20,4},{4,... | collective-permute-start | bytes 1179656 | tf_op jit(solution)/shard_map/ppermute | solution.py:23
  73.4 1.5 %shard_map.43 = (bf16[512,384]{1,0:T(8,128)(2,1)S(1)}, bf16[512,384]{1,0:T(8,128)(2,1)S(1)}) custom-call(s32[4]{0:T(128)S(1)} %pad_add_fusion.place, bf16[2,2,4,112,128]{4,3,2,1,0:T(8,128)(2,1)S(1)} %collective-permute-done.12.first, bf16[2,2,4,112,128]{4,3,2,1,0:T(8,128)(2,1)S(1)} %collective-permute-done.15.last, bf16[4,448,768]{2,1,0:T(8,128)(2,1)S(1)} %shard_map.39.both, ...), custom_call_target="tpu_custom_call" | custom-call | tf_op jit(solution)/shard_map/pallas_call | solution.py:193
  75.3 1.6 %shard_map.45.given = bf16[2048,384]{1,0:T(8,128)(2,1)} custom-call(s32[4]{0:T(128)S(1)} %pad_add_fusion.place, bf16[512,384]{1,0:T(8,128)(2,1)S(1)} %get-tuple-element.34.mine1, bf16[512,384]{1,0:T(8,128)(2,1)S(1)} %get-tuple-element.35.mine2, bf16[512,384]{1,0:T(8,128)(2,1)S(1)} %collective-permute-done.18.theirs1), custom_call_target="tpu_custom_call" | custom-call | tf_op jit(solution)/shard_map/pallas_call | solution.py:193
  76.9 1.3 %shard_map.46 = bf16[2048,384]{1,0:T(8,128)(2,1)} custom-call(s32[4]{0:T(128)S(1)} %pad_add_fusion.place, bf16[512,384]{1,0:T(8,128)(2,1)S(1)} %collective-permute-done.17.theirs2, bf16[2048,384]{1,0:T(8,128)(2,1)} %shard_map.45.given), custom_call_target="tpu_custom_call", output_to_operand_aliasing={{}: (2, {})} | custom-call | tf_op jit(solution)/shard_map/pallas_call | solution.py:193
  (27 shorter events, 5.2 us)
Async XLA Ops:
  0.0 21.5 %collective-permute-start.5 = (bf16[1792,384]{1,0:T(8,128)(2,1)}, bf16[1792,384]{1,0:T(8,128)(2,1)S(1)}, u32[]{:S(2)}, u32[]{:S(2)}) collective-permute-start(bf16[1792,384]{1,0:T(8,128)(2,1)} %own.1), channel_id=1, source_target_pairs={{16,0},{0,16},{17,1},{1,17},{18,2},{2,18},{19,3},{3,19},{20,4},{4,... | collective-permute-start | bytes 4128776 | tf_op jit(solution)/shard_map/ppermute | solution.py:23
  3.3 1.0 %copy-start.1 = (bf16[112,2048]{1,0:T(8,128)(2,1)S(1)}, bf16[112,2048]{1,0:T(8,128)(2,1)}, u32[]{:S(2)}) copy-start(bf16[112,2048]{1,0:T(8,128)(2,1)} %panel.1) | copy-start | bytes 1376260
  4.3 0.7 copy-start.2
  6.1 1.9 %collective-permute-start = (f32[8,112,128]{2,1,0:T(8,128)S(1)}, f32[8,112,128]{2,1,0:T(8,128)S(1)}, u32[]{:S(2)}, u32[]{:S(2)}) collective-permute-start(f32[8,112,128]{2,1,0:T(8,128)S(1)} %get-tuple-element.22), channel_id=1, source_target_pairs={{16,0},{0,16},{17,1},{1,17},{18,2},{2,18},{19,3},{3,19},{20,4},{4,... | collective-permute-start | bytes 1376264 | tf_op jit(solution)/shard_map/ppermute | solution.py:23
  8.6 3.3 %collective-permute-start.1 = (bf16[2,112,128]{2,1,0:T(8,128)(2,1)S(1)}, bf16[2,112,128]{2,1,0:T(8,128)(2,1)S(1)}, u32[]{:S(2)}, u32[]{:S(2)}) collective-permute-start(bf16[2,112,128]{2,1,0:T(8,128)(2,1)S(1)} %get-tuple-element.24), channel_id=1, source_target_pairs={{64,0},{0,64},{192,128},{128,192},{65,1},{1,65},{193,129},{129,193... | collective-permute-start | bytes 172040 | tf_op jit(solution)/shard_map/ppermute | solution.py:27
  8.7 4.3 %collective-permute-start.2 = (bf16[2,112,128]{2,1,0:T(8,128)(2,1)S(1)}, bf16[2,112,128]{2,1,0:T(8,128)(2,1)S(1)}, u32[]{:S(2)}, u32[]{:S(2)}) collective-permute-start(bf16[2,112,128]{2,1,0:T(8,128)(2,1)S(1)} %get-tuple-element.25), channel_id=1, source_target_pairs={{192,0},{128,64},{64,128},{0,192},{193,1},{129,65},{65,129},{1,193... | collective-permute-start | bytes 172040 | tf_op jit(solution)/shard_map/ppermute | solution.py:27
  10.0 4.5 %collective-permute-start.3 = (bf16[2,112,128]{2,1,0:T(8,128)(2,1)S(1)}, bf16[2,112,128]{2,1,0:T(8,128)(2,1)S(1)}, u32[]{:S(2)}, u32[]{:S(2)}) collective-permute-start(bf16[2,112,128]{2,1,0:T(8,128)(2,1)S(1)} %get-tuple-element.26), channel_id=1, source_target_pairs={{128,0},{192,64},{0,128},{64,192},{129,1},{193,65},{1,129},{65,193... | collective-permute-start | bytes 172040 | tf_op jit(solution)/shard_map/ppermute | solution.py:27
  14.5 9.1 %collective-permute-start.4 = (bf16[2,112,128]{2,1,0:T(8,128)(2,1)S(1)}, bf16[2,112,128]{2,1,0:T(8,128)(2,1)S(1)}, u32[]{:S(2)}, u32[]{:S(2)}) collective-permute-start(bf16[2,112,128]{2,1,0:T(8,128)(2,1)S(1)} %fusion), channel_id=1, source_target_pairs={{32,0},{0,32},{33,1},{1,33},{34,2},{2,34},{35,3},{3,35},{36,4},{4,... | collective-permute-start | bytes 172040 | tf_op jit(solution)/shard_map/ppermute | solution.py:27
  21.5 1.3 %copy-start = (bf16[1792,384]{1,0:T(8,128)(2,1)S(1)}, bf16[1792,384]{1,0:T(8,128)(2,1)}, u32[]{:S(2)}) copy-start(bf16[1792,384]{1,0:T(8,128)(2,1)} %own.1) | copy-start | bytes 4128772
  23.7 4.9 %collective-permute-start.8 = (bf16[2,112,128]{2,1,0:T(8,128)(2,1)S(1)}, bf16[2,112,128]{2,1,0:T(8,128)(2,1)S(1)}, u32[]{:S(2)}, u32[]{:S(2)}) collective-permute-start(bf16[2,112,128]{2,1,0:T(8,128)(2,1)S(1)} %add_convert_fusion), channel_id=1, source_target_pairs={{12,0},{8,4},{4,8},{0,12},{13,1},{9,5},{5,9},{1,13},{14,2},{10,6},... | collective-permute-start | bytes 172040 | tf_op jit(solution)/shard_map/ppermute | solution.py:27
  26.1 3.1 %collective-permute-start.6 = (bf16[2,112,128]{2,1,0:T(8,128)(2,1)S(1)}, bf16[2,112,128]{2,1,0:T(8,128)(2,1)S(1)}, u32[]{:S(2)}, u32[]{:S(2)}) collective-permute-start(bf16[2,112,128]{2,1,0:T(8,128)(2,1)S(1)} %add_convert_fusion), channel_id=1, source_target_pairs={{4,0},{0,4},{12,8},{8,12},{5,1},{1,5},{13,9},{9,13},{6,2},{2,6},{1... | collective-permute-start | bytes 172040 | tf_op jit(solution)/shard_map/ppermute | solution.py:27
  26.1 4.2 %collective-permute-start.7 = (bf16[2,112,128]{2,1,0:T(8,128)(2,1)S(1)}, bf16[2,112,128]{2,1,0:T(8,128)(2,1)S(1)}, u32[]{:S(2)}, u32[]{:S(2)}) collective-permute-start(bf16[2,112,128]{2,1,0:T(8,128)(2,1)S(1)} %add_convert_fusion), channel_id=1, source_target_pairs={{8,0},{12,4},{0,8},{4,12},{9,1},{13,5},{1,9},{5,13},{10,2},{14,6},... | collective-permute-start | bytes 172040 | tf_op jit(solution)/shard_map/ppermute | solution.py:27
  30.3 5.0 %collective-permute-start.9 = (bf16[2,4,112,128]{3,2,1,0:T(8,128)(2,1)S(1)}, bf16[2,4,112,128]{3,2,1,0:T(8,128)(2,1)S(1)}, u32[]{:S(2)}, u32[]{:S(2)}) collective-permute-start(bf16[2,4,112,128]{3,2,1,0:T(8,128)(2,1)S(1)} %get-tuple-element.38), channel_id=1, source_target_pairs={{64,0},{65,1},{66,2},{67,3},{68,4},{69,5},{70,6},{71,7},{72,8},{73... | collective-permute-start | bytes 688136 | tf_op jit(solution)/shard_map/ppermute | solution.py:36
  35.3 8.7 %collective-permute-start.13 = (bf16[2,2,4,112,128]{4,3,2,1,0:T(8,128)(2,1)S(1)}, bf16[2,2,4,112,128]{4,3,2,1,0:T(8,128)(2,1)S(1)}, u32[]{:S(2)}, u32[]{:S(2)}) collective-permute-start(bf16[2,2,4,112,128]{4,3,2,1,0:T(8,128)(2,1)S(1)} %pad_maximum_fusion.first), channel_id=1, source_target_pairs={{192,0},{193,1},{194,2},{195,3},{196,4},{197,5},{198,6},{199,7},{2... | collective-permute-start | bytes 1376264 | tf_op jit(solution)/shard_map/ppermute | solution.py:36
  38.2 7.6 %collective-permute-start.10 = (bf16[2,2,4,112,128]{4,3,2,1,0:T(8,128)(2,1)S(1)}, bf16[2,2,4,112,128]{4,3,2,1,0:T(8,128)(2,1)S(1)}, u32[]{:S(2)}, u32[]{:S(2)}) collective-permute-start(bf16[2,2,4,112,128]{4,3,2,1,0:T(8,128)(2,1)S(1)} %pad_maximum_fusion.first), channel_id=1, source_target_pairs={{1,0},{0,1},{3,2},{2,3},{5,4},{4,5},{7,6},{6,7},{9,8},{8,9},{11,10... | collective-permute-start | bytes 1376264 | tf_op jit(solution)/shard_map/ppermute | solution.py:36
  38.5 11.0 %collective-permute-start.11 = (bf16[2,2,4,112,128]{4,3,2,1,0:T(8,128)(2,1)S(1)}, bf16[2,2,4,112,128]{4,3,2,1,0:T(8,128)(2,1)S(1)}, u32[]{:S(2)}, u32[]{:S(2)}) collective-permute-start(bf16[2,2,4,112,128]{4,3,2,1,0:T(8,128)(2,1)S(1)} %pad_maximum_fusion.first), channel_id=1, source_target_pairs={{3,0},{2,1},{1,2},{0,3},{7,4},{6,5},{5,6},{4,7},{11,8},{10,9},{9,1... | collective-permute-start | bytes 1376264 | tf_op jit(solution)/shard_map/ppermute | solution.py:36
  44.0 7.6 %collective-permute-start.14 = (bf16[2,2,4,112,128]{4,3,2,1,0:T(8,128)(2,1)S(1)}, bf16[2,2,4,112,128]{4,3,2,1,0:T(8,128)(2,1)S(1)}, u32[]{:S(2)}, u32[]{:S(2)}) collective-permute-start(bf16[2,2,4,112,128]{4,3,2,1,0:T(8,128)(2,1)S(1)} %collective-permute-done.13.last), channel_id=1, source_target_pairs={{1,0},{0,1},{3,2},{2,3},{5,4},{4,5},{7,6},{6,7},{9,8},{8,9},{11,10... | collective-permute-start | bytes 1376264 | tf_op jit(solution)/shard_map/ppermute | solution.py:36
  44.3 12.5 %collective-permute-start.16 = (bf16[2,2,4,112,128]{4,3,2,1,0:T(8,128)(2,1)S(1)}, bf16[2,2,4,112,128]{4,3,2,1,0:T(8,128)(2,1)S(1)}, u32[]{:S(2)}, u32[]{:S(2)}) collective-permute-start(bf16[2,2,4,112,128]{4,3,2,1,0:T(8,128)(2,1)S(1)} %collective-permute-done.13.last), channel_id=1, source_target_pairs={{3,0},{2,1},{1,2},{0,3},{7,4},{6,5},{5,6},{4,7},{11,8},{10,9},{9,1... | collective-permute-start | bytes 1376264 | tf_op jit(solution)/shard_map/ppermute | solution.py:36
  49.5 9.1 %collective-permute-start.12 = (bf16[2,2,4,112,128]{4,3,2,1,0:T(8,128)(2,1)S(1)}, bf16[2,2,4,112,128]{4,3,2,1,0:T(8,128)(2,1)S(1)}, u32[]{:S(2)}, u32[]{:S(2)}) collective-permute-start(bf16[2,2,4,112,128]{4,3,2,1,0:T(8,128)(2,1)S(1)} %collective-permute-done.11.three), channel_id=1, source_target_pairs={{1,0},{0,1},{3,2},{2,3},{5,4},{4,5},{7,6},{6,7},{9,8},{8,9},{11,10... | collective-permute-start | bytes 1376264 | tf_op jit(solution)/shard_map/ppermute | solution.py:36
  51.7 21.7 %collective-permute-start.15 = (bf16[2,2,4,112,128]{4,3,2,1,0:T(8,128)(2,1)S(1)}, bf16[2,2,4,112,128]{4,3,2,1,0:T(8,128)(2,1)S(1)}, u32[]{:S(2)}, u32[]{:S(2)}) collective-permute-start(bf16[2,2,4,112,128]{4,3,2,1,0:T(8,128)(2,1)S(1)} %collective-permute-done.14.one), channel_id=1, source_target_pairs={{3,0},{2,1},{1,2},{0,3},{7,4},{6,5},{5,6},{4,7},{11,8},{10,9},{9,1... | collective-permute-start | bytes 1376264 | tf_op jit(solution)/shard_map/ppermute | solution.py:36
  59.3 16.0 %collective-permute-start.18 = (bf16[512,384]{1,0:T(8,128)(2,1)S(1)}, bf16[512,384]{1,0:T(8,128)(2,1)S(1)}, u32[]{:S(2)}, u32[]{:S(2)}) collective-permute-start(bf16[512,384]{1,0:T(8,128)(2,1)S(1)} %get-tuple-element.36), channel_id=1, source_target_pairs={{16,0},{0,16},{17,1},{1,17},{18,2},{2,18},{19,3},{3,19},{20,4},{4,... | collective-permute-start | bytes 1179656 | tf_op jit(solution)/shard_map/ppermute | solution.py:23
  74.9 2.0 %collective-permute-start.17 = (bf16[512,384]{1,0:T(8,128)(2,1)S(1)}, bf16[512,384]{1,0:T(8,128)(2,1)S(1)}, u32[]{:S(2)}, u32[]{:S(2)}) collective-permute-start(bf16[512,384]{1,0:T(8,128)(2,1)S(1)} %get-tuple-element.33), channel_id=1, source_target_pairs={{16,0},{0,16},{17,1},{1,17},{18,2},{2,18},{19,3},{3,19},{20,4},{4,... | collective-permute-start | bytes 1179656 | tf_op jit(solution)/shard_map/ppermute | solution.py:23

commit v8 on v7

--- a/solution.py
+++ b/solution.py
@@ -229,12 +229,12 @@
 
     first = jnp.stack([own, turn(own, 0, 1)])
     last = turn(first, 0, 3)
-    one1, three1 = turn(first, 1, 1), turn(first, 1, 3)
     total = jax.ShapeDtypeStruct((1024, 768), F32)
     total_one = call(product_one, total, (place, first, both))
-    last, total_one = lax.optimization_barrier((last, total_one))
-    one2, three2 = turn(last, 1, 1), turn(last, 1, 3)
-    one1, three1 = lax.optimization_barrier((one1, three1))
+    first, total_one = lax.optimization_barrier((first, total_one))
+    one1 = turn(first, 1, 1)
+    first, last, one1 = lax.optimization_barrier((first, last, one1))
+    three1, one2, three2 = turn(first, 1, 3), turn(last, 1, 1), turn(last, 1, 3)
     far1, far2 = turn(three1, 1, 1), turn(one2, 1, 3)
     total_two = call(
         product_two,

time: 78.6 us -> 78.7 us (level)
  waiting for transfers between devices: 21.4 us -> 26.2 us
  starting transfers between devices: 40.7 us -> 36 us
    ppermute x8, waiting for transfers between devices: 14.1 us -> 18.9 us  [turn(): return lax.ppermute(block, ROW + COL, pairs)]
    ppermute x4, starting transfers between devices: 17.9 us -> 13.3 us  [fetch(): lax.ppermute(block, axis, [((i + ahead) % size, i) for i in range(size)])]
  transfers between devices with their start and end apart: 19 -> 19, of which waited for: 12 -> 11; matrix products, arithmetic and copies ran while one was open for 0% -> 0% of each run, Pallas kernels for 14% -> 14%
where the time goes in v8:
time: 78.7 us; the launch traced here: 78.5 us
  starting transfers between devices  36 us (46%)
  waiting for transfers between devices  26.2 us (33%)
  Pallas kernels  12.6 us (16%)
  local copies, waits for them, and re-layouts  3.11 us (4%)
    ppermute x8, waiting for transfers between devices, turn(): return lax.ppermute(block, ROW + COL, pairs)  18.9 us
    ppermute x7, starting transfers between devices, swap(): return lax.ppermute(block, axis, [(i ^ bits, i) for i in range(size)])  14 us
    ppermute x4, starting transfers between devices, fetch(): lax.ppermute(block, axis, [((i + ahead) % size, i) for i in range(size)])  13.3 us
    pallas_call x10, Pallas kernels, call(): pl.pallas_call(kernel, out_shape=out_shape, in_specs=specs or [SMEM] + [V...  12.6 us
    ppermute x8, starting transfers between devices, turn(): return lax.ppermute(block, ROW + COL, pairs)  8.73 us
    ppermute x7, waiting for transfers between devices, swap(): return lax.ppermute(block, axis, [(i ^ bits, i) for i in range(size)])  5.51 us
    unnamed x6, local copies, waits for them, and re-layouts  3.11 us
    ppermute x4, waiting for transfers between devices, fetch(): lax.ppermute(block, axis, [((i + ahead) % size, i) for i in range(size)])  1.81 us
  transfers between devices with their start and end apart: 19, of which 11 were waited for; matrix products, arithmetic and copies ran while one was open for 0% of the time, Pallas kernels for 14%

profile of v8, /device:TPU:1, one launch (start us, length us, event | category | flops | bytes accessed | tf_op | source)
XLA Modules:
  0.0 78.5 jit_solution(17565915287018917091)
XLA Ops:
  0.0 3.2 %collective-permute-start.5 = (bf16[1792,384]{1,0:T(8,128)(2,1)}, bf16[1792,384]{1,0:T(8,128)(2,1)S(1)}, u32[]{:S(2)}, u32[]{:S(2)}) collective-permute-start(bf16[1792,384]{1,0:T(8,128)(2,1)} %own.1), channel_id=1, source_target_pairs={{16,0},{0,16},{17,1},{1,17},{18,2},{2,18},{19,3},{3,19},{20,4},{4,... | collective-permute-start | bytes 4128776 | tf_op jit(solution)/shard_map/ppermute | solution.py:23
  3.3 1.0 %copy-done.1 = bf16[112,2048]{1,0:T(8,128)(2,1)S(1)} copy-done((bf16[112,2048]{1,0:T(8,128)(2,1)S(1)}, bf16[112,2048]{1,0:T(8,128)(2,1)}, u32[]{:S(2)}) %copy-start.1) | copy-done | bytes 458776
  5.1 1.0 %shard_map.37 = (f32[8,112,128]{2,1,0:T(8,128)S(1)}, f32[8,112,128]{2,1,0:T(8,128)S(1)}) custom-call(s32[4]{0:T(128)S(1)} %pad_add_fusion.place, bf16[112,112]{1,0:T(8,128)(2,1)S(1)} %copy-done.2, bf16[112,2048]{1,0:T(8,128)(2,1)S(1)} %copy-done.1), custom_call_target="tpu_custom_call" | custom-call | tf_op jit(solution)/shard_map/pallas_call | solution.py:193
  6.2 1.8 %collective-permute-done.received = f32[8,112,128]{2,1,0:T(8,128)S(1)} collective-permute-done((f32[8,112,128]{2,1,0:T(8,128)S(1)}, f32[8,112,128]{2,1,0:T(8,128)S(1)}, u32[]{:S(2)}, u32[]{:S(2)}) %collective-permute-start) | collective-permute-done | bytes 458784 | tf_op jit(solution)/shard_map/ppermute | solution.py:23
  8.7 1.3 %collective-permute-start.2 = (bf16[2,112,128]{2,1,0:T(8,128)(2,1)S(1)}, bf16[2,112,128]{2,1,0:T(8,128)(2,1)S(1)}, u32[]{:S(2)}, u32[]{:S(2)}) collective-permute-start(bf16[2,112,128]{2,1,0:T(8,128)(2,1)S(1)} %get-tuple-element.26), channel_id=1, source_target_pairs={{192,0},{128,64},{64,128},{0,192},{193,1},{129,65},{65,129},{1,193... | collective-permute-start | bytes 172040 | tf_op jit(solution)/shard_map/ppermute | solution.py:27
  10.0 2.0 %collective-permute-start.3 = (bf16[2,112,128]{2,1,0:T(8,128)(2,1)S(1)}, bf16[2,112,128]{2,1,0:T(8,128)(2,1)S(1)}, u32[]{:S(2)}, u32[]{:S(2)}) collective-permute-start(bf16[2,112,128]{2,1,0:T(8,128)(2,1)S(1)} %get-tuple-element.27), channel_id=1, source_target_pairs={{128,0},{192,64},{0,128},{64,192},{129,1},{193,65},{1,129},{65,193... | collective-permute-start | bytes 172040 | tf_op jit(solution)/shard_map/ppermute | solution.py:27
  11.9 1.1 %collective-permute-done.2 = bf16[2,112,128]{2,1,0:T(8,128)(2,1)S(1)} collective-permute-done((bf16[2,112,128]{2,1,0:T(8,128)(2,1)S(1)}, bf16[2,112,128]{2,1,0:T(8,128)(2,1)S(1)}, u32[]{:S(2)}, u32[]{:S(2)}) %collective-permute-start.2) | collective-permute-done | bytes 57376 | tf_op jit(solution)/shard_map/ppermute | solution.py:27
  13.0 1.5 %collective-permute-done.3 = bf16[2,112,128]{2,1,0:T(8,128)(2,1)S(1)} collective-permute-done((bf16[2,112,128]{2,1,0:T(8,128)(2,1)S(1)}, bf16[2,112,128]{2,1,0:T(8,128)(2,1)S(1)}, u32[]{:S(2)}, u32[]{:S(2)}) %collective-permute-start.3) | collective-permute-done | bytes 57376 | tf_op jit(solution)/shard_map/ppermute | solution.py:27
  14.5 7.0 %collective-permute-start.4 = (bf16[2,112,128]{2,1,0:T(8,128)(2,1)S(1)}, bf16[2,112,128]{2,1,0:T(8,128)(2,1)S(1)}, u32[]{:S(2)}, u32[]{:S(2)}) collective-permute-start(bf16[2,112,128]{2,1,0:T(8,128)(2,1)S(1)} %fusion), channel_id=1, source_target_pairs={{32,0},{0,32},{33,1},{1,33},{34,2},{2,34},{35,3},{3,35},{36,4},{4,... | collective-permute-start | bytes 172040 | tf_op jit(solution)/shard_map/ppermute | solution.py:27
  21.5 1.3 %copy-done = bf16[1792,384]{1,0:T(8,128)(2,1)S(1)} copy-done((bf16[1792,384]{1,0:T(8,128)(2,1)S(1)}, bf16[1792,384]{1,0:T(8,128)(2,1)}, u32[]{:S(2)}) %copy-start) | copy-done | bytes 1376280
  23.7 2.4 %collective-permute-start.8 = (bf16[2,112,128]{2,1,0:T(8,128)(2,1)S(1)}, bf16[2,112,128]{2,1,0:T(8,128)(2,1)S(1)}, u32[]{:S(2)}, u32[]{:S(2)}) collective-permute-start(bf16[2,112,128]{2,1,0:T(8,128)(2,1)S(1)} %add_convert_fusion), channel_id=1, source_target_pairs={{12,0},{8,4},{4,8},{0,12},{13,1},{9,5},{5,9},{1,13},{14,2},{10,6},... | collective-permute-start | bytes 172040 | tf_op jit(solution)/shard_map/ppermute | solution.py:27
  26.1 1.2 %collective-permute-start.6 = (bf16[2,112,128]{2,1,0:T(8,128)(2,1)S(1)}, bf16[2,112,128]{2,1,0:T(8,128)(2,1)S(1)}, u32[]{:S(2)}, u32[]{:S(2)}) collective-permute-start(bf16[2,112,128]{2,1,0:T(8,128)(2,1)S(1)} %add_convert_fusion), channel_id=1, source_target_pairs={{4,0},{0,4},{12,8},{8,12},{5,1},{1,5},{13,9},{9,13},{6,2},{2,6},{1... | collective-permute-start | bytes 172040 | tf_op jit(solution)/shard_map/ppermute | solution.py:27
  27.4 1.3 %collective-permute-done.8 = bf16[2,112,128]{2,1,0:T(8,128)(2,1)S(1)} collective-permute-done((bf16[2,112,128]{2,1,0:T(8,128)(2,1)S(1)}, bf16[2,112,128]{2,1,0:T(8,128)(2,1)S(1)}, u32[]{:S(2)}, u32[]{:S(2)}) %collective-permute-start.8) | collective-permute-done | bytes 57376 | tf_op jit(solution)/shard_map/ppermute | solution.py:27
  28.6 1.7 %collective-permute-done.7 = bf16[2,112,128]{2,1,0:T(8,128)(2,1)S(1)} collective-permute-done((bf16[2,112,128]{2,1,0:T(8,128)(2,1)S(1)}, bf16[2,112,128]{2,1,0:T(8,128)(2,1)S(1)}, u32[]{:S(2)}, u32[]{:S(2)}) %collective-permute-start.7) | collective-permute-done | bytes 57376 | tf_op jit(solution)/shard_map/ppermute | solution.py:27
  30.3 1.4 %collective-permute-start.9 = (bf16[2,4,112,128]{3,2,1,0:T(8,128)(2,1)S(1)}, bf16[2,4,112,128]{3,2,1,0:T(8,128)(2,1)S(1)}, u32[]{:S(2)}, u32[]{:S(2)}) collective-permute-start(bf16[2,4,112,128]{3,2,1,0:T(8,128)(2,1)S(1)} %get-tuple-element.40), channel_id=1, source_target_pairs={{64,0},{65,1},{66,2},{67,3},{68,4},{69,5},{70,6},{71,7},{72,8},{73... | collective-permute-start | bytes 688136 | tf_op jit(solution)/shard_map/ppermute | solution.py:36
  31.7 3.6 %collective-permute-done.9 = bf16[2,4,112,128]{3,2,1,0:T(8,128)(2,1)S(1)} collective-permute-done((bf16[2,4,112,128]{3,2,1,0:T(8,128)(2,1)S(1)}, bf16[2,4,112,128]{3,2,1,0:T(8,128)(2,1)S(1)}, u32[]{:S(2)}, u32[]{:S(2)}) %collective-permute-start.9) | collective-permute-done | bytes 229408 | tf_op jit(solution)/shard_map/ppermute | solution.py:36
  35.4 2.8 %collective-permute-start.10 = (bf16[2,2,4,112,128]{4,3,2,1,0:T(8,128)(2,1)S(1)}, bf16[2,2,4,112,128]{4,3,2,1,0:T(8,128)(2,1)S(1)}, u32[]{:S(2)}, u32[]{:S(2)}) collective-permute-start(bf16[2,2,4,112,128]{4,3,2,1,0:T(8,128)(2,1)S(1)} %pad_maximum_fusion.first), channel_id=1, source_target_pairs={{192,0},{193,1},{194,2},{195,3},{196,4},{197,5},{198,6},{199,7},{2... | collective-permute-start | bytes 1376264 | tf_op jit(solution)/shard_map/ppermute | solution.py:36
  38.2 1.2 %shard_map.40.start = f32[1024,768]{1,0:T(8,128)S(1)} custom-call(s32[4]{0:T(128)S(1)} %pad_add_fusion.place, bf16[2,2,4,112,128]{4,3,2,1,0:T(8,128)(2,1)S(1)} %pad_maximum_fusion.first, bf16[4,448,768]{2,1,0:T(8,128)(2,1)S(1)} %shard_map.39.both), custom_call_target="tpu_custom_call" | custom-call | tf_op jit(solution)/shard_map/pallas_call | solution.py:193
  39.7 4.3 %collective-permute-done.10.last = bf16[2,2,4,112,128]{4,3,2,1,0:T(8,128)(2,1)S(1)} collective-permute-done((bf16[2,2,4,112,128]{4,3,2,1,0:T(8,128)(2,1)S(1)}, bf16[2,2,4,112,128]{4,3,2,1,0:T(8,128)(2,1)S(1)}, u32[]{:S(2)}, u32[]{:S(2)}) %collective-permute-start.10) | collective-permute-done | bytes 458784 | tf_op jit(solution)/shard_map/ppermute | solution.py:36
  44.0 3.0 %collective-permute-done.11.one = bf16[2,2,4,112,128]{4,3,2,1,0:T(8,128)(2,1)S(1)} collective-permute-done((bf16[2,2,4,112,128]{4,3,2,1,0:T(8,128)(2,1)S(1)}, bf16[2,2,4,112,128]{4,3,2,1,0:T(8,128)(2,1)S(1)}, u32[]{:S(2)}, u32[]{:S(2)}) %collective-permute-start.11) | collective-permute-done | bytes 458784 | tf_op jit(solution)/shard_map/ppermute | solution.py:36
  47.0 1.1 %collective-permute-start.12 = (bf16[2,2,4,112,128]{4,3,2,1,0:T(8,128)(2,1)S(1)}, bf16[2,2,4,112,128]{4,3,2,1,0:T(8,128)(2,1)S(1)}, u32[]{:S(2)}, u32[]{:S(2)}) collective-permute-start(bf16[2,2,4,112,128]{4,3,2,1,0:T(8,128)(2,1)S(1)} %pad_maximum_fusion.first), channel_id=1, source_target_pairs={{3,0},{2,1},{1,2},{0,3},{7,4},{6,5},{5,6},{4,7},{11,8},{10,9},{9,1... | collective-permute-start | bytes 1376264 | tf_op jit(solution)/shard_map/ppermute | solution.py:36
  48.1 1.6 %collective-permute-start.16 = (bf16[2,2,4,112,128]{4,3,2,1,0:T(8,128)(2,1)S(1)}, bf16[2,2,4,112,128]{4,3,2,1,0:T(8,128)(2,1)S(1)}, u32[]{:S(2)}, u32[]{:S(2)}) collective-permute-start(bf16[2,2,4,112,128]{4,3,2,1,0:T(8,128)(2,1)S(1)} %collective-permute-done.10.last), channel_id=1, source_target_pairs={{3,0},{2,1},{1,2},{0,3},{7,4},{6,5},{5,6},{4,7},{11,8},{10,9},{9,1... | collective-permute-start | bytes 1376264 | tf_op jit(solution)/shard_map/ppermute | solution.py:36
  49.7 5.9 %collective-permute-done.12.three = bf16[2,2,4,112,128]{4,3,2,1,0:T(8,128)(2,1)S(1)} collective-permute-done((bf16[2,2,4,112,128]{4,3,2,1,0:T(8,128)(2,1)S(1)}, bf16[2,2,4,112,128]{4,3,2,1,0:T(8,128)(2,1)S(1)}, u32[]{:S(2)}, u32[]{:S(2)}) %collective-permute-start.12) | collective-permute-done | bytes 458784 | tf_op jit(solution)/shard_map/ppermute | solution.py:36
  55.6 1.5 %collective-permute-start.15 = (bf16[2,2,4,112,128]{4,3,2,1,0:T(8,128)(2,1)S(1)}, bf16[2,2,4,112,128]{4,3,2,1,0:T(8,128)(2,1)S(1)}, u32[]{:S(2)}, u32[]{:S(2)}) collective-permute-start(bf16[2,2,4,112,128]{4,3,2,1,0:T(8,128)(2,1)S(1)} %collective-permute-done.14.one), channel_id=1, source_target_pairs={{3,0},{2,1},{1,2},{0,3},{7,4},{6,5},{5,6},{4,7},{11,8},{10,9},{9,1... | collective-permute-start | bytes 1376264 | tf_op jit(solution)/shard_map/ppermute | solution.py:36
  57.1 2.3 %shard_map.41.start = f32[1024,768]{1,0:T(8,128)S(1)} custom-call(s32[4]{0:T(128)S(1)} %pad_add_fusion.place, bf16[2,2,4,112,128]{4,3,2,1,0:T(8,128)(2,1)S(1)} %collective-permute-done.10.last, bf16[2,2,4,112,128]{4,3,2,1,0:T(8,128)(2,1)S(1)} %collective-permute-done.11.one, ...), custom_call_target="tpu_custom_call", output_to_operand_aliasing={{}: (5, {})} | custom-call | tf_op jit(solution)/shard_map/pallas_call | solution.py:193
  59.3 1.4 %collective-permute-done.16.three = bf16[2,2,4,112,128]{4,3,2,1,0:T(8,128)(2,1)S(1)} collective-permute-done((bf16[2,2,4,112,128]{4,3,2,1,0:T(8,128)(2,1)S(1)}, bf16[2,2,4,112,128]{4,3,2,1,0:T(8,128)(2,1)S(1)}, u32[]{:S(2)}, u32[]{:S(2)}) %collective-permute-start.16) | collective-permute-done | bytes 458784 | tf_op jit(solution)/shard_map/ppermute | solution.py:36
  60.8 1.7 %shard_map.42.start = f32[1024,768]{1,0:T(8,128)S(1)} custom-call(s32[4]{0:T(128)S(1)} %pad_add_fusion.place, bf16[2,2,4,112,128]{4,3,2,1,0:T(8,128)(2,1)S(1)} %collective-permute-done.14.one, bf16[2,2,4,112,128]{4,3,2,1,0:T(8,128)(2,1)S(1)} %collective-permute-done.16.three, ...), custom_call_target="tpu_custom_call", output_to_operand_aliasing={{}: (4, {})} | custom-call | tf_op jit(solution)/shard_map/pallas_call | solution.py:193
  63.9 8.3 %collective-permute-start.18 = (bf16[512,384]{1,0:T(8,128)(2,1)S(1)}, bf16[512,384]{1,0:T(8,128)(2,1)S(1)}, u32[]{:S(2)}, u32[]{:S(2)}) collective-permute-start(bf16[512,384]{1,0:T(8,128)(2,1)S(1)} %get-tuple-element.38), channel_id=1, source_target_pairs={{16,0},{0,16},{17,1},{1,17},{18,2},{2,18},{19,3},{3,19},{20,4},{4,... | collective-permute-start | bytes 1179656 | tf_op jit(solution)/shard_map/ppermute | solution.py:23
  72.1 1.5 %shard_map.43 = (bf16[512,384]{1,0:T(8,128)(2,1)S(1)}, bf16[512,384]{1,0:T(8,128)(2,1)S(1)}) custom-call(s32[4]{0:T(128)S(1)} %pad_add_fusion.place, bf16[2,2,4,112,128]{4,3,2,1,0:T(8,128)(2,1)S(1)} %collective-permute-done.13.first, bf16[2,2,4,112,128]{4,3,2,1,0:T(8,128)(2,1)S(1)} %collective-permute-done.15.last, bf16[4,448,768]{2,1,0:T(8,128)(2,1)S(1)} %shard_map.39.both, ...), custom_call_target="tpu_custom_call" | custom-call | tf_op jit(solution)/shard_map/pallas_call | solution.py:193
  73.6 1.7 %collective-permute-start.17 = (bf16[512,384]{1,0:T(8,128)(2,1)S(1)}, bf16[512,384]{1,0:T(8,128)(2,1)S(1)}, u32[]{:S(2)}, u32[]{:S(2)}) collective-permute-start(bf16[512,384]{1,0:T(8,128)(2,1)S(1)} %get-tuple-element.35), channel_id=1, source_target_pairs={{16,0},{0,16},{17,1},{1,17},{18,2},{2,18},{19,3},{3,19},{20,4},{4,... | collective-permute-start | bytes 1179656 | tf_op jit(solution)/shard_map/ppermute | solution.py:23
  75.4 1.6 %shard_map.45.given = bf16[2048,384]{1,0:T(8,128)(2,1)} custom-call(s32[4]{0:T(128)S(1)} %pad_add_fusion.place, bf16[512,384]{1,0:T(8,128)(2,1)S(1)} %get-tuple-element.36.mine1, bf16[512,384]{1,0:T(8,128)(2,1)S(1)} %get-tuple-element.37.mine2, bf16[512,384]{1,0:T(8,128)(2,1)S(1)} %collective-permute-done.18.theirs1), custom_call_target="tpu_custom_call" | custom-call | tf_op jit(solution)/shard_map/pallas_call | solution.py:193
  77.0 1.3 %shard_map.46 = bf16[2048,384]{1,0:T(8,128)(2,1)} custom-call(s32[4]{0:T(128)S(1)} %pad_add_fusion.place, bf16[512,384]{1,0:T(8,128)(2,1)S(1)} %collective-permute-done.17.theirs2, bf16[2048,384]{1,0:T(8,128)(2,1)} %shard_map.45.given), custom_call_target="tpu_custom_call", output_to_operand_aliasing={{}: (2, {})} | custom-call | tf_op jit(solution)/shard_map/pallas_call | solution.py:193
  (27 shorter events, 4.3 us)
Async XLA Ops:
  0.0 21.5 %collective-permute-start.5 = (bf16[1792,384]{1,0:T(8,128)(2,1)}, bf16[1792,384]{1,0:T(8,128)(2,1)S(1)}, u32[]{:S(2)}, u32[]{:S(2)}) collective-permute-start(bf16[1792,384]{1,0:T(8,128)(2,1)} %own.1), channel_id=1, source_target_pairs={{16,0},{0,16},{17,1},{1,17},{18,2},{2,18},{19,3},{3,19},{20,4},{4,... | collective-permute-start | bytes 4128776 | tf_op jit(solution)/shard_map/ppermute | solution.py:23
  3.3 1.0 %copy-start.1 = (bf16[112,2048]{1,0:T(8,128)(2,1)S(1)}, bf16[112,2048]{1,0:T(8,128)(2,1)}, u32[]{:S(2)}) copy-start(bf16[112,2048]{1,0:T(8,128)(2,1)} %panel.1) | copy-start | bytes 1376260
  4.3 0.7 copy-start.2
  6.1 1.9 %collective-permute-start = (f32[8,112,128]{2,1,0:T(8,128)S(1)}, f32[8,112,128]{2,1,0:T(8,128)S(1)}, u32[]{:S(2)}, u32[]{:S(2)}) collective-permute-start(f32[8,112,128]{2,1,0:T(8,128)S(1)} %get-tuple-element.23), channel_id=1, source_target_pairs={{16,0},{0,16},{17,1},{1,17},{18,2},{2,18},{19,3},{3,19},{20,4},{4,... | collective-permute-start | bytes 1376264 | tf_op jit(solution)/shard_map/ppermute | solution.py:23
  8.6 3.3 %collective-permute-start.1 = (bf16[2,112,128]{2,1,0:T(8,128)(2,1)S(1)}, bf16[2,112,128]{2,1,0:T(8,128)(2,1)S(1)}, u32[]{:S(2)}, u32[]{:S(2)}) collective-permute-start(bf16[2,112,128]{2,1,0:T(8,128)(2,1)S(1)} %get-tuple-element.25), channel_id=1, source_target_pairs={{64,0},{0,64},{192,128},{128,192},{65,1},{1,65},{193,129},{129,193... | collective-permute-start | bytes 172040 | tf_op jit(solution)/shard_map/ppermute | solution.py:27
  8.7 4.3 %collective-permute-start.2 = (bf16[2,112,128]{2,1,0:T(8,128)(2,1)S(1)}, bf16[2,112,128]{2,1,0:T(8,128)(2,1)S(1)}, u32[]{:S(2)}, u32[]{:S(2)}) collective-permute-start(bf16[2,112,128]{2,1,0:T(8,128)(2,1)S(1)} %get-tuple-element.26), channel_id=1, source_target_pairs={{192,0},{128,64},{64,128},{0,192},{193,1},{129,65},{65,129},{1,193... | collective-permute-start | bytes 172040 | tf_op jit(solution)/shard_map/ppermute | solution.py:27
  10.0 4.5 %collective-permute-start.3 = (bf16[2,112,128]{2,1,0:T(8,128)(2,1)S(1)}, bf16[2,112,128]{2,1,0:T(8,128)(2,1)S(1)}, u32[]{:S(2)}, u32[]{:S(2)}) collective-permute-start(bf16[2,112,128]{2,1,0:T(8,128)(2,1)S(1)} %get-tuple-element.27), channel_id=1, source_target_pairs={{128,0},{192,64},{0,128},{64,192},{129,1},{193,65},{1,129},{65,193... | collective-permute-start | bytes 172040 | tf_op jit(solution)/shard_map/ppermute | solution.py:27
  14.5 9.1 %collective-permute-start.4 = (bf16[2,112,128]{2,1,0:T(8,128)(2,1)S(1)}, bf16[2,112,128]{2,1,0:T(8,128)(2,1)S(1)}, u32[]{:S(2)}, u32[]{:S(2)}) collective-permute-start(bf16[2,112,128]{2,1,0:T(8,128)(2,1)S(1)} %fusion), channel_id=1, source_target_pairs={{32,0},{0,32},{33,1},{1,33},{34,2},{2,34},{35,3},{3,35},{36,4},{4,... | collective-permute-start | bytes 172040 | tf_op jit(solution)/shard_map/ppermute | solution.py:27
  21.5 1.3 %copy-start = (bf16[1792,384]{1,0:T(8,128)(2,1)S(1)}, bf16[1792,384]{1,0:T(8,128)(2,1)}, u32[]{:S(2)}) copy-start(bf16[1792,384]{1,0:T(8,128)(2,1)} %own.1) | copy-start | bytes 4128772
  23.7 4.9 %collective-permute-start.8 = (bf16[2,112,128]{2,1,0:T(8,128)(2,1)S(1)}, bf16[2,112,128]{2,1,0:T(8,128)(2,1)S(1)}, u32[]{:S(2)}, u32[]{:S(2)}) collective-permute-start(bf16[2,112,128]{2,1,0:T(8,128)(2,1)S(1)} %add_convert_fusion), channel_id=1, source_target_pairs={{12,0},{8,4},{4,8},{0,12},{13,1},{9,5},{5,9},{1,13},{14,2},{10,6},... | collective-permute-start | bytes 172040 | tf_op jit(solution)/shard_map/ppermute | solution.py:27
  26.1 4.2 %collective-permute-start.7 = (bf16[2,112,128]{2,1,0:T(8,128)(2,1)S(1)}, bf16[2,112,128]{2,1,0:T(8,128)(2,1)S(1)}, u32[]{:S(2)}, u32[]{:S(2)}) collective-permute-start(bf16[2,112,128]{2,1,0:T(8,128)(2,1)S(1)} %add_convert_fusion), channel_id=1, source_target_pairs={{8,0},{12,4},{0,8},{4,12},{9,1},{13,5},{1,9},{5,13},{10,2},{14,6},... | collective-permute-start | bytes 172040 | tf_op jit(solution)/shard_map/ppermute | solution.py:27
  26.1 4.2 %collective-permute-start.6 = (bf16[2,112,128]{2,1,0:T(8,128)(2,1)S(1)}, bf16[2,112,128]{2,1,0:T(8,128)(2,1)S(1)}, u32[]{:S(2)}, u32[]{:S(2)}) collective-permute-start(bf16[2,112,128]{2,1,0:T(8,128)(2,1)S(1)} %add_convert_fusion), channel_id=1, source_target_pairs={{4,0},{0,4},{12,8},{8,12},{5,1},{1,5},{13,9},{9,13},{6,2},{2,6},{1... | collective-permute-start | bytes 172040 | tf_op jit(solution)/shard_map/ppermute | solution.py:27
  30.3 5.0 %collective-permute-start.9 = (bf16[2,4,112,128]{3,2,1,0:T(8,128)(2,1)S(1)}, bf16[2,4,112,128]{3,2,1,0:T(8,128)(2,1)S(1)}, u32[]{:S(2)}, u32[]{:S(2)}) collective-permute-start(bf16[2,4,112,128]{3,2,1,0:T(8,128)(2,1)S(1)} %get-tuple-element.40), channel_id=1, source_target_pairs={{64,0},{65,1},{66,2},{67,3},{68,4},{69,5},{70,6},{71,7},{72,8},{73... | collective-permute-start | bytes 688136 | tf_op jit(solution)/shard_map/ppermute | solution.py:36
  35.4 8.7 %collective-permute-start.10 = (bf16[2,2,4,112,128]{4,3,2,1,0:T(8,128)(2,1)S(1)}, bf16[2,2,4,112,128]{4,3,2,1,0:T(8,128)(2,1)S(1)}, u32[]{:S(2)}, u32[]{:S(2)}) collective-permute-start(bf16[2,2,4,112,128]{4,3,2,1,0:T(8,128)(2,1)S(1)} %pad_maximum_fusion.first), channel_id=1, source_target_pairs={{192,0},{193,1},{194,2},{195,3},{196,4},{197,5},{198,6},{199,7},{2... | collective-permute-start | bytes 1376264 | tf_op jit(solution)/shard_map/ppermute | solution.py:36
  39.3 7.7 %collective-permute-start.11 = (bf16[2,2,4,112,128]{4,3,2,1,0:T(8,128)(2,1)S(1)}, bf16[2,2,4,112,128]{4,3,2,1,0:T(8,128)(2,1)S(1)}, u32[]{:S(2)}, u32[]{:S(2)}) collective-permute-start(bf16[2,2,4,112,128]{4,3,2,1,0:T(8,128)(2,1)S(1)} %pad_maximum_fusion.first), channel_id=1, source_target_pairs={{1,0},{0,1},{3,2},{2,3},{5,4},{4,5},{7,6},{6,7},{9,8},{8,9},{11,10... | collective-permute-start | bytes 1376264 | tf_op jit(solution)/shard_map/ppermute | solution.py:36
  47.0 8.5 %collective-permute-start.12 = (bf16[2,2,4,112,128]{4,3,2,1,0:T(8,128)(2,1)S(1)}, bf16[2,2,4,112,128]{4,3,2,1,0:T(8,128)(2,1)S(1)}, u32[]{:S(2)}, u32[]{:S(2)}) collective-permute-start(bf16[2,2,4,112,128]{4,3,2,1,0:T(8,128)(2,1)S(1)} %pad_maximum_fusion.first), channel_id=1, source_target_pairs={{3,0},{2,1},{1,2},{0,3},{7,4},{6,5},{5,6},{4,7},{11,8},{10,9},{9,1... | collective-permute-start | bytes 1376264 | tf_op jit(solution)/shard_map/ppermute | solution.py:36
  48.1 7.5 %collective-permute-start.14 = (bf16[2,2,4,112,128]{4,3,2,1,0:T(8,128)(2,1)S(1)}, bf16[2,2,4,112,128]{4,3,2,1,0:T(8,128)(2,1)S(1)}, u32[]{:S(2)}, u32[]{:S(2)}) collective-permute-start(bf16[2,2,4,112,128]{4,3,2,1,0:T(8,128)(2,1)S(1)} %collective-permute-done.10.last), channel_id=1, source_target_pairs={{1,0},{0,1},{3,2},{2,3},{5,4},{4,5},{7,6},{6,7},{9,8},{8,9},{11,10... | collective-permute-start | bytes 1376264 | tf_op jit(solution)/shard_map/ppermute | solution.py:36
  48.1 12.7 %collective-permute-start.16 = (bf16[2,2,4,112,128]{4,3,2,1,0:T(8,128)(2,1)S(1)}, bf16[2,2,4,112,128]{4,3,2,1,0:T(8,128)(2,1)S(1)}, u32[]{:S(2)}, u32[]{:S(2)}) collective-permute-start(bf16[2,2,4,112,128]{4,3,2,1,0:T(8,128)(2,1)S(1)} %collective-permute-done.10.last), channel_id=1, source_target_pairs={{3,0},{2,1},{1,2},{0,3},{7,4},{6,5},{5,6},{4,7},{11,8},{10,9},{9,1... | collective-permute-start | bytes 1376264 | tf_op jit(solution)/shard_map/ppermute | solution.py:36
  55.6 7.6 %collective-permute-start.13 = (bf16[2,2,4,112,128]{4,3,2,1,0:T(8,128)(2,1)S(1)}, bf16[2,2,4,112,128]{4,3,2,1,0:T(8,128)(2,1)S(1)}, u32[]{:S(2)}, u32[]{:S(2)}) collective-permute-start(bf16[2,2,4,112,128]{4,3,2,1,0:T(8,128)(2,1)S(1)} %collective-permute-done.12.three), channel_id=1, source_target_pairs={{1,0},{0,1},{3,2},{2,3},{5,4},{4,5},{7,6},{6,7},{9,8},{8,9},{11,10... | collective-permute-start | bytes 1376264 | tf_op jit(solution)/shard_map/ppermute | solution.py:36
  55.6 16.5 %collective-permute-start.15 = (bf16[2,2,4,112,128]{4,3,2,1,0:T(8,128)(2,1)S(1)}, bf16[2,2,4,112,128]{4,3,2,1,0:T(8,128)(2,1)S(1)}, u32[]{:S(2)}, u32[]{:S(2)}) collective-permute-start(bf16[2,2,4,112,128]{4,3,2,1,0:T(8,128)(2,1)S(1)} %collective-permute-done.14.one), channel_id=1, source_target_pairs={{3,0},{2,1},{1,2},{0,3},{7,4},{6,5},{5,6},{4,7},{11,8},{10,9},{9,1... | collective-permute-start | bytes 1376264 | tf_op jit(solution)/shard_map/ppermute | solution.py:36
  63.9 11.5 %collective-permute-start.18 = (bf16[512,384]{1,0:T(8,128)(2,1)S(1)}, bf16[512,384]{1,0:T(8,128)(2,1)S(1)}, u32[]{:S(2)}, u32[]{:S(2)}) collective-permute-start(bf16[512,384]{1,0:T(8,128)(2,1)S(1)} %get-tuple-element.38), channel_id=1, source_target_pairs={{16,0},{0,16},{17,1},{1,17},{18,2},{2,18},{19,3},{3,19},{20,4},{4,... | collective-permute-start | bytes 1179656 | tf_op jit(solution)/shard_map/ppermute | solution.py:23
  73.6 3.3 %collective-permute-start.17 = (bf16[512,384]{1,0:T(8,128)(2,1)S(1)}, bf16[512,384]{1,0:T(8,128)(2,1)S(1)}, u32[]{:S(2)}, u32[]{:S(2)}) collective-permute-start(bf16[512,384]{1,0:T(8,128)(2,1)S(1)} %get-tuple-element.35), channel_id=1, source_target_pairs={{16,0},{0,16},{17,1},{1,17},{18,2},{2,18},{19,3},{3,19},{20,4},{4,... | collective-permute-start | bytes 1179656 | tf_op jit(solution)/shard_map/ppermute | solution.py:23

commit v9 on v7

--- a/solution.py
+++ b/solution.py
@@ -1,3 +1,4 @@
+import functools
 import itertools
 
 import jax
@@ -151,19 +152,19 @@
         keep(start[rows(0, 2)])
 
 
-def product_five(place, first, last, both, start, mine, theirs):
-    def keep(at, total):
-        mine[at] = total[:, :384].astype(BF16)
-        theirs[at] = total[:, 384:].astype(BF16)
-
-    @on_core(place, 0)
-    def _():
-        keep(rows(0, 2), start[rows(2, 2)] + dot_t(by_x(*slabs(last)), both[3]))
-
-    @on_core(place, 1)
-    def _():
-        keep(rows(0), start[rows(2)])
-        keep(rows(1), dot_t(by_y(*slabs(first), *slabs(last)), deep(both, 0, 4)))
+def product_five(side, place, first, last, both, start, out):
+    columns = pl.ds(side * 384, 384)
+
+    @on_core(place, 0)
+    def _():
+        total = start[rows(2, 2), columns] + dot_t(by_x(*slabs(last)), both[3, :, columns])
+        out[...] = total.astype(BF16)
+
+    @on_core(place, 1)
+    def _():
+        out[rows(0)] = start[rows(2), columns].astype(BF16)
+        left = by_y(*slabs(first), *slabs(last))
+        out[rows(1)] = dot_t(left, both[:, :, columns].reshape(1792, 384)).astype(BF16)
 
 
 def place_rows(place, parts, out, sems):
@@ -227,12 +228,14 @@
     part = (part + share.astype(F32)).astype(BF16)
     own = jnp.stack([part] + [swap(part, "z_lo", 4, bits) for bits in (1, 2, 3)], 1)
 
-    first = jnp.stack([own, turn(own, 0, 1)])
-    last = turn(first, 0, 3)
-    one1, three1 = turn(first, 1, 1), turn(first, 1, 3)
+    near1, near3 = turn(own, 0, 1), turn(own, 0, 3)
+    far = turn(near1, 0, 3)
+    first = jnp.stack([own, near1])
     total = jax.ShapeDtypeStruct((1024, 768), F32)
     total_one = call(product_one, total, (place, first, both))
-    last, total_one = lax.optimization_barrier((last, total_one))
+    first, total_one = lax.optimization_barrier((first, total_one))
+    one1, three1 = turn(first, 1, 1), turn(first, 1, 3)
+    last = jnp.stack([near3, far])
     one2, three2 = turn(last, 1, 1), turn(last, 1, 3)
     one1, three1 = lax.optimization_barrier((one1, three1))
     far1, far2 = turn(three1, 1, 1), turn(one2, 1, 3)
@@ -253,8 +256,9 @@
         product_four, (half, half), (place, far1, both, total_three), (VMEM, VMEM)
     )
     theirs1 = fetch(theirs1, "core", 2, 1)
-    mine2, theirs2 = call(
-        product_five, (half, half), (place, far1, far2, both, total_three), (VMEM, VMEM)
+    mine2, theirs2 = (
+        call(functools.partial(product_five, side), half, (place, far1, far2, both, total_three))
+        for side in (0, 1)
     )
     theirs2 = fetch(theirs2, "core", 2, 1)
 

time: 78.6 us -> 74.8 us (0.952)
  starting transfers between devices: 40.7 us -> 37 us
  waiting for transfers between devices: 21.4 us -> 20.4 us
  Pallas kernels: 12.7 us -> 13.6 us
    ppermute x4, starting transfers between devices: 17.9 us -> 13.2 us  [fetch(): lax.ppermute(block, axis, [((i + ahead) % size, i) for i in range(size)])]
    ppermute x8 -> x9, waiting for transfers between devices: 14.1 us -> 13 us  [turn(): return lax.ppermute(block, ROW + COL, pairs)]
    pallas_call x10 -> x11, Pallas kernels: 12.7 us -> 13.6 us  [call(): pl.pallas_call(kernel, out_shape=out_shape, in_specs=specs or [SMEM] + [V...]
    ppermute x8 -> x9, starting transfers between devices: 8.93 us -> 9.84 us  [turn(): return lax.ppermute(block, ROW + COL, pairs)]
  transfers between devices with their start and end apart: 19 -> 20, of which waited for: 12 -> 13; matrix products, arithmetic and copies ran while one was open for 0% -> 0% of each run, Pallas kernels for 14% -> 16%
where the time goes in v9:
time: 74.8 us; the launch traced here: 74.6 us
  starting transfers between devices  37 us (49%)
  waiting for transfers between devices  20.4 us (27%)
  Pallas kernels  13.6 us (18%)
  local copies, waits for them, and re-layouts  3.11 us (4%)
    ppermute x7, starting transfers between devices, swap(): return lax.ppermute(block, axis, [(i ^ bits, i) for i in range(size)])  14 us
    pallas_call x11, Pallas kernels, call(): pl.pallas_call(kernel, out_shape=out_shape, in_specs=specs or [SMEM] + [V...  13.6 us
    ppermute x4, starting transfers between devices, fetch(): lax.ppermute(block, axis, [((i + ahead) % size, i) for i in range(size)])  13.2 us
    ppermute x9, waiting for transfers between devices, turn(): return lax.ppermute(block, ROW + COL, pairs)  13 us
    ppermute x9, starting transfers between devices, turn(): return lax.ppermute(block, ROW + COL, pairs)  9.84 us
    ppermute x7, waiting for transfers between devices, swap(): return lax.ppermute(block, axis, [(i ^ bits, i) for i in range(size)])  5.51 us
    unnamed x6, local copies, waits for them, and re-layouts  3.11 us
    ppermute x4, waiting for transfers between devices, fetch(): lax.ppermute(block, axis, [((i + ahead) % size, i) for i in range(size)])  1.81 us
  transfers between devices with their start and end apart: 20, of which 13 were waited for; matrix products, arithmetic and copies ran while one was open for 0% of the time, Pallas kernels for 16%

profile of v9, /device:TPU:1, one launch (start us, length us, event | category | flops | bytes accessed | tf_op | source)
XLA Modules:
  0.0 74.6 jit_solution(430168784495920545)
XLA Ops:
  0.0 3.2 %collective-permute-start.5 = (bf16[1792,384]{1,0:T(8,128)(2,1)}, bf16[1792,384]{1,0:T(8,128)(2,1)S(1)}, u32[]{:S(2)}, u32[]{:S(2)}) collective-permute-start(bf16[1792,384]{1,0:T(8,128)(2,1)} %own.1), channel_id=1, source_target_pairs={{16,0},{0,16},{17,1},{1,17},{18,2},{2,18},{19,3},{3,19},{20,4},{4,... | collective-permute-start | bytes 4128776 | tf_op jit(solution)/shard_map/ppermute | solution.py:24
  3.3 1.0 %copy-done.1 = bf16[112,2048]{1,0:T(8,128)(2,1)S(1)} copy-done((bf16[112,2048]{1,0:T(8,128)(2,1)S(1)}, bf16[112,2048]{1,0:T(8,128)(2,1)}, u32[]{:S(2)}) %copy-start.1) | copy-done | bytes 458776
  6.2 1.8 %collective-permute-done.received = f32[8,112,128]{2,1,0:T(8,128)S(1)} collective-permute-done((f32[8,112,128]{2,1,0:T(8,128)S(1)}, f32[8,112,128]{2,1,0:T(8,128)S(1)}, u32[]{:S(2)}, u32[]{:S(2)}) %collective-permute-start) | collective-permute-done | bytes 458784 | tf_op jit(solution)/shard_map/ppermute | solution.py:24
  8.7 1.3 %collective-permute-start.2 = (bf16[2,112,128]{2,1,0:T(8,128)(2,1)S(1)}, bf16[2,112,128]{2,1,0:T(8,128)(2,1)S(1)}, u32[]{:S(2)}, u32[]{:S(2)}) collective-permute-start(bf16[2,112,128]{2,1,0:T(8,128)(2,1)S(1)} %get-tuple-element.23), channel_id=1, source_target_pairs={{192,0},{128,64},{64,128},{0,192},{193,1},{129,65},{65,129},{1,193... | collective-permute-start | bytes 172040 | tf_op jit(solution)/shard_map/ppermute | solution.py:28
  10.0 2.0 %collective-permute-start.3 = (bf16[2,112,128]{2,1,0:T(8,128)(2,1)S(1)}, bf16[2,112,128]{2,1,0:T(8,128)(2,1)S(1)}, u32[]{:S(2)}, u32[]{:S(2)}) collective-permute-start(bf16[2,112,128]{2,1,0:T(8,128)(2,1)S(1)} %get-tuple-element.24), channel_id=1, source_target_pairs={{128,0},{192,64},{0,128},{64,192},{129,1},{193,65},{1,129},{65,193... | collective-permute-start | bytes 172040 | tf_op jit(solution)/shard_map/ppermute | solution.py:28
  11.9 1.1 %collective-permute-done.2 = bf16[2,112,128]{2,1,0:T(8,128)(2,1)S(1)} collective-permute-done((bf16[2,112,128]{2,1,0:T(8,128)(2,1)S(1)}, bf16[2,112,128]{2,1,0:T(8,128)(2,1)S(1)}, u32[]{:S(2)}, u32[]{:S(2)}) %collective-permute-start.2) | collective-permute-done | bytes 57376 | tf_op jit(solution)/shard_map/ppermute | solution.py:28
  13.0 1.5 %collective-permute-done.3 = bf16[2,112,128]{2,1,0:T(8,128)(2,1)S(1)} collective-permute-done((bf16[2,112,128]{2,1,0:T(8,128)(2,1)S(1)}, bf16[2,112,128]{2,1,0:T(8,128)(2,1)S(1)}, u32[]{:S(2)}, u32[]{:S(2)}) %collective-permute-start.3) | collective-permute-done | bytes 57376 | tf_op jit(solution)/shard_map/ppermute | solution.py:28
  14.5 7.0 %collective-permute-start.4 = (bf16[2,112,128]{2,1,0:T(8,128)(2,1)S(1)}, bf16[2,112,128]{2,1,0:T(8,128)(2,1)S(1)}, u32[]{:S(2)}, u32[]{:S(2)}) collective-permute-start(bf16[2,112,128]{2,1,0:T(8,128)(2,1)S(1)} %fusion), channel_id=1, source_target_pairs={{32,0},{0,32},{33,1},{1,33},{34,2},{2,34},{35,3},{3,35},{36,4},{4,... | collective-permute-start | bytes 172040 | tf_op jit(solution)/shard_map/ppermute | solution.py:28
  21.5 1.3 %copy-done = bf16[1792,384]{1,0:T(8,128)(2,1)S(1)} copy-done((bf16[1792,384]{1,0:T(8,128)(2,1)S(1)}, bf16[1792,384]{1,0:T(8,128)(2,1)}, u32[]{:S(2)}) %copy-start) | copy-done | bytes 1376280
  23.7 2.4 %collective-permute-start.8 = (bf16[2,112,128]{2,1,0:T(8,128)(2,1)S(1)}, bf16[2,112,128]{2,1,0:T(8,128)(2,1)S(1)}, u32[]{:S(2)}, u32[]{:S(2)}) collective-permute-start(bf16[2,112,128]{2,1,0:T(8,128)(2,1)S(1)} %add_convert_fusion), channel_id=1, source_target_pairs={{12,0},{8,4},{4,8},{0,12},{13,1},{9,5},{5,9},{1,13},{14,2},{10,6},... | collective-permute-start | bytes 172040 | tf_op jit(solution)/shard_map/ppermute | solution.py:28
  26.1 1.2 %collective-permute-start.7 = (bf16[2,112,128]{2,1,0:T(8,128)(2,1)S(1)}, bf16[2,112,128]{2,1,0:T(8,128)(2,1)S(1)}, u32[]{:S(2)}, u32[]{:S(2)}) collective-permute-start(bf16[2,112,128]{2,1,0:T(8,128)(2,1)S(1)} %add_convert_fusion), channel_id=1, source_target_pairs={{8,0},{12,4},{0,8},{4,12},{9,1},{13,5},{1,9},{5,13},{10,2},{14,6},... | collective-permute-start | bytes 172040 | tf_op jit(solution)/shard_map/ppermute | solution.py:28
  27.4 1.3 %collective-permute-done.8 = bf16[2,112,128]{2,1,0:T(8,128)(2,1)S(1)} collective-permute-done((bf16[2,112,128]{2,1,0:T(8,128)(2,1)S(1)}, bf16[2,112,128]{2,1,0:T(8,128)(2,1)S(1)}, u32[]{:S(2)}, u32[]{:S(2)}) %collective-permute-start.8) | collective-permute-done | bytes 57376 | tf_op jit(solution)/shard_map/ppermute | solution.py:28
  29.3 1.0 %collective-permute-done.7 = bf16[2,112,128]{2,1,0:T(8,128)(2,1)S(1)} collective-permute-done((bf16[2,112,128]{2,1,0:T(8,128)(2,1)S(1)}, bf16[2,112,128]{2,1,0:T(8,128)(2,1)S(1)}, u32[]{:S(2)}, u32[]{:S(2)}) %collective-permute-start.7) | collective-permute-done | bytes 57376 | tf_op jit(solution)/shard_map/ppermute | solution.py:28
  30.3 1.4 %collective-permute-start.9 = (bf16[2,4,112,128]{3,2,1,0:T(8,128)(2,1)S(1)}, bf16[2,4,112,128]{3,2,1,0:T(8,128)(2,1)S(1)}, u32[]{:S(2)}, u32[]{:S(2)}) collective-permute-start(bf16[2,4,112,128]{3,2,1,0:T(8,128)(2,1)S(1)} %get-tuple-element.34), channel_id=1, source_target_pairs={{64,0},{65,1},{66,2},{67,3},{68,4},{69,5},{70,6},{71,7},{72,8},{73... | collective-permute-start | bytes 688136 | tf_op jit(solution)/shard_map/ppermute | solution.py:37
  31.7 1.9 %collective-permute-start.13 = (bf16[2,4,112,128]{3,2,1,0:T(8,128)(2,1)S(1)}, bf16[2,4,112,128]{3,2,1,0:T(8,128)(2,1)S(1)}, u32[]{:S(2)}, u32[]{:S(2)}) collective-permute-start(bf16[2,4,112,128]{3,2,1,0:T(8,128)(2,1)S(1)} %get-tuple-element.34), channel_id=1, source_target_pairs={{192,0},{193,1},{194,2},{195,3},{196,4},{197,5},{198,6},{199,7},{2... | collective-permute-start | bytes 688136 | tf_op jit(solution)/shard_map/ppermute | solution.py:37
  33.6 1.7 %collective-permute-done.9 = bf16[2,4,112,128]{3,2,1,0:T(8,128)(2,1)S(1)} collective-permute-done((bf16[2,4,112,128]{3,2,1,0:T(8,128)(2,1)S(1)}, bf16[2,4,112,128]{3,2,1,0:T(8,128)(2,1)S(1)}, u32[]{:S(2)}, u32[]{:S(2)}) %collective-permute-start.9) | collective-permute-done | bytes 229408 | tf_op jit(solution)/shard_map/ppermute | solution.py:37
  35.3 2.7 %collective-permute-start.14 = (bf16[2,4,112,128]{3,2,1,0:T(8,128)(2,1)S(1)}, bf16[2,4,112,128]{3,2,1,0:T(8,128)(2,1)S(1)}, u32[]{:S(2)}, u32[]{:S(2)}) collective-permute-start(bf16[2,4,112,128]{3,2,1,0:T(8,128)(2,1)S(1)} %collective-permute-done.9), channel_id=1, source_target_pairs={{192,0},{193,1},{194,2},{195,3},{196,4},{197,5},{198,6},{199,7},{2... | collective-permute-start | bytes 688136 | tf_op jit(solution)/shard_map/ppermute | solution.py:37
  38.1 1.2 %shard_map.40.start = f32[1024,768]{1,0:T(8,128)S(1)} custom-call(s32[4]{0:T(128)S(1)} %pad_add_fusion.place, bf16[2,2,4,112,128]{4,3,2,1,0:T(8,128)(2,1)S(1)} %pad_maximum_fusion.first, bf16[4,448,768]{2,1,0:T(8,128)(2,1)S(1)} %shard_map.39.both), custom_call_target="tpu_custom_call" | custom-call | tf_op jit(solution)/shard_map/pallas_call | solution.py:194
  39.6 1.1 %collective-permute-start.11 = (bf16[2,2,4,112,128]{4,3,2,1,0:T(8,128)(2,1)S(1)}, bf16[2,2,4,112,128]{4,3,2,1,0:T(8,128)(2,1)S(1)}, u32[]{:S(2)}, u32[]{:S(2)}) collective-permute-start(bf16[2,2,4,112,128]{4,3,2,1,0:T(8,128)(2,1)S(1)} %pad_maximum_fusion.first), channel_id=1, source_target_pairs={{3,0},{2,1},{1,2},{0,3},{7,4},{6,5},{5,6},{4,7},{11,8},{10,9},{9,1... | collective-permute-start | bytes 1376264 | tf_op jit(solution)/shard_map/ppermute | solution.py:37
  40.8 1.0 %collective-permute-done.14 = bf16[2,4,112,128]{3,2,1,0:T(8,128)(2,1)S(1)} collective-permute-done((bf16[2,4,112,128]{3,2,1,0:T(8,128)(2,1)S(1)}, bf16[2,4,112,128]{3,2,1,0:T(8,128)(2,1)S(1)}, u32[]{:S(2)}, u32[]{:S(2)}) %collective-permute-start.14) | collective-permute-done | bytes 229408 | tf_op jit(solution)/shard_map/ppermute | solution.py:37
  41.9 1.1 %collective-permute-start.17 = (bf16[2,2,4,112,128]{4,3,2,1,0:T(8,128)(2,1)S(1)}, bf16[2,2,4,112,128]{4,3,2,1,0:T(8,128)(2,1)S(1)}, u32[]{:S(2)}, u32[]{:S(2)}) collective-permute-start(bf16[2,2,4,112,128]{4,3,2,1,0:T(8,128)(2,1)S(1)} %pad_maximum_fusion.1.last), channel_id=1, source_target_pairs={{3,0},{2,1},{1,2},{0,3},{7,4},{6,5},{5,6},{4,7},{11,8},{10,9},{9,1... | collective-permute-start | bytes 1376264 | tf_op jit(solution)/shard_map/ppermute | solution.py:37
  43.0 3.9 %collective-permute-done.10.one = bf16[2,2,4,112,128]{4,3,2,1,0:T(8,128)(2,1)S(1)} collective-permute-done((bf16[2,2,4,112,128]{4,3,2,1,0:T(8,128)(2,1)S(1)}, bf16[2,2,4,112,128]{4,3,2,1,0:T(8,128)(2,1)S(1)}, u32[]{:S(2)}, u32[]{:S(2)}) %collective-permute-start.10) | collective-permute-done | bytes 458784 | tf_op jit(solution)/shard_map/ppermute | solution.py:37
  47.0 4.0 %collective-permute-done.11.three = bf16[2,2,4,112,128]{4,3,2,1,0:T(8,128)(2,1)S(1)} collective-permute-done((bf16[2,2,4,112,128]{4,3,2,1,0:T(8,128)(2,1)S(1)}, bf16[2,2,4,112,128]{4,3,2,1,0:T(8,128)(2,1)S(1)}, u32[]{:S(2)}, u32[]{:S(2)}) %collective-permute-start.11) | collective-permute-done | bytes 458784 | tf_op jit(solution)/shard_map/ppermute | solution.py:37
  51.9 1.1 %collective-permute-start.16 = (bf16[2,2,4,112,128]{4,3,2,1,0:T(8,128)(2,1)S(1)}, bf16[2,2,4,112,128]{4,3,2,1,0:T(8,128)(2,1)S(1)}, u32[]{:S(2)}, u32[]{:S(2)}) collective-permute-start(bf16[2,2,4,112,128]{4,3,2,1,0:T(8,128)(2,1)S(1)} %collective-permute-done.15.one), channel_id=1, source_target_pairs={{3,0},{2,1},{1,2},{0,3},{7,4},{6,5},{5,6},{4,7},{11,8},{10,9},{9,1... | collective-permute-start | bytes 1376264 | tf_op jit(solution)/shard_map/ppermute | solution.py:37
  53.0 2.3 %shard_map.41.start = f32[1024,768]{1,0:T(8,128)S(1)} custom-call(s32[4]{0:T(128)S(1)} %pad_add_fusion.place, bf16[2,2,4,112,128]{4,3,2,1,0:T(8,128)(2,1)S(1)} %pad_maximum_fusion.1.last, bf16[2,2,4,112,128]{4,3,2,1,0:T(8,128)(2,1)S(1)} %collective-permute-done.10.one, ...), custom_call_target="tpu_custom_call", output_to_operand_aliasing={{}: (5, {})} | custom-call | tf_op jit(solution)/shard_map/pallas_call | solution.py:194
  55.6 1.8 %shard_map.42.start = f32[1024,768]{1,0:T(8,128)S(1)} custom-call(s32[4]{0:T(128)S(1)} %pad_add_fusion.place, bf16[2,2,4,112,128]{4,3,2,1,0:T(8,128)(2,1)S(1)} %collective-permute-done.15.one, bf16[2,2,4,112,128]{4,3,2,1,0:T(8,128)(2,1)S(1)} %collective-permute-done.17.three, ...), custom_call_target="tpu_custom_call", output_to_operand_aliasing={{}: (4, {})} | custom-call | tf_op jit(solution)/shard_map/pallas_call | solution.py:194
  57.3 1.2 %collective-permute-done.12.first = bf16[2,2,4,112,128]{4,3,2,1,0:T(8,128)(2,1)S(1)} collective-permute-done((bf16[2,2,4,112,128]{4,3,2,1,0:T(8,128)(2,1)S(1)}, bf16[2,2,4,112,128]{4,3,2,1,0:T(8,128)(2,1)S(1)}, u32[]{:S(2)}, u32[]{:S(2)}) %collective-permute-start.12) | collective-permute-done | bytes 458784 | tf_op jit(solution)/shard_map/ppermute | solution.py:37
  59.2 9.3 %collective-permute-start.19 = (bf16[512,384]{1,0:T(8,128)(2,1)S(1)}, bf16[512,384]{1,0:T(8,128)(2,1)S(1)}, u32[]{:S(2)}, u32[]{:S(2)}) collective-permute-start(bf16[512,384]{1,0:T(8,128)(2,1)S(1)} %get-tuple-element.32), channel_id=1, source_target_pairs={{16,0},{0,16},{17,1},{1,17},{18,2},{2,18},{19,3},{3,19},{20,4},{4,... | collective-permute-start | bytes 1179656 | tf_op jit(solution)/shard_map/ppermute | solution.py:24
  68.5 1.2 %shard_map.43 = bf16[512,384]{1,0:T(8,128)(2,1)S(1)} custom-call(s32[4]{0:T(128)S(1)} %pad_add_fusion.place, bf16[2,2,4,112,128]{4,3,2,1,0:T(8,128)(2,1)S(1)} %collective-permute-done.12.first, bf16[2,2,4,112,128]{4,3,2,1,0:T(8,128)(2,1)S(1)} %collective-permute-done.16.last, bf16[4,448,768]{2,1,0:T(8,128)(2,1)S(1)} %shard_map.39.both, ...), custom_call_target="tpu_custom_call" | custom-call | tf_op jit(solution)/shard_map/pallas_call | solution.py:194
  70.3 1.2 %shard_map.45.mine2 = bf16[512,384]{1,0:T(8,128)(2,1)S(1)} custom-call(s32[4]{0:T(128)S(1)} %pad_add_fusion.place, bf16[2,2,4,112,128]{4,3,2,1,0:T(8,128)(2,1)S(1)} %collective-permute-done.12.first, bf16[2,2,4,112,128]{4,3,2,1,0:T(8,128)(2,1)S(1)} %collective-permute-done.16.last, bf16[4,448,768]{2,1,0:T(8,128)(2,1)S(1)} %shard_map.39.both, ...), custom_call_target="tpu_custom_call" | custom-call | tf_op jit(solution)/shard_map/pallas_call | solution.py:194
  71.5 1.6 %shard_map.46.given = bf16[2048,384]{1,0:T(8,128)(2,1)} custom-call(s32[4]{0:T(128)S(1)} %pad_add_fusion.place, bf16[512,384]{1,0:T(8,128)(2,1)S(1)} %get-tuple-element.31.mine1, bf16[512,384]{1,0:T(8,128)(2,1)S(1)} %shard_map.45.mine2, bf16[512,384]{1,0:T(8,128)(2,1)S(1)} %collective-permute-done.19.theirs1), custom_call_target="tpu_custom_call" | custom-call | tf_op jit(solution)/shard_map/pallas_call | solution.py:194
  73.1 1.3 %shard_map.47 = bf16[2048,384]{1,0:T(8,128)(2,1)} custom-call(s32[4]{0:T(128)S(1)} %pad_add_fusion.place, bf16[512,384]{1,0:T(8,128)(2,1)S(1)} %collective-permute-done.18.theirs2, bf16[2048,384]{1,0:T(8,128)(2,1)} %shard_map.46.given), custom_call_target="tpu_custom_call", output_to_operand_aliasing={{}: (2, {})} | custom-call | tf_op jit(solution)/shard_map/pallas_call | solution.py:194
  (31 shorter events, 7.1 us)
Async XLA Ops:
  0.0 21.5 %collective-permute-start.5 = (bf16[1792,384]{1,0:T(8,128)(2,1)}, bf16[1792,384]{1,0:T(8,128)(2,1)S(1)}, u32[]{:S(2)}, u32[]{:S(2)}) collective-permute-start(bf16[1792,384]{1,0:T(8,128)(2,1)} %own.1), channel_id=1, source_target_pairs={{16,0},{0,16},{17,1},{1,17},{18,2},{2,18},{19,3},{3,19},{20,4},{4,... | collective-permute-start | bytes 4128776 | tf_op jit(solution)/shard_map/ppermute | solution.py:24
  3.3 1.0 %copy-start.1 = (bf16[112,2048]{1,0:T(8,128)(2,1)S(1)}, bf16[112,2048]{1,0:T(8,128)(2,1)}, u32[]{:S(2)}) copy-start(bf16[112,2048]{1,0:T(8,128)(2,1)} %panel.1) | copy-start | bytes 1376260
  4.3 0.7 %copy-start.2 = (bf16[112,112]{1,0:T(8,128)(2,1)S(1)}, bf16[112,112]{1,0:T(8,128)(2,1)}, u32[]{:S(2)}) copy-start(bf16[112,112]{1,0:T(8,128)(2,1)} %screening.1) | copy-start | bytes 75268
  6.1 1.9 %collective-permute-start = (f32[8,112,128]{2,1,0:T(8,128)S(1)}, f32[8,112,128]{2,1,0:T(8,128)S(1)}, u32[]{:S(2)}, u32[]{:S(2)}) collective-permute-start(f32[8,112,128]{2,1,0:T(8,128)S(1)} %get-tuple-element.20), channel_id=1, source_target_pairs={{16,0},{0,16},{17,1},{1,17},{18,2},{2,18},{19,3},{3,19},{20,4},{4,... | collective-permute-start | bytes 1376264 | tf_op jit(solution)/shard_map/ppermute | solution.py:24
  8.6 3.3 %collective-permute-start.1 = (bf16[2,112,128]{2,1,0:T(8,128)(2,1)S(1)}, bf16[2,112,128]{2,1,0:T(8,128)(2,1)S(1)}, u32[]{:S(2)}, u32[]{:S(2)}) collective-permute-start(bf16[2,112,128]{2,1,0:T(8,128)(2,1)S(1)} %get-tuple-element.22), channel_id=1, source_target_pairs={{64,0},{0,64},{192,128},{128,192},{65,1},{1,65},{193,129},{129,193... | collective-permute-start | bytes 172040 | tf_op jit(solution)/shard_map/ppermute | solution.py:28
  8.7 4.3 %collective-permute-start.2 = (bf16[2,112,128]{2,1,0:T(8,128)(2,1)S(1)}, bf16[2,112,128]{2,1,0:T(8,128)(2,1)S(1)}, u32[]{:S(2)}, u32[]{:S(2)}) collective-permute-start(bf16[2,112,128]{2,1,0:T(8,128)(2,1)S(1)} %get-tuple-element.23), channel_id=1, source_target_pairs={{192,0},{128,64},{64,128},{0,192},{193,1},{129,65},{65,129},{1,193... | collective-permute-start | bytes 172040 | tf_op jit(solution)/shard_map/ppermute | solution.py:28
  10.0 4.5 %collective-permute-start.3 = (bf16[2,112,128]{2,1,0:T(8,128)(2,1)S(1)}, bf16[2,112,128]{2,1,0:T(8,128)(2,1)S(1)}, u32[]{:S(2)}, u32[]{:S(2)}) collective-permute-start(bf16[2,112,128]{2,1,0:T(8,128)(2,1)S(1)} %get-tuple-element.24), channel_id=1, source_target_pairs={{128,0},{192,64},{0,128},{64,192},{129,1},{193,65},{1,129},{65,193... | collective-permute-start | bytes 172040 | tf_op jit(solution)/shard_map/ppermute | solution.py:28
  14.5 9.1 %collective-permute-start.4 = (bf16[2,112,128]{2,1,0:T(8,128)(2,1)S(1)}, bf16[2,112,128]{2,1,0:T(8,128)(2,1)S(1)}, u32[]{:S(2)}, u32[]{:S(2)}) collective-permute-start(bf16[2,112,128]{2,1,0:T(8,128)(2,1)S(1)} %fusion), channel_id=1, source_target_pairs={{32,0},{0,32},{33,1},{1,33},{34,2},{2,34},{35,3},{3,35},{36,4},{4,... | collective-permute-start | bytes 172040 | tf_op jit(solution)/shard_map/ppermute | solution.py:28
  21.5 1.3 %copy-start = (bf16[1792,384]{1,0:T(8,128)(2,1)S(1)}, bf16[1792,384]{1,0:T(8,128)(2,1)}, u32[]{:S(2)}) copy-start(bf16[1792,384]{1,0:T(8,128)(2,1)} %own.1) | copy-start | bytes 4128772
  23.7 4.9 %collective-permute-start.8 = (bf16[2,112,128]{2,1,0:T(8,128)(2,1)S(1)}, bf16[2,112,128]{2,1,0:T(8,128)(2,1)S(1)}, u32[]{:S(2)}, u32[]{:S(2)}) collective-permute-start(bf16[2,112,128]{2,1,0:T(8,128)(2,1)S(1)} %add_convert_fusion), channel_id=1, source_target_pairs={{12,0},{8,4},{4,8},{0,12},{13,1},{9,5},{5,9},{1,13},{14,2},{10,6},... | collective-permute-start | bytes 172040 | tf_op jit(solution)/shard_map/ppermute | solution.py:28
  26.1 3.1 %collective-permute-start.6 = (bf16[2,112,128]{2,1,0:T(8,128)(2,1)S(1)}, bf16[2,112,128]{2,1,0:T(8,128)(2,1)S(1)}, u32[]{:S(2)}, u32[]{:S(2)}) collective-permute-start(bf16[2,112,128]{2,1,0:T(8,128)(2,1)S(1)} %add_convert_fusion), channel_id=1, source_target_pairs={{4,0},{0,4},{12,8},{8,12},{5,1},{1,5},{13,9},{9,13},{6,2},{2,6},{1... | collective-permute-start | bytes 172040 | tf_op jit(solution)/shard_map/ppermute | solution.py:28
  26.1 4.2 %collective-permute-start.7 = (bf16[2,112,128]{2,1,0:T(8,128)(2,1)S(1)}, bf16[2,112,128]{2,1,0:T(8,128)(2,1)S(1)}, u32[]{:S(2)}, u32[]{:S(2)}) collective-permute-start(bf16[2,112,128]{2,1,0:T(8,128)(2,1)S(1)} %add_convert_fusion), channel_id=1, source_target_pairs={{8,0},{12,4},{0,8},{4,12},{9,1},{13,5},{1,9},{5,13},{10,2},{14,6},... | collective-permute-start | bytes 172040 | tf_op jit(solution)/shard_map/ppermute | solution.py:28
  30.3 5.0 %collective-permute-start.9 = (bf16[2,4,112,128]{3,2,1,0:T(8,128)(2,1)S(1)}, bf16[2,4,112,128]{3,2,1,0:T(8,128)(2,1)S(1)}, u32[]{:S(2)}, u32[]{:S(2)}) collective-permute-start(bf16[2,4,112,128]{3,2,1,0:T(8,128)(2,1)S(1)} %get-tuple-element.34), channel_id=1, source_target_pairs={{64,0},{65,1},{66,2},{67,3},{68,4},{69,5},{70,6},{71,7},{72,8},{73... | collective-permute-start | bytes 688136 | tf_op jit(solution)/shard_map/ppermute | solution.py:37
  31.7 9.0 %collective-permute-start.13 = (bf16[2,4,112,128]{3,2,1,0:T(8,128)(2,1)S(1)}, bf16[2,4,112,128]{3,2,1,0:T(8,128)(2,1)S(1)}, u32[]{:S(2)}, u32[]{:S(2)}) collective-permute-start(bf16[2,4,112,128]{3,2,1,0:T(8,128)(2,1)S(1)} %get-tuple-element.34), channel_id=1, source_target_pairs={{192,0},{193,1},{194,2},{195,3},{196,4},{197,5},{198,6},{199,7},{2... | collective-permute-start | bytes 688136 | tf_op jit(solution)/shard_map/ppermute | solution.py:37
  35.3 6.4 %collective-permute-start.14 = (bf16[2,4,112,128]{3,2,1,0:T(8,128)(2,1)S(1)}, bf16[2,4,112,128]{3,2,1,0:T(8,128)(2,1)S(1)}, u32[]{:S(2)}, u32[]{:S(2)}) collective-permute-start(bf16[2,4,112,128]{3,2,1,0:T(8,128)(2,1)S(1)} %collective-permute-done.9), channel_id=1, source_target_pairs={{192,0},{193,1},{194,2},{195,3},{196,4},{197,5},{198,6},{199,7},{2... | collective-permute-start | bytes 688136 | tf_op jit(solution)/shard_map/ppermute | solution.py:37
  39.2 7.7 %collective-permute-start.10 = (bf16[2,2,4,112,128]{4,3,2,1,0:T(8,128)(2,1)S(1)}, bf16[2,2,4,112,128]{4,3,2,1,0:T(8,128)(2,1)S(1)}, u32[]{:S(2)}, u32[]{:S(2)}) collective-permute-start(bf16[2,2,4,112,128]{4,3,2,1,0:T(8,128)(2,1)S(1)} %pad_maximum_fusion.first), channel_id=1, source_target_pairs={{1,0},{0,1},{3,2},{2,3},{5,4},{4,5},{7,6},{6,7},{9,8},{8,9},{11,10... | collective-permute-start | bytes 1376264 | tf_op jit(solution)/shard_map/ppermute | solution.py:37
  39.6 11.3 %collective-permute-start.11 = (bf16[2,2,4,112,128]{4,3,2,1,0:T(8,128)(2,1)S(1)}, bf16[2,2,4,112,128]{4,3,2,1,0:T(8,128)(2,1)S(1)}, u32[]{:S(2)}, u32[]{:S(2)}) collective-permute-start(bf16[2,2,4,112,128]{4,3,2,1,0:T(8,128)(2,1)S(1)} %pad_maximum_fusion.first), channel_id=1, source_target_pairs={{3,0},{2,1},{1,2},{0,3},{7,4},{6,5},{5,6},{4,7},{11,8},{10,9},{9,1... | collective-permute-start | bytes 1376264 | tf_op jit(solution)/shard_map/ppermute | solution.py:37
  41.8 10.1 %collective-permute-start.15 = (bf16[2,2,4,112,128]{4,3,2,1,0:T(8,128)(2,1)S(1)}, bf16[2,2,4,112,128]{4,3,2,1,0:T(8,128)(2,1)S(1)}, u32[]{:S(2)}, u32[]{:S(2)}) collective-permute-start(bf16[2,2,4,112,128]{4,3,2,1,0:T(8,128)(2,1)S(1)} %pad_maximum_fusion.1.last), channel_id=1, source_target_pairs={{1,0},{0,1},{3,2},{2,3},{5,4},{4,5},{7,6},{6,7},{9,8},{8,9},{11,10... | collective-permute-start | bytes 1376264 | tf_op jit(solution)/shard_map/ppermute | solution.py:37
  41.9 13.7 %collective-permute-start.17 = (bf16[2,2,4,112,128]{4,3,2,1,0:T(8,128)(2,1)S(1)}, bf16[2,2,4,112,128]{4,3,2,1,0:T(8,128)(2,1)S(1)}, u32[]{:S(2)}, u32[]{:S(2)}) collective-permute-start(bf16[2,2,4,112,128]{4,3,2,1,0:T(8,128)(2,1)S(1)} %pad_maximum_fusion.1.last), channel_id=1, source_target_pairs={{3,0},{2,1},{1,2},{0,3},{7,4},{6,5},{5,6},{4,7},{11,8},{10,9},{9,1... | collective-permute-start | bytes 1376264 | tf_op jit(solution)/shard_map/ppermute | solution.py:37
  50.9 7.6 %collective-permute-start.12 = (bf16[2,2,4,112,128]{4,3,2,1,0:T(8,128)(2,1)S(1)}, bf16[2,2,4,112,128]{4,3,2,1,0:T(8,128)(2,1)S(1)}, u32[]{:S(2)}, u32[]{:S(2)}) collective-permute-start(bf16[2,2,4,112,128]{4,3,2,1,0:T(8,128)(2,1)S(1)} %collective-permute-done.11.three), channel_id=1, source_target_pairs={{1,0},{0,1},{3,2},{2,3},{5,4},{4,5},{7,6},{6,7},{9,8},{8,9},{11,10... | collective-permute-start | bytes 1376264 | tf_op jit(solution)/shard_map/ppermute | solution.py:37
  51.9 16.6 %collective-permute-start.16 = (bf16[2,2,4,112,128]{4,3,2,1,0:T(8,128)(2,1)S(1)}, bf16[2,2,4,112,128]{4,3,2,1,0:T(8,128)(2,1)S(1)}, u32[]{:S(2)}, u32[]{:S(2)}) collective-permute-start(bf16[2,2,4,112,128]{4,3,2,1,0:T(8,128)(2,1)S(1)} %collective-permute-done.15.one), channel_id=1, source_target_pairs={{3,0},{2,1},{1,2},{0,3},{7,4},{6,5},{5,6},{4,7},{11,8},{10,9},{9,1... | collective-permute-start | bytes 1376264 | tf_op jit(solution)/shard_map/ppermute | solution.py:37
  59.2 12.3 %collective-permute-start.19 = (bf16[512,384]{1,0:T(8,128)(2,1)S(1)}, bf16[512,384]{1,0:T(8,128)(2,1)S(1)}, u32[]{:S(2)}, u32[]{:S(2)}) collective-permute-start(bf16[512,384]{1,0:T(8,128)(2,1)S(1)} %get-tuple-element.32), channel_id=1, source_target_pairs={{16,0},{0,16},{17,1},{1,17},{18,2},{2,18},{19,3},{3,19},{20,4},{4,... | collective-permute-start | bytes 1179656 | tf_op jit(solution)/shard_map/ppermute | solution.py:24
  69.7 3.4 %collective-permute-start.18 = (bf16[512,384]{1,0:T(8,128)(2,1)S(1)}, bf16[512,384]{1,0:T(8,128)(2,1)S(1)}, u32[]{:S(2)}, u32[]{:S(2)}) collective-permute-start(bf16[512,384]{1,0:T(8,128)(2,1)S(1)} %shard_map.43), channel_id=1, source_target_pairs={{16,0},{0,16},{17,1},{1,17},{18,2},{2,18},{19,3},{3,19},{20,4},{4,... | collective-permute-start | bytes 1179656 | tf_op jit(solution)/shard_map/ppermute | solution.py:24

commit v10 on v9

--- a/solution.py
+++ b/solution.py
@@ -82,10 +82,6 @@
     return jnp.concatenate(halves, 1)
 
 
-def slabs(block):
-    return [block.at[i] for i in range(block.shape[0])]
-
-
 def rows(first, count=1):
     return pl.ds(first * 256, count * 256)
 
@@ -94,76 +90,76 @@
     return both[pl.ds(first, count)].reshape(count * 448, 768)
 
 
-def product_one(place, first, both, out):
-    @on_core(place, 0)
-    def _():
-        out[rows(0, 2)] = dot_t(by_x(*slabs(first)), both[0])
-
-    @on_core(place, 1)
-    def _():
-        out[rows(0)] = dot_t(by_y(*slabs(first)), deep(both, 0, 2))
-
-
-def product_two(place, last, one, three, both, start, out):
-    last, one, three = slabs(last), slabs(one), slabs(three)
-
+def product_one(place, own, near1, both, out):
+    @on_core(place, 0)
+    def _():
+        out[rows(0, 2)] = dot_t(by_x(own, near1), both[0])
+
+    @on_core(place, 1)
+    def _():
+        out[rows(0)] = dot_t(by_y(own, near1), deep(both, 0, 2))
+
+
+def product_two(place, near3, far, own1, near1, own3, near31, both, start, out):
     @on_core(place, 0)
     def _():
         out[rows(0, 2)] = (
-            start[rows(0, 2)] + dot_t(by_x(*one), both[1]) + dot_t(by_x(*three), both[2])
+            start[rows(0, 2)]
+            + dot_t(by_x(own1, near1), both[1])
+            + dot_t(by_x(own3, near31), both[2])
         )
-        out[rows(2, 2)] = dot_t(by_x(*last), both[0])
-
-    @on_core(place, 1)
-    def _():
-        out[rows(0)] = start[rows(0)] + dot_t(by_y(*last), deep(both, 2, 2))
-        out[rows(1)] = dot_t(by_y(*one), deep(both, 0, 2))
-        out[rows(2)] = dot_t(by_y(*three), deep(both, 0, 2))
-
-
-def product_three(place, one, three, both, start, out):
-    one, three = slabs(one), slabs(three)
-
+        out[rows(2, 2)] = dot_t(by_x(near3, far), both[0])
+
+    @on_core(place, 1)
+    def _():
+        out[rows(0)] = start[rows(0)] + dot_t(by_y(near3, far), deep(both, 2, 2))
+        out[rows(1)] = dot_t(by_y(own1, near1), deep(both, 0, 2))
+        out[rows(2)] = dot_t(by_y(own3, near31), deep(both, 0, 2))
+
+
+def product_three(place, near1, far1, near3, far3, both, start, out):
     @on_core(place, 0)
     def _():
         out[rows(0, 2)] = start[rows(0, 2)]
         out[rows(2, 2)] = (
-            start[rows(2, 2)] + dot_t(by_x(*one), both[1]) + dot_t(by_x(*three), both[2])
+            start[rows(2, 2)]
+            + dot_t(by_x(near1, far1), both[1])
+            + dot_t(by_x(near3, far3), both[2])
         )
 
     @on_core(place, 1)
     def _():
         out[rows(0)] = start[rows(0)]
-        out[rows(1)] = start[rows(1)] + dot_t(by_y(*one), deep(both, 2, 2))
-        out[rows(2)] = start[rows(2)] + dot_t(by_y(*three), deep(both, 2, 2))
-
-
-def product_four(place, first, both, start, mine, theirs):
+        out[rows(1)] = start[rows(1)] + dot_t(by_y(near1, far1), deep(both, 2, 2))
+        out[rows(2)] = start[rows(2)] + dot_t(by_y(near3, far3), deep(both, 2, 2))
+
+
+def product_four(place, own, near1, both, start, mine, theirs):
     def keep(total):
         mine[...] = total[:, :384].astype(BF16)
         theirs[...] = total[:, 384:].astype(BF16)
 
     @on_core(place, 0)
     def _():
-        keep(start[rows(0, 2)] + dot_t(by_x(*slabs(first)), both[3]))
+        keep(start[rows(0, 2)] + dot_t(by_x(own, near1), both[3]))
 
     @on_core(place, 1)
     def _():
         keep(start[rows(0, 2)])
 
 
-def product_five(side, place, first, last, both, start, out):
+def product_five(side, place, own, near1, near3, far, both, start, out):
     columns = pl.ds(side * 384, 384)
 
     @on_core(place, 0)
     def _():
-        total = start[rows(2, 2), columns] + dot_t(by_x(*slabs(last)), both[3, :, columns])
+        total = start[rows(2, 2), columns] + dot_t(by_x(near3, far), both[3, :, columns])
         out[...] = total.astype(BF16)
 
     @on_core(place, 1)
     def _():
         out[rows(0)] = start[rows(2), columns].astype(BF16)
-        left = by_y(*slabs(first), *slabs(last))
+        left = by_y(own, near1, near3, far)
         out[rows(1)] = dot_t(left, both[:, :, columns].reshape(1792, 384)).astype(BF16)
 
 
@@ -216,7 +212,7 @@
         (place, keep, fetch(send, "core", 2, 1)),
         (VMEM,) * 4,
     )
-    for bits in (1, 3, 2):
+    for bits in (3, 2, 1):
         part = part + swap(away[bits - 1], "x", 4, bits).astype(F32)
 
     other = fetch(pair_conduction, "core", 2, 1)
@@ -230,34 +226,37 @@
 
     near1, near3 = turn(own, 0, 1), turn(own, 0, 3)
     far = turn(near1, 0, 3)
-    first = jnp.stack([own, near1])
+    one_own, three_own = turn(own, 1, 1), turn(own, 1, 3)
     total = jax.ShapeDtypeStruct((1024, 768), F32)
-    total_one = call(product_one, total, (place, first, both))
-    first, total_one = lax.optimization_barrier((first, total_one))
-    one1, three1 = turn(first, 1, 1), turn(first, 1, 3)
-    last = jnp.stack([near3, far])
-    one2, three2 = turn(last, 1, 1), turn(last, 1, 3)
-    one1, three1 = lax.optimization_barrier((one1, three1))
-    far1, far2 = turn(three1, 1, 1), turn(one2, 1, 3)
+    total_one = call(product_one, total, (place, own, near1, both))
+    one_near1, three_near1 = turn(near1, 1, 1), turn(near1, 1, 3)
+    one_near3, three_near3 = turn(near3, 1, 1), turn(near3, 1, 3)
+    one_far, three_far = turn(far, 1, 1), turn(far, 1, 3)
+    far_own, far_near1 = turn(three_own, 1, 1), turn(three_near1, 1, 1)
+    far_near3, far_far = turn(one_near3, 1, 3), turn(one_far, 1, 3)
     total_two = call(
         product_two,
         total,
-        (place, last, one1, three1, both, total_one),
-        input_output_aliases={5: 0},
+        (place, near3, far, one_own, one_near1, three_own, three_near1, both, total_one),
+        input_output_aliases={8: 0},
     )
     total_three = call(
         product_three,
         total,
-        (place, one2, three2, both, total_two),
-        input_output_aliases={4: 0},
+        (place, one_near3, one_far, three_near3, three_far, both, total_two),
+        input_output_aliases={6: 0},
     )
     half = jax.ShapeDtypeStruct((512, 384), BF16)
     mine1, theirs1 = call(
-        product_four, (half, half), (place, far1, both, total_three), (VMEM, VMEM)
+        product_four, (half, half), (place, far_own, far_near1, both, total_three), (VMEM, VMEM)
     )
     theirs1 = fetch(theirs1, "core", 2, 1)
     mine2, theirs2 = (
-        call(functools.partial(product_five, side), half, (place, far1, far2, both, total_three))
+        call(
+            functools.partial(product_five, side),
+            half,
+            (place, far_own, far_near1, far_near3, far_far, both, total_three),
+        )
         for side in (0, 1)
     )
     theirs2 = fetch(theirs2, "core", 2, 1)

time: 74.8 us -> 71.6 us (0.957)
  waiting for transfers between devices: 20.4 us -> 9.75 us
  starting transfers between devices: 37 us -> 44.5 us
    ppermute x9 -> x15, starting transfers between devices: 9.84 us -> 21.1 us  [turn(): return lax.ppermute(block, ROW + COL, pairs)]
    ppermute x9 -> x15, waiting for transfers between devices: 13 us -> 2.3 us  [turn(): return lax.ppermute(block, ROW + COL, pairs)]
    ppermute x4, starting transfers between devices: 13.2 us -> 10.3 us  [fetch(): lax.ppermute(block, axis, [((i + ahead) % size, i) for i in range(size)])]
    ppermute x7, starting transfers between devices: 14 us -> 13.2 us  [swap(): return lax.ppermute(block, axis, [(i ^ bits, i) for i in range(size)])]
  transfers between devices with their start and end apart: 20 -> 26, of which waited for: 13 -> 10; matrix products, arithmetic and copies ran while one was open for 0% -> 0% of each run, Pallas kernels for 16% -> 17%
where the time goes in v10:
time: 71.6 us; the launch traced here: 71.4 us
  starting transfers between devices  44.5 us (62%)
  Pallas kernels  13.4 us (19%)
  waiting for transfers between devices  9.75 us (14%)
  local copies, waits for them, and re-layouts  3.11 us (4%)
    ppermute x15, starting transfers between devices, turn(): return lax.ppermute(block, ROW + COL, pairs)  21.1 us
    pallas_call x11, Pallas kernels, call(): pl.pallas_call(kernel, out_shape=out_shape, in_specs=specs or [SMEM] + [V...  13.4 us
    ppermute x7, starting transfers between devices, swap(): return lax.ppermute(block, axis, [(i ^ bits, i) for i in range(size)])  13.2 us
    ppermute x4, starting transfers between devices, fetch(): lax.ppermute(block, axis, [((i + ahead) % size, i) for i in range(size)])  10.3 us
    ppermute x7, waiting for transfers between devices, swap(): return lax.ppermute(block, axis, [(i ^ bits, i) for i in range(size)])  5.65 us
    unnamed x6, local copies, waits for them, and re-layouts  3.11 us
    ppermute x15, waiting for transfers between devices, turn(): return lax.ppermute(block, ROW + COL, pairs)  2.3 us
    ppermute x4, waiting for transfers between devices, fetch(): lax.ppermute(block, axis, [((i + ahead) % size, i) for i in range(size)])  1.81 us
  transfers between devices with their start and end apart: 26, of which 10 were waited for; matrix products, arithmetic and copies ran while one was open for 0% of the time, Pallas kernels for 17%

profile of v10, /device:TPU:1, one launch (start us, length us, event | category | flops | bytes accessed | tf_op | source)
XLA Modules:
  0.0 71.4 jit_solution(9212635695237721543)
XLA Ops:
  0.0 3.2 %collective-permute-start.5 = (bf16[1792,384]{1,0:T(8,128)(2,1)}, bf16[1792,384]{1,0:T(8,128)(2,1)S(1)}, u32[]{:S(2)}, u32[]{:S(2)}) collective-permute-start(bf16[1792,384]{1,0:T(8,128)(2,1)} %own.1), channel_id=1, source_target_pairs={{16,0},{0,16},{17,1},{1,17},{18,2},{2,18},{19,3},{3,19},{20,4},{4,... | collective-permute-start | bytes 4128776 | tf_op jit(solution)/shard_map/ppermute | solution.py:24
  3.3 1.0 %copy-done.1 = bf16[112,2048]{1,0:T(8,128)(2,1)S(1)} copy-done((bf16[112,2048]{1,0:T(8,128)(2,1)S(1)}, bf16[112,2048]{1,0:T(8,128)(2,1)}, u32[]{:S(2)}) %copy-start.1) | copy-done | bytes 458776
  5.1 1.0 %shard_map.37 = (f32[8,112,128]{2,1,0:T(8,128)S(1)}, f32[8,112,128]{2,1,0:T(8,128)S(1)}) custom-call(s32[4]{0:T(128)S(1)} %pad_add_fusion.place, bf16[112,112]{1,0:T(8,128)(2,1)S(1)} %copy-done.2, bf16[112,2048]{1,0:T(8,128)(2,1)S(1)} %copy-done.1), custom_call_target="tpu_custom_call" | custom-call | tf_op jit(solution)/shard_map/pallas_call | solution.py:190
  6.2 1.8 %collective-permute-done.received = f32[8,112,128]{2,1,0:T(8,128)S(1)} collective-permute-done((f32[8,112,128]{2,1,0:T(8,128)S(1)}, f32[8,112,128]{2,1,0:T(8,128)S(1)}, u32[]{:S(2)}, u32[]{:S(2)}) %collective-permute-start) | collective-permute-done | bytes 458784 | tf_op jit(solution)/shard_map/ppermute | solution.py:24
  8.6 0.8 %collective-permute-start.1 = (bf16[2,112,128]{2,1,0:T(8,128)(2,1)S(1)}, bf16[2,112,128]{2,1,0:T(8,128)(2,1)S(1)}, u32[]{:S(2)}, u32[]{:S(2)}) collective-permute-start(bf16[2,112,128]{2,1,0:T(8,128)(2,1)S(1)} %get-tuple-element.18), channel_id=1, source_target_pairs={{192,0},{128,64},{64,128},{0,192},{193,1},{129,65},{65,129},{1,193... | collective-permute-start | bytes 172040 | tf_op jit(solution)/shard_map/ppermute | solution.py:28
  9.9 2.0 %collective-permute-start.3 = (bf16[2,112,128]{2,1,0:T(8,128)(2,1)S(1)}, bf16[2,112,128]{2,1,0:T(8,128)(2,1)S(1)}, u32[]{:S(2)}, u32[]{:S(2)}) collective-permute-start(bf16[2,112,128]{2,1,0:T(8,128)(2,1)S(1)} %get-tuple-element.20), channel_id=1, source_target_pairs={{64,0},{0,64},{192,128},{128,192},{65,1},{1,65},{193,129},{129,193... | collective-permute-start | bytes 172040 | tf_op jit(solution)/shard_map/ppermute | solution.py:28
  11.9 1.0 %collective-permute-done.1 = bf16[2,112,128]{2,1,0:T(8,128)(2,1)S(1)} collective-permute-done((bf16[2,112,128]{2,1,0:T(8,128)(2,1)S(1)}, bf16[2,112,128]{2,1,0:T(8,128)(2,1)S(1)}, u32[]{:S(2)}, u32[]{:S(2)}) %collective-permute-start.1) | collective-permute-done | bytes 57376 | tf_op jit(solution)/shard_map/ppermute | solution.py:28
  12.9 1.1 %collective-permute-done.2 = bf16[2,112,128]{2,1,0:T(8,128)(2,1)S(1)} collective-permute-done((bf16[2,112,128]{2,1,0:T(8,128)(2,1)S(1)}, bf16[2,112,128]{2,1,0:T(8,128)(2,1)S(1)}, u32[]{:S(2)}, u32[]{:S(2)}) %collective-permute-start.2) | collective-permute-done | bytes 57376 | tf_op jit(solution)/shard_map/ppermute | solution.py:28
  14.8 6.2 %collective-permute-start.4 = (bf16[2,112,128]{2,1,0:T(8,128)(2,1)S(1)}, bf16[2,112,128]{2,1,0:T(8,128)(2,1)S(1)}, u32[]{:S(2)}, u32[]{:S(2)}) collective-permute-start(bf16[2,112,128]{2,1,0:T(8,128)(2,1)S(1)} %fusion), channel_id=1, source_target_pairs={{32,0},{0,32},{33,1},{1,33},{34,2},{2,34},{35,3},{3,35},{36,4},{4,... | collective-permute-start | bytes 172040 | tf_op jit(solution)/shard_map/ppermute | solution.py:28
  21.0 1.3 %copy-done = bf16[1792,384]{1,0:T(8,128)(2,1)S(1)} copy-done((bf16[1792,384]{1,0:T(8,128)(2,1)S(1)}, bf16[1792,384]{1,0:T(8,128)(2,1)}, u32[]{:S(2)}) %copy-start) | copy-done | bytes 1376280
  23.2 2.4 %collective-permute-start.8 = (bf16[2,112,128]{2,1,0:T(8,128)(2,1)S(1)}, bf16[2,112,128]{2,1,0:T(8,128)(2,1)S(1)}, u32[]{:S(2)}, u32[]{:S(2)}) collective-permute-start(bf16[2,112,128]{2,1,0:T(8,128)(2,1)S(1)} %add_convert_fusion), channel_id=1, source_target_pairs={{12,0},{8,4},{4,8},{0,12},{13,1},{9,5},{5,9},{1,13},{14,2},{10,6},... | collective-permute-start | bytes 172040 | tf_op jit(solution)/shard_map/ppermute | solution.py:28
  25.5 1.3 %collective-permute-start.7 = (bf16[2,112,128]{2,1,0:T(8,128)(2,1)S(1)}, bf16[2,112,128]{2,1,0:T(8,128)(2,1)S(1)}, u32[]{:S(2)}, u32[]{:S(2)}) collective-permute-start(bf16[2,112,128]{2,1,0:T(8,128)(2,1)S(1)} %add_convert_fusion), channel_id=1, source_target_pairs={{8,0},{12,4},{0,8},{4,12},{9,1},{13,5},{1,9},{5,13},{10,2},{14,6},... | collective-permute-start | bytes 172040 | tf_op jit(solution)/shard_map/ppermute | solution.py:28
  26.8 1.3 %collective-permute-done.8 = bf16[2,112,128]{2,1,0:T(8,128)(2,1)S(1)} collective-permute-done((bf16[2,112,128]{2,1,0:T(8,128)(2,1)S(1)}, bf16[2,112,128]{2,1,0:T(8,128)(2,1)S(1)}, u32[]{:S(2)}, u32[]{:S(2)}) %collective-permute-start.8) | collective-permute-done | bytes 57376 | tf_op jit(solution)/shard_map/ppermute | solution.py:28
  28.7 0.9 %collective-permute-done.7 = bf16[2,112,128]{2,1,0:T(8,128)(2,1)S(1)} collective-permute-done((bf16[2,112,128]{2,1,0:T(8,128)(2,1)S(1)}, bf16[2,112,128]{2,1,0:T(8,128)(2,1)S(1)}, u32[]{:S(2)}, u32[]{:S(2)}) %collective-permute-start.7) | collective-permute-done | bytes 57376 | tf_op jit(solution)/shard_map/ppermute | solution.py:28
  29.7 1.4 %collective-permute-start.11 = (bf16[2,4,112,128]{3,2,1,0:T(8,128)(2,1)S(1)}, bf16[2,4,112,128]{3,2,1,0:T(8,128)(2,1)S(1)}, u32[]{:S(2)}, u32[]{:S(2)}) collective-permute-start(bf16[2,4,112,128]{3,2,1,0:T(8,128)(2,1)S(1)} %pad_maximum_fusion.own), channel_id=1, source_target_pairs={{64,0},{65,1},{66,2},{67,3},{68,4},{69,5},{70,6},{71,7},{72,8},{73... | collective-permute-start | bytes 688136 | tf_op jit(solution)/shard_map/ppermute | solution.py:37
  31.1 1.9 %collective-permute-start.14 = (bf16[2,4,112,128]{3,2,1,0:T(8,128)(2,1)S(1)}, bf16[2,4,112,128]{3,2,1,0:T(8,128)(2,1)S(1)}, u32[]{:S(2)}, u32[]{:S(2)}) collective-permute-start(bf16[2,4,112,128]{3,2,1,0:T(8,128)(2,1)S(1)} %pad_maximum_fusion.own), channel_id=1, source_target_pairs={{192,0},{193,1},{194,2},{195,3},{196,4},{197,5},{198,6},{199,7},{2... | collective-permute-start | bytes 688136 | tf_op jit(solution)/shard_map/ppermute | solution.py:37
  33.0 4.1 %collective-permute-start.9 = (bf16[2,4,112,128]{3,2,1,0:T(8,128)(2,1)S(1)}, bf16[2,4,112,128]{3,2,1,0:T(8,128)(2,1)S(1)}, u32[]{:S(2)}, u32[]{:S(2)}) collective-permute-start(bf16[2,4,112,128]{3,2,1,0:T(8,128)(2,1)S(1)} %pad_maximum_fusion.own), channel_id=1, source_target_pairs={{3,0},{2,1},{1,2},{0,3},{7,4},{6,5},{5,6},{4,7},{11,8},{10,9},{9,1... | collective-permute-start | bytes 688136 | tf_op jit(solution)/shard_map/ppermute | solution.py:37
  37.8 1.4 %collective-permute-start.12 = (bf16[2,4,112,128]{3,2,1,0:T(8,128)(2,1)S(1)}, bf16[2,4,112,128]{3,2,1,0:T(8,128)(2,1)S(1)}, u32[]{:S(2)}, u32[]{:S(2)}) collective-permute-start(bf16[2,4,112,128]{3,2,1,0:T(8,128)(2,1)S(1)} %collective-permute-done.11.near1), channel_id=1, source_target_pairs={{3,0},{2,1},{1,2},{0,3},{7,4},{6,5},{5,6},{4,7},{11,8},{10,9},{9,1... | collective-permute-start | bytes 688136 | tf_op jit(solution)/shard_map/ppermute | solution.py:37
  39.2 1.9 %collective-permute-start.23 = (bf16[2,4,112,128]{3,2,1,0:T(8,128)(2,1)S(1)}, bf16[2,4,112,128]{3,2,1,0:T(8,128)(2,1)S(1)}, u32[]{:S(2)}, u32[]{:S(2)}) collective-permute-start(bf16[2,4,112,128]{3,2,1,0:T(8,128)(2,1)S(1)} %collective-permute-done.11.near1), channel_id=1, source_target_pairs={{1,0},{0,1},{3,2},{2,3},{5,4},{4,5},{7,6},{6,7},{9,8},{8,9},{11,10... | collective-permute-start | bytes 688136 | tf_op jit(solution)/shard_map/ppermute | solution.py:37
  41.9 3.4 %collective-permute-start.20 = (bf16[2,4,112,128]{3,2,1,0:T(8,128)(2,1)S(1)}, bf16[2,4,112,128]{3,2,1,0:T(8,128)(2,1)S(1)}, u32[]{:S(2)}, u32[]{:S(2)}) collective-permute-start(bf16[2,4,112,128]{3,2,1,0:T(8,128)(2,1)S(1)} %collective-permute-done.14.near3), channel_id=1, source_target_pairs={{3,0},{2,1},{1,2},{0,3},{7,4},{6,5},{5,6},{4,7},{11,8},{10,9},{9,1... | collective-permute-start | bytes 688136 | tf_op jit(solution)/shard_map/ppermute | solution.py:37
  45.8 2.0 %collective-permute-start.21 = (bf16[2,4,112,128]{3,2,1,0:T(8,128)(2,1)S(1)}, bf16[2,4,112,128]{3,2,1,0:T(8,128)(2,1)S(1)}, u32[]{:S(2)}, u32[]{:S(2)}) collective-permute-start(bf16[2,4,112,128]{3,2,1,0:T(8,128)(2,1)S(1)} %collective-permute-done.17.far), channel_id=1, source_target_pairs={{3,0},{2,1},{1,2},{0,3},{7,4},{6,5},{5,6},{4,7},{11,8},{10,9},{9,1... | collective-permute-start | bytes 688136 | tf_op jit(solution)/shard_map/ppermute | solution.py:37
  47.9 1.5 %collective-permute-start.13 = (bf16[2,4,112,128]{3,2,1,0:T(8,128)(2,1)S(1)}, bf16[2,4,112,128]{3,2,1,0:T(8,128)(2,1)S(1)}, u32[]{:S(2)}, u32[]{:S(2)}) collective-permute-start(bf16[2,4,112,128]{3,2,1,0:T(8,128)(2,1)S(1)} %collective-permute-done.12.near31), channel_id=1, source_target_pairs={{1,0},{0,1},{3,2},{2,3},{5,4},{4,5},{7,6},{6,7},{9,8},{8,9},{11,10... | collective-permute-start | bytes 688136 | tf_op jit(solution)/shard_map/ppermute | solution.py:37
  49.3 1.1 %collective-permute-done.20.near3 = bf16[2,4,112,128]{3,2,1,0:T(8,128)(2,1)S(1)} collective-permute-done((bf16[2,4,112,128]{3,2,1,0:T(8,128)(2,1)S(1)}, bf16[2,4,112,128]{3,2,1,0:T(8,128)(2,1)S(1)}, u32[]{:S(2)}, u32[]{:S(2)}) %collective-permute-start.20) | collective-permute-done | bytes 229408 | tf_op jit(solution)/shard_map/ppermute | solution.py:37
  50.4 2.3 %collective-permute-start.16 = (bf16[2,4,112,128]{3,2,1,0:T(8,128)(2,1)S(1)}, bf16[2,4,112,128]{3,2,1,0:T(8,128)(2,1)S(1)}, u32[]{:S(2)}, u32[]{:S(2)}) collective-permute-start(bf16[2,4,112,128]{3,2,1,0:T(8,128)(2,1)S(1)} %collective-permute-done.15.near1), channel_id=1, source_target_pairs={{3,0},{2,1},{1,2},{0,3},{7,4},{6,5},{5,6},{4,7},{11,8},{10,9},{9,1... | collective-permute-start | bytes 688136 | tf_op jit(solution)/shard_map/ppermute | solution.py:37
  53.1 1.2 %shard_map.40.start = f32[1024,768]{1,0:T(8,128)S(1)} custom-call(s32[4]{0:T(128)S(1)} %pad_add_fusion.place, bf16[2,4,112,128]{3,2,1,0:T(8,128)(2,1)S(1)} %pad_maximum_fusion.own, bf16[2,4,112,128]{3,2,1,0:T(8,128)(2,1)S(1)} %collective-permute-done.11.near1, bf16[4,448,768]{2,1,0:T(8,128)(2,1)S(1)} %shard_map.39.both), custom_call_target="tpu_custom_call" | custom-call | tf_op jit(solution)/shard_map/pallas_call | solution.py:190
  54.2 2.1 %shard_map.41.start = f32[1024,768]{1,0:T(8,128)S(1)} custom-call(s32[4]{0:T(128)S(1)} %pad_add_fusion.place, bf16[2,4,112,128]{3,2,1,0:T(8,128)(2,1)S(1)} %collective-permute-done.14.near3, bf16[2,4,112,128]{3,2,1,0:T(8,128)(2,1)S(1)} %collective-permute-done.17.far, ...), custom_call_target="tpu_custom_call", output_to_operand_aliasing={{}: (8, {})} | custom-call | tf_op jit(solution)/shard_map/pallas_call | solution.py:190
  56.4 1.8 %shard_map.42.start = f32[1024,768]{1,0:T(8,128)S(1)} custom-call(s32[4]{0:T(128)S(1)} %pad_add_fusion.place, bf16[2,4,112,128]{3,2,1,0:T(8,128)(2,1)S(1)} %collective-permute-done.15.near1, bf16[2,4,112,128]{3,2,1,0:T(8,128)(2,1)S(1)} %collective-permute-done.18.far1, ...), custom_call_target="tpu_custom_call", output_to_operand_aliasing={{}: (6, {})} | custom-call | tf_op jit(solution)/shard_map/pallas_call | solution.py:190
  58.8 6.9 %collective-permute-start.25 = (bf16[512,384]{1,0:T(8,128)(2,1)S(1)}, bf16[512,384]{1,0:T(8,128)(2,1)S(1)}, u32[]{:S(2)}, u32[]{:S(2)}) collective-permute-start(bf16[512,384]{1,0:T(8,128)(2,1)S(1)} %get-tuple-element.24), channel_id=1, source_target_pairs={{16,0},{0,16},{17,1},{1,17},{18,2},{2,18},{19,3},{3,19},{20,4},{4,... | collective-permute-start | bytes 1179656 | tf_op jit(solution)/shard_map/ppermute | solution.py:24
  65.7 1.2 %shard_map.43 = bf16[512,384]{1,0:T(8,128)(2,1)S(1)} custom-call(s32[4]{0:T(128)S(1)} %pad_add_fusion.place, bf16[2,4,112,128]{3,2,1,0:T(8,128)(2,1)S(1)} %collective-permute-done.10.own, bf16[2,4,112,128]{3,2,1,0:T(8,128)(2,1)S(1)} %collective-permute-done.13.near1, bf16[2,4,112,128]{3,2,1,0:T(8,128)(2,1)S(1)} %collective-permute-done.16.near3, ...), custom_call_target="tpu_custom_call" | custom-call | tf_op jit(solution)/shard_map/pallas_call | solution.py:190
  67.0 1.2 %shard_map.45.mine2 = bf16[512,384]{1,0:T(8,128)(2,1)S(1)} custom-call(s32[4]{0:T(128)S(1)} %pad_add_fusion.place, bf16[2,4,112,128]{3,2,1,0:T(8,128)(2,1)S(1)} %collective-permute-done.10.own, bf16[2,4,112,128]{3,2,1,0:T(8,128)(2,1)S(1)} %collective-permute-done.13.near1, bf16[2,4,112,128]{3,2,1,0:T(8,128)(2,1)S(1)} %collective-permute-done.16.near3, ...), custom_call_target="tpu_custom_call" | custom-call | tf_op jit(solution)/shard_map/pallas_call | solution.py:190
  68.2 1.6 %shard_map.46.given = bf16[2048,384]{1,0:T(8,128)(2,1)} custom-call(s32[4]{0:T(128)S(1)} %pad_add_fusion.place, bf16[512,384]{1,0:T(8,128)(2,1)S(1)} %get-tuple-element.23.mine1, bf16[512,384]{1,0:T(8,128)(2,1)S(1)} %shard_map.45.mine2, bf16[512,384]{1,0:T(8,128)(2,1)S(1)} %collective-permute-done.25.theirs1), custom_call_target="tpu_custom_call" | custom-call | tf_op jit(solution)/shard_map/pallas_call | solution.py:190
  69.9 1.3 %shard_map.47 = bf16[2048,384]{1,0:T(8,128)(2,1)} custom-call(s32[4]{0:T(128)S(1)} %pad_add_fusion.place, bf16[512,384]{1,0:T(8,128)(2,1)S(1)} %collective-permute-done.24.theirs2, bf16[2048,384]{1,0:T(8,128)(2,1)} %shard_map.46.given), custom_call_target="tpu_custom_call", output_to_operand_aliasing={{}: (2, {})} | custom-call | tf_op jit(solution)/shard_map/pallas_call | solution.py:190
  (41 shorter events, 7.5 us)
Async XLA Ops:
  0.0 21.0 %collective-permute-start.5 = (bf16[1792,384]{1,0:T(8,128)(2,1)}, bf16[1792,384]{1,0:T(8,128)(2,1)S(1)}, u32[]{:S(2)}, u32[]{:S(2)}) collective-permute-start(bf16[1792,384]{1,0:T(8,128)(2,1)} %own.1), channel_id=1, source_target_pairs={{16,0},{0,16},{17,1},{1,17},{18,2},{2,18},{19,3},{3,19},{20,4},{4,... | collective-permute-start | bytes 4128776 | tf_op jit(solution)/shard_map/ppermute | solution.py:24
  3.3 1.0 %copy-start.1 = (bf16[112,2048]{1,0:T(8,128)(2,1)S(1)}, bf16[112,2048]{1,0:T(8,128)(2,1)}, u32[]{:S(2)}) copy-start(bf16[112,2048]{1,0:T(8,128)(2,1)} %panel.1) | copy-start | bytes 1376260
  4.3 0.7 %copy-start.2 = (bf16[112,112]{1,0:T(8,128)(2,1)S(1)}, bf16[112,112]{1,0:T(8,128)(2,1)}, u32[]{:S(2)}) copy-start(bf16[112,112]{1,0:T(8,128)(2,1)} %screening.1) | copy-start | bytes 75268
  6.1 1.9 %collective-permute-start = (f32[8,112,128]{2,1,0:T(8,128)S(1)}, f32[8,112,128]{2,1,0:T(8,128)S(1)}, u32[]{:S(2)}, u32[]{:S(2)}) collective-permute-start(f32[8,112,128]{2,1,0:T(8,128)S(1)} %get-tuple-element.16), channel_id=1, source_target_pairs={{16,0},{0,16},{17,1},{1,17},{18,2},{2,18},{19,3},{3,19},{20,4},{4,... | collective-permute-start | bytes 1376264 | tf_op jit(solution)/shard_map/ppermute | solution.py:24
  8.6 4.3 %collective-permute-start.1 = (bf16[2,112,128]{2,1,0:T(8,128)(2,1)S(1)}, bf16[2,112,128]{2,1,0:T(8,128)(2,1)S(1)}, u32[]{:S(2)}, u32[]{:S(2)}) collective-permute-start(bf16[2,112,128]{2,1,0:T(8,128)(2,1)S(1)} %get-tuple-element.18), channel_id=1, source_target_pairs={{192,0},{128,64},{64,128},{0,192},{193,1},{129,65},{65,129},{1,193... | collective-permute-start | bytes 172040 | tf_op jit(solution)/shard_map/ppermute | solution.py:28
  9.4 4.6 %collective-permute-start.2 = (bf16[2,112,128]{2,1,0:T(8,128)(2,1)S(1)}, bf16[2,112,128]{2,1,0:T(8,128)(2,1)S(1)}, u32[]{:S(2)}, u32[]{:S(2)}) collective-permute-start(bf16[2,112,128]{2,1,0:T(8,128)(2,1)S(1)} %get-tuple-element.19), channel_id=1, source_target_pairs={{128,0},{192,64},{0,128},{64,192},{129,1},{193,65},{1,129},{65,193... | collective-permute-start | bytes 172040 | tf_op jit(solution)/shard_map/ppermute | solution.py:28
  9.9 4.8 %collective-permute-start.3 = (bf16[2,112,128]{2,1,0:T(8,128)(2,1)S(1)}, bf16[2,112,128]{2,1,0:T(8,128)(2,1)S(1)}, u32[]{:S(2)}, u32[]{:S(2)}) collective-permute-start(bf16[2,112,128]{2,1,0:T(8,128)(2,1)S(1)} %get-tuple-element.20), channel_id=1, source_target_pairs={{64,0},{0,64},{192,128},{128,192},{65,1},{1,65},{193,129},{129,193... | collective-permute-start | bytes 172040 | tf_op jit(solution)/shard_map/ppermute | solution.py:28
  14.8 8.3 %collective-permute-start.4 = (bf16[2,112,128]{2,1,0:T(8,128)(2,1)S(1)}, bf16[2,112,128]{2,1,0:T(8,128)(2,1)S(1)}, u32[]{:S(2)}, u32[]{:S(2)}) collective-permute-start(bf16[2,112,128]{2,1,0:T(8,128)(2,1)S(1)} %fusion), channel_id=1, source_target_pairs={{32,0},{0,32},{33,1},{1,33},{34,2},{2,34},{35,3},{3,35},{36,4},{4,... | collective-permute-start | bytes 172040 | tf_op jit(solution)/shard_map/ppermute | solution.py:28
  21.0 1.3 %copy-start = (bf16[1792,384]{1,0:T(8,128)(2,1)S(1)}, bf16[1792,384]{1,0:T(8,128)(2,1)}, u32[]{:S(2)}) copy-start(bf16[1792,384]{1,0:T(8,128)(2,1)} %own.1) | copy-start | bytes 4128772
  23.2 4.9 %collective-permute-start.8 = (bf16[2,112,128]{2,1,0:T(8,128)(2,1)S(1)}, bf16[2,112,128]{2,1,0:T(8,128)(2,1)S(1)}, u32[]{:S(2)}, u32[]{:S(2)}) collective-permute-start(bf16[2,112,128]{2,1,0:T(8,128)(2,1)S(1)} %add_convert_fusion), channel_id=1, source_target_pairs={{12,0},{8,4},{4,8},{0,12},{13,1},{9,5},{5,9},{1,13},{14,2},{10,6},... | collective-permute-start | bytes 172040 | tf_op jit(solution)/shard_map/ppermute | solution.py:28
  25.5 3.2 %collective-permute-start.6 = (bf16[2,112,128]{2,1,0:T(8,128)(2,1)S(1)}, bf16[2,112,128]{2,1,0:T(8,128)(2,1)S(1)}, u32[]{:S(2)}, u32[]{:S(2)}) collective-permute-start(bf16[2,112,128]{2,1,0:T(8,128)(2,1)S(1)} %add_convert_fusion), channel_id=1, source_target_pairs={{4,0},{0,4},{12,8},{8,12},{5,1},{1,5},{13,9},{9,13},{6,2},{2,6},{1... | collective-permute-start | bytes 172040 | tf_op jit(solution)/shard_map/ppermute | solution.py:28
  25.5 4.1 %collective-permute-start.7 = (bf16[2,112,128]{2,1,0:T(8,128)(2,1)S(1)}, bf16[2,112,128]{2,1,0:T(8,128)(2,1)S(1)}, u32[]{:S(2)}, u32[]{:S(2)}) collective-permute-start(bf16[2,112,128]{2,1,0:T(8,128)(2,1)S(1)} %add_convert_fusion), channel_id=1, source_target_pairs={{8,0},{12,4},{0,8},{4,12},{9,1},{13,5},{1,9},{5,13},{10,2},{14,6},... | collective-permute-start | bytes 172040 | tf_op jit(solution)/shard_map/ppermute | solution.py:28
  29.7 7.3 %collective-permute-start.11 = (bf16[2,4,112,128]{3,2,1,0:T(8,128)(2,1)S(1)}, bf16[2,4,112,128]{3,2,1,0:T(8,128)(2,1)S(1)}, u32[]{:S(2)}, u32[]{:S(2)}) collective-permute-start(bf16[2,4,112,128]{3,2,1,0:T(8,128)(2,1)S(1)} %pad_maximum_fusion.own), channel_id=1, source_target_pairs={{64,0},{65,1},{66,2},{67,3},{68,4},{69,5},{70,6},{71,7},{72,8},{73... | collective-permute-start | bytes 688136 | tf_op jit(solution)/shard_map/ppermute | solution.py:37
  31.1 8.2 %collective-permute-start.14 = (bf16[2,4,112,128]{3,2,1,0:T(8,128)(2,1)S(1)}, bf16[2,4,112,128]{3,2,1,0:T(8,128)(2,1)S(1)}, u32[]{:S(2)}, u32[]{:S(2)}) collective-permute-start(bf16[2,4,112,128]{3,2,1,0:T(8,128)(2,1)S(1)} %pad_maximum_fusion.own), channel_id=1, source_target_pairs={{192,0},{193,1},{194,2},{195,3},{196,4},{197,5},{198,6},{199,7},{2... | collective-permute-start | bytes 688136 | tf_op jit(solution)/shard_map/ppermute | solution.py:37
  33.0 8.2 %collective-permute-start.22 = (bf16[2,4,112,128]{3,2,1,0:T(8,128)(2,1)S(1)}, bf16[2,4,112,128]{3,2,1,0:T(8,128)(2,1)S(1)}, u32[]{:S(2)}, u32[]{:S(2)}) collective-permute-start(bf16[2,4,112,128]{3,2,1,0:T(8,128)(2,1)S(1)} %pad_maximum_fusion.own), channel_id=1, source_target_pairs={{1,0},{0,1},{3,2},{2,3},{5,4},{4,5},{7,6},{6,7},{9,8},{8,9},{11,10... | collective-permute-start | bytes 688136 | tf_op jit(solution)/shard_map/ppermute | solution.py:37
  33.0 9.0 %collective-permute-start.9 = (bf16[2,4,112,128]{3,2,1,0:T(8,128)(2,1)S(1)}, bf16[2,4,112,128]{3,2,1,0:T(8,128)(2,1)S(1)}, u32[]{:S(2)}, u32[]{:S(2)}) collective-permute-start(bf16[2,4,112,128]{3,2,1,0:T(8,128)(2,1)S(1)} %pad_maximum_fusion.own), channel_id=1, source_target_pairs={{3,0},{2,1},{1,2},{0,3},{7,4},{6,5},{5,6},{4,7},{11,8},{10,9},{9,1... | collective-permute-start | bytes 688136 | tf_op jit(solution)/shard_map/ppermute | solution.py:37
  37.0 8.3 %collective-permute-start.17 = (bf16[2,4,112,128]{3,2,1,0:T(8,128)(2,1)S(1)}, bf16[2,4,112,128]{3,2,1,0:T(8,128)(2,1)S(1)}, u32[]{:S(2)}, u32[]{:S(2)}) collective-permute-start(bf16[2,4,112,128]{3,2,1,0:T(8,128)(2,1)S(1)} %collective-permute-done.11.near1), channel_id=1, source_target_pairs={{192,0},{193,1},{194,2},{195,3},{196,4},{197,5},{198,6},{199,7},{2... | collective-permute-start | bytes 688136 | tf_op jit(solution)/shard_map/ppermute | solution.py:37
  37.8 8.1 %collective-permute-start.12 = (bf16[2,4,112,128]{3,2,1,0:T(8,128)(2,1)S(1)}, bf16[2,4,112,128]{3,2,1,0:T(8,128)(2,1)S(1)}, u32[]{:S(2)}, u32[]{:S(2)}) collective-permute-start(bf16[2,4,112,128]{3,2,1,0:T(8,128)(2,1)S(1)} %collective-permute-done.11.near1), channel_id=1, source_target_pairs={{3,0},{2,1},{1,2},{0,3},{7,4},{6,5},{5,6},{4,7},{11,8},{10,9},{9,1... | collective-permute-start | bytes 688136 | tf_op jit(solution)/shard_map/ppermute | solution.py:37
  39.2 8.7 %collective-permute-start.23 = (bf16[2,4,112,128]{3,2,1,0:T(8,128)(2,1)S(1)}, bf16[2,4,112,128]{3,2,1,0:T(8,128)(2,1)S(1)}, u32[]{:S(2)}, u32[]{:S(2)}) collective-permute-start(bf16[2,4,112,128]{3,2,1,0:T(8,128)(2,1)S(1)} %collective-permute-done.11.near1), channel_id=1, source_target_pairs={{1,0},{0,1},{3,2},{2,3},{5,4},{4,5},{7,6},{6,7},{9,8},{8,9},{11,10... | collective-permute-start | bytes 688136 | tf_op jit(solution)/shard_map/ppermute | solution.py:37
  41.1 6.7 %collective-permute-start.15 = (bf16[2,4,112,128]{3,2,1,0:T(8,128)(2,1)S(1)}, bf16[2,4,112,128]{3,2,1,0:T(8,128)(2,1)S(1)}, u32[]{:S(2)}, u32[]{:S(2)}) collective-permute-start(bf16[2,4,112,128]{3,2,1,0:T(8,128)(2,1)S(1)} %collective-permute-done.14.near3), channel_id=1, source_target_pairs={{1,0},{0,1},{3,2},{2,3},{5,4},{4,5},{7,6},{6,7},{9,8},{8,9},{11,10... | collective-permute-start | bytes 688136 | tf_op jit(solution)/shard_map/ppermute | solution.py:37
  41.9 8.5 %collective-permute-start.20 = (bf16[2,4,112,128]{3,2,1,0:T(8,128)(2,1)S(1)}, bf16[2,4,112,128]{3,2,1,0:T(8,128)(2,1)S(1)}, u32[]{:S(2)}, u32[]{:S(2)}) collective-permute-start(bf16[2,4,112,128]{3,2,1,0:T(8,128)(2,1)S(1)} %collective-permute-done.14.near3), channel_id=1, source_target_pairs={{3,0},{2,1},{1,2},{0,3},{7,4},{6,5},{5,6},{4,7},{11,8},{10,9},{9,1... | collective-permute-start | bytes 688136 | tf_op jit(solution)/shard_map/ppermute | solution.py:37
  45.3 7.4 %collective-permute-start.18 = (bf16[2,4,112,128]{3,2,1,0:T(8,128)(2,1)S(1)}, bf16[2,4,112,128]{3,2,1,0:T(8,128)(2,1)S(1)}, u32[]{:S(2)}, u32[]{:S(2)}) collective-permute-start(bf16[2,4,112,128]{3,2,1,0:T(8,128)(2,1)S(1)} %collective-permute-done.17.far), channel_id=1, source_target_pairs={{1,0},{0,1},{3,2},{2,3},{5,4},{4,5},{7,6},{6,7},{9,8},{8,9},{11,10... | collective-permute-start | bytes 688136 | tf_op jit(solution)/shard_map/ppermute | solution.py:37
  45.8 10.5 %collective-permute-start.21 = (bf16[2,4,112,128]{3,2,1,0:T(8,128)(2,1)S(1)}, bf16[2,4,112,128]{3,2,1,0:T(8,128)(2,1)S(1)}, u32[]{:S(2)}, u32[]{:S(2)}) collective-permute-start(bf16[2,4,112,128]{3,2,1,0:T(8,128)(2,1)S(1)} %collective-permute-done.17.far), channel_id=1, source_target_pairs={{3,0},{2,1},{1,2},{0,3},{7,4},{6,5},{5,6},{4,7},{11,8},{10,9},{9,1... | collective-permute-start | bytes 688136 | tf_op jit(solution)/shard_map/ppermute | solution.py:37
  47.9 10.3 %collective-permute-start.10 = (bf16[2,4,112,128]{3,2,1,0:T(8,128)(2,1)S(1)}, bf16[2,4,112,128]{3,2,1,0:T(8,128)(2,1)S(1)}, u32[]{:S(2)}, u32[]{:S(2)}) collective-permute-start(bf16[2,4,112,128]{3,2,1,0:T(8,128)(2,1)S(1)} %collective-permute-done.9.own3), channel_id=1, source_target_pairs={{1,0},{0,1},{3,2},{2,3},{5,4},{4,5},{7,6},{6,7},{9,8},{8,9},{11,10... | collective-permute-start | bytes 688136 | tf_op jit(solution)/shard_map/ppermute | solution.py:37
  47.9 10.3 %collective-permute-start.13 = (bf16[2,4,112,128]{3,2,1,0:T(8,128)(2,1)S(1)}, bf16[2,4,112,128]{3,2,1,0:T(8,128)(2,1)S(1)}, u32[]{:S(2)}, u32[]{:S(2)}) collective-permute-start(bf16[2,4,112,128]{3,2,1,0:T(8,128)(2,1)S(1)} %collective-permute-done.12.near31), channel_id=1, source_target_pairs={{1,0},{0,1},{3,2},{2,3},{5,4},{4,5},{7,6},{6,7},{9,8},{8,9},{11,10... | collective-permute-start | bytes 688136 | tf_op jit(solution)/shard_map/ppermute | solution.py:37
  50.4 15.3 %collective-permute-start.16 = (bf16[2,4,112,128]{3,2,1,0:T(8,128)(2,1)S(1)}, bf16[2,4,112,128]{3,2,1,0:T(8,128)(2,1)S(1)}, u32[]{:S(2)}, u32[]{:S(2)}) collective-permute-start(bf16[2,4,112,128]{3,2,1,0:T(8,128)(2,1)S(1)} %collective-permute-done.15.near1), channel_id=1, source_target_pairs={{3,0},{2,1},{1,2},{0,3},{7,4},{6,5},{5,6},{4,7},{11,8},{10,9},{9,1... | collective-permute-start | bytes 688136 | tf_op jit(solution)/shard_map/ppermute | solution.py:37
  52.7 13.0 %collective-permute-start.19 = (bf16[2,4,112,128]{3,2,1,0:T(8,128)(2,1)S(1)}, bf16[2,4,112,128]{3,2,1,0:T(8,128)(2,1)S(1)}, u32[]{:S(2)}, u32[]{:S(2)}) collective-permute-start(bf16[2,4,112,128]{3,2,1,0:T(8,128)(2,1)S(1)} %collective-permute-done.18.far1), channel_id=1, source_target_pairs={{3,0},{2,1},{1,2},{0,3},{7,4},{6,5},{5,6},{4,7},{11,8},{10,9},{9,1... | collective-permute-start | bytes 688136 | tf_op jit(solution)/shard_map/ppermute | solution.py:37
  58.8 9.4 %collective-permute-start.25 = (bf16[512,384]{1,0:T(8,128)(2,1)S(1)}, bf16[512,384]{1,0:T(8,128)(2,1)S(1)}, u32[]{:S(2)}, u32[]{:S(2)}) collective-permute-start(bf16[512,384]{1,0:T(8,128)(2,1)S(1)} %get-tuple-element.24), channel_id=1, source_target_pairs={{16,0},{0,16},{17,1},{1,17},{18,2},{2,18},{19,3},{3,19},{20,4},{4,... | collective-permute-start | bytes 1179656 | tf_op jit(solution)/shard_map/ppermute | solution.py:24
  66.9 3.0 %collective-permute-start.24 = (bf16[512,384]{1,0:T(8,128)(2,1)S(1)}, bf16[512,384]{1,0:T(8,128)(2,1)S(1)}, u32[]{:S(2)}, u32[]{:S(2)}) collective-permute-start(bf16[512,384]{1,0:T(8,128)(2,1)S(1)} %shard_map.43), channel_id=1, source_target_pairs={{16,0},{0,16},{17,1},{1,17},{18,2},{2,18},{19,3},{3,19},{20,4},{4,... | collective-permute-start | bytes 1179656 | tf_op jit(solution)/shard_map/ppermute | solution.py:24

commit v11 on v10

--- a/solution.py
+++ b/solution.py
@@ -90,82 +90,81 @@
     return both[pl.ds(first, count)].reshape(count * 448, 768)
 
 
-def product_one(place, own, near1, both, out):
-    @on_core(place, 0)
-    def _():
-        out[rows(0, 2)] = dot_t(by_x(own, near1), both[0])
-
-    @on_core(place, 1)
-    def _():
-        out[rows(0)] = dot_t(by_y(own, near1), deep(both, 0, 2))
-
-
-def product_two(place, near3, far, own1, near1, own3, near31, both, start, out):
-    @on_core(place, 0)
-    def _():
-        out[rows(0, 2)] = (
-            start[rows(0, 2)]
-            + dot_t(by_x(own1, near1), both[1])
-            + dot_t(by_x(own3, near31), both[2])
+def product_one(place, own, near1, both, low):
+    @on_core(place, 0)
+    def _():
+        low[...] = dot_t(by_x(own, near1), both[0])
+
+    @on_core(place, 1)
+    def _():
+        low[rows(0)] = dot_t(by_y(own, near1), deep(both, 0, 2))
+
+
+def product_two(place, near3, far, own1, near1, own3, near31, both, start, low, high):
+    @on_core(place, 0)
+    def _():
+        low[...] = (
+            start[...] + dot_t(by_x(own1, near1), both[1]) + dot_t(by_x(own3, near31), both[2])
         )
-        out[rows(2, 2)] = dot_t(by_x(near3, far), both[0])
-
-    @on_core(place, 1)
-    def _():
-        out[rows(0)] = start[rows(0)] + dot_t(by_y(near3, far), deep(both, 2, 2))
-        out[rows(1)] = dot_t(by_y(own1, near1), deep(both, 0, 2))
-        out[rows(2)] = dot_t(by_y(own3, near31), deep(both, 0, 2))
-
-
-def product_three(place, near1, far1, near3, far3, both, start, out):
-    @on_core(place, 0)
-    def _():
-        out[rows(0, 2)] = start[rows(0, 2)]
-        out[rows(2, 2)] = (
-            start[rows(2, 2)]
-            + dot_t(by_x(near1, far1), both[1])
-            + dot_t(by_x(near3, far3), both[2])
+        high[...] = dot_t(by_x(near3, far), both[0])
+
+    @on_core(place, 1)
+    def _():
+        low[rows(0)] = start[rows(0)] + dot_t(by_y(near3, far), deep(both, 2, 2))
+        low[rows(1)] = dot_t(by_y(own1, near1), deep(both, 0, 2))
+        high[rows(0)] = dot_t(by_y(own3, near31), deep(both, 0, 2))
+
+
+def product_three(place, near31, far1, own, near1, both, low, mine, theirs):
+    def keep(at, total):
+        mine[at] = total[:, :384].astype(BF16)
+        theirs[at] = total[:, 384:].astype(BF16)
+
+    @on_core(place, 0)
+    def _():
+        keep(rows(0, 2), low[...] + dot_t(by_x(own, near1), both[3]))
+
+    @on_core(place, 1)
+    def _():
+        keep(rows(0), low[rows(0)])
+        keep(rows(1), low[rows(1)] + dot_t(by_y(near31, far1), deep(both, 2, 2)))
+
+
+def product_four(place, near31, far1, near33, far3, both, start, high):
+    @on_core(place, 0)
+    def _():
+        high[...] = (
+            start[...] + dot_t(by_x(near31, far1), both[1]) + dot_t(by_x(near33, far3), both[2])
         )
 
     @on_core(place, 1)
     def _():
-        out[rows(0)] = start[rows(0)]
-        out[rows(1)] = start[rows(1)] + dot_t(by_y(near1, far1), deep(both, 2, 2))
-        out[rows(2)] = start[rows(2)] + dot_t(by_y(near3, far3), deep(both, 2, 2))
-
-
-def product_four(place, own, near1, both, start, mine, theirs):
-    def keep(total):
-        mine[...] = total[:, :384].astype(BF16)
-        theirs[...] = total[:, 384:].astype(BF16)
-
-    @on_core(place, 0)
-    def _():
-        keep(start[rows(0, 2)] + dot_t(by_x(own, near1), both[3]))
-
-    @on_core(place, 1)
-    def _():
-        keep(start[rows(0, 2)])
-
-
-def product_five(side, place, own, near1, near3, far, both, start, out):
+        high[rows(0)] = start[rows(0)] + dot_t(by_y(near33, far3), deep(both, 2, 2))
+
+
+def product_five(side, place, own, near1, near3, far, both, high, out):
     columns = pl.ds(side * 384, 384)
 
     @on_core(place, 0)
     def _():
-        total = start[rows(2, 2), columns] + dot_t(by_x(near3, far), both[3, :, columns])
+        total = high[:, columns] + dot_t(by_x(near3, far), both[3, :, columns])
         out[...] = total.astype(BF16)
 
     @on_core(place, 1)
     def _():
-        out[rows(0)] = start[rows(2), columns].astype(BF16)
+        out[rows(0)] = high[rows(0), columns].astype(BF16)
         left = by_y(own, near1, near3, far)
         out[rows(1)] = dot_t(left, both[:, :, columns].reshape(1792, 384)).astype(BF16)
 
 
-def place_rows(place, parts, out, sems):
+def place_rows(place, mine1, mine2, theirs1, theirs2, out, sems):
     copies = []
-    for block, core, which in parts:
+    for block, core, which in (
+        (mine1, place[2], 0),
+        (mine2, place[2], 1),
+        (theirs1, 1 - place[2], 0),
+        (theirs2, 1 - place[2], 1),
+    ):
         for i in range(2):
             row = core * 1024 + (place[0] ^ ORDER[which * 2 + i]) * 256
             at = pl.ds(pl.multiple_of(row, 256), 256)
@@ -175,15 +174,6 @@
         copy.start()
     for copy in copies:
         copy.wait()
-
-
-def place_first(place, mine1, mine2, theirs1, out, sems):
-    core = place[2]
-    place_rows(place, [(mine1, core, 0), (mine2, core, 1), (theirs1, 1 - core, 0)], out, sems)
-
-
-def place_last(place, theirs2, given, out, sems):
-    place_rows(place, [(theirs2, 1 - place[2], 1)], out, sems)
 
 
 def call(kernel, out_shape, operands, out_specs=VMEM, specs=None, **more):
@@ -227,51 +217,48 @@
     near1, near3 = turn(own, 0, 1), turn(own, 0, 3)
     far = turn(near1, 0, 3)
     one_own, three_own = turn(own, 1, 1), turn(own, 1, 3)
-    total = jax.ShapeDtypeStruct((1024, 768), F32)
-    total_one = call(product_one, total, (place, own, near1, both))
+    total = jax.ShapeDtypeStruct((512, 768), F32)
+    low = call(product_one, total, (place, own, near1, both))
     one_near1, three_near1 = turn(near1, 1, 1), turn(near1, 1, 3)
     one_near3, three_near3 = turn(near3, 1, 1), turn(near3, 1, 3)
     one_far, three_far = turn(far, 1, 1), turn(far, 1, 3)
     far_own, far_near1 = turn(three_own, 1, 1), turn(three_near1, 1, 1)
     far_near3, far_far = turn(one_near3, 1, 3), turn(one_far, 1, 3)
-    total_two = call(
+    low, high = call(
         product_two,
+        (total, total),
+        (place, near3, far, one_own, one_near1, three_own, three_near1, both, low),
+        (VMEM, VMEM),
+    )
+    half = jax.ShapeDtypeStruct((512, 384), BF16)
+    low, three_near3, three_far = lax.optimization_barrier((low, three_near3, three_far))
+    mine1, theirs1 = call(
+        product_three,
+        (half, half),
+        (place, one_near3, one_far, far_own, far_near1, both, low),
+        (VMEM, VMEM),
+    )
+    theirs1 = fetch(theirs1, "core", 2, 1)
+    high = call(
+        product_four,
         total,
-        (place, near3, far, one_own, one_near1, three_own, three_near1, both, total_one),
-        input_output_aliases={8: 0},
-    )
-    total_three = call(
-        product_three,
-        total,
-        (place, one_near3, one_far, three_near3, three_far, both, total_two),
-        input_output_aliases={6: 0},
-    )
-    half = jax.ShapeDtypeStruct((512, 384), BF16)
-    mine1, theirs1 = call(
-        product_four, (half, half), (place, far_own, far_near1, both, total_three), (VMEM, VMEM)
-    )
-    theirs1 = fetch(theirs1, "core", 2, 1)
+        (place, one_near3, one_far, three_near3, three_far, both, high),
+    )
     mine2, theirs2 = (
         call(
             functools.partial(product_five, side),
             half,
-            (place, far_own, far_near1, far_near3, far_far, both, total_three),
+            (place, far_own, far_near1, far_near3, far_far, both, high),
         )
         for side in (0, 1)
     )
     theirs2 = fetch(theirs2, "core", 2, 1)
-
-    out = jax.ShapeDtypeStruct((2048, 384), BF16)
-    sems = dict(scratch_shapes=[pltpu.SemaphoreType.DMA((6,))])
-    kernel = call(place_first, out, (place, mine1, mine2, theirs1), ANY, **sems)
     return call(
-        place_last,
-        out,
-        (place, theirs2, kernel),
+        place_rows,
+        jax.ShapeDtypeStruct((2048, 384), BF16),
+        (place, mine1, mine2, theirs1, theirs2),
         ANY,
-        [SMEM, VMEM, ANY],
-        input_output_aliases={2: 0},
-        **sems,
+        scratch_shapes=[pltpu.SemaphoreType.DMA((8,))],
     )
 
 

time: 71.6 us -> 71.3 us (level)
  waiting for transfers between devices: 9.75 us -> 13 us
  local copies, waits for them, and re-layouts: 3.11 us -> 1.77 us
  Pallas kernels: 13.4 us -> 12.1 us
    ppermute x15, waiting for transfers between devices: 2.3 us -> 4.13 us  [turn(): return lax.ppermute(block, ROW + COL, pairs)]
    pallas_call x11 -> x10, Pallas kernels: 13.4 us -> 12.1 us  [call(): pl.pallas_call(kernel, out_shape=out_shape, in_specs=specs or [SMEM] + [V...]
    unnamed x6, local copies, waits for them, and re-layouts: 3.11 us -> 1.77 us
    ppermute x7, waiting for transfers between devices: 5.65 us -> 6.97 us  [swap(): return lax.ppermute(block, axis, [(i ^ bits, i) for i in range(size)])]
  transfers between devices with their start and end apart: 26 -> 26, of which waited for: 10 -> 12; matrix products, arithmetic and copies ran while one was open for 0% -> 0% of each run, Pallas kernels for 17% -> 15%
where the time goes in v11:
time: 71.3 us; the launch traced here: 71.1 us
  starting transfers between devices  43.8 us (61%)
  waiting for transfers between devices  13 us (18%)
  Pallas kernels  12.1 us (17%)
  local copies, waits for them, and re-layouts  1.77 us (2%)
    ppermute x15, starting transfers between devices, turn(): return lax.ppermute(block, ROW + COL, pairs)  20.6 us
    ppermute x7, starting transfers between devices, swap(): return lax.ppermute(block, axis, [(i ^ bits, i) for i in range(size)])  13.2 us
    pallas_call x10, Pallas kernels, call(): pl.pallas_call(kernel, out_shape=out_shape, in_specs=specs or [SMEM] + [V...  12.1 us
    ppermute x4, starting transfers between devices, fetch(): lax.ppermute(block, axis, [((i + ahead) % size, i) for i in range(size)])  10 us
    ppermute x7, waiting for transfers between devices, swap(): return lax.ppermute(block, axis, [(i ^ bits, i) for i in range(size)])  6.97 us
    ppermute x15, waiting for transfers between devices, turn(): return lax.ppermute(block, ROW + COL, pairs)  4.13 us
    ppermute x4, waiting for transfers between devices, fetch(): lax.ppermute(block, axis, [((i + ahead) % size, i) for i in range(size)])  1.93 us
    unnamed x6, local copies, waits for them, and re-layouts  1.77 us
  transfers between devices with their start and end apart: 26, of which 12 were waited for; matrix products, arithmetic and copies ran while one was open for 0% of the time, Pallas kernels for 15%

profile of v11, /device:TPU:1, one launch (start us, length us, event | category | flops | bytes accessed | tf_op | source)
XLA Modules:
  0.0 71.1 jit_solution(8492880780003139515)
XLA Ops:
  0.0 3.2 %collective-permute-start.5 = (bf16[1792,384]{1,0:T(8,128)(2,1)}, bf16[1792,384]{1,0:T(8,128)(2,1)S(1)}, u32[]{:S(2)}, u32[]{:S(2)}) collective-permute-start(bf16[1792,384]{1,0:T(8,128)(2,1)} %own.1), channel_id=1, source_target_pairs={{16,0},{0,16},{17,1},{1,17},{18,2},{2,18},{19,3},{3,19},{20,4},{4,... | collective-permute-start | bytes 4128776 | tf_op jit(solution)/shard_map/ppermute | solution.py:24
  3.3 1.0 %copy-done.1 = bf16[112,2048]{1,0:T(8,128)(2,1)S(1)} copy-done((bf16[112,2048]{1,0:T(8,128)(2,1)S(1)}, bf16[112,2048]{1,0:T(8,128)(2,1)}, u32[]{:S(2)}) %copy-start.1) | copy-done | bytes 458776
  6.2 1.7 %collective-permute-done.received = f32[8,112,128]{2,1,0:T(8,128)S(1)} collective-permute-done((f32[8,112,128]{2,1,0:T(8,128)S(1)}, f32[8,112,128]{2,1,0:T(8,128)S(1)}, u32[]{:S(2)}, u32[]{:S(2)}) %collective-permute-start) | collective-permute-done | bytes 458784 | tf_op jit(solution)/shard_map/ppermute | solution.py:24
  9.9 2.0 %collective-permute-start.3 = (bf16[2,112,128]{2,1,0:T(8,128)(2,1)S(1)}, bf16[2,112,128]{2,1,0:T(8,128)(2,1)S(1)}, u32[]{:S(2)}, u32[]{:S(2)}) collective-permute-start(bf16[2,112,128]{2,1,0:T(8,128)(2,1)S(1)} %get-tuple-element.25), channel_id=1, source_target_pairs={{64,0},{0,64},{192,128},{128,192},{65,1},{1,65},{193,129},{129,193... | collective-permute-start | bytes 172040 | tf_op jit(solution)/shard_map/ppermute | solution.py:28
  12.9 1.1 %collective-permute-done.2 = bf16[2,112,128]{2,1,0:T(8,128)(2,1)S(1)} collective-permute-done((bf16[2,112,128]{2,1,0:T(8,128)(2,1)S(1)}, bf16[2,112,128]{2,1,0:T(8,128)(2,1)S(1)}, u32[]{:S(2)}, u32[]{:S(2)}) %collective-permute-start.2) | collective-permute-done | bytes 57376 | tf_op jit(solution)/shard_map/ppermute | solution.py:28
  14.8 6.2 %collective-permute-start.4 = (bf16[2,112,128]{2,1,0:T(8,128)(2,1)S(1)}, bf16[2,112,128]{2,1,0:T(8,128)(2,1)S(1)}, u32[]{:S(2)}, u32[]{:S(2)}) collective-permute-start(bf16[2,112,128]{2,1,0:T(8,128)(2,1)S(1)} %fusion), channel_id=1, source_target_pairs={{32,0},{0,32},{33,1},{1,33},{34,2},{2,34},{35,3},{3,35},{36,4},{4,... | collective-permute-start | bytes 172040 | tf_op jit(solution)/shard_map/ppermute | solution.py:28
  22.6 2.9 %collective-permute-start.8 = (bf16[2,112,128]{2,1,0:T(8,128)(2,1)S(1)}, bf16[2,112,128]{2,1,0:T(8,128)(2,1)S(1)}, u32[]{:S(2)}, u32[]{:S(2)}) collective-permute-start(bf16[2,112,128]{2,1,0:T(8,128)(2,1)S(1)} %add_convert_fusion), channel_id=1, source_target_pairs={{12,0},{8,4},{4,8},{0,12},{13,1},{9,5},{5,9},{1,13},{14,2},{10,6},... | collective-permute-start | bytes 172040 | tf_op jit(solution)/shard_map/ppermute | solution.py:28
  26.2 1.3 %collective-permute-done.8 = bf16[2,112,128]{2,1,0:T(8,128)(2,1)S(1)} collective-permute-done((bf16[2,112,128]{2,1,0:T(8,128)(2,1)S(1)}, bf16[2,112,128]{2,1,0:T(8,128)(2,1)S(1)}, u32[]{:S(2)}, u32[]{:S(2)}) %collective-permute-start.8) | collective-permute-done | bytes 57376 | tf_op jit(solution)/shard_map/ppermute | solution.py:28
  27.5 1.0 %collective-permute-done.6 = bf16[2,112,128]{2,1,0:T(8,128)(2,1)S(1)} collective-permute-done((bf16[2,112,128]{2,1,0:T(8,128)(2,1)S(1)}, bf16[2,112,128]{2,1,0:T(8,128)(2,1)S(1)}, u32[]{:S(2)}, u32[]{:S(2)}) %collective-permute-start.6) | collective-permute-done | bytes 57376 | tf_op jit(solution)/shard_map/ppermute | solution.py:28
  28.6 1.0 %collective-permute-done.7 = bf16[2,112,128]{2,1,0:T(8,128)(2,1)S(1)} collective-permute-done((bf16[2,112,128]{2,1,0:T(8,128)(2,1)S(1)}, bf16[2,112,128]{2,1,0:T(8,128)(2,1)S(1)}, u32[]{:S(2)}, u32[]{:S(2)}) %collective-permute-start.7) | collective-permute-done | bytes 57376 | tf_op jit(solution)/shard_map/ppermute | solution.py:28
  29.7 1.4 %collective-permute-start.11 = (bf16[2,4,112,128]{3,2,1,0:T(8,128)(2,1)S(1)}, bf16[2,4,112,128]{3,2,1,0:T(8,128)(2,1)S(1)}, u32[]{:S(2)}, u32[]{:S(2)}) collective-permute-start(bf16[2,4,112,128]{3,2,1,0:T(8,128)(2,1)S(1)} %pad_maximum_fusion.own), channel_id=1, source_target_pairs={{64,0},{65,1},{66,2},{67,3},{68,4},{69,5},{70,6},{71,7},{72,8},{73... | collective-permute-start | bytes 688136 | tf_op jit(solution)/shard_map/ppermute | solution.py:37
  31.0 1.9 %collective-permute-start.14 = (bf16[2,4,112,128]{3,2,1,0:T(8,128)(2,1)S(1)}, bf16[2,4,112,128]{3,2,1,0:T(8,128)(2,1)S(1)}, u32[]{:S(2)}, u32[]{:S(2)}) collective-permute-start(bf16[2,4,112,128]{3,2,1,0:T(8,128)(2,1)S(1)} %pad_maximum_fusion.own), channel_id=1, source_target_pairs={{3,0},{2,1},{1,2},{0,3},{7,4},{6,5},{5,6},{4,7},{11,8},{10,9},{9,1... | collective-permute-start | bytes 688136 | tf_op jit(solution)/shard_map/ppermute | solution.py:37
  32.9 1.9 %collective-permute-start.9 = (bf16[2,4,112,128]{3,2,1,0:T(8,128)(2,1)S(1)}, bf16[2,4,112,128]{3,2,1,0:T(8,128)(2,1)S(1)}, u32[]{:S(2)}, u32[]{:S(2)}) collective-permute-start(bf16[2,4,112,128]{3,2,1,0:T(8,128)(2,1)S(1)} %pad_maximum_fusion.own), channel_id=1, source_target_pairs={{192,0},{193,1},{194,2},{195,3},{196,4},{197,5},{198,6},{199,7},{2... | collective-permute-start | bytes 688136 | tf_op jit(solution)/shard_map/ppermute | solution.py:37
  34.8 1.5 %collective-permute-start.18 = (bf16[2,4,112,128]{3,2,1,0:T(8,128)(2,1)S(1)}, bf16[2,4,112,128]{3,2,1,0:T(8,128)(2,1)S(1)}, u32[]{:S(2)}, u32[]{:S(2)}) collective-permute-start(bf16[2,4,112,128]{3,2,1,0:T(8,128)(2,1)S(1)} %pad_maximum_fusion.own), channel_id=1, source_target_pairs={{1,0},{0,1},{3,2},{2,3},{5,4},{4,5},{7,6},{6,7},{9,8},{8,9},{11,10... | collective-permute-start | bytes 688136 | tf_op jit(solution)/shard_map/ppermute | solution.py:37
  36.3 1.1 %collective-permute-start.12 = (bf16[2,4,112,128]{3,2,1,0:T(8,128)(2,1)S(1)}, bf16[2,4,112,128]{3,2,1,0:T(8,128)(2,1)S(1)}, u32[]{:S(2)}, u32[]{:S(2)}) collective-permute-start(bf16[2,4,112,128]{3,2,1,0:T(8,128)(2,1)S(1)} %collective-permute-done.11.near1), channel_id=1, source_target_pairs={{192,0},{193,1},{194,2},{195,3},{196,4},{197,5},{198,6},{199,7},{2... | collective-permute-start | bytes 688136 | tf_op jit(solution)/shard_map/ppermute | solution.py:37
  37.4 1.9 %collective-permute-start.16 = (bf16[2,4,112,128]{3,2,1,0:T(8,128)(2,1)S(1)}, bf16[2,4,112,128]{3,2,1,0:T(8,128)(2,1)S(1)}, u32[]{:S(2)}, u32[]{:S(2)}) collective-permute-start(bf16[2,4,112,128]{3,2,1,0:T(8,128)(2,1)S(1)} %collective-permute-done.11.near1), channel_id=1, source_target_pairs={{3,0},{2,1},{1,2},{0,3},{7,4},{6,5},{5,6},{4,7},{11,8},{10,9},{9,1... | collective-permute-start | bytes 688136 | tf_op jit(solution)/shard_map/ppermute | solution.py:37
  39.2 1.5 %collective-permute-start.19 = (bf16[2,4,112,128]{3,2,1,0:T(8,128)(2,1)S(1)}, bf16[2,4,112,128]{3,2,1,0:T(8,128)(2,1)S(1)}, u32[]{:S(2)}, u32[]{:S(2)}) collective-permute-start(bf16[2,4,112,128]{3,2,1,0:T(8,128)(2,1)S(1)} %collective-permute-done.11.near1), channel_id=1, source_target_pairs={{1,0},{0,1},{3,2},{2,3},{5,4},{4,5},{7,6},{6,7},{9,8},{8,9},{11,10... | collective-permute-start | bytes 688136 | tf_op jit(solution)/shard_map/ppermute | solution.py:37
  42.9 1.5 %collective-permute-done.12.far = bf16[2,4,112,128]{3,2,1,0:T(8,128)(2,1)S(1)} collective-permute-done((bf16[2,4,112,128]{3,2,1,0:T(8,128)(2,1)S(1)}, bf16[2,4,112,128]{3,2,1,0:T(8,128)(2,1)S(1)}, u32[]{:S(2)}, u32[]{:S(2)}) %collective-permute-start.12) | collective-permute-done | bytes 229408 | tf_op jit(solution)/shard_map/ppermute | solution.py:37
  44.4 1.1 %collective-permute-start.13 = (bf16[2,4,112,128]{3,2,1,0:T(8,128)(2,1)S(1)}, bf16[2,4,112,128]{3,2,1,0:T(8,128)(2,1)S(1)}, u32[]{:S(2)}, u32[]{:S(2)}) collective-permute-start(bf16[2,4,112,128]{3,2,1,0:T(8,128)(2,1)S(1)} %collective-permute-done.12.far), channel_id=1, source_target_pairs={{1,0},{0,1},{3,2},{2,3},{5,4},{4,5},{7,6},{6,7},{9,8},{8,9},{11,10... | collective-permute-start | bytes 688136 | tf_op jit(solution)/shard_map/ppermute | solution.py:37
  45.5 2.2 %collective-permute-start.21 = (bf16[2,4,112,128]{3,2,1,0:T(8,128)(2,1)S(1)}, bf16[2,4,112,128]{3,2,1,0:T(8,128)(2,1)S(1)}, u32[]{:S(2)}, u32[]{:S(2)}) collective-permute-start(bf16[2,4,112,128]{3,2,1,0:T(8,128)(2,1)S(1)} %collective-permute-done.12.far), channel_id=1, source_target_pairs={{3,0},{2,1},{1,2},{0,3},{7,4},{6,5},{5,6},{4,7},{11,8},{10,9},{9,1... | collective-permute-start | bytes 688136 | tf_op jit(solution)/shard_map/ppermute | solution.py:37
  48.1 1.7 %collective-permute-done.20.near33 = bf16[2,4,112,128]{3,2,1,0:T(8,128)(2,1)S(1)} collective-permute-done((bf16[2,4,112,128]{3,2,1,0:T(8,128)(2,1)S(1)}, bf16[2,4,112,128]{3,2,1,0:T(8,128)(2,1)S(1)}, u32[]{:S(2)}, u32[]{:S(2)}) %collective-permute-start.20) | collective-permute-done | bytes 229408 | tf_op jit(solution)/shard_map/ppermute | solution.py:37
  49.8 1.8 %collective-permute-start.17 = (bf16[2,4,112,128]{3,2,1,0:T(8,128)(2,1)S(1)}, bf16[2,4,112,128]{3,2,1,0:T(8,128)(2,1)S(1)}, u32[]{:S(2)}, u32[]{:S(2)}) collective-permute-start(bf16[2,4,112,128]{3,2,1,0:T(8,128)(2,1)S(1)} %collective-permute-done.16.near31), channel_id=1, source_target_pairs={{1,0},{0,1},{3,2},{2,3},{5,4},{4,5},{7,6},{6,7},{9,8},{8,9},{11,10... | collective-permute-start | bytes 688136 | tf_op jit(solution)/shard_map/ppermute | solution.py:37
  51.7 1.0 %collective-permute-start.22 = (bf16[2,4,112,128]{3,2,1,0:T(8,128)(2,1)S(1)}, bf16[2,4,112,128]{3,2,1,0:T(8,128)(2,1)S(1)}, u32[]{:S(2)}, u32[]{:S(2)}) collective-permute-start(bf16[2,4,112,128]{3,2,1,0:T(8,128)(2,1)S(1)} %collective-permute-done.10.near31), channel_id=1, source_target_pairs={{3,0},{2,1},{1,2},{0,3},{7,4},{6,5},{5,6},{4,7},{11,8},{10,9},{9,1... | collective-permute-start | bytes 688136 | tf_op jit(solution)/shard_map/ppermute | solution.py:37
  52.7 1.6 %collective-permute-start.23 = (bf16[2,4,112,128]{3,2,1,0:T(8,128)(2,1)S(1)}, bf16[2,4,112,128]{3,2,1,0:T(8,128)(2,1)S(1)}, u32[]{:S(2)}, u32[]{:S(2)}) collective-permute-start(bf16[2,4,112,128]{3,2,1,0:T(8,128)(2,1)S(1)} %collective-permute-done.13.far1), channel_id=1, source_target_pairs={{3,0},{2,1},{1,2},{0,3},{7,4},{6,5},{5,6},{4,7},{11,8},{10,9},{9,1... | collective-permute-start | bytes 688136 | tf_op jit(solution)/shard_map/ppermute | solution.py:37
  54.3 1.2 %shard_map.40.start = f32[512,768]{1,0:T(8,128)S(1)} custom-call(s32[4]{0:T(128)S(1)} %pad_add_fusion.place, bf16[2,4,112,128]{3,2,1,0:T(8,128)(2,1)S(1)} %pad_maximum_fusion.own, bf16[2,4,112,128]{3,2,1,0:T(8,128)(2,1)S(1)} %collective-permute-done.11.near1, bf16[4,448,768]{2,1,0:T(8,128)(2,1)S(1)} %shard_map.39.both), custom_call_target="tpu_custom_call" | custom-call | tf_op jit(solution)/shard_map/pallas_call | solution.py:180
  55.5 2.0 %shard_map.41 = (f32[512,768]{1,0:T(8,128)S(1)}, f32[512,768]{1,0:T(8,128)S(1)}) custom-call(s32[4]{0:T(128)S(1)} %pad_add_fusion.place, bf16[2,4,112,128]{3,2,1,0:T(8,128)(2,1)S(1)} %collective-permute-done.9.near3, bf16[2,4,112,128]{3,2,1,0:T(8,128)(2,1)S(1)} %collective-permute-done.12.far, bf16[2,4,112,128]{3,2,1,0:T(8,128)(2,1)S(1)} %collective-permute-done.18.own1, ...), custom_call_target="tpu_custom_call" | custom-call | tf_op jit(solution)/shard_map/pallas_call | solution.py:180
  57.5 1.2 %shard_map.42 = (bf16[512,384]{1,0:T(8,128)(2,1)S(1)}, bf16[512,384]{1,0:T(8,128)(2,1)S(1)}) custom-call(s32[4]{0:T(128)S(1)} %pad_add_fusion.place, bf16[2,4,112,128]{3,2,1,0:T(8,128)(2,1)S(1)} %collective-permute-done.10.near31, bf16[2,4,112,128]{3,2,1,0:T(8,128)(2,1)S(1)} %collective-permute-done.13.far1, ...), custom_call_target="tpu_custom_call" | custom-call | tf_op jit(solution)/shard_map/pallas_call | solution.py:180
  58.7 6.2 %collective-permute-start.24 = (bf16[512,384]{1,0:T(8,128)(2,1)S(1)}, bf16[512,384]{1,0:T(8,128)(2,1)S(1)}, u32[]{:S(2)}, u32[]{:S(2)}) collective-permute-start(bf16[512,384]{1,0:T(8,128)(2,1)S(1)} %get-tuple-element.34), channel_id=1, source_target_pairs={{16,0},{0,16},{17,1},{1,17},{18,2},{2,18},{19,3},{3,19},{20,4},{4,... | collective-permute-start | bytes 1179656 | tf_op jit(solution)/shard_map/ppermute | solution.py:24
  65.0 1.2 %shard_map.43.high = f32[512,768]{1,0:T(8,128)S(1)} custom-call(s32[4]{0:T(128)S(1)} %pad_add_fusion.place, bf16[2,4,112,128]{3,2,1,0:T(8,128)(2,1)S(1)} %collective-permute-done.10.near31, bf16[2,4,112,128]{3,2,1,0:T(8,128)(2,1)S(1)} %collective-permute-done.13.far1, bf16[2,4,112,128]{3,2,1,0:T(8,128)(2,1)S(1)} %collective-permute-done.20.near33, ...), custom_call_target="tpu_custom_call" | custom-call | tf_op jit(solution)/shard_map/pallas_call | solution.py:180
  66.2 1.2 %shard_map.45 = bf16[512,384]{1,0:T(8,128)(2,1)S(1)} custom-call(s32[4]{0:T(128)S(1)} %pad_add_fusion.place, bf16[2,4,112,128]{3,2,1,0:T(8,128)(2,1)S(1)} %collective-permute-done.15.own, bf16[2,4,112,128]{3,2,1,0:T(8,128)(2,1)S(1)} %collective-permute-done.17.near1, bf16[2,4,112,128]{3,2,1,0:T(8,128)(2,1)S(1)} %collective-permute-done.22.near3, ...), custom_call_target="tpu_custom_call" | custom-call | tf_op jit(solution)/shard_map/pallas_call | solution.py:180
  67.8 1.2 %shard_map.44.mine2 = bf16[512,384]{1,0:T(8,128)(2,1)S(1)} custom-call(s32[4]{0:T(128)S(1)} %pad_add_fusion.place, bf16[2,4,112,128]{3,2,1,0:T(8,128)(2,1)S(1)} %collective-permute-done.15.own, bf16[2,4,112,128]{3,2,1,0:T(8,128)(2,1)S(1)} %collective-permute-done.17.near1, bf16[2,4,112,128]{3,2,1,0:T(8,128)(2,1)S(1)} %collective-permute-done.22.near3, ...), custom_call_target="tpu_custom_call" | custom-call | tf_op jit(solution)/shard_map/pallas_call | solution.py:180
  69.2 1.7 %shard_map.46 = bf16[2048,384]{1,0:T(8,128)(2,1)} custom-call(s32[4]{0:T(128)S(1)} %pad_add_fusion.place, bf16[512,384]{1,0:T(8,128)(2,1)S(1)} %get-tuple-element.30.mine1, bf16[512,384]{1,0:T(8,128)(2,1)S(1)} %shard_map.44.mine2, bf16[512,384]{1,0:T(8,128)(2,1)S(1)} %collective-permute-done.24.theirs1, bf16[512,384]{1,0:T(8,128)(2,1)S(1)} %collective-permute-done.25.theirs2), custom_call_target="tpu_custom_call" | custom-call | tf_op jit(solution)/shard_map/pallas_call | solution.py:180
  (40 shorter events, 11.2 us)
Async XLA Ops:
  0.0 21.0 %copy-start = (bf16[1792,384]{1,0:T(8,128)(2,1)S(1)}, bf16[1792,384]{1,0:T(8,128)(2,1)}, u32[]{:S(2)}) copy-start(bf16[1792,384]{1,0:T(8,128)(2,1)} %own.1) | copy-start | bytes 4128772
  0.0 21.0 %collective-permute-start.5 = (bf16[1792,384]{1,0:T(8,128)(2,1)}, bf16[1792,384]{1,0:T(8,128)(2,1)S(1)}, u32[]{:S(2)}, u32[]{:S(2)}) collective-permute-start(bf16[1792,384]{1,0:T(8,128)(2,1)} %own.1), channel_id=1, source_target_pairs={{16,0},{0,16},{17,1},{1,17},{18,2},{2,18},{19,3},{3,19},{20,4},{4,... | collective-permute-start | bytes 4128776 | tf_op jit(solution)/shard_map/ppermute | solution.py:24
  3.3 1.0 %copy-start.1 = (bf16[112,2048]{1,0:T(8,128)(2,1)S(1)}, bf16[112,2048]{1,0:T(8,128)(2,1)}, u32[]{:S(2)}) copy-start(bf16[112,2048]{1,0:T(8,128)(2,1)} %panel.1) | copy-start | bytes 1376260
  4.3 0.7 %copy-start.2 = (bf16[112,112]{1,0:T(8,128)(2,1)S(1)}, bf16[112,112]{1,0:T(8,128)(2,1)}, u32[]{:S(2)}) copy-start(bf16[112,112]{1,0:T(8,128)(2,1)} %screening.1) | copy-start | bytes 75268
  6.1 1.9 %collective-permute-start = (f32[8,112,128]{2,1,0:T(8,128)S(1)}, f32[8,112,128]{2,1,0:T(8,128)S(1)}, u32[]{:S(2)}, u32[]{:S(2)}) collective-permute-start(f32[8,112,128]{2,1,0:T(8,128)S(1)} %get-tuple-element.21), channel_id=1, source_target_pairs={{16,0},{0,16},{17,1},{1,17},{18,2},{2,18},{19,3},{3,19},{20,4},{4,... | collective-permute-start | bytes 1376264 | tf_op jit(solution)/shard_map/ppermute | solution.py:24
  8.6 4.3 %collective-permute-start.1 = (bf16[2,112,128]{2,1,0:T(8,128)(2,1)S(1)}, bf16[2,112,128]{2,1,0:T(8,128)(2,1)S(1)}, u32[]{:S(2)}, u32[]{:S(2)}) collective-permute-start(bf16[2,112,128]{2,1,0:T(8,128)(2,1)S(1)} %get-tuple-element.23), channel_id=1, source_target_pairs={{192,0},{128,64},{64,128},{0,192},{193,1},{129,65},{65,129},{1,193... | collective-permute-start | bytes 172040 | tf_op jit(solution)/shard_map/ppermute | solution.py:28
  9.4 4.6 %collective-permute-start.2 = (bf16[2,112,128]{2,1,0:T(8,128)(2,1)S(1)}, bf16[2,112,128]{2,1,0:T(8,128)(2,1)S(1)}, u32[]{:S(2)}, u32[]{:S(2)}) collective-permute-start(bf16[2,112,128]{2,1,0:T(8,128)(2,1)S(1)} %get-tuple-element.24), channel_id=1, source_target_pairs={{128,0},{192,64},{0,128},{64,192},{129,1},{193,65},{1,129},{65,193... | collective-permute-start | bytes 172040 | tf_op jit(solution)/shard_map/ppermute | solution.py:28
  9.9 4.8 %collective-permute-start.3 = (bf16[2,112,128]{2,1,0:T(8,128)(2,1)S(1)}, bf16[2,112,128]{2,1,0:T(8,128)(2,1)S(1)}, u32[]{:S(2)}, u32[]{:S(2)}) collective-permute-start(bf16[2,112,128]{2,1,0:T(8,128)(2,1)S(1)} %get-tuple-element.25), channel_id=1, source_target_pairs={{64,0},{0,64},{192,128},{128,192},{65,1},{1,65},{193,129},{129,193... | collective-permute-start | bytes 172040 | tf_op jit(solution)/shard_map/ppermute | solution.py:28
  14.8 7.8 %collective-permute-start.4 = (bf16[2,112,128]{2,1,0:T(8,128)(2,1)S(1)}, bf16[2,112,128]{2,1,0:T(8,128)(2,1)S(1)}, u32[]{:S(2)}, u32[]{:S(2)}) collective-permute-start(bf16[2,112,128]{2,1,0:T(8,128)(2,1)S(1)} %fusion), channel_id=1, source_target_pairs={{32,0},{0,32},{33,1},{1,33},{34,2},{2,34},{35,3},{3,35},{36,4},{4,... | collective-permute-start | bytes 172040 | tf_op jit(solution)/shard_map/ppermute | solution.py:28
  22.6 4.9 %collective-permute-start.8 = (bf16[2,112,128]{2,1,0:T(8,128)(2,1)S(1)}, bf16[2,112,128]{2,1,0:T(8,128)(2,1)S(1)}, u32[]{:S(2)}, u32[]{:S(2)}) collective-permute-start(bf16[2,112,128]{2,1,0:T(8,128)(2,1)S(1)} %add_convert_fusion), channel_id=1, source_target_pairs={{12,0},{8,4},{4,8},{0,12},{13,1},{9,5},{5,9},{1,13},{14,2},{10,6},... | collective-permute-start | bytes 172040 | tf_op jit(solution)/shard_map/ppermute | solution.py:28
  25.5 3.0 %collective-permute-start.6 = (bf16[2,112,128]{2,1,0:T(8,128)(2,1)S(1)}, bf16[2,112,128]{2,1,0:T(8,128)(2,1)S(1)}, u32[]{:S(2)}, u32[]{:S(2)}) collective-permute-start(bf16[2,112,128]{2,1,0:T(8,128)(2,1)S(1)} %add_convert_fusion), channel_id=1, source_target_pairs={{4,0},{0,4},{12,8},{8,12},{5,1},{1,5},{13,9},{9,13},{6,2},{2,6},{1... | collective-permute-start | bytes 172040 | tf_op jit(solution)/shard_map/ppermute | solution.py:28
  25.5 4.1 %collective-permute-start.7 = (bf16[2,112,128]{2,1,0:T(8,128)(2,1)S(1)}, bf16[2,112,128]{2,1,0:T(8,128)(2,1)S(1)}, u32[]{:S(2)}, u32[]{:S(2)}) collective-permute-start(bf16[2,112,128]{2,1,0:T(8,128)(2,1)S(1)} %add_convert_fusion), channel_id=1, source_target_pairs={{8,0},{12,4},{0,8},{4,12},{9,1},{13,5},{1,9},{5,13},{10,2},{14,6},... | collective-permute-start | bytes 172040 | tf_op jit(solution)/shard_map/ppermute | solution.py:28
  29.7 6.6 %collective-permute-start.11 = (bf16[2,4,112,128]{3,2,1,0:T(8,128)(2,1)S(1)}, bf16[2,4,112,128]{3,2,1,0:T(8,128)(2,1)S(1)}, u32[]{:S(2)}, u32[]{:S(2)}) collective-permute-start(bf16[2,4,112,128]{3,2,1,0:T(8,128)(2,1)S(1)} %pad_maximum_fusion.own), channel_id=1, source_target_pairs={{64,0},{65,1},{66,2},{67,3},{68,4},{69,5},{70,6},{71,7},{72,8},{73... | collective-permute-start | bytes 688136 | tf_op jit(solution)/shard_map/ppermute | solution.py:37
  31.0 8.2 %collective-permute-start.14 = (bf16[2,4,112,128]{3,2,1,0:T(8,128)(2,1)S(1)}, bf16[2,4,112,128]{3,2,1,0:T(8,128)(2,1)S(1)}, u32[]{:S(2)}, u32[]{:S(2)}) collective-permute-start(bf16[2,4,112,128]{3,2,1,0:T(8,128)(2,1)S(1)} %pad_maximum_fusion.own), channel_id=1, source_target_pairs={{3,0},{2,1},{1,2},{0,3},{7,4},{6,5},{5,6},{4,7},{11,8},{10,9},{9,1... | collective-permute-start | bytes 688136 | tf_op jit(solution)/shard_map/ppermute | solution.py:37
  32.9 7.8 %collective-permute-start.9 = (bf16[2,4,112,128]{3,2,1,0:T(8,128)(2,1)S(1)}, bf16[2,4,112,128]{3,2,1,0:T(8,128)(2,1)S(1)}, u32[]{:S(2)}, u32[]{:S(2)}) collective-permute-start(bf16[2,4,112,128]{3,2,1,0:T(8,128)(2,1)S(1)} %pad_maximum_fusion.own), channel_id=1, source_target_pairs={{192,0},{193,1},{194,2},{195,3},{196,4},{197,5},{198,6},{199,7},{2... | collective-permute-start | bytes 688136 | tf_op jit(solution)/shard_map/ppermute | solution.py:37
  34.8 7.3 %collective-permute-start.18 = (bf16[2,4,112,128]{3,2,1,0:T(8,128)(2,1)S(1)}, bf16[2,4,112,128]{3,2,1,0:T(8,128)(2,1)S(1)}, u32[]{:S(2)}, u32[]{:S(2)}) collective-permute-start(bf16[2,4,112,128]{3,2,1,0:T(8,128)(2,1)S(1)} %pad_maximum_fusion.own), channel_id=1, source_target_pairs={{1,0},{0,1},{3,2},{2,3},{5,4},{4,5},{7,6},{6,7},{9,8},{8,9},{11,10... | collective-permute-start | bytes 688136 | tf_op jit(solution)/shard_map/ppermute | solution.py:37
  36.3 8.2 %collective-permute-start.12 = (bf16[2,4,112,128]{3,2,1,0:T(8,128)(2,1)S(1)}, bf16[2,4,112,128]{3,2,1,0:T(8,128)(2,1)S(1)}, u32[]{:S(2)}, u32[]{:S(2)}) collective-permute-start(bf16[2,4,112,128]{3,2,1,0:T(8,128)(2,1)S(1)} %collective-permute-done.11.near1), channel_id=1, source_target_pairs={{192,0},{193,1},{194,2},{195,3},{196,4},{197,5},{198,6},{199,7},{2... | collective-permute-start | bytes 688136 | tf_op jit(solution)/shard_map/ppermute | solution.py:37
  37.4 8.2 %collective-permute-start.16 = (bf16[2,4,112,128]{3,2,1,0:T(8,128)(2,1)S(1)}, bf16[2,4,112,128]{3,2,1,0:T(8,128)(2,1)S(1)}, u32[]{:S(2)}, u32[]{:S(2)}) collective-permute-start(bf16[2,4,112,128]{3,2,1,0:T(8,128)(2,1)S(1)} %collective-permute-done.11.near1), channel_id=1, source_target_pairs={{3,0},{2,1},{1,2},{0,3},{7,4},{6,5},{5,6},{4,7},{11,8},{10,9},{9,1... | collective-permute-start | bytes 688136 | tf_op jit(solution)/shard_map/ppermute | solution.py:37
  39.2 8.5 %collective-permute-start.19 = (bf16[2,4,112,128]{3,2,1,0:T(8,128)(2,1)S(1)}, bf16[2,4,112,128]{3,2,1,0:T(8,128)(2,1)S(1)}, u32[]{:S(2)}, u32[]{:S(2)}) collective-permute-start(bf16[2,4,112,128]{3,2,1,0:T(8,128)(2,1)S(1)} %collective-permute-done.11.near1), channel_id=1, source_target_pairs={{1,0},{0,1},{3,2},{2,3},{5,4},{4,5},{7,6},{6,7},{9,8},{8,9},{11,10... | collective-permute-start | bytes 688136 | tf_op jit(solution)/shard_map/ppermute | solution.py:37
  40.7 9.2 %collective-permute-start.20 = (bf16[2,4,112,128]{3,2,1,0:T(8,128)(2,1)S(1)}, bf16[2,4,112,128]{3,2,1,0:T(8,128)(2,1)S(1)}, u32[]{:S(2)}, u32[]{:S(2)}) collective-permute-start(bf16[2,4,112,128]{3,2,1,0:T(8,128)(2,1)S(1)} %collective-permute-done.9.near3), channel_id=1, source_target_pairs={{3,0},{2,1},{1,2},{0,3},{7,4},{6,5},{5,6},{4,7},{11,8},{10,9},{9,1... | collective-permute-start | bytes 688136 | tf_op jit(solution)/shard_map/ppermute | solution.py:37
  42.1 9.5 %collective-permute-start.10 = (bf16[2,4,112,128]{3,2,1,0:T(8,128)(2,1)S(1)}, bf16[2,4,112,128]{3,2,1,0:T(8,128)(2,1)S(1)}, u32[]{:S(2)}, u32[]{:S(2)}) collective-permute-start(bf16[2,4,112,128]{3,2,1,0:T(8,128)(2,1)S(1)} %collective-permute-done.9.near3), channel_id=1, source_target_pairs={{1,0},{0,1},{3,2},{2,3},{5,4},{4,5},{7,6},{6,7},{9,8},{8,9},{11,10... | collective-permute-start | bytes 688136 | tf_op jit(solution)/shard_map/ppermute | solution.py:37
  44.4 8.3 %collective-permute-start.13 = (bf16[2,4,112,128]{3,2,1,0:T(8,128)(2,1)S(1)}, bf16[2,4,112,128]{3,2,1,0:T(8,128)(2,1)S(1)}, u32[]{:S(2)}, u32[]{:S(2)}) collective-permute-start(bf16[2,4,112,128]{3,2,1,0:T(8,128)(2,1)S(1)} %collective-permute-done.12.far), channel_id=1, source_target_pairs={{1,0},{0,1},{3,2},{2,3},{5,4},{4,5},{7,6},{6,7},{9,8},{8,9},{11,10... | collective-permute-start | bytes 688136 | tf_op jit(solution)/shard_map/ppermute | solution.py:37
  45.5 12.0 %collective-permute-start.21 = (bf16[2,4,112,128]{3,2,1,0:T(8,128)(2,1)S(1)}, bf16[2,4,112,128]{3,2,1,0:T(8,128)(2,1)S(1)}, u32[]{:S(2)}, u32[]{:S(2)}) collective-permute-start(bf16[2,4,112,128]{3,2,1,0:T(8,128)(2,1)S(1)} %collective-permute-done.12.far), channel_id=1, source_target_pairs={{3,0},{2,1},{1,2},{0,3},{7,4},{6,5},{5,6},{4,7},{11,8},{10,9},{9,1... | collective-permute-start | bytes 688136 | tf_op jit(solution)/shard_map/ppermute | solution.py:37
  47.7 9.8 %collective-permute-start.15 = (bf16[2,4,112,128]{3,2,1,0:T(8,128)(2,1)S(1)}, bf16[2,4,112,128]{3,2,1,0:T(8,128)(2,1)S(1)}, u32[]{:S(2)}, u32[]{:S(2)}) collective-permute-start(bf16[2,4,112,128]{3,2,1,0:T(8,128)(2,1)S(1)} %collective-permute-done.14.own3), channel_id=1, source_target_pairs={{1,0},{0,1},{3,2},{2,3},{5,4},{4,5},{7,6},{6,7},{9,8},{8,9},{11,10... | collective-permute-start | bytes 688136 | tf_op jit(solution)/shard_map/ppermute | solution.py:37
  49.8 7.7 %collective-permute-start.17 = (bf16[2,4,112,128]{3,2,1,0:T(8,128)(2,1)S(1)}, bf16[2,4,112,128]{3,2,1,0:T(8,128)(2,1)S(1)}, u32[]{:S(2)}, u32[]{:S(2)}) collective-permute-start(bf16[2,4,112,128]{3,2,1,0:T(8,128)(2,1)S(1)} %collective-permute-done.16.near31), channel_id=1, source_target_pairs={{1,0},{0,1},{3,2},{2,3},{5,4},{4,5},{7,6},{6,7},{9,8},{8,9},{11,10... | collective-permute-start | bytes 688136 | tf_op jit(solution)/shard_map/ppermute | solution.py:37
  51.7 14.5 %collective-permute-start.22 = (bf16[2,4,112,128]{3,2,1,0:T(8,128)(2,1)S(1)}, bf16[2,4,112,128]{3,2,1,0:T(8,128)(2,1)S(1)}, u32[]{:S(2)}, u32[]{:S(2)}) collective-permute-start(bf16[2,4,112,128]{3,2,1,0:T(8,128)(2,1)S(1)} %collective-permute-done.10.near31), channel_id=1, source_target_pairs={{3,0},{2,1},{1,2},{0,3},{7,4},{6,5},{5,6},{4,7},{11,8},{10,9},{9,1... | collective-permute-start | bytes 688136 | tf_op jit(solution)/shard_map/ppermute | solution.py:37
  52.7 13.5 %collective-permute-start.23 = (bf16[2,4,112,128]{3,2,1,0:T(8,128)(2,1)S(1)}, bf16[2,4,112,128]{3,2,1,0:T(8,128)(2,1)S(1)}, u32[]{:S(2)}, u32[]{:S(2)}) collective-permute-start(bf16[2,4,112,128]{3,2,1,0:T(8,128)(2,1)S(1)} %collective-permute-done.13.far1), channel_id=1, source_target_pairs={{3,0},{2,1},{1,2},{0,3},{7,4},{6,5},{5,6},{4,7},{11,8},{10,9},{9,1... | collective-permute-start | bytes 688136 | tf_op jit(solution)/shard_map/ppermute | solution.py:37
  58.7 10.3 %collective-permute-start.24 = (bf16[512,384]{1,0:T(8,128)(2,1)S(1)}, bf16[512,384]{1,0:T(8,128)(2,1)S(1)}, u32[]{:S(2)}, u32[]{:S(2)}) collective-permute-start(bf16[512,384]{1,0:T(8,128)(2,1)S(1)} %get-tuple-element.34), channel_id=1, source_target_pairs={{16,0},{0,16},{17,1},{1,17},{18,2},{2,18},{19,3},{3,19},{20,4},{4,... | collective-permute-start | bytes 1179656 | tf_op jit(solution)/shard_map/ppermute | solution.py:24
  67.4 1.8 %collective-permute-start.25 = (bf16[512,384]{1,0:T(8,128)(2,1)S(1)}, bf16[512,384]{1,0:T(8,128)(2,1)S(1)}, u32[]{:S(2)}, u32[]{:S(2)}) collective-permute-start(bf16[512,384]{1,0:T(8,128)(2,1)S(1)} %shard_map.45), channel_id=1, source_target_pairs={{16,0},{0,16},{17,1},{1,17},{18,2},{2,18},{19,3},{3,19},{20,4},{4,... | collective-permute-start | bytes 1179656 | tf_op jit(solution)/shard_map/ppermute | solution.py:24

commit v12 on v11

--- a/solution.py
+++ b/solution.py
@@ -90,28 +90,28 @@
     return both[pl.ds(first, count)].reshape(count * 448, 768)
 
 
-def product_one(place, own, near1, both, low):
-    @on_core(place, 0)
-    def _():
-        low[...] = dot_t(by_x(own, near1), both[0])
-
-    @on_core(place, 1)
-    def _():
-        low[rows(0)] = dot_t(by_y(own, near1), deep(both, 0, 2))
-
-
-def product_two(place, near3, far, own1, near1, own3, near31, both, start, low, high):
-    @on_core(place, 0)
-    def _():
-        low[...] = (
-            start[...] + dot_t(by_x(own1, near1), both[1]) + dot_t(by_x(own3, near31), both[2])
-        )
+def product_one(place, own, both, out):
+    @on_core(place, 0)
+    def _():
+        out[...] = dot_t(by_x(own), both[0])
+
+    @on_core(place, 1)
+    def _():
+        out[...] = dot_t(by_y(own), both[0])
+
+
+def product_two(place, near1, near3, far, own1, near11, own3, near31, both, start, low, high):
+    @on_core(place, 0)
+    def _():
+        total = dot_t(by_x(own1, near11), both[1]) + dot_t(by_x(own3, near31), both[2])
+        low[rows(0)] = start[...] + total[:256]
+        low[rows(1)] = dot_t(by_x(near1), both[0]) + total[256:]
         high[...] = dot_t(by_x(near3, far), both[0])
 
     @on_core(place, 1)
     def _():
-        low[rows(0)] = start[rows(0)] + dot_t(by_y(near3, far), deep(both, 2, 2))
-        low[rows(1)] = dot_t(by_y(own1, near1), deep(both, 0, 2))
+        low[rows(0)] = start[...] + dot_t(by_y(near1, near3, far), deep(both, 1, 3))
+        low[rows(1)] = dot_t(by_y(own1, near11), deep(both, 0, 2))
         high[rows(0)] = dot_t(by_y(own3, near31), deep(both, 0, 2))
 
 
@@ -215,11 +215,13 @@
     own = jnp.stack([part] + [swap(part, "z_lo", 4, bits) for bits in (1, 2, 3)], 1)
 
     near1, near3 = turn(own, 0, 1), turn(own, 0, 3)
+    total = jax.ShapeDtypeStruct((512, 768), F32)
+    start = call(product_one, jax.ShapeDtypeStruct((256, 768), F32), (place, own, both))
+    near1, start = lax.optimization_barrier((near1, start))
     far = turn(near1, 0, 3)
     one_own, three_own = turn(own, 1, 1), turn(own, 1, 3)
-    total = jax.ShapeDtypeStruct((512, 768), F32)
-    low = call(product_one, total, (place, own, near1, both))
     one_near1, three_near1 = turn(near1, 1, 1), turn(near1, 1, 3)
+    near3, one_own = lax.optimization_barrier((near3, one_own))
     one_near3, three_near3 = turn(near3, 1, 1), turn(near3, 1, 3)
     one_far, three_far = turn(far, 1, 1), turn(far, 1, 3)
     far_own, far_near1 = turn(three_own, 1, 1), turn(three_near1, 1, 1)
@@ -227,7 +229,7 @@
     low, high = call(
         product_two,
         (total, total),
-        (place, near3, far, one_own, one_near1, three_own, three_near1, both, low),
+        (place, near1, near3, far, one_own, one_near1, three_own, three_near1, both, start),
         (VMEM, VMEM),
     )
     half = jax.ShapeDtypeStruct((512, 384), BF16)

time: 71.3 us -> 70.7 us (level)
  starting transfers between devices: 43.8 us -> 40.7 us
  waiting for transfers between devices: 13 us -> 15.5 us
    ppermute x15, starting transfers between devices: 20.6 us -> 17 us  [turn(): return lax.ppermute(block, ROW + COL, pairs)]
    ppermute x15, waiting for transfers between devices: 4.13 us -> 6.69 us  [turn(): return lax.ppermute(block, ROW + COL, pairs)]
where the time goes in v12:
time: 70.7 us; the launch traced here: 70.5 us
  starting transfers between devices  40.7 us (58%)
  waiting for transfers between devices  15.5 us (22%)
  Pallas kernels  12.1 us (17%)
  local copies, waits for them, and re-layouts  1.77 us (3%)
    ppermute x15, starting transfers between devices, turn(): return lax.ppermute(block, ROW + COL, pairs)  17 us
    ppermute x7, starting transfers between devices, swap(): return lax.ppermute(block, axis, [(i ^ bits, i) for i in range(size)])  13.2 us
    pallas_call x10, Pallas kernels, call(): pl.pallas_call(kernel, out_shape=out_shape, in_specs=specs or [SMEM] + [V...  12.1 us
    ppermute x4, starting transfers between devices, fetch(): lax.ppermute(block, axis, [((i + ahead) % size, i) for i in range(size)])  10.5 us
    ppermute x7, waiting for transfers between devices, swap(): return lax.ppermute(block, axis, [(i ^ bits, i) for i in range(size)])  6.97 us
    ppermute x15, waiting for transfers between devices, turn(): return lax.ppermute(block, ROW + COL, pairs)  6.69 us
    ppermute x4, waiting for transfers between devices, fetch(): lax.ppermute(block, axis, [((i + ahead) % size, i) for i in range(size)])  1.83 us
    unnamed x6, local copies, waits for them, and re-layouts  1.77 us
  transfers between devices with their start and end apart: 26, of which 12 were waited for; matrix products, arithmetic and copies ran while one was open for 0% of the time, Pallas kernels for 15%

profile of v12, /device:TPU:1, one launch (start us, length us, event | category | flops | bytes accessed | tf_op | source)
XLA Modules:
  0.0 70.5 jit_solution(10544021488288823521)
XLA Ops:
  0.0 3.2 %collective-permute-start.5 = (bf16[1792,384]{1,0:T(8,128)(2,1)}, bf16[1792,384]{1,0:T(8,128)(2,1)S(1)}, u32[]{:S(2)}, u32[]{:S(2)}) collective-permute-start(bf16[1792,384]{1,0:T(8,128)(2,1)} %own.1), channel_id=1, source_target_pairs={{16,0},{0,16},{17,1},{1,17},{18,2},{2,18},{19,3},{3,19},{20,4},{4,... | collective-permute-start | bytes 4128776 | tf_op jit(solution)/shard_map/ppermute | solution.py:24
  3.3 1.0 %copy-done.1 = bf16[112,2048]{1,0:T(8,128)(2,1)S(1)} copy-done((bf16[112,2048]{1,0:T(8,128)(2,1)S(1)}, bf16[112,2048]{1,0:T(8,128)(2,1)}, u32[]{:S(2)}) %copy-start.1) | copy-done | bytes 458776
  5.1 1.0 %shard_map.37 = (f32[8,112,128]{2,1,0:T(8,128)S(1)}, f32[8,112,128]{2,1,0:T(8,128)S(1)}) custom-call(s32[4]{0:T(128)S(1)} %pad_add_fusion.place, bf16[112,112]{1,0:T(8,128)(2,1)S(1)} %copy-done.2, bf16[112,2048]{1,0:T(8,128)(2,1)S(1)} %copy-done.1), custom_call_target="tpu_custom_call" | custom-call | tf_op jit(solution)/shard_map/pallas_call | solution.py:180
  6.2 1.7 %collective-permute-done.received = f32[8,112,128]{2,1,0:T(8,128)S(1)} collective-permute-done((f32[8,112,128]{2,1,0:T(8,128)S(1)}, f32[8,112,128]{2,1,0:T(8,128)S(1)}, u32[]{:S(2)}, u32[]{:S(2)}) %collective-permute-start) | collective-permute-done | bytes 458784 | tf_op jit(solution)/shard_map/ppermute | solution.py:24
  8.6 0.8 %collective-permute-start.1 = (bf16[2,112,128]{2,1,0:T(8,128)(2,1)S(1)}, bf16[2,112,128]{2,1,0:T(8,128)(2,1)S(1)}, u32[]{:S(2)}, u32[]{:S(2)}) collective-permute-start(bf16[2,112,128]{2,1,0:T(8,128)(2,1)S(1)} %get-tuple-element.27), channel_id=1, source_target_pairs={{192,0},{128,64},{64,128},{0,192},{193,1},{129,65},{65,129},{1,193... | collective-permute-start | bytes 172040 | tf_op jit(solution)/shard_map/ppermute | solution.py:28
  9.9 2.0 %collective-permute-start.3 = (bf16[2,112,128]{2,1,0:T(8,128)(2,1)S(1)}, bf16[2,112,128]{2,1,0:T(8,128)(2,1)S(1)}, u32[]{:S(2)}, u32[]{:S(2)}) collective-permute-start(bf16[2,112,128]{2,1,0:T(8,128)(2,1)S(1)} %get-tuple-element.29), channel_id=1, source_target_pairs={{64,0},{0,64},{192,128},{128,192},{65,1},{1,65},{193,129},{129,193... | collective-permute-start | bytes 172040 | tf_op jit(solution)/shard_map/ppermute | solution.py:28
  11.9 1.0 %collective-permute-done.1 = bf16[2,112,128]{2,1,0:T(8,128)(2,1)S(1)} collective-permute-done((bf16[2,112,128]{2,1,0:T(8,128)(2,1)S(1)}, bf16[2,112,128]{2,1,0:T(8,128)(2,1)S(1)}, u32[]{:S(2)}, u32[]{:S(2)}) %collective-permute-start.1) | collective-permute-done | bytes 57376 | tf_op jit(solution)/shard_map/ppermute | solution.py:28
  12.9 1.1 %collective-permute-done.2 = bf16[2,112,128]{2,1,0:T(8,128)(2,1)S(1)} collective-permute-done((bf16[2,112,128]{2,1,0:T(8,128)(2,1)S(1)}, bf16[2,112,128]{2,1,0:T(8,128)(2,1)S(1)}, u32[]{:S(2)}, u32[]{:S(2)}) %collective-permute-start.2) | collective-permute-done | bytes 57376 | tf_op jit(solution)/shard_map/ppermute | solution.py:28
  14.8 6.2 %collective-permute-start.4 = (bf16[2,112,128]{2,1,0:T(8,128)(2,1)S(1)}, bf16[2,112,128]{2,1,0:T(8,128)(2,1)S(1)}, u32[]{:S(2)}, u32[]{:S(2)}) collective-permute-start(bf16[2,112,128]{2,1,0:T(8,128)(2,1)S(1)} %fusion), channel_id=1, source_target_pairs={{32,0},{0,32},{33,1},{1,33},{34,2},{2,34},{35,3},{3,35},{36,4},{4,... | collective-permute-start | bytes 172040 | tf_op jit(solution)/shard_map/ppermute | solution.py:28
  21.0 0.8 %shard_map.39.both = bf16[4,448,768]{2,1,0:T(8,128)(2,1)S(1)} custom-call(s32[4]{0:T(128)S(1)} %pad_add_fusion.place, bf16[1792,384]{1,0:T(8,128)(2,1)S(1)} %copy-done, bf16[1792,384]{1,0:T(8,128)(2,1)S(1)} %collective-permute-done.5.other), custom_call_target="tpu_custom_call" | custom-call | tf_op jit(solution)/shard_map/pallas_call | solution.py:180
  22.6 2.9 %collective-permute-start.8 = (bf16[2,112,128]{2,1,0:T(8,128)(2,1)S(1)}, bf16[2,112,128]{2,1,0:T(8,128)(2,1)S(1)}, u32[]{:S(2)}, u32[]{:S(2)}) collective-permute-start(bf16[2,112,128]{2,1,0:T(8,128)(2,1)S(1)} %add_convert_fusion), channel_id=1, source_target_pairs={{12,0},{8,4},{4,8},{0,12},{13,1},{9,5},{5,9},{1,13},{14,2},{10,6},... | collective-permute-start | bytes 172040 | tf_op jit(solution)/shard_map/ppermute | solution.py:28
  26.2 1.3 %collective-permute-done.8 = bf16[2,112,128]{2,1,0:T(8,128)(2,1)S(1)} collective-permute-done((bf16[2,112,128]{2,1,0:T(8,128)(2,1)S(1)}, bf16[2,112,128]{2,1,0:T(8,128)(2,1)S(1)}, u32[]{:S(2)}, u32[]{:S(2)}) %collective-permute-start.8) | collective-permute-done | bytes 57376 | tf_op jit(solution)/shard_map/ppermute | solution.py:28
  27.5 1.0 %collective-permute-done.6 = bf16[2,112,128]{2,1,0:T(8,128)(2,1)S(1)} collective-permute-done((bf16[2,112,128]{2,1,0:T(8,128)(2,1)S(1)}, bf16[2,112,128]{2,1,0:T(8,128)(2,1)S(1)}, u32[]{:S(2)}, u32[]{:S(2)}) %collective-permute-start.6) | collective-permute-done | bytes 57376 | tf_op jit(solution)/shard_map/ppermute | solution.py:28
  28.6 1.0 %collective-permute-done.7 = bf16[2,112,128]{2,1,0:T(8,128)(2,1)S(1)} collective-permute-done((bf16[2,112,128]{2,1,0:T(8,128)(2,1)S(1)}, bf16[2,112,128]{2,1,0:T(8,128)(2,1)S(1)}, u32[]{:S(2)}, u32[]{:S(2)}) %collective-permute-start.7) | collective-permute-done | bytes 57376 | tf_op jit(solution)/shard_map/ppermute | solution.py:28
  29.7 1.4 %collective-permute-start.12 = (bf16[2,4,112,128]{3,2,1,0:T(8,128)(2,1)S(1)}, bf16[2,4,112,128]{3,2,1,0:T(8,128)(2,1)S(1)}, u32[]{:S(2)}, u32[]{:S(2)}) collective-permute-start(bf16[2,4,112,128]{3,2,1,0:T(8,128)(2,1)S(1)} %pad_maximum_fusion.own), channel_id=1, source_target_pairs={{64,0},{65,1},{66,2},{67,3},{68,4},{69,5},{70,6},{71,7},{72,8},{73... | collective-permute-start | bytes 688136 | tf_op jit(solution)/shard_map/ppermute | solution.py:37
  31.0 1.9 %collective-permute-start.9 = (bf16[2,4,112,128]{3,2,1,0:T(8,128)(2,1)S(1)}, bf16[2,4,112,128]{3,2,1,0:T(8,128)(2,1)S(1)}, u32[]{:S(2)}, u32[]{:S(2)}) collective-permute-start(bf16[2,4,112,128]{3,2,1,0:T(8,128)(2,1)S(1)} %pad_maximum_fusion.own), channel_id=1, source_target_pairs={{192,0},{193,1},{194,2},{195,3},{196,4},{197,5},{198,6},{199,7},{2... | collective-permute-start | bytes 688136 | tf_op jit(solution)/shard_map/ppermute | solution.py:37
  33.0 3.9 %collective-permute-start.15 = (bf16[2,4,112,128]{3,2,1,0:T(8,128)(2,1)S(1)}, bf16[2,4,112,128]{3,2,1,0:T(8,128)(2,1)S(1)}, u32[]{:S(2)}, u32[]{:S(2)}) collective-permute-start(bf16[2,4,112,128]{3,2,1,0:T(8,128)(2,1)S(1)} %pad_maximum_fusion.own), channel_id=1, source_target_pairs={{3,0},{2,1},{1,2},{0,3},{7,4},{6,5},{5,6},{4,7},{11,8},{10,9},{9,1... | collective-permute-start | bytes 688136 | tf_op jit(solution)/shard_map/ppermute | solution.py:37
  36.9 1.0 %shard_map.40.start = f32[256,768]{1,0:T(8,128)S(1)} custom-call(s32[4]{0:T(128)S(1)} %pad_add_fusion.place, bf16[2,4,112,128]{3,2,1,0:T(8,128)(2,1)S(1)} %pad_maximum_fusion.own, bf16[4,448,768]{2,1,0:T(8,128)(2,1)S(1)} %shard_map.39.both), custom_call_target="tpu_custom_call" | custom-call | tf_op jit(solution)/shard_map/pallas_call | solution.py:180
  37.8 1.1 %collective-permute-start.13 = (bf16[2,4,112,128]{3,2,1,0:T(8,128)(2,1)S(1)}, bf16[2,4,112,128]{3,2,1,0:T(8,128)(2,1)S(1)}, u32[]{:S(2)}, u32[]{:S(2)}) collective-permute-start(bf16[2,4,112,128]{3,2,1,0:T(8,128)(2,1)S(1)} %collective-permute-done.12.near1), channel_id=1, source_target_pairs={{192,0},{193,1},{194,2},{195,3},{196,4},{197,5},{198,6},{199,7},{2... | collective-permute-start | bytes 688136 | tf_op jit(solution)/shard_map/ppermute | solution.py:37
  39.2 1.5 %collective-permute-start.19 = (bf16[2,4,112,128]{3,2,1,0:T(8,128)(2,1)S(1)}, bf16[2,4,112,128]{3,2,1,0:T(8,128)(2,1)S(1)}, u32[]{:S(2)}, u32[]{:S(2)}) collective-permute-start(bf16[2,4,112,128]{3,2,1,0:T(8,128)(2,1)S(1)} %collective-permute-done.12.near1), channel_id=1, source_target_pairs={{1,0},{0,1},{3,2},{2,3},{5,4},{4,5},{7,6},{6,7},{9,8},{8,9},{11,10... | collective-permute-start | bytes 688136 | tf_op jit(solution)/shard_map/ppermute | solution.py:37
  40.7 1.0 %collective-permute-start.20 = (bf16[2,4,112,128]{3,2,1,0:T(8,128)(2,1)S(1)}, bf16[2,4,112,128]{3,2,1,0:T(8,128)(2,1)S(1)}, u32[]{:S(2)}, u32[]{:S(2)}) collective-permute-start(bf16[2,4,112,128]{3,2,1,0:T(8,128)(2,1)S(1)} %collective-permute-done.9.near3), channel_id=1, source_target_pairs={{3,0},{2,1},{1,2},{0,3},{7,4},{6,5},{5,6},{4,7},{11,8},{10,9},{9,1... | collective-permute-start | bytes 688136 | tf_op jit(solution)/shard_map/ppermute | solution.py:37
  42.4 4.0 %collective-permute-done.13.far = bf16[2,4,112,128]{3,2,1,0:T(8,128)(2,1)S(1)} collective-permute-done((bf16[2,4,112,128]{3,2,1,0:T(8,128)(2,1)S(1)}, bf16[2,4,112,128]{3,2,1,0:T(8,128)(2,1)S(1)}, u32[]{:S(2)}, u32[]{:S(2)}) %collective-permute-start.13) | collective-permute-done | bytes 229408 | tf_op jit(solution)/shard_map/ppermute | solution.py:37
  46.4 2.5 %collective-permute-start.21 = (bf16[2,4,112,128]{3,2,1,0:T(8,128)(2,1)S(1)}, bf16[2,4,112,128]{3,2,1,0:T(8,128)(2,1)S(1)}, u32[]{:S(2)}, u32[]{:S(2)}) collective-permute-start(bf16[2,4,112,128]{3,2,1,0:T(8,128)(2,1)S(1)} %collective-permute-done.13.far), channel_id=1, source_target_pairs={{3,0},{2,1},{1,2},{0,3},{7,4},{6,5},{5,6},{4,7},{11,8},{10,9},{9,1... | collective-permute-start | bytes 688136 | tf_op jit(solution)/shard_map/ppermute | solution.py:37
  49.0 1.9 %collective-permute-done.20.near33 = bf16[2,4,112,128]{3,2,1,0:T(8,128)(2,1)S(1)} collective-permute-done((bf16[2,4,112,128]{3,2,1,0:T(8,128)(2,1)S(1)}, bf16[2,4,112,128]{3,2,1,0:T(8,128)(2,1)S(1)}, u32[]{:S(2)}, u32[]{:S(2)}) %collective-permute-start.20) | collective-permute-done | bytes 229408 | tf_op jit(solution)/shard_map/ppermute | solution.py:37
  50.9 2.2 %collective-permute-start.22 = (bf16[2,4,112,128]{3,2,1,0:T(8,128)(2,1)S(1)}, bf16[2,4,112,128]{3,2,1,0:T(8,128)(2,1)S(1)}, u32[]{:S(2)}, u32[]{:S(2)}) collective-permute-start(bf16[2,4,112,128]{3,2,1,0:T(8,128)(2,1)S(1)} %collective-permute-done.11.near31), channel_id=1, source_target_pairs={{3,0},{2,1},{1,2},{0,3},{7,4},{6,5},{5,6},{4,7},{11,8},{10,9},{9,1... | collective-permute-start | bytes 688136 | tf_op jit(solution)/shard_map/ppermute | solution.py:37
  53.6 2.2 %shard_map.41 = (f32[512,768]{1,0:T(8,128)S(1)}, f32[512,768]{1,0:T(8,128)S(1)}) custom-call(s32[4]{0:T(128)S(1)} %pad_add_fusion.place, bf16[2,4,112,128]{3,2,1,0:T(8,128)(2,1)S(1)} %collective-permute-done.12.near1, bf16[2,4,112,128]{3,2,1,0:T(8,128)(2,1)S(1)} %collective-permute-done.9.near3, bf16[2,4,112,128]{3,2,1,0:T(8,128)(2,1)S(1)} %collective-permute-done.13.far, ...), custom_call_target="tpu_custom_call" | custom-call | tf_op jit(solution)/shard_map/pallas_call | solution.py:180
  56.6 1.2 %shard_map.42 = (bf16[512,384]{1,0:T(8,128)(2,1)S(1)}, bf16[512,384]{1,0:T(8,128)(2,1)S(1)}) custom-call(s32[4]{0:T(128)S(1)} %pad_add_fusion.place, bf16[2,4,112,128]{3,2,1,0:T(8,128)(2,1)S(1)} %collective-permute-done.11.near31, bf16[2,4,112,128]{3,2,1,0:T(8,128)(2,1)S(1)} %collective-permute-done.14.far1, ...), custom_call_target="tpu_custom_call" | custom-call | tf_op jit(solution)/shard_map/pallas_call | solution.py:180
  57.8 6.4 %collective-permute-start.24 = (bf16[512,384]{1,0:T(8,128)(2,1)S(1)}, bf16[512,384]{1,0:T(8,128)(2,1)S(1)}, u32[]{:S(2)}, u32[]{:S(2)}) collective-permute-start(bf16[512,384]{1,0:T(8,128)(2,1)S(1)} %get-tuple-element.42), channel_id=1, source_target_pairs={{16,0},{0,16},{17,1},{1,17},{18,2},{2,18},{19,3},{3,19},{20,4},{4,... | collective-permute-start | bytes 1179656 | tf_op jit(solution)/shard_map/ppermute | solution.py:24
  64.2 1.2 %shard_map.43.high = f32[512,768]{1,0:T(8,128)S(1)} custom-call(s32[4]{0:T(128)S(1)} %pad_add_fusion.place, bf16[2,4,112,128]{3,2,1,0:T(8,128)(2,1)S(1)} %collective-permute-done.11.near31, bf16[2,4,112,128]{3,2,1,0:T(8,128)(2,1)S(1)} %collective-permute-done.14.far1, bf16[2,4,112,128]{3,2,1,0:T(8,128)(2,1)S(1)} %collective-permute-done.20.near33, ...), custom_call_target="tpu_custom_call" | custom-call | tf_op jit(solution)/shard_map/pallas_call | solution.py:180
  65.4 1.2 %shard_map.45 = bf16[512,384]{1,0:T(8,128)(2,1)S(1)} custom-call(s32[4]{0:T(128)S(1)} %pad_add_fusion.place, bf16[2,4,112,128]{3,2,1,0:T(8,128)(2,1)S(1)} %collective-permute-done.16.own, bf16[2,4,112,128]{3,2,1,0:T(8,128)(2,1)S(1)} %collective-permute-done.18.near1, bf16[2,4,112,128]{3,2,1,0:T(8,128)(2,1)S(1)} %collective-permute-done.22.near3, ...), custom_call_target="tpu_custom_call" | custom-call | tf_op jit(solution)/shard_map/pallas_call | solution.py:180
  67.3 1.2 %shard_map.44.mine2 = bf16[512,384]{1,0:T(8,128)(2,1)S(1)} custom-call(s32[4]{0:T(128)S(1)} %pad_add_fusion.place, bf16[2,4,112,128]{3,2,1,0:T(8,128)(2,1)S(1)} %collective-permute-done.16.own, bf16[2,4,112,128]{3,2,1,0:T(8,128)(2,1)S(1)} %collective-permute-done.18.near1, bf16[2,4,112,128]{3,2,1,0:T(8,128)(2,1)S(1)} %collective-permute-done.22.near3, ...), custom_call_target="tpu_custom_call" | custom-call | tf_op jit(solution)/shard_map/pallas_call | solution.py:180
  68.6 1.7 %shard_map.46 = bf16[2048,384]{1,0:T(8,128)(2,1)} custom-call(s32[4]{0:T(128)S(1)} %pad_add_fusion.place, bf16[512,384]{1,0:T(8,128)(2,1)S(1)} %get-tuple-element.38.mine1, bf16[512,384]{1,0:T(8,128)(2,1)S(1)} %shard_map.44.mine2, bf16[512,384]{1,0:T(8,128)(2,1)S(1)} %collective-permute-done.24.theirs1, bf16[512,384]{1,0:T(8,128)(2,1)S(1)} %collective-permute-done.25.theirs2), custom_call_target="tpu_custom_call" | custom-call | tf_op jit(solution)/shard_map/pallas_call | solution.py:180
  (40 shorter events, 7.5 us)
Async XLA Ops:
  0.0 21.0 %copy-start = (bf16[1792,384]{1,0:T(8,128)(2,1)S(1)}, bf16[1792,384]{1,0:T(8,128)(2,1)}, u32[]{:S(2)}) copy-start(bf16[1792,384]{1,0:T(8,128)(2,1)} %own.1) | copy-start | bytes 4128772
  0.0 21.0 %collective-permute-start.5 = (bf16[1792,384]{1,0:T(8,128)(2,1)}, bf16[1792,384]{1,0:T(8,128)(2,1)S(1)}, u32[]{:S(2)}, u32[]{:S(2)}) collective-permute-start(bf16[1792,384]{1,0:T(8,128)(2,1)} %own.1), channel_id=1, source_target_pairs={{16,0},{0,16},{17,1},{1,17},{18,2},{2,18},{19,3},{3,19},{20,4},{4,... | collective-permute-start | bytes 4128776 | tf_op jit(solution)/shard_map/ppermute | solution.py:24
  3.3 1.0 %copy-start.1 = (bf16[112,2048]{1,0:T(8,128)(2,1)S(1)}, bf16[112,2048]{1,0:T(8,128)(2,1)}, u32[]{:S(2)}) copy-start(bf16[112,2048]{1,0:T(8,128)(2,1)} %panel.1) | copy-start | bytes 1376260
  4.3 0.7 %copy-start.2 = (bf16[112,112]{1,0:T(8,128)(2,1)S(1)}, bf16[112,112]{1,0:T(8,128)(2,1)}, u32[]{:S(2)}) copy-start(bf16[112,112]{1,0:T(8,128)(2,1)} %screening.1) | copy-start | bytes 75268
  6.1 1.9 %collective-permute-start = (f32[8,112,128]{2,1,0:T(8,128)S(1)}, f32[8,112,128]{2,1,0:T(8,128)S(1)}, u32[]{:S(2)}, u32[]{:S(2)}) collective-permute-start(f32[8,112,128]{2,1,0:T(8,128)S(1)} %get-tuple-element.25), channel_id=1, source_target_pairs={{16,0},{0,16},{17,1},{1,17},{18,2},{2,18},{19,3},{3,19},{20,4},{4,... | collective-permute-start | bytes 1376264 | tf_op jit(solution)/shard_map/ppermute | solution.py:24
  8.6 4.3 %collective-permute-start.1 = (bf16[2,112,128]{2,1,0:T(8,128)(2,1)S(1)}, bf16[2,112,128]{2,1,0:T(8,128)(2,1)S(1)}, u32[]{:S(2)}, u32[]{:S(2)}) collective-permute-start(bf16[2,112,128]{2,1,0:T(8,128)(2,1)S(1)} %get-tuple-element.27), channel_id=1, source_target_pairs={{192,0},{128,64},{64,128},{0,192},{193,1},{129,65},{65,129},{1,193... | collective-permute-start | bytes 172040 | tf_op jit(solution)/shard_map/ppermute | solution.py:28
  9.4 4.6 %collective-permute-start.2 = (bf16[2,112,128]{2,1,0:T(8,128)(2,1)S(1)}, bf16[2,112,128]{2,1,0:T(8,128)(2,1)S(1)}, u32[]{:S(2)}, u32[]{:S(2)}) collective-permute-start(bf16[2,112,128]{2,1,0:T(8,128)(2,1)S(1)} %get-tuple-element.28), channel_id=1, source_target_pairs={{128,0},{192,64},{0,128},{64,192},{129,1},{193,65},{1,129},{65,193... | collective-permute-start | bytes 172040 | tf_op jit(solution)/shard_map/ppermute | solution.py:28
  9.9 4.8 %collective-permute-start.3 = (bf16[2,112,128]{2,1,0:T(8,128)(2,1)S(1)}, bf16[2,112,128]{2,1,0:T(8,128)(2,1)S(1)}, u32[]{:S(2)}, u32[]{:S(2)}) collective-permute-start(bf16[2,112,128]{2,1,0:T(8,128)(2,1)S(1)} %get-tuple-element.29), channel_id=1, source_target_pairs={{64,0},{0,64},{192,128},{128,192},{65,1},{1,65},{193,129},{129,193... | collective-permute-start | bytes 172040 | tf_op jit(solution)/shard_map/ppermute | solution.py:28
  14.8 7.8 %collective-permute-start.4 = (bf16[2,112,128]{2,1,0:T(8,128)(2,1)S(1)}, bf16[2,112,128]{2,1,0:T(8,128)(2,1)S(1)}, u32[]{:S(2)}, u32[]{:S(2)}) collective-permute-start(bf16[2,112,128]{2,1,0:T(8,128)(2,1)S(1)} %fusion), channel_id=1, source_target_pairs={{32,0},{0,32},{33,1},{1,33},{34,2},{2,34},{35,3},{3,35},{36,4},{4,... | collective-permute-start | bytes 172040 | tf_op jit(solution)/shard_map/ppermute | solution.py:28
  22.6 4.9 %collective-permute-start.8 = (bf16[2,112,128]{2,1,0:T(8,128)(2,1)S(1)}, bf16[2,112,128]{2,1,0:T(8,128)(2,1)S(1)}, u32[]{:S(2)}, u32[]{:S(2)}) collective-permute-start(bf16[2,112,128]{2,1,0:T(8,128)(2,1)S(1)} %add_convert_fusion), channel_id=1, source_target_pairs={{12,0},{8,4},{4,8},{0,12},{13,1},{9,5},{5,9},{1,13},{14,2},{10,6},... | collective-permute-start | bytes 172040 | tf_op jit(solution)/shard_map/ppermute | solution.py:28
  25.5 3.0 %collective-permute-start.6 = (bf16[2,112,128]{2,1,0:T(8,128)(2,1)S(1)}, bf16[2,112,128]{2,1,0:T(8,128)(2,1)S(1)}, u32[]{:S(2)}, u32[]{:S(2)}) collective-permute-start(bf16[2,112,128]{2,1,0:T(8,128)(2,1)S(1)} %add_convert_fusion), channel_id=1, source_target_pairs={{4,0},{0,4},{12,8},{8,12},{5,1},{1,5},{13,9},{9,13},{6,2},{2,6},{1... | collective-permute-start | bytes 172040 | tf_op jit(solution)/shard_map/ppermute | solution.py:28
  25.5 4.1 %collective-permute-start.7 = (bf16[2,112,128]{2,1,0:T(8,128)(2,1)S(1)}, bf16[2,112,128]{2,1,0:T(8,128)(2,1)S(1)}, u32[]{:S(2)}, u32[]{:S(2)}) collective-permute-start(bf16[2,112,128]{2,1,0:T(8,128)(2,1)S(1)} %add_convert_fusion), channel_id=1, source_target_pairs={{8,0},{12,4},{0,8},{4,12},{9,1},{13,5},{1,9},{5,13},{10,2},{14,6},... | collective-permute-start | bytes 172040 | tf_op jit(solution)/shard_map/ppermute | solution.py:28
  29.7 8.2 %collective-permute-start.12 = (bf16[2,4,112,128]{3,2,1,0:T(8,128)(2,1)S(1)}, bf16[2,4,112,128]{3,2,1,0:T(8,128)(2,1)S(1)}, u32[]{:S(2)}, u32[]{:S(2)}) collective-permute-start(bf16[2,4,112,128]{3,2,1,0:T(8,128)(2,1)S(1)} %pad_maximum_fusion.own), channel_id=1, source_target_pairs={{64,0},{65,1},{66,2},{67,3},{68,4},{69,5},{70,6},{71,7},{72,8},{73... | collective-permute-start | bytes 688136 | tf_op jit(solution)/shard_map/ppermute | solution.py:37
  31.0 8.2 %collective-permute-start.10 = (bf16[2,4,112,128]{3,2,1,0:T(8,128)(2,1)S(1)}, bf16[2,4,112,128]{3,2,1,0:T(8,128)(2,1)S(1)}, u32[]{:S(2)}, u32[]{:S(2)}) collective-permute-start(bf16[2,4,112,128]{3,2,1,0:T(8,128)(2,1)S(1)} %pad_maximum_fusion.own), channel_id=1, source_target_pairs={{1,0},{0,1},{3,2},{2,3},{5,4},{4,5},{7,6},{6,7},{9,8},{8,9},{11,10... | collective-permute-start | bytes 688136 | tf_op jit(solution)/shard_map/ppermute | solution.py:37
  31.0 9.6 %collective-permute-start.9 = (bf16[2,4,112,128]{3,2,1,0:T(8,128)(2,1)S(1)}, bf16[2,4,112,128]{3,2,1,0:T(8,128)(2,1)S(1)}, u32[]{:S(2)}, u32[]{:S(2)}) collective-permute-start(bf16[2,4,112,128]{3,2,1,0:T(8,128)(2,1)S(1)} %pad_maximum_fusion.own), channel_id=1, source_target_pairs={{192,0},{193,1},{194,2},{195,3},{196,4},{197,5},{198,6},{199,7},{2... | collective-permute-start | bytes 688136 | tf_op jit(solution)/shard_map/ppermute | solution.py:37
  33.0 8.8 %collective-permute-start.15 = (bf16[2,4,112,128]{3,2,1,0:T(8,128)(2,1)S(1)}, bf16[2,4,112,128]{3,2,1,0:T(8,128)(2,1)S(1)}, u32[]{:S(2)}, u32[]{:S(2)}) collective-permute-start(bf16[2,4,112,128]{3,2,1,0:T(8,128)(2,1)S(1)} %pad_maximum_fusion.own), channel_id=1, source_target_pairs={{3,0},{2,1},{1,2},{0,3},{7,4},{6,5},{5,6},{4,7},{11,8},{10,9},{9,1... | collective-permute-start | bytes 688136 | tf_op jit(solution)/shard_map/ppermute | solution.py:37
  37.8 8.6 %collective-permute-start.13 = (bf16[2,4,112,128]{3,2,1,0:T(8,128)(2,1)S(1)}, bf16[2,4,112,128]{3,2,1,0:T(8,128)(2,1)S(1)}, u32[]{:S(2)}, u32[]{:S(2)}) collective-permute-start(bf16[2,4,112,128]{3,2,1,0:T(8,128)(2,1)S(1)} %collective-permute-done.12.near1), channel_id=1, source_target_pairs={{192,0},{193,1},{194,2},{195,3},{196,4},{197,5},{198,6},{199,7},{2... | collective-permute-start | bytes 688136 | tf_op jit(solution)/shard_map/ppermute | solution.py:37
  38.9 7.5 %collective-permute-start.17 = (bf16[2,4,112,128]{3,2,1,0:T(8,128)(2,1)S(1)}, bf16[2,4,112,128]{3,2,1,0:T(8,128)(2,1)S(1)}, u32[]{:S(2)}, u32[]{:S(2)}) collective-permute-start(bf16[2,4,112,128]{3,2,1,0:T(8,128)(2,1)S(1)} %collective-permute-done.12.near1), channel_id=1, source_target_pairs={{3,0},{2,1},{1,2},{0,3},{7,4},{6,5},{5,6},{4,7},{11,8},{10,9},{9,1... | collective-permute-start | bytes 688136 | tf_op jit(solution)/shard_map/ppermute | solution.py:37
  39.2 9.7 %collective-permute-start.19 = (bf16[2,4,112,128]{3,2,1,0:T(8,128)(2,1)S(1)}, bf16[2,4,112,128]{3,2,1,0:T(8,128)(2,1)S(1)}, u32[]{:S(2)}, u32[]{:S(2)}) collective-permute-start(bf16[2,4,112,128]{3,2,1,0:T(8,128)(2,1)S(1)} %collective-permute-done.12.near1), channel_id=1, source_target_pairs={{1,0},{0,1},{3,2},{2,3},{5,4},{4,5},{7,6},{6,7},{9,8},{8,9},{11,10... | collective-permute-start | bytes 688136 | tf_op jit(solution)/shard_map/ppermute | solution.py:37
  40.7 10.2 %collective-permute-start.20 = (bf16[2,4,112,128]{3,2,1,0:T(8,128)(2,1)S(1)}, bf16[2,4,112,128]{3,2,1,0:T(8,128)(2,1)S(1)}, u32[]{:S(2)}, u32[]{:S(2)}) collective-permute-start(bf16[2,4,112,128]{3,2,1,0:T(8,128)(2,1)S(1)} %collective-permute-done.9.near3), channel_id=1, source_target_pairs={{3,0},{2,1},{1,2},{0,3},{7,4},{6,5},{5,6},{4,7},{11,8},{10,9},{9,1... | collective-permute-start | bytes 688136 | tf_op jit(solution)/shard_map/ppermute | solution.py:37
  41.7 9.2 %collective-permute-start.11 = (bf16[2,4,112,128]{3,2,1,0:T(8,128)(2,1)S(1)}, bf16[2,4,112,128]{3,2,1,0:T(8,128)(2,1)S(1)}, u32[]{:S(2)}, u32[]{:S(2)}) collective-permute-start(bf16[2,4,112,128]{3,2,1,0:T(8,128)(2,1)S(1)} %collective-permute-done.9.near3), channel_id=1, source_target_pairs={{1,0},{0,1},{3,2},{2,3},{5,4},{4,5},{7,6},{6,7},{9,8},{8,9},{11,10... | collective-permute-start | bytes 688136 | tf_op jit(solution)/shard_map/ppermute | solution.py:37
  46.4 6.7 %collective-permute-start.14 = (bf16[2,4,112,128]{3,2,1,0:T(8,128)(2,1)S(1)}, bf16[2,4,112,128]{3,2,1,0:T(8,128)(2,1)S(1)}, u32[]{:S(2)}, u32[]{:S(2)}) collective-permute-start(bf16[2,4,112,128]{3,2,1,0:T(8,128)(2,1)S(1)} %collective-permute-done.13.far), channel_id=1, source_target_pairs={{1,0},{0,1},{3,2},{2,3},{5,4},{4,5},{7,6},{6,7},{9,8},{8,9},{11,10... | collective-permute-start | bytes 688136 | tf_op jit(solution)/shard_map/ppermute | solution.py:37
  46.4 9.4 %collective-permute-start.21 = (bf16[2,4,112,128]{3,2,1,0:T(8,128)(2,1)S(1)}, bf16[2,4,112,128]{3,2,1,0:T(8,128)(2,1)S(1)}, u32[]{:S(2)}, u32[]{:S(2)}) collective-permute-start(bf16[2,4,112,128]{3,2,1,0:T(8,128)(2,1)S(1)} %collective-permute-done.13.far), channel_id=1, source_target_pairs={{3,0},{2,1},{1,2},{0,3},{7,4},{6,5},{5,6},{4,7},{11,8},{10,9},{9,1... | collective-permute-start | bytes 688136 | tf_op jit(solution)/shard_map/ppermute | solution.py:37
  49.0 6.9 %collective-permute-start.16 = (bf16[2,4,112,128]{3,2,1,0:T(8,128)(2,1)S(1)}, bf16[2,4,112,128]{3,2,1,0:T(8,128)(2,1)S(1)}, u32[]{:S(2)}, u32[]{:S(2)}) collective-permute-start(bf16[2,4,112,128]{3,2,1,0:T(8,128)(2,1)S(1)} %collective-permute-done.15.own3), channel_id=1, source_target_pairs={{1,0},{0,1},{3,2},{2,3},{5,4},{4,5},{7,6},{6,7},{9,8},{8,9},{11,10... | collective-permute-start | bytes 688136 | tf_op jit(solution)/shard_map/ppermute | solution.py:37
  50.9 5.7 %collective-permute-start.18 = (bf16[2,4,112,128]{3,2,1,0:T(8,128)(2,1)S(1)}, bf16[2,4,112,128]{3,2,1,0:T(8,128)(2,1)S(1)}, u32[]{:S(2)}, u32[]{:S(2)}) collective-permute-start(bf16[2,4,112,128]{3,2,1,0:T(8,128)(2,1)S(1)} %collective-permute-done.17.near31), channel_id=1, source_target_pairs={{1,0},{0,1},{3,2},{2,3},{5,4},{4,5},{7,6},{6,7},{9,8},{8,9},{11,10... | collective-permute-start | bytes 688136 | tf_op jit(solution)/shard_map/ppermute | solution.py:37
  50.9 14.5 %collective-permute-start.22 = (bf16[2,4,112,128]{3,2,1,0:T(8,128)(2,1)S(1)}, bf16[2,4,112,128]{3,2,1,0:T(8,128)(2,1)S(1)}, u32[]{:S(2)}, u32[]{:S(2)}) collective-permute-start(bf16[2,4,112,128]{3,2,1,0:T(8,128)(2,1)S(1)} %collective-permute-done.11.near31), channel_id=1, source_target_pairs={{3,0},{2,1},{1,2},{0,3},{7,4},{6,5},{5,6},{4,7},{11,8},{10,9},{9,1... | collective-permute-start | bytes 688136 | tf_op jit(solution)/shard_map/ppermute | solution.py:37
  53.1 12.3 %collective-permute-start.23 = (bf16[2,4,112,128]{3,2,1,0:T(8,128)(2,1)S(1)}, bf16[2,4,112,128]{3,2,1,0:T(8,128)(2,1)S(1)}, u32[]{:S(2)}, u32[]{:S(2)}) collective-permute-start(bf16[2,4,112,128]{3,2,1,0:T(8,128)(2,1)S(1)} %collective-permute-done.14.far1), channel_id=1, source_target_pairs={{3,0},{2,1},{1,2},{0,3},{7,4},{6,5},{5,6},{4,7},{11,8},{10,9},{9,1... | collective-permute-start | bytes 688136 | tf_op jit(solution)/shard_map/ppermute | solution.py:37
  57.8 10.8 %collective-permute-start.24 = (bf16[512,384]{1,0:T(8,128)(2,1)S(1)}, bf16[512,384]{1,0:T(8,128)(2,1)S(1)}, u32[]{:S(2)}, u32[]{:S(2)}) collective-permute-start(bf16[512,384]{1,0:T(8,128)(2,1)S(1)} %get-tuple-element.42), channel_id=1, source_target_pairs={{16,0},{0,16},{17,1},{1,17},{18,2},{2,18},{19,3},{3,19},{20,4},{4,... | collective-permute-start | bytes 1179656 | tf_op jit(solution)/shard_map/ppermute | solution.py:24
  66.6 2.0 %collective-permute-start.25 = (bf16[512,384]{1,0:T(8,128)(2,1)S(1)}, bf16[512,384]{1,0:T(8,128)(2,1)S(1)}, u32[]{:S(2)}, u32[]{:S(2)}) collective-permute-start(bf16[512,384]{1,0:T(8,128)(2,1)S(1)} %shard_map.45), channel_id=1, source_target_pairs={{16,0},{0,16},{17,1},{1,17},{18,2},{2,18},{19,3},{3,19},{20,4},{4,... | collective-permute-start | bytes 1179656 | tf_op jit(solution)/shard_map/ppermute | solution.py:24

commit v13 on v12

--- a/solution.py
+++ b/solution.py
@@ -232,8 +232,13 @@
         (place, near1, near3, far, one_own, one_near1, three_own, three_near1, both, start),
         (VMEM, VMEM),
     )
+    high = call(
+        product_four,
+        total,
+        (place, one_near3, one_far, three_near3, three_far, both, high),
+    )
+    far_near1, high = lax.optimization_barrier((far_near1, high))
     half = jax.ShapeDtypeStruct((512, 384), BF16)
-    low, three_near3, three_far = lax.optimization_barrier((low, three_near3, three_far))
     mine1, theirs1 = call(
         product_three,
         (half, half),
@@ -241,11 +246,6 @@
         (VMEM, VMEM),
     )
     theirs1 = fetch(theirs1, "core", 2, 1)
-    high = call(
-        product_four,
-        total,
-        (place, one_near3, one_far, three_near3, three_far, both, high),
-    )
     mine2, theirs2 = (
         call(
             functools.partial(product_five, side),

time: 70.7 us -> 70.7 us (level)
  waiting for transfers between devices: 15.5 us -> 11.2 us
  starting transfers between devices: 40.7 us -> 45 us
    ppermute x15, waiting for transfers between devices: 6.69 us -> 2.44 us  [turn(): return lax.ppermute(block, ROW + COL, pairs)]
    ppermute x15, starting transfers between devices: 17 us -> 20.2 us  [turn(): return lax.ppermute(block, ROW + COL, pairs)]
    ppermute x4, starting transfers between devices: 10.5 us -> 11.6 us  [fetch(): lax.ppermute(block, axis, [((i + ahead) % size, i) for i in range(size)])]
where the time goes in v13:
time: 70.7 us; the launch traced here: 70.5 us
  starting transfers between devices  45 us (64%)
  Pallas kernels  12.1 us (17%)
  waiting for transfers between devices  11.2 us (16%)
  local copies, waits for them, and re-layouts  1.77 us (3%)
    ppermute x15, starting transfers between devices, turn(): return lax.ppermute(block, ROW + COL, pairs)  20.2 us
    ppermute x7, starting transfers between devices, swap(): return lax.ppermute(block, axis, [(i ^ bits, i) for i in range(size)])  13.2 us
    pallas_call x10, Pallas kernels, call(): pl.pallas_call(kernel, out_shape=out_shape, in_specs=specs or [SMEM] + [V...  12.1 us
    ppermute x4, starting transfers between devices, fetch(): lax.ppermute(block, axis, [((i + ahead) % size, i) for i in range(size)])  11.6 us
    ppermute x7, waiting for transfers between devices, swap(): return lax.ppermute(block, axis, [(i ^ bits, i) for i in range(size)])  6.97 us
    ppermute x15, waiting for transfers between devices, turn(): return lax.ppermute(block, ROW + COL, pairs)  2.44 us
    ppermute x4, waiting for transfers between devices, fetch(): lax.ppermute(block, axis, [((i + ahead) % size, i) for i in range(size)])  1.83 us
    unnamed x6, local copies, waits for them, and re-layouts  1.77 us
  transfers between devices with their start and end apart: 26, of which 12 were waited for; matrix products, arithmetic and copies ran while one was open for 0% of the time, Pallas kernels for 15%

profile of v13, /device:TPU:1, one launch (start us, length us, event | category | flops | bytes accessed | tf_op | source)
XLA Modules:
  0.0 70.5 jit_solution(16933692091328584719)
XLA Ops:
  0.0 3.2 %collective-permute-start.5 = (bf16[1792,384]{1,0:T(8,128)(2,1)}, bf16[1792,384]{1,0:T(8,128)(2,1)S(1)}, u32[]{:S(2)}, u32[]{:S(2)}) collective-permute-start(bf16[1792,384]{1,0:T(8,128)(2,1)} %own.1), channel_id=1, source_target_pairs={{16,0},{0,16},{17,1},{1,17},{18,2},{2,18},{19,3},{3,19},{20,4},{4,... | collective-permute-start | bytes 4128776 | tf_op jit(solution)/shard_map/ppermute | solution.py:24
  3.3 1.0 %copy-done.1 = bf16[112,2048]{1,0:T(8,128)(2,1)S(1)} copy-done((bf16[112,2048]{1,0:T(8,128)(2,1)S(1)}, bf16[112,2048]{1,0:T(8,128)(2,1)}, u32[]{:S(2)}) %copy-start.1) | copy-done | bytes 458776
  5.1 1.0 %shard_map.37 = (f32[8,112,128]{2,1,0:T(8,128)S(1)}, f32[8,112,128]{2,1,0:T(8,128)S(1)}) custom-call(s32[4]{0:T(128)S(1)} %pad_add_fusion.place, bf16[112,112]{1,0:T(8,128)(2,1)S(1)} %copy-done.2, bf16[112,2048]{1,0:T(8,128)(2,1)S(1)} %copy-done.1), custom_call_target="tpu_custom_call" | custom-call | tf_op jit(solution)/shard_map/pallas_call | solution.py:180
  6.2 1.7 %collective-permute-done.received = f32[8,112,128]{2,1,0:T(8,128)S(1)} collective-permute-done((f32[8,112,128]{2,1,0:T(8,128)S(1)}, f32[8,112,128]{2,1,0:T(8,128)S(1)}, u32[]{:S(2)}, u32[]{:S(2)}) %collective-permute-start) | collective-permute-done | bytes 458784 | tf_op jit(solution)/shard_map/ppermute | solution.py:24
  8.6 0.8 %collective-permute-start.1 = (bf16[2,112,128]{2,1,0:T(8,128)(2,1)S(1)}, bf16[2,112,128]{2,1,0:T(8,128)(2,1)S(1)}, u32[]{:S(2)}, u32[]{:S(2)}) collective-permute-start(bf16[2,112,128]{2,1,0:T(8,128)(2,1)S(1)} %get-tuple-element.26), channel_id=1, source_target_pairs={{192,0},{128,64},{64,128},{0,192},{193,1},{129,65},{65,129},{1,193... | collective-permute-start | bytes 172040 | tf_op jit(solution)/shard_map/ppermute | solution.py:28
  9.9 2.0 %collective-permute-start.3 = (bf16[2,112,128]{2,1,0:T(8,128)(2,1)S(1)}, bf16[2,112,128]{2,1,0:T(8,128)(2,1)S(1)}, u32[]{:S(2)}, u32[]{:S(2)}) collective-permute-start(bf16[2,112,128]{2,1,0:T(8,128)(2,1)S(1)} %get-tuple-element.28), channel_id=1, source_target_pairs={{64,0},{0,64},{192,128},{128,192},{65,1},{1,65},{193,129},{129,193... | collective-permute-start | bytes 172040 | tf_op jit(solution)/shard_map/ppermute | solution.py:28
  11.9 1.0 %collective-permute-done.1 = bf16[2,112,128]{2,1,0:T(8,128)(2,1)S(1)} collective-permute-done((bf16[2,112,128]{2,1,0:T(8,128)(2,1)S(1)}, bf16[2,112,128]{2,1,0:T(8,128)(2,1)S(1)}, u32[]{:S(2)}, u32[]{:S(2)}) %collective-permute-start.1) | collective-permute-done | bytes 57376 | tf_op jit(solution)/shard_map/ppermute | solution.py:28
  12.9 1.1 %collective-permute-done.2 = bf16[2,112,128]{2,1,0:T(8,128)(2,1)S(1)} collective-permute-done((bf16[2,112,128]{2,1,0:T(8,128)(2,1)S(1)}, bf16[2,112,128]{2,1,0:T(8,128)(2,1)S(1)}, u32[]{:S(2)}, u32[]{:S(2)}) %collective-permute-start.2) | collective-permute-done | bytes 57376 | tf_op jit(solution)/shard_map/ppermute | solution.py:28
  14.8 6.2 %collective-permute-start.4 = (bf16[2,112,128]{2,1,0:T(8,128)(2,1)S(1)}, bf16[2,112,128]{2,1,0:T(8,128)(2,1)S(1)}, u32[]{:S(2)}, u32[]{:S(2)}) collective-permute-start(bf16[2,112,128]{2,1,0:T(8,128)(2,1)S(1)} %fusion), channel_id=1, source_target_pairs={{32,0},{0,32},{33,1},{1,33},{34,2},{2,34},{35,3},{3,35},{36,4},{4,... | collective-permute-start | bytes 172040 | tf_op jit(solution)/shard_map/ppermute | solution.py:28
  22.6 2.9 %collective-permute-start.8 = (bf16[2,112,128]{2,1,0:T(8,128)(2,1)S(1)}, bf16[2,112,128]{2,1,0:T(8,128)(2,1)S(1)}, u32[]{:S(2)}, u32[]{:S(2)}) collective-permute-start(bf16[2,112,128]{2,1,0:T(8,128)(2,1)S(1)} %add_convert_fusion), channel_id=1, source_target_pairs={{12,0},{8,4},{4,8},{0,12},{13,1},{9,5},{5,9},{1,13},{14,2},{10,6},... | collective-permute-start | bytes 172040 | tf_op jit(solution)/shard_map/ppermute | solution.py:28
  26.2 1.3 %collective-permute-done.8 = bf16[2,112,128]{2,1,0:T(8,128)(2,1)S(1)} collective-permute-done((bf16[2,112,128]{2,1,0:T(8,128)(2,1)S(1)}, bf16[2,112,128]{2,1,0:T(8,128)(2,1)S(1)}, u32[]{:S(2)}, u32[]{:S(2)}) %collective-permute-start.8) | collective-permute-done | bytes 57376 | tf_op jit(solution)/shard_map/ppermute | solution.py:28
  27.5 1.0 %collective-permute-done.6 = bf16[2,112,128]{2,1,0:T(8,128)(2,1)S(1)} collective-permute-done((bf16[2,112,128]{2,1,0:T(8,128)(2,1)S(1)}, bf16[2,112,128]{2,1,0:T(8,128)(2,1)S(1)}, u32[]{:S(2)}, u32[]{:S(2)}) %collective-permute-start.6) | collective-permute-done | bytes 57376 | tf_op jit(solution)/shard_map/ppermute | solution.py:28
  28.6 1.0 %collective-permute-done.7 = bf16[2,112,128]{2,1,0:T(8,128)(2,1)S(1)} collective-permute-done((bf16[2,112,128]{2,1,0:T(8,128)(2,1)S(1)}, bf16[2,112,128]{2,1,0:T(8,128)(2,1)S(1)}, u32[]{:S(2)}, u32[]{:S(2)}) %collective-permute-start.7) | collective-permute-done | bytes 57376 | tf_op jit(solution)/shard_map/ppermute | solution.py:28
  29.7 1.4 %collective-permute-start.12 = (bf16[2,4,112,128]{3,2,1,0:T(8,128)(2,1)S(1)}, bf16[2,4,112,128]{3,2,1,0:T(8,128)(2,1)S(1)}, u32[]{:S(2)}, u32[]{:S(2)}) collective-permute-start(bf16[2,4,112,128]{3,2,1,0:T(8,128)(2,1)S(1)} %pad_maximum_fusion.own), channel_id=1, source_target_pairs={{64,0},{65,1},{66,2},{67,3},{68,4},{69,5},{70,6},{71,7},{72,8},{73... | collective-permute-start | bytes 688136 | tf_op jit(solution)/shard_map/ppermute | solution.py:37
  31.0 1.9 %collective-permute-start.9 = (bf16[2,4,112,128]{3,2,1,0:T(8,128)(2,1)S(1)}, bf16[2,4,112,128]{3,2,1,0:T(8,128)(2,1)S(1)}, u32[]{:S(2)}, u32[]{:S(2)}) collective-permute-start(bf16[2,4,112,128]{3,2,1,0:T(8,128)(2,1)S(1)} %pad_maximum_fusion.own), channel_id=1, source_target_pairs={{192,0},{193,1},{194,2},{195,3},{196,4},{197,5},{198,6},{199,7},{2... | collective-permute-start | bytes 688136 | tf_op jit(solution)/shard_map/ppermute | solution.py:37
  33.0 3.9 %collective-permute-start.15 = (bf16[2,4,112,128]{3,2,1,0:T(8,128)(2,1)S(1)}, bf16[2,4,112,128]{3,2,1,0:T(8,128)(2,1)S(1)}, u32[]{:S(2)}, u32[]{:S(2)}) collective-permute-start(bf16[2,4,112,128]{3,2,1,0:T(8,128)(2,1)S(1)} %pad_maximum_fusion.own), channel_id=1, source_target_pairs={{3,0},{2,1},{1,2},{0,3},{7,4},{6,5},{5,6},{4,7},{11,8},{10,9},{9,1... | collective-permute-start | bytes 688136 | tf_op jit(solution)/shard_map/ppermute | solution.py:37
  36.9 1.0 %shard_map.40.start = f32[256,768]{1,0:T(8,128)S(1)} custom-call(s32[4]{0:T(128)S(1)} %pad_add_fusion.place, bf16[2,4,112,128]{3,2,1,0:T(8,128)(2,1)S(1)} %pad_maximum_fusion.own, bf16[4,448,768]{2,1,0:T(8,128)(2,1)S(1)} %shard_map.39.both), custom_call_target="tpu_custom_call" | custom-call | tf_op jit(solution)/shard_map/pallas_call | solution.py:180
  37.8 1.1 %collective-permute-start.13 = (bf16[2,4,112,128]{3,2,1,0:T(8,128)(2,1)S(1)}, bf16[2,4,112,128]{3,2,1,0:T(8,128)(2,1)S(1)}, u32[]{:S(2)}, u32[]{:S(2)}) collective-permute-start(bf16[2,4,112,128]{3,2,1,0:T(8,128)(2,1)S(1)} %collective-permute-done.12.near1), channel_id=1, source_target_pairs={{192,0},{193,1},{194,2},{195,3},{196,4},{197,5},{198,6},{199,7},{2... | collective-permute-start | bytes 688136 | tf_op jit(solution)/shard_map/ppermute | solution.py:37
  39.2 1.5 %collective-permute-start.21 = (bf16[2,4,112,128]{3,2,1,0:T(8,128)(2,1)S(1)}, bf16[2,4,112,128]{3,2,1,0:T(8,128)(2,1)S(1)}, u32[]{:S(2)}, u32[]{:S(2)}) collective-permute-start(bf16[2,4,112,128]{3,2,1,0:T(8,128)(2,1)S(1)} %collective-permute-done.12.near1), channel_id=1, source_target_pairs={{1,0},{0,1},{3,2},{2,3},{5,4},{4,5},{7,6},{6,7},{9,8},{8,9},{11,10... | collective-permute-start | bytes 688136 | tf_op jit(solution)/shard_map/ppermute | solution.py:37
  41.0 3.4 %collective-permute-start.19 = (bf16[2,4,112,128]{3,2,1,0:T(8,128)(2,1)S(1)}, bf16[2,4,112,128]{3,2,1,0:T(8,128)(2,1)S(1)}, u32[]{:S(2)}, u32[]{:S(2)}) collective-permute-start(bf16[2,4,112,128]{3,2,1,0:T(8,128)(2,1)S(1)} %collective-permute-done.9.near3), channel_id=1, source_target_pairs={{3,0},{2,1},{1,2},{0,3},{7,4},{6,5},{5,6},{4,7},{11,8},{10,9},{9,1... | collective-permute-start | bytes 688136 | tf_op jit(solution)/shard_map/ppermute | solution.py:37
  44.5 1.9 %collective-permute-done.13.far = bf16[2,4,112,128]{3,2,1,0:T(8,128)(2,1)S(1)} collective-permute-done((bf16[2,4,112,128]{3,2,1,0:T(8,128)(2,1)S(1)}, bf16[2,4,112,128]{3,2,1,0:T(8,128)(2,1)S(1)}, u32[]{:S(2)}, u32[]{:S(2)}) %collective-permute-start.13) | collective-permute-done | bytes 229408 | tf_op jit(solution)/shard_map/ppermute | solution.py:37
  46.4 2.5 %collective-permute-start.20 = (bf16[2,4,112,128]{3,2,1,0:T(8,128)(2,1)S(1)}, bf16[2,4,112,128]{3,2,1,0:T(8,128)(2,1)S(1)}, u32[]{:S(2)}, u32[]{:S(2)}) collective-permute-start(bf16[2,4,112,128]{3,2,1,0:T(8,128)(2,1)S(1)} %collective-permute-done.13.far), channel_id=1, source_target_pairs={{3,0},{2,1},{1,2},{0,3},{7,4},{6,5},{5,6},{4,7},{11,8},{10,9},{9,1... | collective-permute-start | bytes 688136 | tf_op jit(solution)/shard_map/ppermute | solution.py:37
  49.0 1.5 %collective-permute-start.16 = (bf16[2,4,112,128]{3,2,1,0:T(8,128)(2,1)S(1)}, bf16[2,4,112,128]{3,2,1,0:T(8,128)(2,1)S(1)}, u32[]{:S(2)}, u32[]{:S(2)}) collective-permute-start(bf16[2,4,112,128]{3,2,1,0:T(8,128)(2,1)S(1)} %collective-permute-done.15.own3), channel_id=1, source_target_pairs={{1,0},{0,1},{3,2},{2,3},{5,4},{4,5},{7,6},{6,7},{9,8},{8,9},{11,10... | collective-permute-start | bytes 688136 | tf_op jit(solution)/shard_map/ppermute | solution.py:37
  50.6 2.5 %collective-permute-start.22 = (bf16[2,4,112,128]{3,2,1,0:T(8,128)(2,1)S(1)}, bf16[2,4,112,128]{3,2,1,0:T(8,128)(2,1)S(1)}, u32[]{:S(2)}, u32[]{:S(2)}) collective-permute-start(bf16[2,4,112,128]{3,2,1,0:T(8,128)(2,1)S(1)} %collective-permute-done.11.near31), channel_id=1, source_target_pairs={{3,0},{2,1},{1,2},{0,3},{7,4},{6,5},{5,6},{4,7},{11,8},{10,9},{9,1... | collective-permute-start | bytes 688136 | tf_op jit(solution)/shard_map/ppermute | solution.py:37
  53.3 2.2 %shard_map.41 = (f32[512,768]{1,0:T(8,128)S(1)}, f32[512,768]{1,0:T(8,128)S(1)}) custom-call(s32[4]{0:T(128)S(1)} %pad_add_fusion.place, bf16[2,4,112,128]{3,2,1,0:T(8,128)(2,1)S(1)} %collective-permute-done.12.near1, bf16[2,4,112,128]{3,2,1,0:T(8,128)(2,1)S(1)} %collective-permute-done.9.near3, bf16[2,4,112,128]{3,2,1,0:T(8,128)(2,1)S(1)} %collective-permute-done.13.far, ...), custom_call_target="tpu_custom_call" | custom-call | tf_op jit(solution)/shard_map/pallas_call | solution.py:180
  55.5 1.2 %shard_map.42.high = f32[512,768]{1,0:T(8,128)S(1)} custom-call(s32[4]{0:T(128)S(1)} %pad_add_fusion.place, bf16[2,4,112,128]{3,2,1,0:T(8,128)(2,1)S(1)} %collective-permute-done.11.near31, bf16[2,4,112,128]{3,2,1,0:T(8,128)(2,1)S(1)} %collective-permute-done.14.far1, bf16[2,4,112,128]{3,2,1,0:T(8,128)(2,1)S(1)} %collective-permute-done.19.near33, ...), custom_call_target="tpu_custom_call" | custom-call | tf_op jit(solution)/shard_map/pallas_call | solution.py:180
  56.7 1.2 %shard_map.43 = (bf16[512,384]{1,0:T(8,128)(2,1)S(1)}, bf16[512,384]{1,0:T(8,128)(2,1)S(1)}) custom-call(s32[4]{0:T(128)S(1)} %pad_add_fusion.place, bf16[2,4,112,128]{3,2,1,0:T(8,128)(2,1)S(1)} %collective-permute-done.11.near31, bf16[2,4,112,128]{3,2,1,0:T(8,128)(2,1)S(1)} %collective-permute-done.14.far1, ...), custom_call_target="tpu_custom_call" | custom-call | tf_op jit(solution)/shard_map/pallas_call | solution.py:180
  57.9 7.0 %collective-permute-start.24 = (bf16[512,384]{1,0:T(8,128)(2,1)S(1)}, bf16[512,384]{1,0:T(8,128)(2,1)S(1)}, u32[]{:S(2)}, u32[]{:S(2)}) collective-permute-start(bf16[512,384]{1,0:T(8,128)(2,1)S(1)} %get-tuple-element.40), channel_id=1, source_target_pairs={{16,0},{0,16},{17,1},{1,17},{18,2},{2,18},{19,3},{3,19},{20,4},{4,... | collective-permute-start | bytes 1179656 | tf_op jit(solution)/shard_map/ppermute | solution.py:24
  64.9 1.2 %shard_map.45 = bf16[512,384]{1,0:T(8,128)(2,1)S(1)} custom-call(s32[4]{0:T(128)S(1)} %pad_add_fusion.place, bf16[2,4,112,128]{3,2,1,0:T(8,128)(2,1)S(1)} %collective-permute-done.16.own, bf16[2,4,112,128]{3,2,1,0:T(8,128)(2,1)S(1)} %collective-permute-done.18.near1, bf16[2,4,112,128]{3,2,1,0:T(8,128)(2,1)S(1)} %collective-permute-done.22.near3, ...), custom_call_target="tpu_custom_call" | custom-call | tf_op jit(solution)/shard_map/pallas_call | solution.py:180
  66.1 1.2 %collective-permute-start.25 = (bf16[512,384]{1,0:T(8,128)(2,1)S(1)}, bf16[512,384]{1,0:T(8,128)(2,1)S(1)}, u32[]{:S(2)}, u32[]{:S(2)}) collective-permute-start(bf16[512,384]{1,0:T(8,128)(2,1)S(1)} %shard_map.45), channel_id=1, source_target_pairs={{16,0},{0,16},{17,1},{1,17},{18,2},{2,18},{19,3},{3,19},{20,4},{4,... | collective-permute-start | bytes 1179656 | tf_op jit(solution)/shard_map/ppermute | solution.py:24
  67.3 1.2 %shard_map.44.mine2 = bf16[512,384]{1,0:T(8,128)(2,1)S(1)} custom-call(s32[4]{0:T(128)S(1)} %pad_add_fusion.place, bf16[2,4,112,128]{3,2,1,0:T(8,128)(2,1)S(1)} %collective-permute-done.16.own, bf16[2,4,112,128]{3,2,1,0:T(8,128)(2,1)S(1)} %collective-permute-done.18.near1, bf16[2,4,112,128]{3,2,1,0:T(8,128)(2,1)S(1)} %collective-permute-done.22.near3, ...), custom_call_target="tpu_custom_call" | custom-call | tf_op jit(solution)/shard_map/pallas_call | solution.py:180
  68.6 1.7 %shard_map.46 = bf16[2048,384]{1,0:T(8,128)(2,1)} custom-call(s32[4]{0:T(128)S(1)} %pad_add_fusion.place, bf16[512,384]{1,0:T(8,128)(2,1)S(1)} %get-tuple-element.38.mine1, bf16[512,384]{1,0:T(8,128)(2,1)S(1)} %shard_map.44.mine2, bf16[512,384]{1,0:T(8,128)(2,1)S(1)} %collective-permute-done.24.theirs1, bf16[512,384]{1,0:T(8,128)(2,1)S(1)} %collective-permute-done.25.theirs2), custom_call_target="tpu_custom_call" | custom-call | tf_op jit(solution)/shard_map/pallas_call | solution.py:180
  (40 shorter events, 6.4 us)
Async XLA Ops:
  0.0 21.0 %copy-start = (bf16[1792,384]{1,0:T(8,128)(2,1)S(1)}, bf16[1792,384]{1,0:T(8,128)(2,1)}, u32[]{:S(2)}) copy-start(bf16[1792,384]{1,0:T(8,128)(2,1)} %own.1) | copy-start | bytes 4128772
  0.0 21.0 %collective-permute-start.5 = (bf16[1792,384]{1,0:T(8,128)(2,1)}, bf16[1792,384]{1,0:T(8,128)(2,1)S(1)}, u32[]{:S(2)}, u32[]{:S(2)}) collective-permute-start(bf16[1792,384]{1,0:T(8,128)(2,1)} %own.1), channel_id=1, source_target_pairs={{16,0},{0,16},{17,1},{1,17},{18,2},{2,18},{19,3},{3,19},{20,4},{4,... | collective-permute-start | bytes 4128776 | tf_op jit(solution)/shard_map/ppermute | solution.py:24
  3.3 1.0 %copy-start.1 = (bf16[112,2048]{1,0:T(8,128)(2,1)S(1)}, bf16[112,2048]{1,0:T(8,128)(2,1)}, u32[]{:S(2)}) copy-start(bf16[112,2048]{1,0:T(8,128)(2,1)} %panel.1) | copy-start | bytes 1376260
  4.3 0.7 %copy-start.2 = (bf16[112,112]{1,0:T(8,128)(2,1)S(1)}, bf16[112,112]{1,0:T(8,128)(2,1)}, u32[]{:S(2)}) copy-start(bf16[112,112]{1,0:T(8,128)(2,1)} %screening.1) | copy-start | bytes 75268
  6.1 1.9 %collective-permute-start = (f32[8,112,128]{2,1,0:T(8,128)S(1)}, f32[8,112,128]{2,1,0:T(8,128)S(1)}, u32[]{:S(2)}, u32[]{:S(2)}) collective-permute-start(f32[8,112,128]{2,1,0:T(8,128)S(1)} %get-tuple-element.24), channel_id=1, source_target_pairs={{16,0},{0,16},{17,1},{1,17},{18,2},{2,18},{19,3},{3,19},{20,4},{4,... | collective-permute-start | bytes 1376264 | tf_op jit(solution)/shard_map/ppermute | solution.py:24
  8.6 4.3 %collective-permute-start.1 = (bf16[2,112,128]{2,1,0:T(8,128)(2,1)S(1)}, bf16[2,112,128]{2,1,0:T(8,128)(2,1)S(1)}, u32[]{:S(2)}, u32[]{:S(2)}) collective-permute-start(bf16[2,112,128]{2,1,0:T(8,128)(2,1)S(1)} %get-tuple-element.26), channel_id=1, source_target_pairs={{192,0},{128,64},{64,128},{0,192},{193,1},{129,65},{65,129},{1,193... | collective-permute-start | bytes 172040 | tf_op jit(solution)/shard_map/ppermute | solution.py:28
  9.4 4.6 %collective-permute-start.2 = (bf16[2,112,128]{2,1,0:T(8,128)(2,1)S(1)}, bf16[2,112,128]{2,1,0:T(8,128)(2,1)S(1)}, u32[]{:S(2)}, u32[]{:S(2)}) collective-permute-start(bf16[2,112,128]{2,1,0:T(8,128)(2,1)S(1)} %get-tuple-element.27), channel_id=1, source_target_pairs={{128,0},{192,64},{0,128},{64,192},{129,1},{193,65},{1,129},{65,193... | collective-permute-start | bytes 172040 | tf_op jit(solution)/shard_map/ppermute | solution.py:28
  9.9 4.8 %collective-permute-start.3 = (bf16[2,112,128]{2,1,0:T(8,128)(2,1)S(1)}, bf16[2,112,128]{2,1,0:T(8,128)(2,1)S(1)}, u32[]{:S(2)}, u32[]{:S(2)}) collective-permute-start(bf16[2,112,128]{2,1,0:T(8,128)(2,1)S(1)} %get-tuple-element.28), channel_id=1, source_target_pairs={{64,0},{0,64},{192,128},{128,192},{65,1},{1,65},{193,129},{129,193... | collective-permute-start | bytes 172040 | tf_op jit(solution)/shard_map/ppermute | solution.py:28
  14.8 7.8 %collective-permute-start.4 = (bf16[2,112,128]{2,1,0:T(8,128)(2,1)S(1)}, bf16[2,112,128]{2,1,0:T(8,128)(2,1)S(1)}, u32[]{:S(2)}, u32[]{:S(2)}) collective-permute-start(bf16[2,112,128]{2,1,0:T(8,128)(2,1)S(1)} %fusion), channel_id=1, source_target_pairs={{32,0},{0,32},{33,1},{1,33},{34,2},{2,34},{35,3},{3,35},{36,4},{4,... | collective-permute-start | bytes 172040 | tf_op jit(solution)/shard_map/ppermute | solution.py:28
  22.6 4.9 %collective-permute-start.8 = (bf16[2,112,128]{2,1,0:T(8,128)(2,1)S(1)}, bf16[2,112,128]{2,1,0:T(8,128)(2,1)S(1)}, u32[]{:S(2)}, u32[]{:S(2)}) collective-permute-start(bf16[2,112,128]{2,1,0:T(8,128)(2,1)S(1)} %add_convert_fusion), channel_id=1, source_target_pairs={{12,0},{8,4},{4,8},{0,12},{13,1},{9,5},{5,9},{1,13},{14,2},{10,6},... | collective-permute-start | bytes 172040 | tf_op jit(solution)/shard_map/ppermute | solution.py:28
  25.5 3.0 %collective-permute-start.6 = (bf16[2,112,128]{2,1,0:T(8,128)(2,1)S(1)}, bf16[2,112,128]{2,1,0:T(8,128)(2,1)S(1)}, u32[]{:S(2)}, u32[]{:S(2)}) collective-permute-start(bf16[2,112,128]{2,1,0:T(8,128)(2,1)S(1)} %add_convert_fusion), channel_id=1, source_target_pairs={{4,0},{0,4},{12,8},{8,12},{5,1},{1,5},{13,9},{9,13},{6,2},{2,6},{1... | collective-permute-start | bytes 172040 | tf_op jit(solution)/shard_map/ppermute | solution.py:28
  25.5 4.1 %collective-permute-start.7 = (bf16[2,112,128]{2,1,0:T(8,128)(2,1)S(1)}, bf16[2,112,128]{2,1,0:T(8,128)(2,1)S(1)}, u32[]{:S(2)}, u32[]{:S(2)}) collective-permute-start(bf16[2,112,128]{2,1,0:T(8,128)(2,1)S(1)} %add_convert_fusion), channel_id=1, source_target_pairs={{8,0},{12,4},{0,8},{4,12},{9,1},{13,5},{1,9},{5,13},{10,2},{14,6},... | collective-permute-start | bytes 172040 | tf_op jit(solution)/shard_map/ppermute | solution.py:28
  29.7 8.2 %collective-permute-start.12 = (bf16[2,4,112,128]{3,2,1,0:T(8,128)(2,1)S(1)}, bf16[2,4,112,128]{3,2,1,0:T(8,128)(2,1)S(1)}, u32[]{:S(2)}, u32[]{:S(2)}) collective-permute-start(bf16[2,4,112,128]{3,2,1,0:T(8,128)(2,1)S(1)} %pad_maximum_fusion.own), channel_id=1, source_target_pairs={{64,0},{65,1},{66,2},{67,3},{68,4},{69,5},{70,6},{71,7},{72,8},{73... | collective-permute-start | bytes 688136 | tf_op jit(solution)/shard_map/ppermute | solution.py:37
  31.0 8.2 %collective-permute-start.10 = (bf16[2,4,112,128]{3,2,1,0:T(8,128)(2,1)S(1)}, bf16[2,4,112,128]{3,2,1,0:T(8,128)(2,1)S(1)}, u32[]{:S(2)}, u32[]{:S(2)}) collective-permute-start(bf16[2,4,112,128]{3,2,1,0:T(8,128)(2,1)S(1)} %pad_maximum_fusion.own), channel_id=1, source_target_pairs={{1,0},{0,1},{3,2},{2,3},{5,4},{4,5},{7,6},{6,7},{9,8},{8,9},{11,10... | collective-permute-start | bytes 688136 | tf_op jit(solution)/shard_map/ppermute | solution.py:37
  31.0 9.6 %collective-permute-start.9 = (bf16[2,4,112,128]{3,2,1,0:T(8,128)(2,1)S(1)}, bf16[2,4,112,128]{3,2,1,0:T(8,128)(2,1)S(1)}, u32[]{:S(2)}, u32[]{:S(2)}) collective-permute-start(bf16[2,4,112,128]{3,2,1,0:T(8,128)(2,1)S(1)} %pad_maximum_fusion.own), channel_id=1, source_target_pairs={{192,0},{193,1},{194,2},{195,3},{196,4},{197,5},{198,6},{199,7},{2... | collective-permute-start | bytes 688136 | tf_op jit(solution)/shard_map/ppermute | solution.py:37
  33.0 8.1 %collective-permute-start.15 = (bf16[2,4,112,128]{3,2,1,0:T(8,128)(2,1)S(1)}, bf16[2,4,112,128]{3,2,1,0:T(8,128)(2,1)S(1)}, u32[]{:S(2)}, u32[]{:S(2)}) collective-permute-start(bf16[2,4,112,128]{3,2,1,0:T(8,128)(2,1)S(1)} %pad_maximum_fusion.own), channel_id=1, source_target_pairs={{3,0},{2,1},{1,2},{0,3},{7,4},{6,5},{5,6},{4,7},{11,8},{10,9},{9,1... | collective-permute-start | bytes 688136 | tf_op jit(solution)/shard_map/ppermute | solution.py:37
  37.8 8.6 %collective-permute-start.13 = (bf16[2,4,112,128]{3,2,1,0:T(8,128)(2,1)S(1)}, bf16[2,4,112,128]{3,2,1,0:T(8,128)(2,1)S(1)}, u32[]{:S(2)}, u32[]{:S(2)}) collective-permute-start(bf16[2,4,112,128]{3,2,1,0:T(8,128)(2,1)S(1)} %collective-permute-done.12.near1), channel_id=1, source_target_pairs={{192,0},{193,1},{194,2},{195,3},{196,4},{197,5},{198,6},{199,7},{2... | collective-permute-start | bytes 688136 | tf_op jit(solution)/shard_map/ppermute | solution.py:37
  38.9 7.5 %collective-permute-start.17 = (bf16[2,4,112,128]{3,2,1,0:T(8,128)(2,1)S(1)}, bf16[2,4,112,128]{3,2,1,0:T(8,128)(2,1)S(1)}, u32[]{:S(2)}, u32[]{:S(2)}) collective-permute-start(bf16[2,4,112,128]{3,2,1,0:T(8,128)(2,1)S(1)} %collective-permute-done.12.near1), channel_id=1, source_target_pairs={{3,0},{2,1},{1,2},{0,3},{7,4},{6,5},{5,6},{4,7},{11,8},{10,9},{9,1... | collective-permute-start | bytes 688136 | tf_op jit(solution)/shard_map/ppermute | solution.py:37
  39.2 9.7 %collective-permute-start.21 = (bf16[2,4,112,128]{3,2,1,0:T(8,128)(2,1)S(1)}, bf16[2,4,112,128]{3,2,1,0:T(8,128)(2,1)S(1)}, u32[]{:S(2)}, u32[]{:S(2)}) collective-permute-start(bf16[2,4,112,128]{3,2,1,0:T(8,128)(2,1)S(1)} %collective-permute-done.12.near1), channel_id=1, source_target_pairs={{1,0},{0,1},{3,2},{2,3},{5,4},{4,5},{7,6},{6,7},{9,8},{8,9},{11,10... | collective-permute-start | bytes 688136 | tf_op jit(solution)/shard_map/ppermute | solution.py:37
  40.7 8.3 %collective-permute-start.11 = (bf16[2,4,112,128]{3,2,1,0:T(8,128)(2,1)S(1)}, bf16[2,4,112,128]{3,2,1,0:T(8,128)(2,1)S(1)}, u32[]{:S(2)}, u32[]{:S(2)}) collective-permute-start(bf16[2,4,112,128]{3,2,1,0:T(8,128)(2,1)S(1)} %collective-permute-done.9.near3), channel_id=1, source_target_pairs={{1,0},{0,1},{3,2},{2,3},{5,4},{4,5},{7,6},{6,7},{9,8},{8,9},{11,10... | collective-permute-start | bytes 688136 | tf_op jit(solution)/shard_map/ppermute | solution.py:37
  41.0 9.6 %collective-permute-start.19 = (bf16[2,4,112,128]{3,2,1,0:T(8,128)(2,1)S(1)}, bf16[2,4,112,128]{3,2,1,0:T(8,128)(2,1)S(1)}, u32[]{:S(2)}, u32[]{:S(2)}) collective-permute-start(bf16[2,4,112,128]{3,2,1,0:T(8,128)(2,1)S(1)} %collective-permute-done.9.near3), channel_id=1, source_target_pairs={{3,0},{2,1},{1,2},{0,3},{7,4},{6,5},{5,6},{4,7},{11,8},{10,9},{9,1... | collective-permute-start | bytes 688136 | tf_op jit(solution)/shard_map/ppermute | solution.py:37
  46.4 6.7 %collective-permute-start.14 = (bf16[2,4,112,128]{3,2,1,0:T(8,128)(2,1)S(1)}, bf16[2,4,112,128]{3,2,1,0:T(8,128)(2,1)S(1)}, u32[]{:S(2)}, u32[]{:S(2)}) collective-permute-start(bf16[2,4,112,128]{3,2,1,0:T(8,128)(2,1)S(1)} %collective-permute-done.13.far), channel_id=1, source_target_pairs={{1,0},{0,1},{3,2},{2,3},{5,4},{4,5},{7,6},{6,7},{9,8},{8,9},{11,10... | collective-permute-start | bytes 688136 | tf_op jit(solution)/shard_map/ppermute | solution.py:37
  46.4 9.1 %collective-permute-start.20 = (bf16[2,4,112,128]{3,2,1,0:T(8,128)(2,1)S(1)}, bf16[2,4,112,128]{3,2,1,0:T(8,128)(2,1)S(1)}, u32[]{:S(2)}, u32[]{:S(2)}) collective-permute-start(bf16[2,4,112,128]{3,2,1,0:T(8,128)(2,1)S(1)} %collective-permute-done.13.far), channel_id=1, source_target_pairs={{3,0},{2,1},{1,2},{0,3},{7,4},{6,5},{5,6},{4,7},{11,8},{10,9},{9,1... | collective-permute-start | bytes 688136 | tf_op jit(solution)/shard_map/ppermute | solution.py:37
  49.0 7.7 %collective-permute-start.18 = (bf16[2,4,112,128]{3,2,1,0:T(8,128)(2,1)S(1)}, bf16[2,4,112,128]{3,2,1,0:T(8,128)(2,1)S(1)}, u32[]{:S(2)}, u32[]{:S(2)}) collective-permute-start(bf16[2,4,112,128]{3,2,1,0:T(8,128)(2,1)S(1)} %collective-permute-done.17.near31), channel_id=1, source_target_pairs={{1,0},{0,1},{3,2},{2,3},{5,4},{4,5},{7,6},{6,7},{9,8},{8,9},{11,10... | collective-permute-start | bytes 688136 | tf_op jit(solution)/shard_map/ppermute | solution.py:37
  49.0 7.7 %collective-permute-start.16 = (bf16[2,4,112,128]{3,2,1,0:T(8,128)(2,1)S(1)}, bf16[2,4,112,128]{3,2,1,0:T(8,128)(2,1)S(1)}, u32[]{:S(2)}, u32[]{:S(2)}) collective-permute-start(bf16[2,4,112,128]{3,2,1,0:T(8,128)(2,1)S(1)} %collective-permute-done.15.own3), channel_id=1, source_target_pairs={{1,0},{0,1},{3,2},{2,3},{5,4},{4,5},{7,6},{6,7},{9,8},{8,9},{11,10... | collective-permute-start | bytes 688136 | tf_op jit(solution)/shard_map/ppermute | solution.py:37
  50.6 14.3 %collective-permute-start.22 = (bf16[2,4,112,128]{3,2,1,0:T(8,128)(2,1)S(1)}, bf16[2,4,112,128]{3,2,1,0:T(8,128)(2,1)S(1)}, u32[]{:S(2)}, u32[]{:S(2)}) collective-permute-start(bf16[2,4,112,128]{3,2,1,0:T(8,128)(2,1)S(1)} %collective-permute-done.11.near31), channel_id=1, source_target_pairs={{3,0},{2,1},{1,2},{0,3},{7,4},{6,5},{5,6},{4,7},{11,8},{10,9},{9,1... | collective-permute-start | bytes 688136 | tf_op jit(solution)/shard_map/ppermute | solution.py:37
  53.1 11.8 %collective-permute-start.23 = (bf16[2,4,112,128]{3,2,1,0:T(8,128)(2,1)S(1)}, bf16[2,4,112,128]{3,2,1,0:T(8,128)(2,1)S(1)}, u32[]{:S(2)}, u32[]{:S(2)}) collective-permute-start(bf16[2,4,112,128]{3,2,1,0:T(8,128)(2,1)S(1)} %collective-permute-done.14.far1), channel_id=1, source_target_pairs={{3,0},{2,1},{1,2},{0,3},{7,4},{6,5},{5,6},{4,7},{11,8},{10,9},{9,1... | collective-permute-start | bytes 688136 | tf_op jit(solution)/shard_map/ppermute | solution.py:37
  57.9 10.6 %collective-permute-start.24 = (bf16[512,384]{1,0:T(8,128)(2,1)S(1)}, bf16[512,384]{1,0:T(8,128)(2,1)S(1)}, u32[]{:S(2)}, u32[]{:S(2)}) collective-permute-start(bf16[512,384]{1,0:T(8,128)(2,1)S(1)} %get-tuple-element.40), channel_id=1, source_target_pairs={{16,0},{0,16},{17,1},{1,17},{18,2},{2,18},{19,3},{3,19},{20,4},{4,... | collective-permute-start | bytes 1179656 | tf_op jit(solution)/shard_map/ppermute | solution.py:24
  66.1 2.5 %collective-permute-start.25 = (bf16[512,384]{1,0:T(8,128)(2,1)S(1)}, bf16[512,384]{1,0:T(8,128)(2,1)S(1)}, u32[]{:S(2)}, u32[]{:S(2)}) collective-permute-start(bf16[512,384]{1,0:T(8,128)(2,1)S(1)} %shard_map.45), channel_id=1, source_target_pairs={{16,0},{0,16},{17,1},{1,17},{18,2},{2,18},{19,3},{3,19},{20,4},{4,... | collective-permute-start | bytes 1179656 | tf_op jit(solution)/shard_map/ppermute | solution.py:24

commit v14 on v13

--- a/solution.py
+++ b/solution.py
@@ -46,7 +46,7 @@
     for out, base in ((send, 1 - core), (keep, core)):
         for slab in range(8):
             columns = pl.ds(pl.multiple_of(base * 1024 + slab * 128, 128), 128)
-            out[slab] = dot_t(screening[...], panel[:, columns])
+            out[slab] = dot_t(screening[...].astype(BF16), panel[:, columns])
 
 
 def add_cores(place, keep, received, mine, *away):
@@ -193,7 +193,7 @@
     place = jnp.stack([x, y, core, z_lo]).astype(jnp.int32)
 
     slabs = jax.ShapeDtypeStruct((8, 112, 128), F32)
-    keep, send = call(partial_sums, (slabs, slabs), (place, screening, pair_valence), (VMEM, VMEM))
+    keep, send = call(partial_sums, (slabs, slabs), (place, screening.astype(F32), pair_valence), (VMEM, VMEM))
     two = jax.ShapeDtypeStruct((2, 112, 128), F32)
     sent = jax.ShapeDtypeStruct((2, 112, 128), BF16)
     part, *away = call(

time: 70.7 us -> 70.6 us (level)
  other arithmetic: 0.19 us -> 0.94 us
  local copies, waits for them, and re-layouts: 1.77 us -> 1.02 us
    convert_element_type x0 -> x1, other arithmetic: none -> 0.75 us  [per_device(): screening.astype(F32)]
    unnamed x6 -> x4, local copies, waits for them, and re-layouts: 1.77 us -> 1.02 us
  transfers between devices with their start and end apart: 26 -> 26, of which waited for: 12 -> 11; matrix products, arithmetic and copies ran while one was open for 0% -> 1% of each run, Pallas kernels for 15% -> 15%
where the time goes in v14:
time: 70.6 us; the launch traced here: 70.4 us
  starting transfers between devices  45.2 us (64%)
  Pallas kernels  12.1 us (17%)
  waiting for transfers between devices  10.9 us (15%)
  local copies, waits for them, and re-layouts  1.02 us (1%)
  other arithmetic  0.94 us (1%)
    ppermute x15, starting transfers between devices, turn(): return lax.ppermute(block, ROW + COL, pairs)  20.8 us
    ppermute x7, starting transfers between devices, swap(): return lax.ppermute(block, axis, [(i ^ bits, i) for i in range(size)])  13.2 us
    pallas_call x10, Pallas kernels, call(): pl.pallas_call(kernel, out_shape=out_shape, in_specs=specs or [SMEM] + [V...  12.1 us
    ppermute x4, starting transfers between devices, fetch(): lax.ppermute(block, axis, [((i + ahead) % size, i) for i in range(size)])  11.2 us
    ppermute x7, waiting for transfers between devices, swap(): return lax.ppermute(block, axis, [(i ^ bits, i) for i in range(size)])  6.97 us
    ppermute x15, waiting for transfers between devices, turn(): return lax.ppermute(block, ROW + COL, pairs)  2.11 us
    ppermute x4, waiting for transfers between devices, fetch(): lax.ppermute(block, axis, [((i + ahead) % size, i) for i in range(size)])  1.82 us
  transfers between devices with their start and end apart: 26, of which 11 were waited for; matrix products, arithmetic and copies ran while one was open for 1% of the time, Pallas kernels for 15%

profile of v14, /device:TPU:1, one launch (start us, length us, event | category | flops | bytes accessed | tf_op | source)
XLA Modules:
  0.0 70.4 jit_solution(18341146144983775121)
XLA Ops:
  0.0 3.2 %collective-permute-start.5 = (bf16[1792,384]{1,0:T(8,128)(2,1)}, bf16[1792,384]{1,0:T(8,128)(2,1)S(1)}, u32[]{:S(2)}, u32[]{:S(2)}) collective-permute-start(bf16[1792,384]{1,0:T(8,128)(2,1)} %own.1), channel_id=1, source_target_pairs={{16,0},{0,16},{17,1},{1,17},{18,2},{2,18},{19,3},{3,19},{20,4},{4,... | collective-permute-start | bytes 4128776 | tf_op jit(solution)/shard_map/ppermute | solution.py:24
  4.1 1.0 %copy-done.1 = bf16[112,2048]{1,0:T(8,128)(2,1)S(1)} copy-done((bf16[112,2048]{1,0:T(8,128)(2,1)S(1)}, bf16[112,2048]{1,0:T(8,128)(2,1)}, u32[]{:S(2)}) %copy-start.1) | copy-done | bytes 458776
  5.1 1.0 %shard_map.37 = (f32[8,112,128]{2,1,0:T(8,128)S(1)}, f32[8,112,128]{2,1,0:T(8,128)S(1)}) custom-call(s32[4]{0:T(128)S(1)} %pad_add_fusion.place, f32[112,112]{1,0:T(8,128)S(1)} %convert_element_type.21.screening, bf16[112,2048]{1,0:T(8,128)(2,1)S(1)} %copy-done.1), custom_call_target="tpu_custom_call" | custom-call | tf_op jit(solution)/shard_map/pallas_call | solution.py:180
  6.3 1.7 %collective-permute-done.received = f32[8,112,128]{2,1,0:T(8,128)S(1)} collective-permute-done((f32[8,112,128]{2,1,0:T(8,128)S(1)}, f32[8,112,128]{2,1,0:T(8,128)S(1)}, u32[]{:S(2)}, u32[]{:S(2)}) %collective-permute-start) | collective-permute-done | bytes 458784 | tf_op jit(solution)/shard_map/ppermute | solution.py:24
  8.6 0.8 %collective-permute-start.1 = (bf16[2,112,128]{2,1,0:T(8,128)(2,1)S(1)}, bf16[2,112,128]{2,1,0:T(8,128)(2,1)S(1)}, u32[]{:S(2)}, u32[]{:S(2)}) collective-permute-start(bf16[2,112,128]{2,1,0:T(8,128)(2,1)S(1)} %get-tuple-element.26), channel_id=1, source_target_pairs={{192,0},{128,64},{64,128},{0,192},{193,1},{129,65},{65,129},{1,193... | collective-permute-start | bytes 172040 | tf_op jit(solution)/shard_map/ppermute | solution.py:28
  9.9 2.0 %collective-permute-start.3 = (bf16[2,112,128]{2,1,0:T(8,128)(2,1)S(1)}, bf16[2,112,128]{2,1,0:T(8,128)(2,1)S(1)}, u32[]{:S(2)}, u32[]{:S(2)}) collective-permute-start(bf16[2,112,128]{2,1,0:T(8,128)(2,1)S(1)} %get-tuple-element.28), channel_id=1, source_target_pairs={{64,0},{0,64},{192,128},{128,192},{65,1},{1,65},{193,129},{129,193... | collective-permute-start | bytes 172040 | tf_op jit(solution)/shard_map/ppermute | solution.py:28
  11.9 1.0 %collective-permute-done.1 = bf16[2,112,128]{2,1,0:T(8,128)(2,1)S(1)} collective-permute-done((bf16[2,112,128]{2,1,0:T(8,128)(2,1)S(1)}, bf16[2,112,128]{2,1,0:T(8,128)(2,1)S(1)}, u32[]{:S(2)}, u32[]{:S(2)}) %collective-permute-start.1) | collective-permute-done | bytes 57376 | tf_op jit(solution)/shard_map/ppermute | solution.py:28
  12.9 1.1 %collective-permute-done.2 = bf16[2,112,128]{2,1,0:T(8,128)(2,1)S(1)} collective-permute-done((bf16[2,112,128]{2,1,0:T(8,128)(2,1)S(1)}, bf16[2,112,128]{2,1,0:T(8,128)(2,1)S(1)}, u32[]{:S(2)}, u32[]{:S(2)}) %collective-permute-start.2) | collective-permute-done | bytes 57376 | tf_op jit(solution)/shard_map/ppermute | solution.py:28
  14.8 6.2 %collective-permute-start.4 = (bf16[2,112,128]{2,1,0:T(8,128)(2,1)S(1)}, bf16[2,112,128]{2,1,0:T(8,128)(2,1)S(1)}, u32[]{:S(2)}, u32[]{:S(2)}) collective-permute-start(bf16[2,112,128]{2,1,0:T(8,128)(2,1)S(1)} %fusion), channel_id=1, source_target_pairs={{32,0},{0,32},{33,1},{1,33},{34,2},{2,34},{35,3},{3,35},{36,4},{4,... | collective-permute-start | bytes 172040 | tf_op jit(solution)/shard_map/ppermute | solution.py:28
  22.6 2.9 %collective-permute-start.8 = (bf16[2,112,128]{2,1,0:T(8,128)(2,1)S(1)}, bf16[2,112,128]{2,1,0:T(8,128)(2,1)S(1)}, u32[]{:S(2)}, u32[]{:S(2)}) collective-permute-start(bf16[2,112,128]{2,1,0:T(8,128)(2,1)S(1)} %add_convert_fusion), channel_id=1, source_target_pairs={{12,0},{8,4},{4,8},{0,12},{13,1},{9,5},{5,9},{1,13},{14,2},{10,6},... | collective-permute-start | bytes 172040 | tf_op jit(solution)/shard_map/ppermute | solution.py:28
  26.2 1.3 %collective-permute-done.8 = bf16[2,112,128]{2,1,0:T(8,128)(2,1)S(1)} collective-permute-done((bf16[2,112,128]{2,1,0:T(8,128)(2,1)S(1)}, bf16[2,112,128]{2,1,0:T(8,128)(2,1)S(1)}, u32[]{:S(2)}, u32[]{:S(2)}) %collective-permute-start.8) | collective-permute-done | bytes 57376 | tf_op jit(solution)/shard_map/ppermute | solution.py:28
  27.5 1.0 %collective-permute-done.6 = bf16[2,112,128]{2,1,0:T(8,128)(2,1)S(1)} collective-permute-done((bf16[2,112,128]{2,1,0:T(8,128)(2,1)S(1)}, bf16[2,112,128]{2,1,0:T(8,128)(2,1)S(1)}, u32[]{:S(2)}, u32[]{:S(2)}) %collective-permute-start.6) | collective-permute-done | bytes 57376 | tf_op jit(solution)/shard_map/ppermute | solution.py:28
  28.6 1.0 %collective-permute-done.7 = bf16[2,112,128]{2,1,0:T(8,128)(2,1)S(1)} collective-permute-done((bf16[2,112,128]{2,1,0:T(8,128)(2,1)S(1)}, bf16[2,112,128]{2,1,0:T(8,128)(2,1)S(1)}, u32[]{:S(2)}, u32[]{:S(2)}) %collective-permute-start.7) | collective-permute-done | bytes 57376 | tf_op jit(solution)/shard_map/ppermute | solution.py:28
  29.7 1.4 %collective-permute-start.12 = (bf16[2,4,112,128]{3,2,1,0:T(8,128)(2,1)S(1)}, bf16[2,4,112,128]{3,2,1,0:T(8,128)(2,1)S(1)}, u32[]{:S(2)}, u32[]{:S(2)}) collective-permute-start(bf16[2,4,112,128]{3,2,1,0:T(8,128)(2,1)S(1)} %pad_maximum_fusion.own), channel_id=1, source_target_pairs={{64,0},{65,1},{66,2},{67,3},{68,4},{69,5},{70,6},{71,7},{72,8},{73... | collective-permute-start | bytes 688136 | tf_op jit(solution)/shard_map/ppermute | solution.py:37
  31.0 1.9 %collective-permute-start.9 = (bf16[2,4,112,128]{3,2,1,0:T(8,128)(2,1)S(1)}, bf16[2,4,112,128]{3,2,1,0:T(8,128)(2,1)S(1)}, u32[]{:S(2)}, u32[]{:S(2)}) collective-permute-start(bf16[2,4,112,128]{3,2,1,0:T(8,128)(2,1)S(1)} %pad_maximum_fusion.own), channel_id=1, source_target_pairs={{192,0},{193,1},{194,2},{195,3},{196,4},{197,5},{198,6},{199,7},{2... | collective-permute-start | bytes 688136 | tf_op jit(solution)/shard_map/ppermute | solution.py:37
  33.0 4.1 %collective-permute-start.15 = (bf16[2,4,112,128]{3,2,1,0:T(8,128)(2,1)S(1)}, bf16[2,4,112,128]{3,2,1,0:T(8,128)(2,1)S(1)}, u32[]{:S(2)}, u32[]{:S(2)}) collective-permute-start(bf16[2,4,112,128]{3,2,1,0:T(8,128)(2,1)S(1)} %pad_maximum_fusion.own), channel_id=1, source_target_pairs={{3,0},{2,1},{1,2},{0,3},{7,4},{6,5},{5,6},{4,7},{11,8},{10,9},{9,1... | collective-permute-start | bytes 688136 | tf_op jit(solution)/shard_map/ppermute | solution.py:37
  37.0 1.0 %shard_map.40.start = f32[256,768]{1,0:T(8,128)S(1)} custom-call(s32[4]{0:T(128)S(1)} %pad_add_fusion.place, bf16[2,4,112,128]{3,2,1,0:T(8,128)(2,1)S(1)} %pad_maximum_fusion.own, bf16[4,448,768]{2,1,0:T(8,128)(2,1)S(1)} %shard_map.39.both), custom_call_target="tpu_custom_call" | custom-call | tf_op jit(solution)/shard_map/pallas_call | solution.py:180
  38.0 0.9 %collective-permute-start.13 = (bf16[2,4,112,128]{3,2,1,0:T(8,128)(2,1)S(1)}, bf16[2,4,112,128]{3,2,1,0:T(8,128)(2,1)S(1)}, u32[]{:S(2)}, u32[]{:S(2)}) collective-permute-start(bf16[2,4,112,128]{3,2,1,0:T(8,128)(2,1)S(1)} %collective-permute-done.12.near1), channel_id=1, source_target_pairs={{192,0},{193,1},{194,2},{195,3},{196,4},{197,5},{198,6},{199,7},{2... | collective-permute-start | bytes 688136 | tf_op jit(solution)/shard_map/ppermute | solution.py:37
  39.2 1.9 %collective-permute-start.21 = (bf16[2,4,112,128]{3,2,1,0:T(8,128)(2,1)S(1)}, bf16[2,4,112,128]{3,2,1,0:T(8,128)(2,1)S(1)}, u32[]{:S(2)}, u32[]{:S(2)}) collective-permute-start(bf16[2,4,112,128]{3,2,1,0:T(8,128)(2,1)S(1)} %collective-permute-done.12.near1), channel_id=1, source_target_pairs={{1,0},{0,1},{3,2},{2,3},{5,4},{4,5},{7,6},{6,7},{9,8},{8,9},{11,10... | collective-permute-start | bytes 688136 | tf_op jit(solution)/shard_map/ppermute | solution.py:37
  41.4 3.4 %collective-permute-start.19 = (bf16[2,4,112,128]{3,2,1,0:T(8,128)(2,1)S(1)}, bf16[2,4,112,128]{3,2,1,0:T(8,128)(2,1)S(1)}, u32[]{:S(2)}, u32[]{:S(2)}) collective-permute-start(bf16[2,4,112,128]{3,2,1,0:T(8,128)(2,1)S(1)} %collective-permute-done.9.near3), channel_id=1, source_target_pairs={{3,0},{2,1},{1,2},{0,3},{7,4},{6,5},{5,6},{4,7},{11,8},{10,9},{9,1... | collective-permute-start | bytes 688136 | tf_op jit(solution)/shard_map/ppermute | solution.py:37
  44.8 1.9 %collective-permute-done.13.far = bf16[2,4,112,128]{3,2,1,0:T(8,128)(2,1)S(1)} collective-permute-done((bf16[2,4,112,128]{3,2,1,0:T(8,128)(2,1)S(1)}, bf16[2,4,112,128]{3,2,1,0:T(8,128)(2,1)S(1)}, u32[]{:S(2)}, u32[]{:S(2)}) %collective-permute-start.13) | collective-permute-done | bytes 229408 | tf_op jit(solution)/shard_map/ppermute | solution.py:37
  46.7 2.6 %collective-permute-start.20 = (bf16[2,4,112,128]{3,2,1,0:T(8,128)(2,1)S(1)}, bf16[2,4,112,128]{3,2,1,0:T(8,128)(2,1)S(1)}, u32[]{:S(2)}, u32[]{:S(2)}) collective-permute-start(bf16[2,4,112,128]{3,2,1,0:T(8,128)(2,1)S(1)} %collective-permute-done.13.far), channel_id=1, source_target_pairs={{3,0},{2,1},{1,2},{0,3},{7,4},{6,5},{5,6},{4,7},{11,8},{10,9},{9,1... | collective-permute-start | bytes 688136 | tf_op jit(solution)/shard_map/ppermute | solution.py:37
  49.3 1.5 %collective-permute-start.16 = (bf16[2,4,112,128]{3,2,1,0:T(8,128)(2,1)S(1)}, bf16[2,4,112,128]{3,2,1,0:T(8,128)(2,1)S(1)}, u32[]{:S(2)}, u32[]{:S(2)}) collective-permute-start(bf16[2,4,112,128]{3,2,1,0:T(8,128)(2,1)S(1)} %collective-permute-done.15.own3), channel_id=1, source_target_pairs={{1,0},{0,1},{3,2},{2,3},{5,4},{4,5},{7,6},{6,7},{9,8},{8,9},{11,10... | collective-permute-start | bytes 688136 | tf_op jit(solution)/shard_map/ppermute | solution.py:37
  50.8 2.4 %collective-permute-start.22 = (bf16[2,4,112,128]{3,2,1,0:T(8,128)(2,1)S(1)}, bf16[2,4,112,128]{3,2,1,0:T(8,128)(2,1)S(1)}, u32[]{:S(2)}, u32[]{:S(2)}) collective-permute-start(bf16[2,4,112,128]{3,2,1,0:T(8,128)(2,1)S(1)} %collective-permute-done.11.near31), channel_id=1, source_target_pairs={{3,0},{2,1},{1,2},{0,3},{7,4},{6,5},{5,6},{4,7},{11,8},{10,9},{9,1... | collective-permute-start | bytes 688136 | tf_op jit(solution)/shard_map/ppermute | solution.py:37
  53.5 2.2 %shard_map.41 = (f32[512,768]{1,0:T(8,128)S(1)}, f32[512,768]{1,0:T(8,128)S(1)}) custom-call(s32[4]{0:T(128)S(1)} %pad_add_fusion.place, bf16[2,4,112,128]{3,2,1,0:T(8,128)(2,1)S(1)} %collective-permute-done.12.near1, bf16[2,4,112,128]{3,2,1,0:T(8,128)(2,1)S(1)} %collective-permute-done.9.near3, bf16[2,4,112,128]{3,2,1,0:T(8,128)(2,1)S(1)} %collective-permute-done.13.far, ...), custom_call_target="tpu_custom_call" | custom-call | tf_op jit(solution)/shard_map/pallas_call | solution.py:180
  55.7 1.2 %shard_map.42.high = f32[512,768]{1,0:T(8,128)S(1)} custom-call(s32[4]{0:T(128)S(1)} %pad_add_fusion.place, bf16[2,4,112,128]{3,2,1,0:T(8,128)(2,1)S(1)} %collective-permute-done.11.near31, bf16[2,4,112,128]{3,2,1,0:T(8,128)(2,1)S(1)} %collective-permute-done.14.far1, bf16[2,4,112,128]{3,2,1,0:T(8,128)(2,1)S(1)} %collective-permute-done.19.near33, ...), custom_call_target="tpu_custom_call" | custom-call | tf_op jit(solution)/shard_map/pallas_call | solution.py:180
  56.9 1.2 %shard_map.43 = (bf16[512,384]{1,0:T(8,128)(2,1)S(1)}, bf16[512,384]{1,0:T(8,128)(2,1)S(1)}) custom-call(s32[4]{0:T(128)S(1)} %pad_add_fusion.place, bf16[2,4,112,128]{3,2,1,0:T(8,128)(2,1)S(1)} %collective-permute-done.11.near31, bf16[2,4,112,128]{3,2,1,0:T(8,128)(2,1)S(1)} %collective-permute-done.14.far1, ...), custom_call_target="tpu_custom_call" | custom-call | tf_op jit(solution)/shard_map/pallas_call | solution.py:180
  58.1 6.6 %collective-permute-start.24 = (bf16[512,384]{1,0:T(8,128)(2,1)S(1)}, bf16[512,384]{1,0:T(8,128)(2,1)S(1)}, u32[]{:S(2)}, u32[]{:S(2)}) collective-permute-start(bf16[512,384]{1,0:T(8,128)(2,1)S(1)} %get-tuple-element.40), channel_id=1, source_target_pairs={{16,0},{0,16},{17,1},{1,17},{18,2},{2,18},{19,3},{3,19},{20,4},{4,... | collective-permute-start | bytes 1179656 | tf_op jit(solution)/shard_map/ppermute | solution.py:24
  64.8 1.2 %shard_map.45 = bf16[512,384]{1,0:T(8,128)(2,1)S(1)} custom-call(s32[4]{0:T(128)S(1)} %pad_add_fusion.place, bf16[2,4,112,128]{3,2,1,0:T(8,128)(2,1)S(1)} %collective-permute-done.16.own, bf16[2,4,112,128]{3,2,1,0:T(8,128)(2,1)S(1)} %collective-permute-done.18.near1, bf16[2,4,112,128]{3,2,1,0:T(8,128)(2,1)S(1)} %collective-permute-done.22.near3, ...), custom_call_target="tpu_custom_call" | custom-call | tf_op jit(solution)/shard_map/pallas_call | solution.py:180
  66.0 1.2 %collective-permute-start.25 = (bf16[512,384]{1,0:T(8,128)(2,1)S(1)}, bf16[512,384]{1,0:T(8,128)(2,1)S(1)}, u32[]{:S(2)}, u32[]{:S(2)}) collective-permute-start(bf16[512,384]{1,0:T(8,128)(2,1)S(1)} %shard_map.45), channel_id=1, source_target_pairs={{16,0},{0,16},{17,1},{1,17},{18,2},{2,18},{19,3},{3,19},{20,4},{4,... | collective-permute-start | bytes 1179656 | tf_op jit(solution)/shard_map/ppermute | solution.py:24
  67.2 1.2 %shard_map.44.mine2 = bf16[512,384]{1,0:T(8,128)(2,1)S(1)} custom-call(s32[4]{0:T(128)S(1)} %pad_add_fusion.place, bf16[2,4,112,128]{3,2,1,0:T(8,128)(2,1)S(1)} %collective-permute-done.16.own, bf16[2,4,112,128]{3,2,1,0:T(8,128)(2,1)S(1)} %collective-permute-done.18.near1, bf16[2,4,112,128]{3,2,1,0:T(8,128)(2,1)S(1)} %collective-permute-done.22.near3, ...), custom_call_target="tpu_custom_call" | custom-call | tf_op jit(solution)/shard_map/pallas_call | solution.py:180
  68.5 1.7 %shard_map.46 = bf16[2048,384]{1,0:T(8,128)(2,1)} custom-call(s32[4]{0:T(128)S(1)} %pad_add_fusion.place, bf16[512,384]{1,0:T(8,128)(2,1)S(1)} %get-tuple-element.38.mine1, bf16[512,384]{1,0:T(8,128)(2,1)S(1)} %shard_map.44.mine2, bf16[512,384]{1,0:T(8,128)(2,1)S(1)} %collective-permute-done.24.theirs1, bf16[512,384]{1,0:T(8,128)(2,1)S(1)} %collective-permute-done.25.theirs2), custom_call_target="tpu_custom_call" | custom-call | tf_op jit(solution)/shard_map/pallas_call | solution.py:180
  (39 shorter events, 6.2 us)
Async XLA Ops:
  0.0 21.0 %copy-start = (bf16[1792,384]{1,0:T(8,128)(2,1)S(1)}, bf16[1792,384]{1,0:T(8,128)(2,1)}, u32[]{:S(2)}) copy-start(bf16[1792,384]{1,0:T(8,128)(2,1)} %own.1) | copy-start | bytes 4128772
  0.0 21.0 %collective-permute-start.5 = (bf16[1792,384]{1,0:T(8,128)(2,1)}, bf16[1792,384]{1,0:T(8,128)(2,1)S(1)}, u32[]{:S(2)}, u32[]{:S(2)}) collective-permute-start(bf16[1792,384]{1,0:T(8,128)(2,1)} %own.1), channel_id=1, source_target_pairs={{16,0},{0,16},{17,1},{1,17},{18,2},{2,18},{19,3},{3,19},{20,4},{4,... | collective-permute-start | bytes 4128776 | tf_op jit(solution)/shard_map/ppermute | solution.py:24
  4.1 1.0 %copy-start.1 = (bf16[112,2048]{1,0:T(8,128)(2,1)S(1)}, bf16[112,2048]{1,0:T(8,128)(2,1)}, u32[]{:S(2)}) copy-start(bf16[112,2048]{1,0:T(8,128)(2,1)} %panel.1) | copy-start | bytes 1376260
  6.1 1.9 %collective-permute-start = (f32[8,112,128]{2,1,0:T(8,128)S(1)}, f32[8,112,128]{2,1,0:T(8,128)S(1)}, u32[]{:S(2)}, u32[]{:S(2)}) collective-permute-start(f32[8,112,128]{2,1,0:T(8,128)S(1)} %get-tuple-element.24), channel_id=1, source_target_pairs={{16,0},{0,16},{17,1},{1,17},{18,2},{2,18},{19,3},{3,19},{20,4},{4,... | collective-permute-start | bytes 1376264 | tf_op jit(solution)/shard_map/ppermute | solution.py:24
  8.6 4.3 %collective-permute-start.1 = (bf16[2,112,128]{2,1,0:T(8,128)(2,1)S(1)}, bf16[2,112,128]{2,1,0:T(8,128)(2,1)S(1)}, u32[]{:S(2)}, u32[]{:S(2)}) collective-permute-start(bf16[2,112,128]{2,1,0:T(8,128)(2,1)S(1)} %get-tuple-element.26), channel_id=1, source_target_pairs={{192,0},{128,64},{64,128},{0,192},{193,1},{129,65},{65,129},{1,193... | collective-permute-start | bytes 172040 | tf_op jit(solution)/shard_map/ppermute | solution.py:28
  9.4 4.6 %collective-permute-start.2 = (bf16[2,112,128]{2,1,0:T(8,128)(2,1)S(1)}, bf16[2,112,128]{2,1,0:T(8,128)(2,1)S(1)}, u32[]{:S(2)}, u32[]{:S(2)}) collective-permute-start(bf16[2,112,128]{2,1,0:T(8,128)(2,1)S(1)} %get-tuple-element.27), channel_id=1, source_target_pairs={{128,0},{192,64},{0,128},{64,192},{129,1},{193,65},{1,129},{65,193... | collective-permute-start | bytes 172040 | tf_op jit(solution)/shard_map/ppermute | solution.py:28
  9.9 4.8 %collective-permute-start.3 = (bf16[2,112,128]{2,1,0:T(8,128)(2,1)S(1)}, bf16[2,112,128]{2,1,0:T(8,128)(2,1)S(1)}, u32[]{:S(2)}, u32[]{:S(2)}) collective-permute-start(bf16[2,112,128]{2,1,0:T(8,128)(2,1)S(1)} %get-tuple-element.28), channel_id=1, source_target_pairs={{64,0},{0,64},{192,128},{128,192},{65,1},{1,65},{193,129},{129,193... | collective-permute-start | bytes 172040 | tf_op jit(solution)/shard_map/ppermute | solution.py:28
  14.8 7.8 %collective-permute-start.4 = (bf16[2,112,128]{2,1,0:T(8,128)(2,1)S(1)}, bf16[2,112,128]{2,1,0:T(8,128)(2,1)S(1)}, u32[]{:S(2)}, u32[]{:S(2)}) collective-permute-start(bf16[2,112,128]{2,1,0:T(8,128)(2,1)S(1)} %fusion), channel_id=1, source_target_pairs={{32,0},{0,32},{33,1},{1,33},{34,2},{2,34},{35,3},{3,35},{36,4},{4,... | collective-permute-start | bytes 172040 | tf_op jit(solution)/shard_map/ppermute | solution.py:28
  22.6 4.9 %collective-permute-start.8 = (bf16[2,112,128]{2,1,0:T(8,128)(2,1)S(1)}, bf16[2,112,128]{2,1,0:T(8,128)(2,1)S(1)}, u32[]{:S(2)}, u32[]{:S(2)}) collective-permute-start(bf16[2,112,128]{2,1,0:T(8,128)(2,1)S(1)} %add_convert_fusion), channel_id=1, source_target_pairs={{12,0},{8,4},{4,8},{0,12},{13,1},{9,5},{5,9},{1,13},{14,2},{10,6},... | collective-permute-start | bytes 172040 | tf_op jit(solution)/shard_map/ppermute | solution.py:28
  25.5 3.0 %collective-permute-start.6 = (bf16[2,112,128]{2,1,0:T(8,128)(2,1)S(1)}, bf16[2,112,128]{2,1,0:T(8,128)(2,1)S(1)}, u32[]{:S(2)}, u32[]{:S(2)}) collective-permute-start(bf16[2,112,128]{2,1,0:T(8,128)(2,1)S(1)} %add_convert_fusion), channel_id=1, source_target_pairs={{4,0},{0,4},{12,8},{8,12},{5,1},{1,5},{13,9},{9,13},{6,2},{2,6},{1... | collective-permute-start | bytes 172040 | tf_op jit(solution)/shard_map/ppermute | solution.py:28
  25.6 4.1 %collective-permute-start.7 = (bf16[2,112,128]{2,1,0:T(8,128)(2,1)S(1)}, bf16[2,112,128]{2,1,0:T(8,128)(2,1)S(1)}, u32[]{:S(2)}, u32[]{:S(2)}) collective-permute-start(bf16[2,112,128]{2,1,0:T(8,128)(2,1)S(1)} %add_convert_fusion), channel_id=1, source_target_pairs={{8,0},{12,4},{0,8},{4,12},{9,1},{13,5},{1,9},{5,13},{10,2},{14,6},... | collective-permute-start | bytes 172040 | tf_op jit(solution)/shard_map/ppermute | solution.py:28
  29.7 8.3 %collective-permute-start.12 = (bf16[2,4,112,128]{3,2,1,0:T(8,128)(2,1)S(1)}, bf16[2,4,112,128]{3,2,1,0:T(8,128)(2,1)S(1)}, u32[]{:S(2)}, u32[]{:S(2)}) collective-permute-start(bf16[2,4,112,128]{3,2,1,0:T(8,128)(2,1)S(1)} %pad_maximum_fusion.own), channel_id=1, source_target_pairs={{64,0},{65,1},{66,2},{67,3},{68,4},{69,5},{70,6},{71,7},{72,8},{73... | collective-permute-start | bytes 688136 | tf_op jit(solution)/shard_map/ppermute | solution.py:37
  31.0 8.2 %collective-permute-start.10 = (bf16[2,4,112,128]{3,2,1,0:T(8,128)(2,1)S(1)}, bf16[2,4,112,128]{3,2,1,0:T(8,128)(2,1)S(1)}, u32[]{:S(2)}, u32[]{:S(2)}) collective-permute-start(bf16[2,4,112,128]{3,2,1,0:T(8,128)(2,1)S(1)} %pad_maximum_fusion.own), channel_id=1, source_target_pairs={{1,0},{0,1},{3,2},{2,3},{5,4},{4,5},{7,6},{6,7},{9,8},{8,9},{11,10... | collective-permute-start | bytes 688136 | tf_op jit(solution)/shard_map/ppermute | solution.py:37
  31.0 10.1 %collective-permute-start.9 = (bf16[2,4,112,128]{3,2,1,0:T(8,128)(2,1)S(1)}, bf16[2,4,112,128]{3,2,1,0:T(8,128)(2,1)S(1)}, u32[]{:S(2)}, u32[]{:S(2)}) collective-permute-start(bf16[2,4,112,128]{3,2,1,0:T(8,128)(2,1)S(1)} %pad_maximum_fusion.own), channel_id=1, source_target_pairs={{192,0},{193,1},{194,2},{195,3},{196,4},{197,5},{198,6},{199,7},{2... | collective-permute-start | bytes 688136 | tf_op jit(solution)/shard_map/ppermute | solution.py:37
  33.0 8.5 %collective-permute-start.15 = (bf16[2,4,112,128]{3,2,1,0:T(8,128)(2,1)S(1)}, bf16[2,4,112,128]{3,2,1,0:T(8,128)(2,1)S(1)}, u32[]{:S(2)}, u32[]{:S(2)}) collective-permute-start(bf16[2,4,112,128]{3,2,1,0:T(8,128)(2,1)S(1)} %pad_maximum_fusion.own), channel_id=1, source_target_pairs={{3,0},{2,1},{1,2},{0,3},{7,4},{6,5},{5,6},{4,7},{11,8},{10,9},{9,1... | collective-permute-start | bytes 688136 | tf_op jit(solution)/shard_map/ppermute | solution.py:37
  38.0 8.7 %collective-permute-start.13 = (bf16[2,4,112,128]{3,2,1,0:T(8,128)(2,1)S(1)}, bf16[2,4,112,128]{3,2,1,0:T(8,128)(2,1)S(1)}, u32[]{:S(2)}, u32[]{:S(2)}) collective-permute-start(bf16[2,4,112,128]{3,2,1,0:T(8,128)(2,1)S(1)} %collective-permute-done.12.near1), channel_id=1, source_target_pairs={{192,0},{193,1},{194,2},{195,3},{196,4},{197,5},{198,6},{199,7},{2... | collective-permute-start | bytes 688136 | tf_op jit(solution)/shard_map/ppermute | solution.py:37
  38.9 7.8 %collective-permute-start.17 = (bf16[2,4,112,128]{3,2,1,0:T(8,128)(2,1)S(1)}, bf16[2,4,112,128]{3,2,1,0:T(8,128)(2,1)S(1)}, u32[]{:S(2)}, u32[]{:S(2)}) collective-permute-start(bf16[2,4,112,128]{3,2,1,0:T(8,128)(2,1)S(1)} %collective-permute-done.12.near1), channel_id=1, source_target_pairs={{3,0},{2,1},{1,2},{0,3},{7,4},{6,5},{5,6},{4,7},{11,8},{10,9},{9,1... | collective-permute-start | bytes 688136 | tf_op jit(solution)/shard_map/ppermute | solution.py:37
  39.2 10.1 %collective-permute-start.21 = (bf16[2,4,112,128]{3,2,1,0:T(8,128)(2,1)S(1)}, bf16[2,4,112,128]{3,2,1,0:T(8,128)(2,1)S(1)}, u32[]{:S(2)}, u32[]{:S(2)}) collective-permute-start(bf16[2,4,112,128]{3,2,1,0:T(8,128)(2,1)S(1)} %collective-permute-done.12.near1), channel_id=1, source_target_pairs={{1,0},{0,1},{3,2},{2,3},{5,4},{4,5},{7,6},{6,7},{9,8},{8,9},{11,10... | collective-permute-start | bytes 688136 | tf_op jit(solution)/shard_map/ppermute | solution.py:37
  41.1 8.2 %collective-permute-start.11 = (bf16[2,4,112,128]{3,2,1,0:T(8,128)(2,1)S(1)}, bf16[2,4,112,128]{3,2,1,0:T(8,128)(2,1)S(1)}, u32[]{:S(2)}, u32[]{:S(2)}) collective-permute-start(bf16[2,4,112,128]{3,2,1,0:T(8,128)(2,1)S(1)} %collective-permute-done.9.near3), channel_id=1, source_target_pairs={{1,0},{0,1},{3,2},{2,3},{5,4},{4,5},{7,6},{6,7},{9,8},{8,9},{11,10... | collective-permute-start | bytes 688136 | tf_op jit(solution)/shard_map/ppermute | solution.py:37
  41.4 9.4 %collective-permute-start.19 = (bf16[2,4,112,128]{3,2,1,0:T(8,128)(2,1)S(1)}, bf16[2,4,112,128]{3,2,1,0:T(8,128)(2,1)S(1)}, u32[]{:S(2)}, u32[]{:S(2)}) collective-permute-start(bf16[2,4,112,128]{3,2,1,0:T(8,128)(2,1)S(1)} %collective-permute-done.9.near3), channel_id=1, source_target_pairs={{3,0},{2,1},{1,2},{0,3},{7,4},{6,5},{5,6},{4,7},{11,8},{10,9},{9,1... | collective-permute-start | bytes 688136 | tf_op jit(solution)/shard_map/ppermute | solution.py:37
  46.7 6.6 %collective-permute-start.14 = (bf16[2,4,112,128]{3,2,1,0:T(8,128)(2,1)S(1)}, bf16[2,4,112,128]{3,2,1,0:T(8,128)(2,1)S(1)}, u32[]{:S(2)}, u32[]{:S(2)}) collective-permute-start(bf16[2,4,112,128]{3,2,1,0:T(8,128)(2,1)S(1)} %collective-permute-done.13.far), channel_id=1, source_target_pairs={{1,0},{0,1},{3,2},{2,3},{5,4},{4,5},{7,6},{6,7},{9,8},{8,9},{11,10... | collective-permute-start | bytes 688136 | tf_op jit(solution)/shard_map/ppermute | solution.py:37
  46.7 9.0 %collective-permute-start.20 = (bf16[2,4,112,128]{3,2,1,0:T(8,128)(2,1)S(1)}, bf16[2,4,112,128]{3,2,1,0:T(8,128)(2,1)S(1)}, u32[]{:S(2)}, u32[]{:S(2)}) collective-permute-start(bf16[2,4,112,128]{3,2,1,0:T(8,128)(2,1)S(1)} %collective-permute-done.13.far), channel_id=1, source_target_pairs={{3,0},{2,1},{1,2},{0,3},{7,4},{6,5},{5,6},{4,7},{11,8},{10,9},{9,1... | collective-permute-start | bytes 688136 | tf_op jit(solution)/shard_map/ppermute | solution.py:37
  49.3 7.6 %collective-permute-start.18 = (bf16[2,4,112,128]{3,2,1,0:T(8,128)(2,1)S(1)}, bf16[2,4,112,128]{3,2,1,0:T(8,128)(2,1)S(1)}, u32[]{:S(2)}, u32[]{:S(2)}) collective-permute-start(bf16[2,4,112,128]{3,2,1,0:T(8,128)(2,1)S(1)} %collective-permute-done.17.near31), channel_id=1, source_target_pairs={{1,0},{0,1},{3,2},{2,3},{5,4},{4,5},{7,6},{6,7},{9,8},{8,9},{11,10... | collective-permute-start | bytes 688136 | tf_op jit(solution)/shard_map/ppermute | solution.py:37
  49.3 7.6 %collective-permute-start.16 = (bf16[2,4,112,128]{3,2,1,0:T(8,128)(2,1)S(1)}, bf16[2,4,112,128]{3,2,1,0:T(8,128)(2,1)S(1)}, u32[]{:S(2)}, u32[]{:S(2)}) collective-permute-start(bf16[2,4,112,128]{3,2,1,0:T(8,128)(2,1)S(1)} %collective-permute-done.15.own3), channel_id=1, source_target_pairs={{1,0},{0,1},{3,2},{2,3},{5,4},{4,5},{7,6},{6,7},{9,8},{8,9},{11,10... | collective-permute-start | bytes 688136 | tf_op jit(solution)/shard_map/ppermute | solution.py:37
  50.8 14.0 %collective-permute-start.22 = (bf16[2,4,112,128]{3,2,1,0:T(8,128)(2,1)S(1)}, bf16[2,4,112,128]{3,2,1,0:T(8,128)(2,1)S(1)}, u32[]{:S(2)}, u32[]{:S(2)}) collective-permute-start(bf16[2,4,112,128]{3,2,1,0:T(8,128)(2,1)S(1)} %collective-permute-done.11.near31), channel_id=1, source_target_pairs={{3,0},{2,1},{1,2},{0,3},{7,4},{6,5},{5,6},{4,7},{11,8},{10,9},{9,1... | collective-permute-start | bytes 688136 | tf_op jit(solution)/shard_map/ppermute | solution.py:37
  53.2 11.5 %collective-permute-start.23 = (bf16[2,4,112,128]{3,2,1,0:T(8,128)(2,1)S(1)}, bf16[2,4,112,128]{3,2,1,0:T(8,128)(2,1)S(1)}, u32[]{:S(2)}, u32[]{:S(2)}) collective-permute-start(bf16[2,4,112,128]{3,2,1,0:T(8,128)(2,1)S(1)} %collective-permute-done.14.far1), channel_id=1, source_target_pairs={{3,0},{2,1},{1,2},{0,3},{7,4},{6,5},{5,6},{4,7},{11,8},{10,9},{9,1... | collective-permute-start | bytes 688136 | tf_op jit(solution)/shard_map/ppermute | solution.py:37
  58.1 10.3 %collective-permute-start.24 = (bf16[512,384]{1,0:T(8,128)(2,1)S(1)}, bf16[512,384]{1,0:T(8,128)(2,1)S(1)}, u32[]{:S(2)}, u32[]{:S(2)}) collective-permute-start(bf16[512,384]{1,0:T(8,128)(2,1)S(1)} %get-tuple-element.40), channel_id=1, source_target_pairs={{16,0},{0,16},{17,1},{1,17},{18,2},{2,18},{19,3},{3,19},{20,4},{4,... | collective-permute-start | bytes 1179656 | tf_op jit(solution)/shard_map/ppermute | solution.py:24
  66.0 2.5 %collective-permute-start.25 = (bf16[512,384]{1,0:T(8,128)(2,1)S(1)}, bf16[512,384]{1,0:T(8,128)(2,1)S(1)}, u32[]{:S(2)}, u32[]{:S(2)}) collective-permute-start(bf16[512,384]{1,0:T(8,128)(2,1)S(1)} %shard_map.45), channel_id=1, source_target_pairs={{16,0},{0,16},{17,1},{1,17},{18,2},{2,18},{19,3},{3,19},{20,4},{4,... | collective-permute-start | bytes 1179656 | tf_op jit(solution)/shard_map/ppermute | solution.py:24

commit v15 on v13

--- a/solution.py
+++ b/solution.py
@@ -220,6 +220,7 @@
     near1, start = lax.optimization_barrier((near1, start))
     far = turn(near1, 0, 3)
     one_own, three_own = turn(own, 1, 1), turn(own, 1, 3)
+    near1, near3 = lax.optimization_barrier((near1, near3))
     one_near1, three_near1 = turn(near1, 1, 1), turn(near1, 1, 3)
     near3, one_own = lax.optimization_barrier((near3, one_own))
     one_near3, three_near3 = turn(near3, 1, 1), turn(near3, 1, 3)

time: 70.7 us -> 69.9 us (0.989)
  starting transfers between devices: 45 us -> 42.8 us
  waiting for transfers between devices: 11.2 us -> 12.6 us
    ppermute x15, starting transfers between devices: 20.2 us -> 18.7 us  [turn(): return lax.ppermute(block, ROW + COL, pairs)]
    ppermute x15, waiting for transfers between devices: 2.44 us -> 3.79 us  [turn(): return lax.ppermute(block, ROW + COL, pairs)]
where the time goes in v15:
time: 69.9 us; the launch traced here: 69.7 us
  starting transfers between devices  42.8 us (61%)
  waiting for transfers between devices  12.6 us (18%)
  Pallas kernels  12.1 us (17%)
  local copies, waits for them, and re-layouts  1.77 us (3%)
    ppermute x15, starting transfers between devices, turn(): return lax.ppermute(block, ROW + COL, pairs)  18.7 us
    ppermute x7, starting transfers between devices, swap(): return lax.ppermute(block, axis, [(i ^ bits, i) for i in range(size)])  13.2 us
    pallas_call x10, Pallas kernels, call(): pl.pallas_call(kernel, out_shape=out_shape, in_specs=specs or [SMEM] + [V...  12.1 us
    ppermute x4, starting transfers between devices, fetch(): lax.ppermute(block, axis, [((i + ahead) % size, i) for i in range(size)])  10.9 us
    ppermute x7, waiting for transfers between devices, swap(): return lax.ppermute(block, axis, [(i ^ bits, i) for i in range(size)])  6.97 us
    ppermute x15, waiting for transfers between devices, turn(): return lax.ppermute(block, ROW + COL, pairs)  3.79 us
    ppermute x4, waiting for transfers between devices, fetch(): lax.ppermute(block, axis, [((i + ahead) % size, i) for i in range(size)])  1.83 us
    unnamed x6, local copies, waits for them, and re-layouts  1.77 us
  transfers between devices with their start and end apart: 26, of which 12 were waited for; matrix products, arithmetic and copies ran while one was open for 0% of the time, Pallas kernels for 15%

profile of v15, /device:TPU:1, one launch (start us, length us, event | category | flops | bytes accessed | tf_op | source)
XLA Modules:
  0.0 69.7 jit_solution(12073724158535786062)
XLA Ops:
  0.0 3.2 %collective-permute-start.5 = (bf16[1792,384]{1,0:T(8,128)(2,1)}, bf16[1792,384]{1,0:T(8,128)(2,1)S(1)}, u32[]{:S(2)}, u32[]{:S(2)}) collective-permute-start(bf16[1792,384]{1,0:T(8,128)(2,1)} %own.1), channel_id=1, source_target_pairs={{16,0},{0,16},{17,1},{1,17},{18,2},{2,18},{19,3},{3,19},{20,4},{4,... | collective-permute-start | bytes 4128776 | tf_op jit(solution)/shard_map/ppermute | solution.py:24
  3.3 1.0 %copy-done.1 = bf16[112,2048]{1,0:T(8,128)(2,1)S(1)} copy-done((bf16[112,2048]{1,0:T(8,128)(2,1)S(1)}, bf16[112,2048]{1,0:T(8,128)(2,1)}, u32[]{:S(2)}) %copy-start.1) | copy-done | bytes 458776
  5.1 1.0 %shard_map.37 = (f32[8,112,128]{2,1,0:T(8,128)S(1)}, f32[8,112,128]{2,1,0:T(8,128)S(1)}) custom-call(s32[4]{0:T(128)S(1)} %pad_add_fusion.place, bf16[112,112]{1,0:T(8,128)(2,1)S(1)} %copy-done.2, bf16[112,2048]{1,0:T(8,128)(2,1)S(1)} %copy-done.1), custom_call_target="tpu_custom_call" | custom-call | tf_op jit(solution)/shard_map/pallas_call | solution.py:180
  6.2 1.7 %collective-permute-done.received = f32[8,112,128]{2,1,0:T(8,128)S(1)} collective-permute-done((f32[8,112,128]{2,1,0:T(8,128)S(1)}, f32[8,112,128]{2,1,0:T(8,128)S(1)}, u32[]{:S(2)}, u32[]{:S(2)}) %collective-permute-start) | collective-permute-done | bytes 458784 | tf_op jit(solution)/shard_map/ppermute | solution.py:24
  9.9 2.0 %collective-permute-start.3 = (bf16[2,112,128]{2,1,0:T(8,128)(2,1)S(1)}, bf16[2,112,128]{2,1,0:T(8,128)(2,1)S(1)}, u32[]{:S(2)}, u32[]{:S(2)}) collective-permute-start(bf16[2,112,128]{2,1,0:T(8,128)(2,1)S(1)} %get-tuple-element.30), channel_id=1, source_target_pairs={{64,0},{0,64},{192,128},{128,192},{65,1},{1,65},{193,129},{129,193... | collective-permute-start | bytes 172040 | tf_op jit(solution)/shard_map/ppermute | solution.py:28
  11.9 1.0 %collective-permute-done.1 = bf16[2,112,128]{2,1,0:T(8,128)(2,1)S(1)} collective-permute-done((bf16[2,112,128]{2,1,0:T(8,128)(2,1)S(1)}, bf16[2,112,128]{2,1,0:T(8,128)(2,1)S(1)}, u32[]{:S(2)}, u32[]{:S(2)}) %collective-permute-start.1) | collective-permute-done | bytes 57376 | tf_op jit(solution)/shard_map/ppermute | solution.py:28
  12.9 1.1 %collective-permute-done.2 = bf16[2,112,128]{2,1,0:T(8,128)(2,1)S(1)} collective-permute-done((bf16[2,112,128]{2,1,0:T(8,128)(2,1)S(1)}, bf16[2,112,128]{2,1,0:T(8,128)(2,1)S(1)}, u32[]{:S(2)}, u32[]{:S(2)}) %collective-permute-start.2) | collective-permute-done | bytes 57376 | tf_op jit(solution)/shard_map/ppermute | solution.py:28
  14.8 6.2 %collective-permute-start.4 = (bf16[2,112,128]{2,1,0:T(8,128)(2,1)S(1)}, bf16[2,112,128]{2,1,0:T(8,128)(2,1)S(1)}, u32[]{:S(2)}, u32[]{:S(2)}) collective-permute-start(bf16[2,112,128]{2,1,0:T(8,128)(2,1)S(1)} %fusion), channel_id=1, source_target_pairs={{32,0},{0,32},{33,1},{1,33},{34,2},{2,34},{35,3},{3,35},{36,4},{4,... | collective-permute-start | bytes 172040 | tf_op jit(solution)/shard_map/ppermute | solution.py:28
  22.6 2.9 %collective-permute-start.8 = (bf16[2,112,128]{2,1,0:T(8,128)(2,1)S(1)}, bf16[2,112,128]{2,1,0:T(8,128)(2,1)S(1)}, u32[]{:S(2)}, u32[]{:S(2)}) collective-permute-start(bf16[2,112,128]{2,1,0:T(8,128)(2,1)S(1)} %add_convert_fusion), channel_id=1, source_target_pairs={{12,0},{8,4},{4,8},{0,12},{13,1},{9,5},{5,9},{1,13},{14,2},{10,6},... | collective-permute-start | bytes 172040 | tf_op jit(solution)/shard_map/ppermute | solution.py:28
  26.2 1.3 %collective-permute-done.8 = bf16[2,112,128]{2,1,0:T(8,128)(2,1)S(1)} collective-permute-done((bf16[2,112,128]{2,1,0:T(8,128)(2,1)S(1)}, bf16[2,112,128]{2,1,0:T(8,128)(2,1)S(1)}, u32[]{:S(2)}, u32[]{:S(2)}) %collective-permute-start.8) | collective-permute-done | bytes 57376 | tf_op jit(solution)/shard_map/ppermute | solution.py:28
  27.5 1.0 %collective-permute-done.6 = bf16[2,112,128]{2,1,0:T(8,128)(2,1)S(1)} collective-permute-done((bf16[2,112,128]{2,1,0:T(8,128)(2,1)S(1)}, bf16[2,112,128]{2,1,0:T(8,128)(2,1)S(1)}, u32[]{:S(2)}, u32[]{:S(2)}) %collective-permute-start.6) | collective-permute-done | bytes 57376 | tf_op jit(solution)/shard_map/ppermute | solution.py:28
  28.6 1.0 %collective-permute-done.7 = bf16[2,112,128]{2,1,0:T(8,128)(2,1)S(1)} collective-permute-done((bf16[2,112,128]{2,1,0:T(8,128)(2,1)S(1)}, bf16[2,112,128]{2,1,0:T(8,128)(2,1)S(1)}, u32[]{:S(2)}, u32[]{:S(2)}) %collective-permute-start.7) | collective-permute-done | bytes 57376 | tf_op jit(solution)/shard_map/ppermute | solution.py:28
  29.7 1.4 %collective-permute-start.9 = (bf16[2,4,112,128]{3,2,1,0:T(8,128)(2,1)S(1)}, bf16[2,4,112,128]{3,2,1,0:T(8,128)(2,1)S(1)}, u32[]{:S(2)}, u32[]{:S(2)}) collective-permute-start(bf16[2,4,112,128]{3,2,1,0:T(8,128)(2,1)S(1)} %pad_maximum_fusion.own), channel_id=1, source_target_pairs={{64,0},{65,1},{66,2},{67,3},{68,4},{69,5},{70,6},{71,7},{72,8},{73... | collective-permute-start | bytes 688136 | tf_op jit(solution)/shard_map/ppermute | solution.py:37
  31.0 1.9 %collective-permute-start.10 = (bf16[2,4,112,128]{3,2,1,0:T(8,128)(2,1)S(1)}, bf16[2,4,112,128]{3,2,1,0:T(8,128)(2,1)S(1)}, u32[]{:S(2)}, u32[]{:S(2)}) collective-permute-start(bf16[2,4,112,128]{3,2,1,0:T(8,128)(2,1)S(1)} %pad_maximum_fusion.own), channel_id=1, source_target_pairs={{192,0},{193,1},{194,2},{195,3},{196,4},{197,5},{198,6},{199,7},{2... | collective-permute-start | bytes 688136 | tf_op jit(solution)/shard_map/ppermute | solution.py:37
  33.0 3.9 %collective-permute-start.15 = (bf16[2,4,112,128]{3,2,1,0:T(8,128)(2,1)S(1)}, bf16[2,4,112,128]{3,2,1,0:T(8,128)(2,1)S(1)}, u32[]{:S(2)}, u32[]{:S(2)}) collective-permute-start(bf16[2,4,112,128]{3,2,1,0:T(8,128)(2,1)S(1)} %pad_maximum_fusion.own), channel_id=1, source_target_pairs={{3,0},{2,1},{1,2},{0,3},{7,4},{6,5},{5,6},{4,7},{11,8},{10,9},{9,1... | collective-permute-start | bytes 688136 | tf_op jit(solution)/shard_map/ppermute | solution.py:37
  37.8 1.1 %collective-permute-start.13 = (bf16[2,4,112,128]{3,2,1,0:T(8,128)(2,1)S(1)}, bf16[2,4,112,128]{3,2,1,0:T(8,128)(2,1)S(1)}, u32[]{:S(2)}, u32[]{:S(2)}) collective-permute-start(bf16[2,4,112,128]{3,2,1,0:T(8,128)(2,1)S(1)} %collective-permute-done.9.near1), channel_id=1, source_target_pairs={{192,0},{193,1},{194,2},{195,3},{196,4},{197,5},{198,6},{199,7},{2... | collective-permute-start | bytes 688136 | tf_op jit(solution)/shard_map/ppermute | solution.py:37
  39.2 1.5 %collective-permute-start.21 = (bf16[2,4,112,128]{3,2,1,0:T(8,128)(2,1)S(1)}, bf16[2,4,112,128]{3,2,1,0:T(8,128)(2,1)S(1)}, u32[]{:S(2)}, u32[]{:S(2)}) collective-permute-start(bf16[2,4,112,128]{3,2,1,0:T(8,128)(2,1)S(1)} %collective-permute-done.9.near1), channel_id=1, source_target_pairs={{1,0},{0,1},{3,2},{2,3},{5,4},{4,5},{7,6},{6,7},{9,8},{8,9},{11,10... | collective-permute-start | bytes 688136 | tf_op jit(solution)/shard_map/ppermute | solution.py:37
  40.7 1.2 %collective-permute-done.15.own3 = bf16[2,4,112,128]{3,2,1,0:T(8,128)(2,1)S(1)} collective-permute-done((bf16[2,4,112,128]{3,2,1,0:T(8,128)(2,1)S(1)}, bf16[2,4,112,128]{3,2,1,0:T(8,128)(2,1)S(1)}, u32[]{:S(2)}, u32[]{:S(2)}) %collective-permute-start.15) | collective-permute-done | bytes 229408 | tf_op jit(solution)/shard_map/ppermute | solution.py:37
  41.9 3.4 %collective-permute-start.19 = (bf16[2,4,112,128]{3,2,1,0:T(8,128)(2,1)S(1)}, bf16[2,4,112,128]{3,2,1,0:T(8,128)(2,1)S(1)}, u32[]{:S(2)}, u32[]{:S(2)}) collective-permute-start(bf16[2,4,112,128]{3,2,1,0:T(8,128)(2,1)S(1)} %collective-permute-done.10.near3), channel_id=1, source_target_pairs={{3,0},{2,1},{1,2},{0,3},{7,4},{6,5},{5,6},{4,7},{11,8},{10,9},{9,1... | collective-permute-start | bytes 688136 | tf_op jit(solution)/shard_map/ppermute | solution.py:37
  45.3 1.1 %collective-permute-done.13.far = bf16[2,4,112,128]{3,2,1,0:T(8,128)(2,1)S(1)} collective-permute-done((bf16[2,4,112,128]{3,2,1,0:T(8,128)(2,1)S(1)}, bf16[2,4,112,128]{3,2,1,0:T(8,128)(2,1)S(1)}, u32[]{:S(2)}, u32[]{:S(2)}) %collective-permute-start.13) | collective-permute-done | bytes 229408 | tf_op jit(solution)/shard_map/ppermute | solution.py:37
  46.4 1.1 %collective-permute-start.20 = (bf16[2,4,112,128]{3,2,1,0:T(8,128)(2,1)S(1)}, bf16[2,4,112,128]{3,2,1,0:T(8,128)(2,1)S(1)}, u32[]{:S(2)}, u32[]{:S(2)}) collective-permute-start(bf16[2,4,112,128]{3,2,1,0:T(8,128)(2,1)S(1)} %collective-permute-done.13.far), channel_id=1, source_target_pairs={{3,0},{2,1},{1,2},{0,3},{7,4},{6,5},{5,6},{4,7},{11,8},{10,9},{9,1... | collective-permute-start | bytes 688136 | tf_op jit(solution)/shard_map/ppermute | solution.py:37
  48.0 1.0 %collective-permute-start.16 = (bf16[2,4,112,128]{3,2,1,0:T(8,128)(2,1)S(1)}, bf16[2,4,112,128]{3,2,1,0:T(8,128)(2,1)S(1)}, u32[]{:S(2)}, u32[]{:S(2)}) collective-permute-start(bf16[2,4,112,128]{3,2,1,0:T(8,128)(2,1)S(1)} %collective-permute-done.15.own3), channel_id=1, source_target_pairs={{1,0},{0,1},{3,2},{2,3},{5,4},{4,5},{7,6},{6,7},{9,8},{8,9},{11,10... | collective-permute-start | bytes 688136 | tf_op jit(solution)/shard_map/ppermute | solution.py:37
  49.0 1.5 %collective-permute-done.19.near33 = bf16[2,4,112,128]{3,2,1,0:T(8,128)(2,1)S(1)} collective-permute-done((bf16[2,4,112,128]{3,2,1,0:T(8,128)(2,1)S(1)}, bf16[2,4,112,128]{3,2,1,0:T(8,128)(2,1)S(1)}, u32[]{:S(2)}, u32[]{:S(2)}) %collective-permute-start.19) | collective-permute-done | bytes 229408 | tf_op jit(solution)/shard_map/ppermute | solution.py:37
  50.4 2.0 %collective-permute-start.22 = (bf16[2,4,112,128]{3,2,1,0:T(8,128)(2,1)S(1)}, bf16[2,4,112,128]{3,2,1,0:T(8,128)(2,1)S(1)}, u32[]{:S(2)}, u32[]{:S(2)}) collective-permute-start(bf16[2,4,112,128]{3,2,1,0:T(8,128)(2,1)S(1)} %collective-permute-done.12.near31), channel_id=1, source_target_pairs={{3,0},{2,1},{1,2},{0,3},{7,4},{6,5},{5,6},{4,7},{11,8},{10,9},{9,1... | collective-permute-start | bytes 688136 | tf_op jit(solution)/shard_map/ppermute | solution.py:37
  53.1 2.2 %shard_map.41 = (f32[512,768]{1,0:T(8,128)S(1)}, f32[512,768]{1,0:T(8,128)S(1)}) custom-call(s32[4]{0:T(128)S(1)} %pad_add_fusion.place, bf16[2,4,112,128]{3,2,1,0:T(8,128)(2,1)S(1)} %collective-permute-done.9.near1, bf16[2,4,112,128]{3,2,1,0:T(8,128)(2,1)S(1)} %collective-permute-done.10.near3, bf16[2,4,112,128]{3,2,1,0:T(8,128)(2,1)S(1)} %collective-permute-done.13.far, ...), custom_call_target="tpu_custom_call" | custom-call | tf_op jit(solution)/shard_map/pallas_call | solution.py:180
  55.3 1.2 %shard_map.42.high = f32[512,768]{1,0:T(8,128)S(1)} custom-call(s32[4]{0:T(128)S(1)} %pad_add_fusion.place, bf16[2,4,112,128]{3,2,1,0:T(8,128)(2,1)S(1)} %collective-permute-done.12.near31, bf16[2,4,112,128]{3,2,1,0:T(8,128)(2,1)S(1)} %collective-permute-done.14.far1, bf16[2,4,112,128]{3,2,1,0:T(8,128)(2,1)S(1)} %collective-permute-done.19.near33, ...), custom_call_target="tpu_custom_call" | custom-call | tf_op jit(solution)/shard_map/pallas_call | solution.py:180
  56.5 1.2 %shard_map.43 = (bf16[512,384]{1,0:T(8,128)(2,1)S(1)}, bf16[512,384]{1,0:T(8,128)(2,1)S(1)}) custom-call(s32[4]{0:T(128)S(1)} %pad_add_fusion.place, bf16[2,4,112,128]{3,2,1,0:T(8,128)(2,1)S(1)} %collective-permute-done.12.near31, bf16[2,4,112,128]{3,2,1,0:T(8,128)(2,1)S(1)} %collective-permute-done.14.far1, ...), custom_call_target="tpu_custom_call" | custom-call | tf_op jit(solution)/shard_map/pallas_call | solution.py:180
  57.7 6.3 %collective-permute-start.24 = (bf16[512,384]{1,0:T(8,128)(2,1)S(1)}, bf16[512,384]{1,0:T(8,128)(2,1)S(1)}, u32[]{:S(2)}, u32[]{:S(2)}) collective-permute-start(bf16[512,384]{1,0:T(8,128)(2,1)S(1)} %get-tuple-element.44), channel_id=1, source_target_pairs={{16,0},{0,16},{17,1},{1,17},{18,2},{2,18},{19,3},{3,19},{20,4},{4,... | collective-permute-start | bytes 1179656 | tf_op jit(solution)/shard_map/ppermute | solution.py:24
  64.0 1.2 %shard_map.45 = bf16[512,384]{1,0:T(8,128)(2,1)S(1)} custom-call(s32[4]{0:T(128)S(1)} %pad_add_fusion.place, bf16[2,4,112,128]{3,2,1,0:T(8,128)(2,1)S(1)} %collective-permute-done.16.own, bf16[2,4,112,128]{3,2,1,0:T(8,128)(2,1)S(1)} %collective-permute-done.18.near1, bf16[2,4,112,128]{3,2,1,0:T(8,128)(2,1)S(1)} %collective-permute-done.22.near3, ...), custom_call_target="tpu_custom_call" | custom-call | tf_op jit(solution)/shard_map/pallas_call | solution.py:180
  65.3 1.2 %collective-permute-start.25 = (bf16[512,384]{1,0:T(8,128)(2,1)S(1)}, bf16[512,384]{1,0:T(8,128)(2,1)S(1)}, u32[]{:S(2)}, u32[]{:S(2)}) collective-permute-start(bf16[512,384]{1,0:T(8,128)(2,1)S(1)} %shard_map.45), channel_id=1, source_target_pairs={{16,0},{0,16},{17,1},{1,17},{18,2},{2,18},{19,3},{3,19},{20,4},{4,... | collective-permute-start | bytes 1179656 | tf_op jit(solution)/shard_map/ppermute | solution.py:24
  66.4 1.2 %shard_map.44.mine2 = bf16[512,384]{1,0:T(8,128)(2,1)S(1)} custom-call(s32[4]{0:T(128)S(1)} %pad_add_fusion.place, bf16[2,4,112,128]{3,2,1,0:T(8,128)(2,1)S(1)} %collective-permute-done.16.own, bf16[2,4,112,128]{3,2,1,0:T(8,128)(2,1)S(1)} %collective-permute-done.18.near1, bf16[2,4,112,128]{3,2,1,0:T(8,128)(2,1)S(1)} %collective-permute-done.22.near3, ...), custom_call_target="tpu_custom_call" | custom-call | tf_op jit(solution)/shard_map/pallas_call | solution.py:180
  67.8 1.7 %shard_map.46 = bf16[2048,384]{1,0:T(8,128)(2,1)} custom-call(s32[4]{0:T(128)S(1)} %pad_add_fusion.place, bf16[512,384]{1,0:T(8,128)(2,1)S(1)} %get-tuple-element.42.mine1, bf16[512,384]{1,0:T(8,128)(2,1)S(1)} %shard_map.44.mine2, bf16[512,384]{1,0:T(8,128)(2,1)S(1)} %collective-permute-done.24.theirs1, bf16[512,384]{1,0:T(8,128)(2,1)S(1)} %collective-permute-done.25.theirs2), custom_call_target="tpu_custom_call" | custom-call | tf_op jit(solution)/shard_map/pallas_call | solution.py:180
  (40 shorter events, 8.7 us)
Async XLA Ops:
  0.0 21.0 %copy-start = (bf16[1792,384]{1,0:T(8,128)(2,1)S(1)}, bf16[1792,384]{1,0:T(8,128)(2,1)}, u32[]{:S(2)}) copy-start(bf16[1792,384]{1,0:T(8,128)(2,1)} %own.1) | copy-start | bytes 4128772
  0.0 21.0 %collective-permute-start.5 = (bf16[1792,384]{1,0:T(8,128)(2,1)}, bf16[1792,384]{1,0:T(8,128)(2,1)S(1)}, u32[]{:S(2)}, u32[]{:S(2)}) collective-permute-start(bf16[1792,384]{1,0:T(8,128)(2,1)} %own.1), channel_id=1, source_target_pairs={{16,0},{0,16},{17,1},{1,17},{18,2},{2,18},{19,3},{3,19},{20,4},{4,... | collective-permute-start | bytes 4128776 | tf_op jit(solution)/shard_map/ppermute | solution.py:24
  3.3 1.0 %copy-start.1 = (bf16[112,2048]{1,0:T(8,128)(2,1)S(1)}, bf16[112,2048]{1,0:T(8,128)(2,1)}, u32[]{:S(2)}) copy-start(bf16[112,2048]{1,0:T(8,128)(2,1)} %panel.1) | copy-start | bytes 1376260
  4.3 0.7 %copy-start.2 = (bf16[112,112]{1,0:T(8,128)(2,1)S(1)}, bf16[112,112]{1,0:T(8,128)(2,1)}, u32[]{:S(2)}) copy-start(bf16[112,112]{1,0:T(8,128)(2,1)} %screening.1) | copy-start | bytes 75268
  6.1 1.9 %collective-permute-start = (f32[8,112,128]{2,1,0:T(8,128)S(1)}, f32[8,112,128]{2,1,0:T(8,128)S(1)}, u32[]{:S(2)}, u32[]{:S(2)}) collective-permute-start(f32[8,112,128]{2,1,0:T(8,128)S(1)} %get-tuple-element.26), channel_id=1, source_target_pairs={{16,0},{0,16},{17,1},{1,17},{18,2},{2,18},{19,3},{3,19},{20,4},{4,... | collective-permute-start | bytes 1376264 | tf_op jit(solution)/shard_map/ppermute | solution.py:24
  8.6 4.3 %collective-permute-start.1 = (bf16[2,112,128]{2,1,0:T(8,128)(2,1)S(1)}, bf16[2,112,128]{2,1,0:T(8,128)(2,1)S(1)}, u32[]{:S(2)}, u32[]{:S(2)}) collective-permute-start(bf16[2,112,128]{2,1,0:T(8,128)(2,1)S(1)} %get-tuple-element.28), channel_id=1, source_target_pairs={{192,0},{128,64},{64,128},{0,192},{193,1},{129,65},{65,129},{1,193... | collective-permute-start | bytes 172040 | tf_op jit(solution)/shard_map/ppermute | solution.py:28
  9.4 4.6 %collective-permute-start.2 = (bf16[2,112,128]{2,1,0:T(8,128)(2,1)S(1)}, bf16[2,112,128]{2,1,0:T(8,128)(2,1)S(1)}, u32[]{:S(2)}, u32[]{:S(2)}) collective-permute-start(bf16[2,112,128]{2,1,0:T(8,128)(2,1)S(1)} %get-tuple-element.29), channel_id=1, source_target_pairs={{128,0},{192,64},{0,128},{64,192},{129,1},{193,65},{1,129},{65,193... | collective-permute-start | bytes 172040 | tf_op jit(solution)/shard_map/ppermute | solution.py:28
  9.9 4.8 %collective-permute-start.3 = (bf16[2,112,128]{2,1,0:T(8,128)(2,1)S(1)}, bf16[2,112,128]{2,1,0:T(8,128)(2,1)S(1)}, u32[]{:S(2)}, u32[]{:S(2)}) collective-permute-start(bf16[2,112,128]{2,1,0:T(8,128)(2,1)S(1)} %get-tuple-element.30), channel_id=1, source_target_pairs={{64,0},{0,64},{192,128},{128,192},{65,1},{1,65},{193,129},{129,193... | collective-permute-start | bytes 172040 | tf_op jit(solution)/shard_map/ppermute | solution.py:28
  14.8 7.8 %collective-permute-start.4 = (bf16[2,112,128]{2,1,0:T(8,128)(2,1)S(1)}, bf16[2,112,128]{2,1,0:T(8,128)(2,1)S(1)}, u32[]{:S(2)}, u32[]{:S(2)}) collective-permute-start(bf16[2,112,128]{2,1,0:T(8,128)(2,1)S(1)} %fusion), channel_id=1, source_target_pairs={{32,0},{0,32},{33,1},{1,33},{34,2},{2,34},{35,3},{3,35},{36,4},{4,... | collective-permute-start | bytes 172040 | tf_op jit(solution)/shard_map/ppermute | solution.py:28
  22.6 4.9 %collective-permute-start.8 = (bf16[2,112,128]{2,1,0:T(8,128)(2,1)S(1)}, bf16[2,112,128]{2,1,0:T(8,128)(2,1)S(1)}, u32[]{:S(2)}, u32[]{:S(2)}) collective-permute-start(bf16[2,112,128]{2,1,0:T(8,128)(2,1)S(1)} %add_convert_fusion), channel_id=1, source_target_pairs={{12,0},{8,4},{4,8},{0,12},{13,1},{9,5},{5,9},{1,13},{14,2},{10,6},... | collective-permute-start | bytes 172040 | tf_op jit(solution)/shard_map/ppermute | solution.py:28
  25.5 3.0 %collective-permute-start.6 = (bf16[2,112,128]{2,1,0:T(8,128)(2,1)S(1)}, bf16[2,112,128]{2,1,0:T(8,128)(2,1)S(1)}, u32[]{:S(2)}, u32[]{:S(2)}) collective-permute-start(bf16[2,112,128]{2,1,0:T(8,128)(2,1)S(1)} %add_convert_fusion), channel_id=1, source_target_pairs={{4,0},{0,4},{12,8},{8,12},{5,1},{1,5},{13,9},{9,13},{6,2},{2,6},{1... | collective-permute-start | bytes 172040 | tf_op jit(solution)/shard_map/ppermute | solution.py:28
  25.5 4.1 %collective-permute-start.7 = (bf16[2,112,128]{2,1,0:T(8,128)(2,1)S(1)}, bf16[2,112,128]{2,1,0:T(8,128)(2,1)S(1)}, u32[]{:S(2)}, u32[]{:S(2)}) collective-permute-start(bf16[2,112,128]{2,1,0:T(8,128)(2,1)S(1)} %add_convert_fusion), channel_id=1, source_target_pairs={{8,0},{12,4},{0,8},{4,12},{9,1},{13,5},{1,9},{5,13},{10,2},{14,6},... | collective-permute-start | bytes 172040 | tf_op jit(solution)/shard_map/ppermute | solution.py:28
  29.7 8.2 %collective-permute-start.9 = (bf16[2,4,112,128]{3,2,1,0:T(8,128)(2,1)S(1)}, bf16[2,4,112,128]{3,2,1,0:T(8,128)(2,1)S(1)}, u32[]{:S(2)}, u32[]{:S(2)}) collective-permute-start(bf16[2,4,112,128]{3,2,1,0:T(8,128)(2,1)S(1)} %pad_maximum_fusion.own), channel_id=1, source_target_pairs={{64,0},{65,1},{66,2},{67,3},{68,4},{69,5},{70,6},{71,7},{72,8},{73... | collective-permute-start | bytes 688136 | tf_op jit(solution)/shard_map/ppermute | solution.py:37
  31.0 7.8 %collective-permute-start.10 = (bf16[2,4,112,128]{3,2,1,0:T(8,128)(2,1)S(1)}, bf16[2,4,112,128]{3,2,1,0:T(8,128)(2,1)S(1)}, u32[]{:S(2)}, u32[]{:S(2)}) collective-permute-start(bf16[2,4,112,128]{3,2,1,0:T(8,128)(2,1)S(1)} %pad_maximum_fusion.own), channel_id=1, source_target_pairs={{192,0},{193,1},{194,2},{195,3},{196,4},{197,5},{198,6},{199,7},{2... | collective-permute-start | bytes 688136 | tf_op jit(solution)/shard_map/ppermute | solution.py:37
  32.9 7.7 %collective-permute-start.11 = (bf16[2,4,112,128]{3,2,1,0:T(8,128)(2,1)S(1)}, bf16[2,4,112,128]{3,2,1,0:T(8,128)(2,1)S(1)}, u32[]{:S(2)}, u32[]{:S(2)}) collective-permute-start(bf16[2,4,112,128]{3,2,1,0:T(8,128)(2,1)S(1)} %pad_maximum_fusion.own), channel_id=1, source_target_pairs={{1,0},{0,1},{3,2},{2,3},{5,4},{4,5},{7,6},{6,7},{9,8},{8,9},{11,10... | collective-permute-start | bytes 688136 | tf_op jit(solution)/shard_map/ppermute | solution.py:37
  33.0 9.0 %collective-permute-start.15 = (bf16[2,4,112,128]{3,2,1,0:T(8,128)(2,1)S(1)}, bf16[2,4,112,128]{3,2,1,0:T(8,128)(2,1)S(1)}, u32[]{:S(2)}, u32[]{:S(2)}) collective-permute-start(bf16[2,4,112,128]{3,2,1,0:T(8,128)(2,1)S(1)} %pad_maximum_fusion.own), channel_id=1, source_target_pairs={{3,0},{2,1},{1,2},{0,3},{7,4},{6,5},{5,6},{4,7},{11,8},{10,9},{9,1... | collective-permute-start | bytes 688136 | tf_op jit(solution)/shard_map/ppermute | solution.py:37
  37.8 8.6 %collective-permute-start.13 = (bf16[2,4,112,128]{3,2,1,0:T(8,128)(2,1)S(1)}, bf16[2,4,112,128]{3,2,1,0:T(8,128)(2,1)S(1)}, u32[]{:S(2)}, u32[]{:S(2)}) collective-permute-start(bf16[2,4,112,128]{3,2,1,0:T(8,128)(2,1)S(1)} %collective-permute-done.9.near1), channel_id=1, source_target_pairs={{192,0},{193,1},{194,2},{195,3},{196,4},{197,5},{198,6},{199,7},{2... | collective-permute-start | bytes 688136 | tf_op jit(solution)/shard_map/ppermute | solution.py:37
  38.9 7.5 %collective-permute-start.17 = (bf16[2,4,112,128]{3,2,1,0:T(8,128)(2,1)S(1)}, bf16[2,4,112,128]{3,2,1,0:T(8,128)(2,1)S(1)}, u32[]{:S(2)}, u32[]{:S(2)}) collective-permute-start(bf16[2,4,112,128]{3,2,1,0:T(8,128)(2,1)S(1)} %collective-permute-done.9.near1), channel_id=1, source_target_pairs={{3,0},{2,1},{1,2},{0,3},{7,4},{6,5},{5,6},{4,7},{11,8},{10,9},{9,1... | collective-permute-start | bytes 688136 | tf_op jit(solution)/shard_map/ppermute | solution.py:37
  39.2 8.3 %collective-permute-start.21 = (bf16[2,4,112,128]{3,2,1,0:T(8,128)(2,1)S(1)}, bf16[2,4,112,128]{3,2,1,0:T(8,128)(2,1)S(1)}, u32[]{:S(2)}, u32[]{:S(2)}) collective-permute-start(bf16[2,4,112,128]{3,2,1,0:T(8,128)(2,1)S(1)} %collective-permute-done.9.near1), channel_id=1, source_target_pairs={{1,0},{0,1},{3,2},{2,3},{5,4},{4,5},{7,6},{6,7},{9,8},{8,9},{11,10... | collective-permute-start | bytes 688136 | tf_op jit(solution)/shard_map/ppermute | solution.py:37
  40.7 7.3 %collective-permute-start.12 = (bf16[2,4,112,128]{3,2,1,0:T(8,128)(2,1)S(1)}, bf16[2,4,112,128]{3,2,1,0:T(8,128)(2,1)S(1)}, u32[]{:S(2)}, u32[]{:S(2)}) collective-permute-start(bf16[2,4,112,128]{3,2,1,0:T(8,128)(2,1)S(1)} %collective-permute-done.10.near3), channel_id=1, source_target_pairs={{1,0},{0,1},{3,2},{2,3},{5,4},{4,5},{7,6},{6,7},{9,8},{8,9},{11,10... | collective-permute-start | bytes 688136 | tf_op jit(solution)/shard_map/ppermute | solution.py:37
  41.9 8.5 %collective-permute-start.19 = (bf16[2,4,112,128]{3,2,1,0:T(8,128)(2,1)S(1)}, bf16[2,4,112,128]{3,2,1,0:T(8,128)(2,1)S(1)}, u32[]{:S(2)}, u32[]{:S(2)}) collective-permute-start(bf16[2,4,112,128]{3,2,1,0:T(8,128)(2,1)S(1)} %collective-permute-done.10.near3), channel_id=1, source_target_pairs={{3,0},{2,1},{1,2},{0,3},{7,4},{6,5},{5,6},{4,7},{11,8},{10,9},{9,1... | collective-permute-start | bytes 688136 | tf_op jit(solution)/shard_map/ppermute | solution.py:37
  46.4 6.0 %collective-permute-start.14 = (bf16[2,4,112,128]{3,2,1,0:T(8,128)(2,1)S(1)}, bf16[2,4,112,128]{3,2,1,0:T(8,128)(2,1)S(1)}, u32[]{:S(2)}, u32[]{:S(2)}) collective-permute-start(bf16[2,4,112,128]{3,2,1,0:T(8,128)(2,1)S(1)} %collective-permute-done.13.far), channel_id=1, source_target_pairs={{1,0},{0,1},{3,2},{2,3},{5,4},{4,5},{7,6},{6,7},{9,8},{8,9},{11,10... | collective-permute-start | bytes 688136 | tf_op jit(solution)/shard_map/ppermute | solution.py:37
  46.4 8.9 %collective-permute-start.20 = (bf16[2,4,112,128]{3,2,1,0:T(8,128)(2,1)S(1)}, bf16[2,4,112,128]{3,2,1,0:T(8,128)(2,1)S(1)}, u32[]{:S(2)}, u32[]{:S(2)}) collective-permute-start(bf16[2,4,112,128]{3,2,1,0:T(8,128)(2,1)S(1)} %collective-permute-done.13.far), channel_id=1, source_target_pairs={{3,0},{2,1},{1,2},{0,3},{7,4},{6,5},{5,6},{4,7},{11,8},{10,9},{9,1... | collective-permute-start | bytes 688136 | tf_op jit(solution)/shard_map/ppermute | solution.py:37
  47.5 9.0 %collective-permute-start.18 = (bf16[2,4,112,128]{3,2,1,0:T(8,128)(2,1)S(1)}, bf16[2,4,112,128]{3,2,1,0:T(8,128)(2,1)S(1)}, u32[]{:S(2)}, u32[]{:S(2)}) collective-permute-start(bf16[2,4,112,128]{3,2,1,0:T(8,128)(2,1)S(1)} %collective-permute-done.17.near31), channel_id=1, source_target_pairs={{1,0},{0,1},{3,2},{2,3},{5,4},{4,5},{7,6},{6,7},{9,8},{8,9},{11,10... | collective-permute-start | bytes 688136 | tf_op jit(solution)/shard_map/ppermute | solution.py:37
  48.0 8.6 %collective-permute-start.16 = (bf16[2,4,112,128]{3,2,1,0:T(8,128)(2,1)S(1)}, bf16[2,4,112,128]{3,2,1,0:T(8,128)(2,1)S(1)}, u32[]{:S(2)}, u32[]{:S(2)}) collective-permute-start(bf16[2,4,112,128]{3,2,1,0:T(8,128)(2,1)S(1)} %collective-permute-done.15.own3), channel_id=1, source_target_pairs={{1,0},{0,1},{3,2},{2,3},{5,4},{4,5},{7,6},{6,7},{9,8},{8,9},{11,10... | collective-permute-start | bytes 688136 | tf_op jit(solution)/shard_map/ppermute | solution.py:37
  50.4 13.6 %collective-permute-start.22 = (bf16[2,4,112,128]{3,2,1,0:T(8,128)(2,1)S(1)}, bf16[2,4,112,128]{3,2,1,0:T(8,128)(2,1)S(1)}, u32[]{:S(2)}, u32[]{:S(2)}) collective-permute-start(bf16[2,4,112,128]{3,2,1,0:T(8,128)(2,1)S(1)} %collective-permute-done.12.near31), channel_id=1, source_target_pairs={{3,0},{2,1},{1,2},{0,3},{7,4},{6,5},{5,6},{4,7},{11,8},{10,9},{9,1... | collective-permute-start | bytes 688136 | tf_op jit(solution)/shard_map/ppermute | solution.py:37
  52.4 11.6 %collective-permute-start.23 = (bf16[2,4,112,128]{3,2,1,0:T(8,128)(2,1)S(1)}, bf16[2,4,112,128]{3,2,1,0:T(8,128)(2,1)S(1)}, u32[]{:S(2)}, u32[]{:S(2)}) collective-permute-start(bf16[2,4,112,128]{3,2,1,0:T(8,128)(2,1)S(1)} %collective-permute-done.14.far1), channel_id=1, source_target_pairs={{3,0},{2,1},{1,2},{0,3},{7,4},{6,5},{5,6},{4,7},{11,8},{10,9},{9,1... | collective-permute-start | bytes 688136 | tf_op jit(solution)/shard_map/ppermute | solution.py:37
  57.7 9.9 %collective-permute-start.24 = (bf16[512,384]{1,0:T(8,128)(2,1)S(1)}, bf16[512,384]{1,0:T(8,128)(2,1)S(1)}, u32[]{:S(2)}, u32[]{:S(2)}) collective-permute-start(bf16[512,384]{1,0:T(8,128)(2,1)S(1)} %get-tuple-element.44), channel_id=1, source_target_pairs={{16,0},{0,16},{17,1},{1,17},{18,2},{2,18},{19,3},{3,19},{20,4},{4,... | collective-permute-start | bytes 1179656 | tf_op jit(solution)/shard_map/ppermute | solution.py:24
  65.3 2.5 %collective-permute-start.25 = (bf16[512,384]{1,0:T(8,128)(2,1)S(1)}, bf16[512,384]{1,0:T(8,128)(2,1)S(1)}, u32[]{:S(2)}, u32[]{:S(2)}) collective-permute-start(bf16[512,384]{1,0:T(8,128)(2,1)S(1)} %shard_map.45), channel_id=1, source_target_pairs={{16,0},{0,16},{17,1},{1,17},{18,2},{2,18},{19,3},{3,19},{20,4},{4,... | collective-permute-start | bytes 1179656 | tf_op jit(solution)/shard_map/ppermute | solution.py:24

commit v16 on v13

--- a/solution.py
+++ b/solution.py
@@ -217,11 +217,10 @@
     near1, near3 = turn(own, 0, 1), turn(own, 0, 3)
     total = jax.ShapeDtypeStruct((512, 768), F32)
     start = call(product_one, jax.ShapeDtypeStruct((256, 768), F32), (place, own, both))
-    near1, start = lax.optimization_barrier((near1, start))
     far = turn(near1, 0, 3)
     one_own, three_own = turn(own, 1, 1), turn(own, 1, 3)
+    near1, near3, start = lax.optimization_barrier((near1, near3, start))
     one_near1, three_near1 = turn(near1, 1, 1), turn(near1, 1, 3)
-    near3, one_own = lax.optimization_barrier((near3, one_own))
     one_near3, three_near3 = turn(near3, 1, 1), turn(near3, 1, 3)
     one_far, three_far = turn(far, 1, 1), turn(far, 1, 3)
     far_own, far_near1 = turn(three_own, 1, 1), turn(three_near1, 1, 1)

time: 70.7 us -> 70.4 us (level)
  transfers between devices with their start and end apart: 26 -> 26, of which waited for: 12 -> 14; matrix products, arithmetic and copies ran while one was open for 0% -> 0% of each run, Pallas kernels for 15% -> 15%
where the time goes in v16:
time: 70.4 us; the launch traced here: 70.2 us
  starting transfers between devices  44.6 us (63%)
  Pallas kernels  12.1 us (17%)
  waiting for transfers between devices  11.3 us (16%)
  local copies, waits for them, and re-layouts  1.77 us (3%)
    ppermute x15, starting transfers between devices, turn(): return lax.ppermute(block, ROW + COL, pairs)  20 us
    ppermute x7, starting transfers between devices, swap(): return lax.ppermute(block, axis, [(i ^ bits, i) for i in range(size)])  13.2 us
    pallas_call x10, Pallas kernels, call(): pl.pallas_call(kernel, out_shape=out_shape, in_specs=specs or [SMEM] + [V...  12.1 us
    ppermute x4, starting transfers between devices, fetch(): lax.ppermute(block, axis, [((i + ahead) % size, i) for i in range(size)])  11.3 us
    ppermute x7, waiting for transfers between devices, swap(): return lax.ppermute(block, axis, [(i ^ bits, i) for i in range(size)])  6.97 us
    ppermute x15, waiting for transfers between devices, turn(): return lax.ppermute(block, ROW + COL, pairs)  2.53 us
    ppermute x4, waiting for transfers between devices, fetch(): lax.ppermute(block, axis, [((i + ahead) % size, i) for i in range(size)])  1.83 us
    unnamed x6, local copies, waits for them, and re-layouts  1.77 us
  transfers between devices with their start and end apart: 26, of which 14 were waited for; matrix products, arithmetic and copies ran while one was open for 0% of the time, Pallas kernels for 15%

profile of v16, /device:TPU:1, one launch (start us, length us, event | category | flops | bytes accessed | tf_op | source)
XLA Modules:
  0.0 70.2 jit_solution(10100352121466063932)
XLA Ops:
  0.0 3.2 %collective-permute-start.5 = (bf16[1792,384]{1,0:T(8,128)(2,1)}, bf16[1792,384]{1,0:T(8,128)(2,1)S(1)}, u32[]{:S(2)}, u32[]{:S(2)}) collective-permute-start(bf16[1792,384]{1,0:T(8,128)(2,1)} %own.1), channel_id=1, source_target_pairs={{16,0},{0,16},{17,1},{1,17},{18,2},{2,18},{19,3},{3,19},{20,4},{4,... | collective-permute-start | bytes 4128776 | tf_op jit(solution)/shard_map/ppermute | solution.py:24
  3.3 1.0 %copy-done.1 = bf16[112,2048]{1,0:T(8,128)(2,1)S(1)} copy-done((bf16[112,2048]{1,0:T(8,128)(2,1)S(1)}, bf16[112,2048]{1,0:T(8,128)(2,1)}, u32[]{:S(2)}) %copy-start.1) | copy-done | bytes 458776
  5.1 1.0 %shard_map.37 = (f32[8,112,128]{2,1,0:T(8,128)S(1)}, f32[8,112,128]{2,1,0:T(8,128)S(1)}) custom-call(s32[4]{0:T(128)S(1)} %pad_add_fusion.place, bf16[112,112]{1,0:T(8,128)(2,1)S(1)} %copy-done.2, bf16[112,2048]{1,0:T(8,128)(2,1)S(1)} %copy-done.1), custom_call_target="tpu_custom_call" | custom-call | tf_op jit(solution)/shard_map/pallas_call | solution.py:180
  6.2 1.7 %collective-permute-done.received = f32[8,112,128]{2,1,0:T(8,128)S(1)} collective-permute-done((f32[8,112,128]{2,1,0:T(8,128)S(1)}, f32[8,112,128]{2,1,0:T(8,128)S(1)}, u32[]{:S(2)}, u32[]{:S(2)}) %collective-permute-start) | collective-permute-done | bytes 458784 | tf_op jit(solution)/shard_map/ppermute | solution.py:24
  9.9 2.0 %collective-permute-start.3 = (bf16[2,112,128]{2,1,0:T(8,128)(2,1)S(1)}, bf16[2,112,128]{2,1,0:T(8,128)(2,1)S(1)}, u32[]{:S(2)}, u32[]{:S(2)}) collective-permute-start(bf16[2,112,128]{2,1,0:T(8,128)(2,1)S(1)} %get-tuple-element.27), channel_id=1, source_target_pairs={{64,0},{0,64},{192,128},{128,192},{65,1},{1,65},{193,129},{129,193... | collective-permute-start | bytes 172040 | tf_op jit(solution)/shard_map/ppermute | solution.py:28
  11.9 1.0 %collective-permute-done.1 = bf16[2,112,128]{2,1,0:T(8,128)(2,1)S(1)} collective-permute-done((bf16[2,112,128]{2,1,0:T(8,128)(2,1)S(1)}, bf16[2,112,128]{2,1,0:T(8,128)(2,1)S(1)}, u32[]{:S(2)}, u32[]{:S(2)}) %collective-permute-start.1) | collective-permute-done | bytes 57376 | tf_op jit(solution)/shard_map/ppermute | solution.py:28
  12.9 1.1 %collective-permute-done.2 = bf16[2,112,128]{2,1,0:T(8,128)(2,1)S(1)} collective-permute-done((bf16[2,112,128]{2,1,0:T(8,128)(2,1)S(1)}, bf16[2,112,128]{2,1,0:T(8,128)(2,1)S(1)}, u32[]{:S(2)}, u32[]{:S(2)}) %collective-permute-start.2) | collective-permute-done | bytes 57376 | tf_op jit(solution)/shard_map/ppermute | solution.py:28
  14.8 6.2 %collective-permute-start.4 = (bf16[2,112,128]{2,1,0:T(8,128)(2,1)S(1)}, bf16[2,112,128]{2,1,0:T(8,128)(2,1)S(1)}, u32[]{:S(2)}, u32[]{:S(2)}) collective-permute-start(bf16[2,112,128]{2,1,0:T(8,128)(2,1)S(1)} %fusion), channel_id=1, source_target_pairs={{32,0},{0,32},{33,1},{1,33},{34,2},{2,34},{35,3},{3,35},{36,4},{4,... | collective-permute-start | bytes 172040 | tf_op jit(solution)/shard_map/ppermute | solution.py:28
  22.6 2.9 %collective-permute-start.8 = (bf16[2,112,128]{2,1,0:T(8,128)(2,1)S(1)}, bf16[2,112,128]{2,1,0:T(8,128)(2,1)S(1)}, u32[]{:S(2)}, u32[]{:S(2)}) collective-permute-start(bf16[2,112,128]{2,1,0:T(8,128)(2,1)S(1)} %add_convert_fusion), channel_id=1, source_target_pairs={{12,0},{8,4},{4,8},{0,12},{13,1},{9,5},{5,9},{1,13},{14,2},{10,6},... | collective-permute-start | bytes 172040 | tf_op jit(solution)/shard_map/ppermute | solution.py:28
  26.2 1.3 %collective-permute-done.8 = bf16[2,112,128]{2,1,0:T(8,128)(2,1)S(1)} collective-permute-done((bf16[2,112,128]{2,1,0:T(8,128)(2,1)S(1)}, bf16[2,112,128]{2,1,0:T(8,128)(2,1)S(1)}, u32[]{:S(2)}, u32[]{:S(2)}) %collective-permute-start.8) | collective-permute-done | bytes 57376 | tf_op jit(solution)/shard_map/ppermute | solution.py:28
  27.5 1.0 %collective-permute-done.6 = bf16[2,112,128]{2,1,0:T(8,128)(2,1)S(1)} collective-permute-done((bf16[2,112,128]{2,1,0:T(8,128)(2,1)S(1)}, bf16[2,112,128]{2,1,0:T(8,128)(2,1)S(1)}, u32[]{:S(2)}, u32[]{:S(2)}) %collective-permute-start.6) | collective-permute-done | bytes 57376 | tf_op jit(solution)/shard_map/ppermute | solution.py:28
  28.6 1.0 %collective-permute-done.7 = bf16[2,112,128]{2,1,0:T(8,128)(2,1)S(1)} collective-permute-done((bf16[2,112,128]{2,1,0:T(8,128)(2,1)S(1)}, bf16[2,112,128]{2,1,0:T(8,128)(2,1)S(1)}, u32[]{:S(2)}, u32[]{:S(2)}) %collective-permute-start.7) | collective-permute-done | bytes 57376 | tf_op jit(solution)/shard_map/ppermute | solution.py:28
  29.7 1.4 %collective-permute-start.9 = (bf16[2,4,112,128]{3,2,1,0:T(8,128)(2,1)S(1)}, bf16[2,4,112,128]{3,2,1,0:T(8,128)(2,1)S(1)}, u32[]{:S(2)}, u32[]{:S(2)}) collective-permute-start(bf16[2,4,112,128]{3,2,1,0:T(8,128)(2,1)S(1)} %pad_maximum_fusion.own), channel_id=1, source_target_pairs={{64,0},{65,1},{66,2},{67,3},{68,4},{69,5},{70,6},{71,7},{72,8},{73... | collective-permute-start | bytes 688136 | tf_op jit(solution)/shard_map/ppermute | solution.py:37
  31.0 1.9 %collective-permute-start.10 = (bf16[2,4,112,128]{3,2,1,0:T(8,128)(2,1)S(1)}, bf16[2,4,112,128]{3,2,1,0:T(8,128)(2,1)S(1)}, u32[]{:S(2)}, u32[]{:S(2)}) collective-permute-start(bf16[2,4,112,128]{3,2,1,0:T(8,128)(2,1)S(1)} %pad_maximum_fusion.own), channel_id=1, source_target_pairs={{192,0},{193,1},{194,2},{195,3},{196,4},{197,5},{198,6},{199,7},{2... | collective-permute-start | bytes 688136 | tf_op jit(solution)/shard_map/ppermute | solution.py:37
  32.9 1.9 %collective-permute-start.14 = (bf16[2,4,112,128]{3,2,1,0:T(8,128)(2,1)S(1)}, bf16[2,4,112,128]{3,2,1,0:T(8,128)(2,1)S(1)}, u32[]{:S(2)}, u32[]{:S(2)}) collective-permute-start(bf16[2,4,112,128]{3,2,1,0:T(8,128)(2,1)S(1)} %pad_maximum_fusion.own), channel_id=1, source_target_pairs={{3,0},{2,1},{1,2},{0,3},{7,4},{6,5},{5,6},{4,7},{11,8},{10,9},{9,1... | collective-permute-start | bytes 688136 | tf_op jit(solution)/shard_map/ppermute | solution.py:37
  34.8 1.5 %collective-permute-start.20 = (bf16[2,4,112,128]{3,2,1,0:T(8,128)(2,1)S(1)}, bf16[2,4,112,128]{3,2,1,0:T(8,128)(2,1)S(1)}, u32[]{:S(2)}, u32[]{:S(2)}) collective-permute-start(bf16[2,4,112,128]{3,2,1,0:T(8,128)(2,1)S(1)} %pad_maximum_fusion.own), channel_id=1, source_target_pairs={{1,0},{0,1},{3,2},{2,3},{5,4},{4,5},{7,6},{6,7},{9,8},{8,9},{11,10... | collective-permute-start | bytes 688136 | tf_op jit(solution)/shard_map/ppermute | solution.py:37
  36.3 1.1 %collective-permute-start.12 = (bf16[2,4,112,128]{3,2,1,0:T(8,128)(2,1)S(1)}, bf16[2,4,112,128]{3,2,1,0:T(8,128)(2,1)S(1)}, u32[]{:S(2)}, u32[]{:S(2)}) collective-permute-start(bf16[2,4,112,128]{3,2,1,0:T(8,128)(2,1)S(1)} %collective-permute-done.9.near1), channel_id=1, source_target_pairs={{192,0},{193,1},{194,2},{195,3},{196,4},{197,5},{198,6},{199,7},{2... | collective-permute-start | bytes 688136 | tf_op jit(solution)/shard_map/ppermute | solution.py:37
  38.3 1.9 %collective-permute-start.16 = (bf16[2,4,112,128]{3,2,1,0:T(8,128)(2,1)S(1)}, bf16[2,4,112,128]{3,2,1,0:T(8,128)(2,1)S(1)}, u32[]{:S(2)}, u32[]{:S(2)}) collective-permute-start(bf16[2,4,112,128]{3,2,1,0:T(8,128)(2,1)S(1)} %collective-permute-done.9.near1), channel_id=1, source_target_pairs={{3,0},{2,1},{1,2},{0,3},{7,4},{6,5},{5,6},{4,7},{11,8},{10,9},{9,1... | collective-permute-start | bytes 688136 | tf_op jit(solution)/shard_map/ppermute | solution.py:37
  40.3 1.5 %collective-permute-start.21 = (bf16[2,4,112,128]{3,2,1,0:T(8,128)(2,1)S(1)}, bf16[2,4,112,128]{3,2,1,0:T(8,128)(2,1)S(1)}, u32[]{:S(2)}, u32[]{:S(2)}) collective-permute-start(bf16[2,4,112,128]{3,2,1,0:T(8,128)(2,1)S(1)} %collective-permute-done.9.near1), channel_id=1, source_target_pairs={{1,0},{0,1},{3,2},{2,3},{5,4},{4,5},{7,6},{6,7},{9,8},{8,9},{11,10... | collective-permute-start | bytes 688136 | tf_op jit(solution)/shard_map/ppermute | solution.py:37
  42.1 2.1 %collective-permute-start.18 = (bf16[2,4,112,128]{3,2,1,0:T(8,128)(2,1)S(1)}, bf16[2,4,112,128]{3,2,1,0:T(8,128)(2,1)S(1)}, u32[]{:S(2)}, u32[]{:S(2)}) collective-permute-start(bf16[2,4,112,128]{3,2,1,0:T(8,128)(2,1)S(1)} %collective-permute-done.10.near3), channel_id=1, source_target_pairs={{3,0},{2,1},{1,2},{0,3},{7,4},{6,5},{5,6},{4,7},{11,8},{10,9},{9,1... | collective-permute-start | bytes 688136 | tf_op jit(solution)/shard_map/ppermute | solution.py:37
  44.8 2.4 %collective-permute-start.19 = (bf16[2,4,112,128]{3,2,1,0:T(8,128)(2,1)S(1)}, bf16[2,4,112,128]{3,2,1,0:T(8,128)(2,1)S(1)}, u32[]{:S(2)}, u32[]{:S(2)}) collective-permute-start(bf16[2,4,112,128]{3,2,1,0:T(8,128)(2,1)S(1)} %collective-permute-done.12.far), channel_id=1, source_target_pairs={{3,0},{2,1},{1,2},{0,3},{7,4},{6,5},{5,6},{4,7},{11,8},{10,9},{9,1... | collective-permute-start | bytes 688136 | tf_op jit(solution)/shard_map/ppermute | solution.py:37
  47.9 1.5 %collective-permute-start.15 = (bf16[2,4,112,128]{3,2,1,0:T(8,128)(2,1)S(1)}, bf16[2,4,112,128]{3,2,1,0:T(8,128)(2,1)S(1)}, u32[]{:S(2)}, u32[]{:S(2)}) collective-permute-start(bf16[2,4,112,128]{3,2,1,0:T(8,128)(2,1)S(1)} %collective-permute-done.14.own3), channel_id=1, source_target_pairs={{1,0},{0,1},{3,2},{2,3},{5,4},{4,5},{7,6},{6,7},{9,8},{8,9},{11,10... | collective-permute-start | bytes 688136 | tf_op jit(solution)/shard_map/ppermute | solution.py:37
  49.3 1.2 %collective-permute-done.18.near33 = bf16[2,4,112,128]{3,2,1,0:T(8,128)(2,1)S(1)} collective-permute-done((bf16[2,4,112,128]{3,2,1,0:T(8,128)(2,1)S(1)}, bf16[2,4,112,128]{3,2,1,0:T(8,128)(2,1)S(1)}, u32[]{:S(2)}, u32[]{:S(2)}) %collective-permute-start.18) | collective-permute-done | bytes 229408 | tf_op jit(solution)/shard_map/ppermute | solution.py:37
  50.5 1.9 %collective-permute-start.22 = (bf16[2,4,112,128]{3,2,1,0:T(8,128)(2,1)S(1)}, bf16[2,4,112,128]{3,2,1,0:T(8,128)(2,1)S(1)}, u32[]{:S(2)}, u32[]{:S(2)}) collective-permute-start(bf16[2,4,112,128]{3,2,1,0:T(8,128)(2,1)S(1)} %collective-permute-done.11.near31), channel_id=1, source_target_pairs={{3,0},{2,1},{1,2},{0,3},{7,4},{6,5},{5,6},{4,7},{11,8},{10,9},{9,1... | collective-permute-start | bytes 688136 | tf_op jit(solution)/shard_map/ppermute | solution.py:37
  53.2 2.2 %shard_map.41 = (f32[512,768]{1,0:T(8,128)S(1)}, f32[512,768]{1,0:T(8,128)S(1)}) custom-call(s32[4]{0:T(128)S(1)} %pad_add_fusion.place, bf16[2,4,112,128]{3,2,1,0:T(8,128)(2,1)S(1)} %collective-permute-done.9.near1, bf16[2,4,112,128]{3,2,1,0:T(8,128)(2,1)S(1)} %collective-permute-done.10.near3, bf16[2,4,112,128]{3,2,1,0:T(8,128)(2,1)S(1)} %collective-permute-done.12.far, ...), custom_call_target="tpu_custom_call" | custom-call | tf_op jit(solution)/shard_map/pallas_call | solution.py:180
  55.4 1.2 %shard_map.42.high = f32[512,768]{1,0:T(8,128)S(1)} custom-call(s32[4]{0:T(128)S(1)} %pad_add_fusion.place, bf16[2,4,112,128]{3,2,1,0:T(8,128)(2,1)S(1)} %collective-permute-done.11.near31, bf16[2,4,112,128]{3,2,1,0:T(8,128)(2,1)S(1)} %collective-permute-done.13.far1, bf16[2,4,112,128]{3,2,1,0:T(8,128)(2,1)S(1)} %collective-permute-done.18.near33, ...), custom_call_target="tpu_custom_call" | custom-call | tf_op jit(solution)/shard_map/pallas_call | solution.py:180
  56.6 1.2 %shard_map.43 = (bf16[512,384]{1,0:T(8,128)(2,1)S(1)}, bf16[512,384]{1,0:T(8,128)(2,1)S(1)}) custom-call(s32[4]{0:T(128)S(1)} %pad_add_fusion.place, bf16[2,4,112,128]{3,2,1,0:T(8,128)(2,1)S(1)} %collective-permute-done.11.near31, bf16[2,4,112,128]{3,2,1,0:T(8,128)(2,1)S(1)} %collective-permute-done.13.far1, ...), custom_call_target="tpu_custom_call" | custom-call | tf_op jit(solution)/shard_map/pallas_call | solution.py:180
  57.8 6.8 %collective-permute-start.24 = (bf16[512,384]{1,0:T(8,128)(2,1)S(1)}, bf16[512,384]{1,0:T(8,128)(2,1)S(1)}, u32[]{:S(2)}, u32[]{:S(2)}) collective-permute-start(bf16[512,384]{1,0:T(8,128)(2,1)S(1)} %get-tuple-element.38), channel_id=1, source_target_pairs={{16,0},{0,16},{17,1},{1,17},{18,2},{2,18},{19,3},{3,19},{20,4},{4,... | collective-permute-start | bytes 1179656 | tf_op jit(solution)/shard_map/ppermute | solution.py:24
  64.7 1.2 %shard_map.45 = bf16[512,384]{1,0:T(8,128)(2,1)S(1)} custom-call(s32[4]{0:T(128)S(1)} %pad_add_fusion.place, bf16[2,4,112,128]{3,2,1,0:T(8,128)(2,1)S(1)} %collective-permute-done.15.own, bf16[2,4,112,128]{3,2,1,0:T(8,128)(2,1)S(1)} %collective-permute-done.17.near1, bf16[2,4,112,128]{3,2,1,0:T(8,128)(2,1)S(1)} %collective-permute-done.22.near3, ...), custom_call_target="tpu_custom_call" | custom-call | tf_op jit(solution)/shard_map/pallas_call | solution.py:180
  65.9 1.1 %collective-permute-start.25 = (bf16[512,384]{1,0:T(8,128)(2,1)S(1)}, bf16[512,384]{1,0:T(8,128)(2,1)S(1)}, u32[]{:S(2)}, u32[]{:S(2)}) collective-permute-start(bf16[512,384]{1,0:T(8,128)(2,1)S(1)} %shard_map.45), channel_id=1, source_target_pairs={{16,0},{0,16},{17,1},{1,17},{18,2},{2,18},{19,3},{3,19},{20,4},{4,... | collective-permute-start | bytes 1179656 | tf_op jit(solution)/shard_map/ppermute | solution.py:24
  67.0 1.2 %shard_map.44.mine2 = bf16[512,384]{1,0:T(8,128)(2,1)S(1)} custom-call(s32[4]{0:T(128)S(1)} %pad_add_fusion.place, bf16[2,4,112,128]{3,2,1,0:T(8,128)(2,1)S(1)} %collective-permute-done.15.own, bf16[2,4,112,128]{3,2,1,0:T(8,128)(2,1)S(1)} %collective-permute-done.17.near1, bf16[2,4,112,128]{3,2,1,0:T(8,128)(2,1)S(1)} %collective-permute-done.22.near3, ...), custom_call_target="tpu_custom_call" | custom-call | tf_op jit(solution)/shard_map/pallas_call | solution.py:180
  68.3 1.7 %shard_map.46 = bf16[2048,384]{1,0:T(8,128)(2,1)} custom-call(s32[4]{0:T(128)S(1)} %pad_add_fusion.place, bf16[512,384]{1,0:T(8,128)(2,1)S(1)} %get-tuple-element.36.mine1, bf16[512,384]{1,0:T(8,128)(2,1)S(1)} %shard_map.44.mine2, bf16[512,384]{1,0:T(8,128)(2,1)S(1)} %collective-permute-done.24.theirs1, bf16[512,384]{1,0:T(8,128)(2,1)S(1)} %collective-permute-done.25.theirs2), custom_call_target="tpu_custom_call" | custom-call | tf_op jit(solution)/shard_map/pallas_call | solution.py:180
  (40 shorter events, 9.6 us)
Async XLA Ops:
  0.0 21.0 %copy-start = (bf16[1792,384]{1,0:T(8,128)(2,1)S(1)}, bf16[1792,384]{1,0:T(8,128)(2,1)}, u32[]{:S(2)}) copy-start(bf16[1792,384]{1,0:T(8,128)(2,1)} %own.1) | copy-start | bytes 4128772
  0.0 21.0 %collective-permute-start.5 = (bf16[1792,384]{1,0:T(8,128)(2,1)}, bf16[1792,384]{1,0:T(8,128)(2,1)S(1)}, u32[]{:S(2)}, u32[]{:S(2)}) collective-permute-start(bf16[1792,384]{1,0:T(8,128)(2,1)} %own.1), channel_id=1, source_target_pairs={{16,0},{0,16},{17,1},{1,17},{18,2},{2,18},{19,3},{3,19},{20,4},{4,... | collective-permute-start | bytes 4128776 | tf_op jit(solution)/shard_map/ppermute | solution.py:24
  3.3 1.0 %copy-start.1 = (bf16[112,2048]{1,0:T(8,128)(2,1)S(1)}, bf16[112,2048]{1,0:T(8,128)(2,1)}, u32[]{:S(2)}) copy-start(bf16[112,2048]{1,0:T(8,128)(2,1)} %panel.1) | copy-start | bytes 1376260
  4.3 0.7 %copy-start.2 = (bf16[112,112]{1,0:T(8,128)(2,1)S(1)}, bf16[112,112]{1,0:T(8,128)(2,1)}, u32[]{:S(2)}) copy-start(bf16[112,112]{1,0:T(8,128)(2,1)} %screening.1) | copy-start | bytes 75268
  6.1 1.9 %collective-permute-start = (f32[8,112,128]{2,1,0:T(8,128)S(1)}, f32[8,112,128]{2,1,0:T(8,128)S(1)}, u32[]{:S(2)}, u32[]{:S(2)}) collective-permute-start(f32[8,112,128]{2,1,0:T(8,128)S(1)} %get-tuple-element.23), channel_id=1, source_target_pairs={{16,0},{0,16},{17,1},{1,17},{18,2},{2,18},{19,3},{3,19},{20,4},{4,... | collective-permute-start | bytes 1376264 | tf_op jit(solution)/shard_map/ppermute | solution.py:24
  8.6 4.3 %collective-permute-start.1 = (bf16[2,112,128]{2,1,0:T(8,128)(2,1)S(1)}, bf16[2,112,128]{2,1,0:T(8,128)(2,1)S(1)}, u32[]{:S(2)}, u32[]{:S(2)}) collective-permute-start(bf16[2,112,128]{2,1,0:T(8,128)(2,1)S(1)} %get-tuple-element.25), channel_id=1, source_target_pairs={{192,0},{128,64},{64,128},{0,192},{193,1},{129,65},{65,129},{1,193... | collective-permute-start | bytes 172040 | tf_op jit(solution)/shard_map/ppermute | solution.py:28
  9.4 4.6 %collective-permute-start.2 = (bf16[2,112,128]{2,1,0:T(8,128)(2,1)S(1)}, bf16[2,112,128]{2,1,0:T(8,128)(2,1)S(1)}, u32[]{:S(2)}, u32[]{:S(2)}) collective-permute-start(bf16[2,112,128]{2,1,0:T(8,128)(2,1)S(1)} %get-tuple-element.26), channel_id=1, source_target_pairs={{128,0},{192,64},{0,128},{64,192},{129,1},{193,65},{1,129},{65,193... | collective-permute-start | bytes 172040 | tf_op jit(solution)/shard_map/ppermute | solution.py:28
  9.9 4.8 %collective-permute-start.3 = (bf16[2,112,128]{2,1,0:T(8,128)(2,1)S(1)}, bf16[2,112,128]{2,1,0:T(8,128)(2,1)S(1)}, u32[]{:S(2)}, u32[]{:S(2)}) collective-permute-start(bf16[2,112,128]{2,1,0:T(8,128)(2,1)S(1)} %get-tuple-element.27), channel_id=1, source_target_pairs={{64,0},{0,64},{192,128},{128,192},{65,1},{1,65},{193,129},{129,193... | collective-permute-start | bytes 172040 | tf_op jit(solution)/shard_map/ppermute | solution.py:28
  14.8 7.8 %collective-permute-start.4 = (bf16[2,112,128]{2,1,0:T(8,128)(2,1)S(1)}, bf16[2,112,128]{2,1,0:T(8,128)(2,1)S(1)}, u32[]{:S(2)}, u32[]{:S(2)}) collective-permute-start(bf16[2,112,128]{2,1,0:T(8,128)(2,1)S(1)} %fusion), channel_id=1, source_target_pairs={{32,0},{0,32},{33,1},{1,33},{34,2},{2,34},{35,3},{3,35},{36,4},{4,... | collective-permute-start | bytes 172040 | tf_op jit(solution)/shard_map/ppermute | solution.py:28
  22.6 4.9 %collective-permute-start.8 = (bf16[2,112,128]{2,1,0:T(8,128)(2,1)S(1)}, bf16[2,112,128]{2,1,0:T(8,128)(2,1)S(1)}, u32[]{:S(2)}, u32[]{:S(2)}) collective-permute-start(bf16[2,112,128]{2,1,0:T(8,128)(2,1)S(1)} %add_convert_fusion), channel_id=1, source_target_pairs={{12,0},{8,4},{4,8},{0,12},{13,1},{9,5},{5,9},{1,13},{14,2},{10,6},... | collective-permute-start | bytes 172040 | tf_op jit(solution)/shard_map/ppermute | solution.py:28
  25.5 3.0 %collective-permute-start.6 = (bf16[2,112,128]{2,1,0:T(8,128)(2,1)S(1)}, bf16[2,112,128]{2,1,0:T(8,128)(2,1)S(1)}, u32[]{:S(2)}, u32[]{:S(2)}) collective-permute-start(bf16[2,112,128]{2,1,0:T(8,128)(2,1)S(1)} %add_convert_fusion), channel_id=1, source_target_pairs={{4,0},{0,4},{12,8},{8,12},{5,1},{1,5},{13,9},{9,13},{6,2},{2,6},{1... | collective-permute-start | bytes 172040 | tf_op jit(solution)/shard_map/ppermute | solution.py:28
  25.5 4.1 %collective-permute-start.7 = (bf16[2,112,128]{2,1,0:T(8,128)(2,1)S(1)}, bf16[2,112,128]{2,1,0:T(8,128)(2,1)S(1)}, u32[]{:S(2)}, u32[]{:S(2)}) collective-permute-start(bf16[2,112,128]{2,1,0:T(8,128)(2,1)S(1)} %add_convert_fusion), channel_id=1, source_target_pairs={{8,0},{12,4},{0,8},{4,12},{9,1},{13,5},{1,9},{5,13},{10,2},{14,6},... | collective-permute-start | bytes 172040 | tf_op jit(solution)/shard_map/ppermute | solution.py:28
  29.7 6.6 %collective-permute-start.9 = (bf16[2,4,112,128]{3,2,1,0:T(8,128)(2,1)S(1)}, bf16[2,4,112,128]{3,2,1,0:T(8,128)(2,1)S(1)}, u32[]{:S(2)}, u32[]{:S(2)}) collective-permute-start(bf16[2,4,112,128]{3,2,1,0:T(8,128)(2,1)S(1)} %pad_maximum_fusion.own), channel_id=1, source_target_pairs={{64,0},{65,1},{66,2},{67,3},{68,4},{69,5},{70,6},{71,7},{72,8},{73... | collective-permute-start | bytes 688136 | tf_op jit(solution)/shard_map/ppermute | solution.py:37
  31.0 7.3 %collective-permute-start.10 = (bf16[2,4,112,128]{3,2,1,0:T(8,128)(2,1)S(1)}, bf16[2,4,112,128]{3,2,1,0:T(8,128)(2,1)S(1)}, u32[]{:S(2)}, u32[]{:S(2)}) collective-permute-start(bf16[2,4,112,128]{3,2,1,0:T(8,128)(2,1)S(1)} %pad_maximum_fusion.own), channel_id=1, source_target_pairs={{192,0},{193,1},{194,2},{195,3},{196,4},{197,5},{198,6},{199,7},{2... | collective-permute-start | bytes 688136 | tf_op jit(solution)/shard_map/ppermute | solution.py:37
  32.9 8.8 %collective-permute-start.14 = (bf16[2,4,112,128]{3,2,1,0:T(8,128)(2,1)S(1)}, bf16[2,4,112,128]{3,2,1,0:T(8,128)(2,1)S(1)}, u32[]{:S(2)}, u32[]{:S(2)}) collective-permute-start(bf16[2,4,112,128]{3,2,1,0:T(8,128)(2,1)S(1)} %pad_maximum_fusion.own), channel_id=1, source_target_pairs={{3,0},{2,1},{1,2},{0,3},{7,4},{6,5},{5,6},{4,7},{11,8},{10,9},{9,1... | collective-permute-start | bytes 688136 | tf_op jit(solution)/shard_map/ppermute | solution.py:37
  34.8 7.3 %collective-permute-start.20 = (bf16[2,4,112,128]{3,2,1,0:T(8,128)(2,1)S(1)}, bf16[2,4,112,128]{3,2,1,0:T(8,128)(2,1)S(1)}, u32[]{:S(2)}, u32[]{:S(2)}) collective-permute-start(bf16[2,4,112,128]{3,2,1,0:T(8,128)(2,1)S(1)} %pad_maximum_fusion.own), channel_id=1, source_target_pairs={{1,0},{0,1},{3,2},{2,3},{5,4},{4,5},{7,6},{6,7},{9,8},{8,9},{11,10... | collective-permute-start | bytes 688136 | tf_op jit(solution)/shard_map/ppermute | solution.py:37
  36.3 8.4 %collective-permute-start.12 = (bf16[2,4,112,128]{3,2,1,0:T(8,128)(2,1)S(1)}, bf16[2,4,112,128]{3,2,1,0:T(8,128)(2,1)S(1)}, u32[]{:S(2)}, u32[]{:S(2)}) collective-permute-start(bf16[2,4,112,128]{3,2,1,0:T(8,128)(2,1)S(1)} %collective-permute-done.9.near1), channel_id=1, source_target_pairs={{192,0},{193,1},{194,2},{195,3},{196,4},{197,5},{198,6},{199,7},{2... | collective-permute-start | bytes 688136 | tf_op jit(solution)/shard_map/ppermute | solution.py:37
  38.3 6.5 %collective-permute-start.16 = (bf16[2,4,112,128]{3,2,1,0:T(8,128)(2,1)S(1)}, bf16[2,4,112,128]{3,2,1,0:T(8,128)(2,1)S(1)}, u32[]{:S(2)}, u32[]{:S(2)}) collective-permute-start(bf16[2,4,112,128]{3,2,1,0:T(8,128)(2,1)S(1)} %collective-permute-done.9.near1), channel_id=1, source_target_pairs={{3,0},{2,1},{1,2},{0,3},{7,4},{6,5},{5,6},{4,7},{11,8},{10,9},{9,1... | collective-permute-start | bytes 688136 | tf_op jit(solution)/shard_map/ppermute | solution.py:37
  40.3 6.9 %collective-permute-start.21 = (bf16[2,4,112,128]{3,2,1,0:T(8,128)(2,1)S(1)}, bf16[2,4,112,128]{3,2,1,0:T(8,128)(2,1)S(1)}, u32[]{:S(2)}, u32[]{:S(2)}) collective-permute-start(bf16[2,4,112,128]{3,2,1,0:T(8,128)(2,1)S(1)} %collective-permute-done.9.near1), channel_id=1, source_target_pairs={{1,0},{0,1},{3,2},{2,3},{5,4},{4,5},{7,6},{6,7},{9,8},{8,9},{11,10... | collective-permute-start | bytes 688136 | tf_op jit(solution)/shard_map/ppermute | solution.py:37
  41.7 6.2 %collective-permute-start.11 = (bf16[2,4,112,128]{3,2,1,0:T(8,128)(2,1)S(1)}, bf16[2,4,112,128]{3,2,1,0:T(8,128)(2,1)S(1)}, u32[]{:S(2)}, u32[]{:S(2)}) collective-permute-start(bf16[2,4,112,128]{3,2,1,0:T(8,128)(2,1)S(1)} %collective-permute-done.10.near3), channel_id=1, source_target_pairs={{1,0},{0,1},{3,2},{2,3},{5,4},{4,5},{7,6},{6,7},{9,8},{8,9},{11,10... | collective-permute-start | bytes 688136 | tf_op jit(solution)/shard_map/ppermute | solution.py:37
  42.1 8.4 %collective-permute-start.18 = (bf16[2,4,112,128]{3,2,1,0:T(8,128)(2,1)S(1)}, bf16[2,4,112,128]{3,2,1,0:T(8,128)(2,1)S(1)}, u32[]{:S(2)}, u32[]{:S(2)}) collective-permute-start(bf16[2,4,112,128]{3,2,1,0:T(8,128)(2,1)S(1)} %collective-permute-done.10.near3), channel_id=1, source_target_pairs={{3,0},{2,1},{1,2},{0,3},{7,4},{6,5},{5,6},{4,7},{11,8},{10,9},{9,1... | collective-permute-start | bytes 688136 | tf_op jit(solution)/shard_map/ppermute | solution.py:37
  44.6 7.8 %collective-permute-start.13 = (bf16[2,4,112,128]{3,2,1,0:T(8,128)(2,1)S(1)}, bf16[2,4,112,128]{3,2,1,0:T(8,128)(2,1)S(1)}, u32[]{:S(2)}, u32[]{:S(2)}) collective-permute-start(bf16[2,4,112,128]{3,2,1,0:T(8,128)(2,1)S(1)} %collective-permute-done.12.far), channel_id=1, source_target_pairs={{1,0},{0,1},{3,2},{2,3},{5,4},{4,5},{7,6},{6,7},{9,8},{8,9},{11,10... | collective-permute-start | bytes 688136 | tf_op jit(solution)/shard_map/ppermute | solution.py:37
  44.8 10.6 %collective-permute-start.19 = (bf16[2,4,112,128]{3,2,1,0:T(8,128)(2,1)S(1)}, bf16[2,4,112,128]{3,2,1,0:T(8,128)(2,1)S(1)}, u32[]{:S(2)}, u32[]{:S(2)}) collective-permute-start(bf16[2,4,112,128]{3,2,1,0:T(8,128)(2,1)S(1)} %collective-permute-done.12.far), channel_id=1, source_target_pairs={{3,0},{2,1},{1,2},{0,3},{7,4},{6,5},{5,6},{4,7},{11,8},{10,9},{9,1... | collective-permute-start | bytes 688136 | tf_op jit(solution)/shard_map/ppermute | solution.py:37
  47.2 9.4 %collective-permute-start.17 = (bf16[2,4,112,128]{3,2,1,0:T(8,128)(2,1)S(1)}, bf16[2,4,112,128]{3,2,1,0:T(8,128)(2,1)S(1)}, u32[]{:S(2)}, u32[]{:S(2)}) collective-permute-start(bf16[2,4,112,128]{3,2,1,0:T(8,128)(2,1)S(1)} %collective-permute-done.16.near31), channel_id=1, source_target_pairs={{1,0},{0,1},{3,2},{2,3},{5,4},{4,5},{7,6},{6,7},{9,8},{8,9},{11,10... | collective-permute-start | bytes 688136 | tf_op jit(solution)/shard_map/ppermute | solution.py:37
  47.9 8.7 %collective-permute-start.15 = (bf16[2,4,112,128]{3,2,1,0:T(8,128)(2,1)S(1)}, bf16[2,4,112,128]{3,2,1,0:T(8,128)(2,1)S(1)}, u32[]{:S(2)}, u32[]{:S(2)}) collective-permute-start(bf16[2,4,112,128]{3,2,1,0:T(8,128)(2,1)S(1)} %collective-permute-done.14.own3), channel_id=1, source_target_pairs={{1,0},{0,1},{3,2},{2,3},{5,4},{4,5},{7,6},{6,7},{9,8},{8,9},{11,10... | collective-permute-start | bytes 688136 | tf_op jit(solution)/shard_map/ppermute | solution.py:37
  50.5 14.1 %collective-permute-start.22 = (bf16[2,4,112,128]{3,2,1,0:T(8,128)(2,1)S(1)}, bf16[2,4,112,128]{3,2,1,0:T(8,128)(2,1)S(1)}, u32[]{:S(2)}, u32[]{:S(2)}) collective-permute-start(bf16[2,4,112,128]{3,2,1,0:T(8,128)(2,1)S(1)} %collective-permute-done.11.near31), channel_id=1, source_target_pairs={{3,0},{2,1},{1,2},{0,3},{7,4},{6,5},{5,6},{4,7},{11,8},{10,9},{9,1... | collective-permute-start | bytes 688136 | tf_op jit(solution)/shard_map/ppermute | solution.py:37
  52.5 12.2 %collective-permute-start.23 = (bf16[2,4,112,128]{3,2,1,0:T(8,128)(2,1)S(1)}, bf16[2,4,112,128]{3,2,1,0:T(8,128)(2,1)S(1)}, u32[]{:S(2)}, u32[]{:S(2)}) collective-permute-start(bf16[2,4,112,128]{3,2,1,0:T(8,128)(2,1)S(1)} %collective-permute-done.13.far1), channel_id=1, source_target_pairs={{3,0},{2,1},{1,2},{0,3},{7,4},{6,5},{5,6},{4,7},{11,8},{10,9},{9,1... | collective-permute-start | bytes 688136 | tf_op jit(solution)/shard_map/ppermute | solution.py:37
  57.8 10.4 %collective-permute-start.24 = (bf16[512,384]{1,0:T(8,128)(2,1)S(1)}, bf16[512,384]{1,0:T(8,128)(2,1)S(1)}, u32[]{:S(2)}, u32[]{:S(2)}) collective-permute-start(bf16[512,384]{1,0:T(8,128)(2,1)S(1)} %get-tuple-element.38), channel_id=1, source_target_pairs={{16,0},{0,16},{17,1},{1,17},{18,2},{2,18},{19,3},{3,19},{20,4},{4,... | collective-permute-start | bytes 1179656 | tf_op jit(solution)/shard_map/ppermute | solution.py:24
  65.9 2.4 %collective-permute-start.25 = (bf16[512,384]{1,0:T(8,128)(2,1)S(1)}, bf16[512,384]{1,0:T(8,128)(2,1)S(1)}, u32[]{:S(2)}, u32[]{:S(2)}) collective-permute-start(bf16[512,384]{1,0:T(8,128)(2,1)S(1)} %shard_map.45), channel_id=1, source_target_pairs={{16,0},{0,16},{17,1},{1,17},{18,2},{2,18},{19,3},{3,19},{20,4},{4,... | collective-permute-start | bytes 1179656 | tf_op jit(solution)/shard_map/ppermute | solution.py:24
